TPU v7x, 32 devices: a whole 2x2x4 slice. The times are simulated.
32 devices in a mesh: dom: 4 (over x, core), ctx: 8 (over z, y).
Axes of the slice: x: 2, y: 2, z: 4, core: 2. Of those that a mesh axis runs over, the one named last changes fastest.
Arguments:
- q_new: bfloat16 [4096, 4096], P(('dom', 'ctx')), may hold values from -40 to 40
- kv_new: bfloat16 [4096, 2, 512], P(('dom', 'ctx')), may hold values from -5 to 5
- prompt_kv: bfloat16 [512, 2, 512], P('ctx'), may hold values from -5 to 5
- cache_kv: bfloat16 [32, 64, 2, 512], P('dom', 'ctx'), may hold values from -5 to 5
- ancestors: int32 [32], replicated, may hold values from 0 to 31, as said below
- lengths: int32 [32], replicated, may hold values from 1 to 8, as said below
Outputs:
- attended: bfloat16 [4096, 4096], P(('dom', 'ctx'))
Inputs may be any that keep to these rules, and one draw needn't show every extreme that they name: The 32 particles form 4 groups of 8 consecutive ones; within a group, each run of 4 consecutive particles takes all its ancestors from one group, and the runs of a group take them from different groups (its own among the possible ones). Ancestors repeat freely. `lengths`: both ends are reached.
All inputs are finite; a program needn't handle non-finite values.
Results may differ from a plain program's by a relative error of at most 0.022.
Values may be sent and summed in bfloat16 or wider, within the bound.
No kernel may reach another device: no remote copies, remote signals or barrier semaphores. Data moves between devices by JAX's collectives and lax.ppermute only.
A program may use at most 128 MiB of HBM per device.

v0:
```python
import jax
import jax.numpy as jnp
from jax import lax
from jax.sharding import PartitionSpec as P

HD = 128
H = 32
KVH = 4
SPAN = 128
PAGE = 8
GQ = 8


NEGATIVE = -1e30


def fresh_state(leading):
    return (
        jnp.full(leading, NEGATIVE, jnp.float32),
        jnp.zeros(leading, jnp.float32),
        jnp.zeros(leading + (HD,), jnp.float32),
    )


def absorb(running, queries, key_part, value_part, visible):
    maxima, totals, accumulated = running
    scores = jnp.einsum(
        "rgjd,kgd->rgjk", queries, key_part, preferred_element_type=jnp.float32
    ) * HD ** (-0.5)
    if visible is not None:
        scores = jnp.where(visible, scores, NEGATIVE)
    new_max = jnp.maximum(maxima, jnp.max(scores, axis=-1))
    weights = jnp.exp(scores - new_max[..., None])
    if visible is not None:
        weights = jnp.where(visible, weights, 0.0)
    factor = jnp.exp(maxima - new_max)
    totals = factor * totals + jnp.sum(weights, axis=-1)
    accumulated = factor[..., None] * accumulated + jnp.einsum(
        "rgjk,kgd->rgjd",
        weights.astype(jnp.bfloat16),
        value_part,
        preferred_element_type=jnp.float32,
    )
    return (new_max, totals, accumulated)


def absorb_blocks(running, queries, key_rows, value_rows, visible):
    query_count = queries.shape[0] * queries.shape[1] * queries.shape[2]
    key_block = max(128, 2**21 // query_count)
    length = key_rows.shape[0]
    for begin_at in range(0, length, key_block):
        end_at = min(begin_at + key_block, length)
        window = None if visible is None else visible
        running = absorb(
            running, queries, key_rows[begin_at:end_at], value_rows[begin_at:end_at], window
        )
    return running


def on_device(q_new, kv_new, prompt_kv, cache_kv, ancestors, lengths):
    dom_count = lax.axis_size("dom")
    ctx_count = lax.axis_size("ctx")
    dom_index = lax.axis_index("dom")
    ctx_index = lax.axis_index("ctx")
    group_size = cache_kv.shape[0]
    per_device = group_size // ctx_count
    capacity = 2 * group_size // dom_count
    page_rows = cache_kv.shape[1]
    kv_width = cache_kv.shape[3]
    source_group = (ancestors // group_size).reshape(dom_count, group_size)
    source_local = (ancestors % group_size).reshape(dom_count, group_size)
    from_here = (source_group == dom_index).astype(jnp.int32)
    ranking = jnp.cumsum(from_here, axis=1) - 1
    slot_ids = jnp.arange(capacity, dtype=jnp.int32)
    chosen = (from_here[:, :, None] == 1) & (ranking[:, :, None] == slot_ids[None, None, :])
    slot_local = jnp.sum(jnp.where(chosen, source_local[:, :, None], 0), axis=1)
    outgoing = cache_kv[slot_local.reshape(-1)].reshape(dom_count, capacity, page_rows, 2, kv_width)
    incoming = lax.all_to_all(outgoing, "dom", split_axis=0, concat_axis=0, tiled=True)
    own_source = lax.dynamic_index_in_dim(source_group, dom_index, 0, keepdims=False)
    group_ids = jnp.arange(dom_count, dtype=jnp.int32)
    matches = (own_source[:, None] == group_ids[None, :]).astype(jnp.int32)
    own_rank = jnp.sum(matches * (jnp.cumsum(matches, axis=0) - 1), axis=1)
    copied = incoming.reshape(dom_count * capacity, page_rows, 2, kv_width)[
        own_source * capacity + own_rank
    ]
    gathered_pages = lax.all_to_all(copied, "ctx", split_axis=0, concat_axis=1, tiled=True)
    particle_ids = (
        dom_index * group_size + ctx_index * per_device + jnp.arange(per_device, dtype=jnp.int32)
    )
    anchors = jnp.take(ancestors, particle_ids)
    page_limit = jnp.take(lengths, anchors) * PAGE
    row_count = per_device * SPAN
    queries = q_new.reshape(row_count, KVH, GQ, HD)
    fresh_kv = kv_new.reshape(per_device, SPAN, 2, KVH, HD)
    positions = jnp.arange(SPAN, dtype=jnp.int32)
    causal = (positions[None, :] <= positions[:, None])[:, None, None, :]
    gen_rows = gathered_pages.shape[1]
    cache_positions = jnp.arange(gen_rows, dtype=jnp.int32)
    running = fresh_state((SPAN, KVH, GQ))
    running = absorb_blocks(running, queries, fresh_kv[0, :, 0], fresh_kv[0, :, 1], causal)
    member_pages = gathered_pages[0].reshape(gen_rows, 2, KVH, HD)
    visible = (cache_positions < page_limit[0])[None, None, None, :]
    running = absorb_blocks(running, queries, member_pages[:, 0], member_pages[:, 1], visible)
    pieces = [running]
    local_state = tuple(
        (
            jnp.concatenate([member_state[number] for member_state in pieces], axis=0)
            for number in range(3)
        )
    )
    shard_rows = lax.all_gather(prompt_kv, "ctx", axis=0, tiled=True)
    shard_kv = shard_rows.reshape(shard_rows.shape[0], 2, KVH, HD)
    final_state = absorb_blocks(local_state, queries, shard_kv[:, 0], shard_kv[:, 1], None)
    output = (final_state[2] / final_state[1][..., None]).astype(jnp.bfloat16)
    return output.reshape(row_count, H * HD)


def solution(mesh):
    placed = (
        P(("dom", "ctx"), None),
        P(("dom", "ctx"), None, None),
        P("ctx", None, None),
        P("dom", "ctx", None, None),
        P(),
        P(),
    )
    return jax.shard_map(
        on_device, mesh=mesh, in_specs=placed, out_specs=P(("dom", "ctx"), None), check_vma=False
    )
```

profile of v0, /device:TPU:0, one launch (start us, length us, event | category | flops | bytes accessed | tf_op | source)
XLA Modules:
  0.0 72.7 jit_solution(3507986692822301191)
XLA Ops:
  6.5 0.0 copy-start
  6.5 0.0 all-gather.2.cloned.1.call-start
  6.5 0.7 all-gather.2.cloned.1.call-update
  7.3 0.7 and_select_fusion.1
  7.9 0.1 reshape.177
  8.0 0.2 reduce_window_sum.22
  8.2 0.1 broadcast_in_dim.92
  8.3 0.1 select_reduce_fusion
  8.4 0.1 reshape.178
  8.6 0.0 copy-done
  8.6 0.0 copy-start.8
  8.6 1.1 %gather_fusion = bf16[16,8,2,512]{3,2,1,0:T(2,128)(2,1)S(1)} fusion(bf16[8,8,2,512]{3,2,1,0:T(2,128)(2,1)S(1)} %copy-done, s32[1024]{0:T(1024)S(1)} %pad_clamp_fusion.1), kind=kCustom, calls=%fused_computation | custom fusion | bytes 524352 | tf_op jit(solution)/shard_map/gather | solution.py:77
  9.7 0.7 %copy.58 = bf16[4,4,8,2,512]{4,2,3,1,0:T(8,128)(2,1)} copy(bf16[4,4,8,2,512]{4,3,2,1,0:T(2,128)(2,1)S(1)} %bitcast.120) | data formatting | bytes 524288 | tf_op jit(solution)/shard_map/reshape | solution.py:77
  10.4 4.2 %all-to-all-start = ((bf16[4,4,8,2,512]{4,2,3,1,0:T(8,128)(2,1)}), bf16[4,4,8,2,512]{4,2,3,1,0:T(8,128)(2,1)S(1)}, u32[]{:S(2)}, u32[]{:S(2)}) async-start(bf16[4,4,8,2,512]{4,2,3,1,0:T(8,128)(2,1)} %copy.58), calls=%async_computation | async-start | bytes 524288 | tf_op jit(solution)/shard_map/all_to_all | solution.py:78
  14.6 1.2 %dynamic-slice.4 = s32[1]{0:T(128)} dynamic-slice(s32[32]{0:T(128)} %param.10, s32[]{:T(128)} %bitcast.6), dynamic_slice_sizes={1} | dynamic-slice | bytes 12 | tf_op jit(solution)/shard_map/jit(_take)/gather | solution.py:90
  16.4 0.2 reduce_window_sum.23
  16.6 1.1 %copy.55 = bf16[128,2,512]{0,2,1:T(8,128)(2,1)S(1)} copy(bf16[128,2,512]{2,1,0:T(2,128)(2,1)} %param.7) | data formatting | bytes 524288 | tf_op args[1]
  17.8 0.0 copy-done.2
  17.8 0.2 copy.81
  18.0 0.0 copy-done.8
  18.1 0.6 dynamic-slice.5
  19.3 0.0 copy-start.6
  19.3 1.3 %all-to-all-done = bf16[4,4,8,2,512]{4,2,3,1,0:T(8,128)(2,1)S(1)} async-done(((bf16[4,4,8,2,512]{4,2,3,1,0:T(8,128)(2,1)}), bf16[4,4,8,2,512]{4,2,3,1,0:T(8,128)(2,1)S(1)}, u32[]{:S(2)}, u32[]{:S(2)}) %all-to-all-start) | async-done | bytes 262176 | tf_op jit(solution)/shard_map/all_to_all | solution.py:78
  20.6 1.2 %gather_fusion.1 = bf16[8,8,2,512]{3,1,2,0:T(8,128)(2,1)} fusion(bf16[16,8,2,512]{3,1,2,0:T(8,128)(2,1)S(1)} %bitcast.125, s32[1024]{0:T(1024)S(1)} %pad_clamp_fusion), kind=kCustom, calls=%fused_computation.1 | custom fusion | bytes 262176 | tf_op jit(solution)/shard_map/gather | solution.py:83
  21.9 6.5 %all-to-all-start.1 = ((bf16[8,8,2,512]{3,1,2,0:T(8,128)(2,1)}), bf16[8,8,2,512]{3,1,2,0:T(8,128)(2,1)S(1)}, u32[]{:S(2)}, u32[]{:S(2)}) async-start(bf16[8,8,2,512]{3,1,2,0:T(8,128)(2,1)} %gather_fusion.1), calls=%async_computation.1 | async-start | bytes 262144 | tf_op jit(solution)/shard_map/all_to_all | solution.py:86
  28.3 2.6 %fusion.11 = (f32[128,4,8]{0,2,1:T(8,128)}, f32[4,128,128,8]{2,1,3,0:T(8,128)}) fusion(pred[128,128]{0,1:T(8,128)(4,1)S(1)} %iota_compare_fusion, bf16[128,4,8,128]{3,2,1,0:T(8,128)(2,1)S(1)} %bitcast.115, bf16[1,128,2,4,128]{1,4,3,2,0:T(8,128)(2,1)S(1)} %bitcast.123), kind=kOutput, calls=%fused_computation.19 | convolution fusion | flops 135786496 | bytes 3309568 | tf_op jit(solution)/shard_map/rgjd,kgd->rgjk/dot_general | solution.py:27
  30.9 4.8 %all-to-all-done.1 = bf16[8,8,2,512]{3,1,2,0:T(8,128)(2,1)S(1)} async-done(((bf16[8,8,2,512]{3,1,2,0:T(8,128)(2,1)}), bf16[8,8,2,512]{3,1,2,0:T(8,128)(2,1)S(1)}, u32[]{:S(2)}, u32[]{:S(2)}) %all-to-all-start.1) | async-done | bytes 131104 | tf_op jit(solution)/shard_map/all_to_all | solution.py:86
  35.7 0.7 fusion.47
  36.4 0.0 copy-done.6
  36.4 1.2 %fusion.48 = (f32[128,4,8]{0,2,1:T(8,128)}, f32[128,4,8,64]{0,3,2,1:T(8,128)S(1)}) fusion(bf16[128,4,8,128]{3,2,1,0:T(8,128)(2,1)S(1)} %bitcast.116, bf16[64,1,4,128]{3,2,0,1:T(4,128)(2,1)S(1)} %get-tuple-element.35, pred[64]{0:T(512)(128)(4,1)S(1)} %iota_compare_fusion.3), kind=kOutput, calls=%fused_computation.86 | convolution fusion | flops 67891200 | bytes 2179136 | tf_op jit(solution)/shard_map/rgjd,kgd->rgjk/dot_general | solution.py:27
  37.6 16.2 %all-gather.2.cloned.1.call-done = bf16[512,2,512]{2,1,0:T(2,128)(2,1)} async-done(((bf16[64,2,512]{2,1,0:T(2,128)(2,1)}), bf16[512,2,512]{2,1,0:T(2,128)(2,1)}) %all-gather.2.cloned.1.call-update) | async-done | bytes 1048592 | tf_op jit(solution)/shard_map/all_gather | solution.py:111
  53.8 2.4 %copy.62 = bf16[512,2,512]{0,2,1:T(8,128)(2,1)S(1)} copy(bf16[512,2,512]{2,1,0:T(2,128)(2,1)} %all-gather.2.cloned.1.call-done) | data formatting | bytes 2097152 | tf_op jit(solution)/shard_map/all_gather | solution.py:111
  56.2 0.0 copy-start.4
  56.2 0.0 copy-start.5
  56.2 1.4 %bitcast_reduce_fusion = (f32[128,4,8]{0,2,1:T(8,128)S(1)}, f32[4,512,128,8]{2,1,3,0:T(8,128)S(1)}) fusion(bf16[128,4,8,128]{3,2,1,0:T(8,128)(2,1)S(1)} %bitcast.117, bf16[512,2,4,128]{0,3,2,1:T(8,128)(2,1)S(1)} %bitcast.118), kind=kOutput, calls=%fused_computation.3 | convolution fusion | flops 541061120 | bytes 9977856 | tf_op jit(solution)/shard_map/rgjd,kgd->rgjk/dot_general | solution.py:27
  57.6 0.0 copy-done.4
  57.6 0.0 copy-done.5
  57.7 1.6 %fusion.1 = f32[128,4,8]{0,2,1:T(8,128)S(1)} fusion(f32[4,512,128,8]{2,1,3,0:T(8,128)S(1)} %get-tuple-element.41, f32[128,4,8]{0,2,1:T(8,128)S(1)} %get-tuple-element.30), kind=kLoop, calls=%fused_computation.5 | loop fusion | flops 6287360 | bytes 8421376 | tf_op jit(solution)/shard_map/reduce_sum | solution.py:37
  59.2 0.0 copy-start.7
  59.2 0.0 copy-start.3
  59.3 1.9 %fusion.3 = f32[4,128,8,128]{1,3,2,0:T(8,128)S(1)} fusion(f32[4,512,128,8]{2,1,3,0:T(8,128)S(1)} %get-tuple-element.41, f32[128,4,8]{0,2,1:T(8,128)S(1)} %get-tuple-element.30, bf16[512,2,4,128]{0,3,2,1:T(8,128)(2,1)S(1)} %bitcast.119), kind=kOutput, calls=%fused_computation.7 | convolution fusion | flops 543162368 | bytes 11026432 | tf_op jit(solution)/shard_map/rgjk,kgd->rgjd/dot_general | solution.py:38
  61.2 0.0 copy-done.7
  61.2 0.2 fusion.22
  61.4 0.5 fusion.29
  62.0 0.8 %copy-done.1 = f32[4,128,128,8]{2,1,3,0:T(8,128)S(1)} copy-done((f32[4,128,128,8]{2,1,3,0:T(8,128)S(1)}, f32[4,128,128,8]{2,1,3,0:T(8,128)}, u32[]{:S(2)}) %copy-start.1) | copy-done | bytes 2097176
  62.8 0.6 fusion.12
  63.4 1.1 %fusion.8 = bf16[128,4,8,128]{0,3,2,1:T(8,128)(2,1)S(1)} fusion(f32[4,128,8,128]{1,3,2,0:T(8,128)S(1)} %fusion.3, f32[4,128,128,8]{2,1,3,0:T(8,128)S(1)} %fusion.29, f32[4,128,128,8]{2,1,3,0:T(8,128)S(1)} %copy-done.1, f32[128,4,8]{0,2,1:T(8,128)S(1)} %get-tuple-element.27, f32[128,4,8]{0,2,1:T(8,128)S(1)} %get-tuple-element.37, ...), kind=kOutput, calls=%fused_computation.12 | convolution fusion | flops 140509184 | bytes 7569408 | tf_op jit(solution)/shard_map/rgjk,kgd->rgjd/dot_general | solution.py:38
  64.5 1.3 %copy.68 = bf16[128,4096]{1,0:T(8,128)(2,1)} copy(bf16[128,4096]{0,1:T(8,128)(2,1)S(1)} %bitcast.122) | data formatting | bytes 2097152 | tf_op jit(solution)/shard_map/reshape | solution.py:115
  (18 shorter events, 0.2 us)
Async XLA Ops:
  6.5 2.0 %copy-start = (bf16[8,8,2,512]{3,2,1,0:T(2,128)(2,1)S(1)}, bf16[8,8,2,512]{3,2,1,0:T(2,128)(2,1)}, u32[]{:S(2)}) copy-start(bf16[8,8,2,512]{3,2,1,0:T(2,128)(2,1)} %param.9) | copy-start | bytes 393220
  6.5 11.2 %copy-start.2 = (bf16[128,4096]{1,0:T(8,128)(2,1)S(1)}, bf16[128,4096]{1,0:T(8,128)(2,1)}, u32[]{:S(2)}) copy-start(bf16[128,4096]{1,0:T(8,128)(2,1)} %param.6) | copy-start | bytes 3145732
  6.5 47.2 %all-gather.2.cloned.1.call-start = ((), (), s32[]{:S(2)}) async-start(), calls=%async_computation.2 | async-start | bytes 1179648 | tf_op jit(solution)/shard_map/all_gather | solution.py:111
  8.6 9.5 %copy-start.8 = (s32[32]{0:T(128)S(1)}, s32[32]{0:T(128)}, u32[]{:S(2)}) copy-start(s32[32]{0:T(128)} %param.11) | copy-start | bytes 388
  10.4 10.2 %all-to-all-start = ((bf16[4,4,8,2,512]{4,2,3,1,0:T(8,128)(2,1)}), bf16[4,4,8,2,512]{4,2,3,1,0:T(8,128)(2,1)S(1)}, u32[]{:S(2)}, u32[]{:S(2)}) async-start(bf16[4,4,8,2,512]{4,2,3,1,0:T(8,128)(2,1)} %copy.58), calls=%async_computation | async-start | bytes 524288 | tf_op jit(solution)/shard_map/all_to_all | solution.py:78
  19.3 17.1 %copy-start.6 = (pred[64]{0:T(512)(128)(4,1)}, pred[64]{0:T(512)(128)(4,1)S(1)}, u32[]{:S(2)}) copy-start(pred[64]{0:T(512)(128)(4,1)S(1)} %iota_compare_fusion.3) | copy-start | bytes 196
  21.9 13.8 %all-to-all-start.1 = ((bf16[8,8,2,512]{3,1,2,0:T(8,128)(2,1)}), bf16[8,8,2,512]{3,1,2,0:T(8,128)(2,1)S(1)}, u32[]{:S(2)}, u32[]{:S(2)}) async-start(bf16[8,8,2,512]{3,1,2,0:T(8,128)(2,1)} %gather_fusion.1), calls=%async_computation.1 | async-start | bytes 262144 | tf_op jit(solution)/shard_map/all_to_all | solution.py:86
  56.2 1.4 %copy-start.4 = (f32[128,4,8]{0,2,1:T(8,128)S(1)}, f32[128,4,8]{0,2,1:T(8,128)}, u32[]{:S(2)}) copy-start(f32[128,4,8]{0,2,1:T(8,128)} %get-tuple-element.44) | copy-start | bytes 49156
  56.2 1.4 %copy-start.5 = (f32[128,4,8]{0,2,1:T(8,128)S(1)}, f32[128,4,8]{0,2,1:T(8,128)}, u32[]{:S(2)}) copy-start(f32[128,4,8]{0,2,1:T(8,128)} %get-tuple-element.42) | copy-start | bytes 49156
  59.2 1.9 %copy-start.7 = (pred[64]{0:T(512)(128)(4,1)S(1)}, pred[64]{0:T(512)(128)(4,1)}, u32[]{:S(2)}) copy-start(pred[64]{0:T(512)(128)(4,1)} %copy-done.6) | copy-start | bytes 196
  59.2 2.2 %copy-start.3 = (bf16[64,1,4,128]{3,2,0,1:T(4,128)(2,1)S(1)}, bf16[64,1,4,128]{3,2,0,1:T(4,128)(2,1)}, u32[]{:S(2)}) copy-start(bf16[64,1,4,128]{3,2,0,1:T(4,128)(2,1)} %get-tuple-element.34) | copy-start | bytes 196612
  61.2 1.6 %copy-start.1 = (f32[4,128,128,8]{2,1,3,0:T(8,128)S(1)}, f32[4,128,128,8]{2,1,3,0:T(8,128)}, u32[]{:S(2)}) copy-start(f32[4,128,128,8]{2,1,3,0:T(8,128)} %get-tuple-element.45) | copy-start | bytes 6291460
Sparse Core Ops, SparseCore 0:
  9.5 44.2 all-gather.1
where the time goes:
time: 73.1 us; the launch traced here: 72.7 us
  waiting for transfers between devices  23 us (31%)
  between operations  14.8 us (20%)
  local copies, waits for them, and re-layouts  11.8 us (16%)
  starting transfers between devices  10.7 us (15%)
  matrix products  8.71 us (12%)
  other arithmetic  3.68 us (5%)
    all_gather x1, waiting for transfers between devices, on_device(): shard_rows = lax.all_gather(prompt_kv, 'ctx', axis=0, tiled=True)  16.2 us
    all_to_all x1, starting transfers between devices, on_device(): lax.all_to_all(copied, 'ctx', split_axis=0, concat_axis=1, tiled=True)  6.45 us
    dot_general x3, matrix products, absorb(): jnp.einsum('rgjd,kgd->rgjk', queries, key_part, preferred_element_type=jn...  5.17 us
    all_to_all x1, waiting for transfers between devices, on_device(): lax.all_to_all(copied, 'ctx', split_axis=0, concat_axis=1, tiled=True)  4.76 us
    all_to_all x1, starting transfers between devices, on_device(): lax.all_to_all(outgoing, 'dom', split_axis=0, concat_axis=0, tiled=True)  4.21 us
    dot_general x3, matrix products, absorb(): jnp.einsum('rgjk,kgd->rgjd', weights.astype(jnp.bfloat16), value_part, pr...  3.54 us
    all_gather x1, local copies, waits for them, and re-layouts, on_device(): shard_rows = lax.all_gather(prompt_kv, 'ctx', axis=0, tiled=True)  2.44 us
    reduce_sum x3, other arithmetic, absorb(): totals = factor * totals + jnp.sum(weights, axis=-1)  2.36 us
  transfers between devices with their start and end apart: 3, of which 3 were waited for; matrix products, arithmetic and copies ran while one was open for 17% of the time, Pallas kernels for 0%

commit v1 on v0

v1 whole, which is shorter than its diff:
```python
import functools

import jax
import jax.numpy as jnp
from jax import lax
from jax.experimental import pallas as pl
from jax.experimental.pallas import tpu as pltpu
from jax.sharding import PartitionSpec as P

HD = 128
SPAN = 128
PAGE = 8
RUN = 4
Z = 4
NEGATIVE = -1e30
SCALE2 = HD ** (-0.5) * 1.4426950408889634
VMEM = pl.BlockSpec(memory_space=pltpu.VMEM)
SMEM = pl.BlockSpec(memory_space=pltpu.SMEM)


def params():
    return pltpu.CompilerParams(vmem_limit_bytes=40 * 2**20)


def pack_kernel(dom_count, anc_ref, prompt_ref, cache_ref, half_ref, out_ref):
    group = cache_ref.shape[0]
    dom = lax.axis_index("dom")
    rows, width = half_ref.shape
    half_ref[...] = prompt_ref[pl.ds(pl.multiple_of((dom % 2) * rows, rows), rows)].reshape(rows, width)
    runs = group // RUN

    def one(step, carry):
        first = step * RUN
        anchor = anc_ref[first]

        @pl.when(anchor // group == dom)
        def _():
            for slot in range(RUN):
                local = anc_ref[first + slot] % group
                out_ref[step // runs, slot] = cache_ref[local].reshape(cache_ref.shape[1], width)

        return carry

    lax.fori_loop(0, dom_count * runs, one, 0)


def route_kernel(anc_ref, in_ref, out_ref):
    group = out_ref.shape[0]
    dom = lax.axis_index("dom")
    for run in range(group // RUN):
        source = anc_ref[dom * group + run * RUN] // group
        out_ref[pl.ds(run * RUN, RUN)] = in_ref[source]


def head_rows(q_ref, g, gq):
    return jnp.concatenate(
        [q_ref[:, (g * gq + j) * HD : (g * gq + j + 1) * HD] for j in range(gq)], axis=0
    )


def dot_nt(a, b):
    return lax.dot_general(a, b, (((1,), (1,)), ((), ())), preferred_element_type=jnp.float32)


def dot_nn(a, b):
    return lax.dot_general(a, b, (((1,), (0,)), ((), ())), preferred_element_type=jnp.float32)


def main_kernel(q_ref, new_ref, *refs):
    *pieces, acc_ref, max_ref, sum_ref = refs
    width = new_ref.shape[2]
    kvh = width // HD
    gq = q_ref.shape[1] // width
    new = new_ref[...].reshape(SPAN, 2 * width)
    ones = jnp.ones((SPAN + sum(p.shape[0] for p in pieces), HD), jnp.bfloat16)
    token = lax.broadcasted_iota(jnp.int32, (SPAN, SPAN), 0)
    key = lax.broadcasted_iota(jnp.int32, (SPAN, SPAN), 1)
    causal = key <= token
    for g in range(kvh):
        k_at = slice(g * HD, (g + 1) * HD)
        v_at = slice(width + g * HD, width + (g + 1) * HD)
        keys = jnp.concatenate([new[:, k_at]] + [p[:, k_at] for p in pieces], axis=0)
        values = jnp.concatenate([new[:, v_at]] + [p[:, v_at] for p in pieces], axis=0)
        values = jnp.concatenate([values, ones], axis=1)
        scores = dot_nt(head_rows(q_ref, g, gq), keys)
        weights, tops = [], []
        for j in range(gq):
            s = scores[j * SPAN : (j + 1) * SPAN]
            s_new = jnp.where(causal, s[:, :SPAN], NEGATIVE)
            s_old = s[:, SPAN:]
            top = s_new
            for at in range(0, s_old.shape[1], HD):
                top = jnp.maximum(top, s_old[:, at : at + HD])
            top = jnp.max(top, axis=1, keepdims=True)
            s = jnp.concatenate([s_new, s_old], axis=1)
            weights.append(jnp.exp2((s - top) * SCALE2).astype(jnp.bfloat16))
            tops.append(top)
        out = dot_nn(jnp.concatenate(weights, axis=0), values)
        for j in range(gq):
            at = slice((g * gq + j) * HD, (g * gq + j + 1) * HD)
            rows = slice(j * SPAN, (j + 1) * SPAN)
            acc_ref[:, at] = out[rows, :HD]
            sum_ref[:, at] = out[rows, HD:]
            max_ref[:, at] = jnp.broadcast_to(tops[j], (SPAN, HD))


def merge_kernel(particle_group, anc_ref, len_ref, q_ref, cache_ref, acc_ref, max_ref, sum_ref, out_ref, stage, sems):
    width = cache_ref.shape[1] // 2
    gen = cache_ref.shape[0]
    kvh = width // HD
    gq = q_ref.shape[1] // width
    particle = lax.axis_index("dom") * particle_group + lax.axis_index("ctx")
    limit = len_ref[anc_ref[particle]] * PAGE
    visible = lax.broadcasted_iota(jnp.int32, (SPAN, gen), 1) < limit
    ones = jnp.ones((gen, HD), jnp.bfloat16)
    copies = []
    for g in range(kvh):
        keys = cache_ref[:, g * HD : (g + 1) * HD]
        values = jnp.concatenate([cache_ref[:, width + g * HD : width + (g + 1) * HD], ones], axis=1)
        scores = dot_nt(head_rows(q_ref, g, gq), keys)
        weights, factors = [], []
        for j in range(gq):
            at = slice((g * gq + j) * HD, (g * gq + j + 1) * HD)
            s = jnp.where(visible, scores[j * SPAN : (j + 1) * SPAN], NEGATIVE)
            before = max_ref[:, at]
            top = jnp.maximum(before, jnp.max(s, axis=1, keepdims=True))
            wide = top[:, :gen] if gen <= HD else jnp.concatenate([top] * (gen // HD), axis=1)
            weights.append(jnp.exp2((s - wide) * SCALE2).astype(jnp.bfloat16))
            factors.append(jnp.exp2((before - top) * SCALE2))
        out = dot_nn(jnp.concatenate(weights, axis=0), values)
        for j in range(gq):
            at = slice((g * gq + j) * HD, (g * gq + j + 1) * HD)
            rows = slice(j * SPAN, (j + 1) * SPAN)
            total = sum_ref[:, at] * factors[j] + out[rows, HD:]
            value = acc_ref[:, at] * factors[j] + out[rows, :HD]
            stage[:, at] = (value / total).astype(jnp.bfloat16)
        columns = pl.ds(g * gq * HD, gq * HD)
        copy = pltpu.make_async_copy(stage.at[:, columns], out_ref.at[:, columns], sems.at[g])
        copy.start()
        copies.append(copy)
    for copy in copies:
        copy.wait()


def swap(x, axis, partner):
    return lax.ppermute(x, axis, [(i, partner(i)) for i in range(lax.axis_size(axis))])


def on_device(q_new, kv_new, prompt_kv, cache_kv, ancestors, lengths):
    dom_count = lax.axis_size("dom")
    ctx_count = lax.axis_size("ctx")
    group, page_rows, _, width = cache_kv.shape
    y_count = ctx_count // Z
    tokens, q_width = q_new.shape
    kvh = width // HD
    shape = jax.ShapeDtypeStruct
    half, outgoing = pl.pallas_call(
        functools.partial(pack_kernel, dom_count),
        out_shape=(
            shape((prompt_kv.shape[0] // 2, 2 * width), jnp.bfloat16),
            shape((dom_count, RUN, page_rows, 2 * width), jnp.bfloat16),
        ),
        in_specs=[SMEM, VMEM, VMEM],
        out_specs=(VMEM, VMEM),
        compiler_params=params(),
        name="pack",
    )(ancestors, prompt_kv, cache_kv)

    pieces = [half] + [swap(half, "ctx", lambda i, k=k: i ^ (k * y_count)) for k in range(1, Z)]
    pieces += [swap(p, "ctx", lambda i, k=k: i ^ k) for k in range(1, y_count) for p in pieces[:Z]]
    pieces += [swap(p, "dom", lambda i: i ^ 1) for p in pieces]

    incoming = lax.all_to_all(outgoing, "dom", split_axis=0, concat_axis=0, tiled=True)
    routed = pl.pallas_call(
        route_kernel,
        out_shape=shape((group, page_rows, 2 * width), jnp.bfloat16),
        in_specs=[SMEM, VMEM],
        out_specs=VMEM,
        compiler_params=params(),
        name="route",
    )(ancestors, incoming)
    pages = lax.all_to_all(routed, "ctx", split_axis=0, concat_axis=0, tiled=True)
    pages = pages.reshape(ctx_count * page_rows, 2 * width)

    key_count = SPAN + sum(p.shape[0] for p in pieces)
    flops = 4 * tokens * q_width * key_count
    acc, top, total = pl.pallas_call(
        main_kernel,
        out_shape=(shape((tokens, q_width), jnp.float32),) * 3,
        in_specs=[VMEM] * (2 + len(pieces)),
        out_specs=(VMEM,) * 3,
        compiler_params=params(),
        cost_estimate=pl.CostEstimate(
            flops=flops, bytes_accessed=2**23, transcendentals=tokens * q_width // HD * key_count
        ),
        name="prompt_and_new",
    )(q_new, kv_new, *pieces)
    return pl.pallas_call(
        functools.partial(merge_kernel, group),
        out_shape=shape((tokens, q_width), jnp.bfloat16),
        in_specs=[SMEM, SMEM] + [VMEM] * 5,
        out_specs=pl.BlockSpec(memory_space=pl.ANY),
        scratch_shapes=[pltpu.VMEM((tokens, q_width), jnp.bfloat16), pltpu.SemaphoreType.DMA((kvh,))],
        compiler_params=params(),
        name="cache_and_merge",
    )(ancestors, lengths, q_new, pages, acc, top, total)


def solution(mesh):
    placed = (
        P(("dom", "ctx"), None),
        P(("dom", "ctx"), None, None),
        P("ctx", None, None),
        P("dom", "ctx", None, None),
        P(),
        P(),
    )
    return jax.shard_map(
        on_device, mesh=mesh, in_specs=placed, out_specs=P(("dom", "ctx"), None), check_vma=False
    )
```

time: 73.1 us -> 54.6 us (0.75)
  waiting for transfers between devices: 23 us -> 5.24 us
  between operations: 14.8 us -> 0.12 us
  Pallas kernels: 0 us -> 9.96 us
  matrix products: 8.71 us -> 0 us
  local copies, waits for them, and re-layouts: 11.8 us -> 20.1 us
  starting transfers between devices: 10.7 us -> 18.4 us
  other arithmetic: 3.68 us -> 0 us
    unnamed x20 -> x54, local copies, waits for them, and re-layouts: 2.25 us -> 20.1 us
    all_gather x1 -> x0, waiting for transfers between devices: 16.2 us -> none  [on_device(): shard_rows = lax.all_gather(prompt_kv, 'ctx', axis=0, tiled=True)]
    ppermute x0 -> x15, starting transfers between devices: none -> 10.2 us  [swap(): lax.ppermute(x, axis, [(i, partner(i)) for i in range(lax.axis_size(axis))])]
    pallas_call x0 -> x4, Pallas kernels: none -> 9.96 us  [the longest x1 4.09 us: on_device(): pl.pallas_call(main_kernel, out_shape=(shape((tokens, q_width), jnp.float...]
    dot_general x6 -> x0, matrix products: 8.71 us -> none  [the longest x3 5.17 us: absorb(): jnp.einsum('rgjd,kgd->rgjk', queries, key_part, preferred_element_type=jn...]
    ppermute x0 -> x15, waiting for transfers between devices: none -> 5.23 us  [swap(): lax.ppermute(x, axis, [(i, partner(i)) for i in range(lax.axis_size(axis))])]
    all_to_all x1, waiting for transfers between devices: 4.76 us -> 0.01 us  [on_device(): lax.all_to_all(routed, 'ctx', split_axis=0, concat_axis=0, tiled=True)]
    gather x4 -> x0, local copies, waits for them, and re-layouts: 4.09 us -> none  [the longest x1 1.23 us: on_device(): anchors = jnp.take(ancestors, particle_ids)]
  transfers between devices with their start and end apart: 3 -> 17, of which waited for: 3 -> 3; matrix products, arithmetic and copies ran while one was open for 17% -> 0% of each run, Pallas kernels for 0% -> 10%
where the time goes in v1:
time: 54.6 us; the launch traced here: 53.8 us
  local copies, waits for them, and re-layouts  20.1 us (37%)
  starting transfers between devices  18.4 us (34%)
  Pallas kernels  9.96 us (18%)
  waiting for transfers between devices  5.24 us (10%)
    unnamed x54, local copies, waits for them, and re-layouts  20.1 us
    ppermute x15, starting transfers between devices, swap(): lax.ppermute(x, axis, [(i, partner(i)) for i in range(lax.axis_size(axis))])  10.2 us
    ppermute x15, waiting for transfers between devices, swap(): lax.ppermute(x, axis, [(i, partner(i)) for i in range(lax.axis_size(axis))])  5.23 us
    all_to_all x1, starting transfers between devices, on_device(): lax.all_to_all(outgoing, 'dom', split_axis=0, concat_axis=0, tiled=True)  4.24 us
    pallas_call x1, Pallas kernels, on_device(): pl.pallas_call(main_kernel, out_shape=(shape((tokens, q_width), jnp.float...  4.09 us
    all_to_all x1, starting transfers between devices, on_device(): lax.all_to_all(routed, 'ctx', split_axis=0, concat_axis=0, tiled=True)  3.96 us
    pallas_call x1, Pallas kernels, on_device(): pl.pallas_call(functools.partial(merge_kernel, group), out_shape=shape((t...  3.17 us
    pallas_call x1, Pallas kernels, on_device(): pl.pallas_call(functools.partial(pack_kernel, dom_count), out_shape=(shap...  1.47 us
  transfers between devices with their start and end apart: 17, of which 3 were waited for; matrix products, arithmetic and copies ran while one was open for 0% of the time, Pallas kernels for 10%

profile of v1, /device:TPU:0, one launch (start us, length us, event | category | flops | bytes accessed | tf_op | source)
XLA Modules:
  0.0 53.8 jit_solution(13121520549427549335)
XLA Ops:
  0.0 0.9 %copy-done.6 = bf16[64,2,512]{2,1,0:T(2,128)(2,1)S(1)} copy-done((bf16[64,2,512]{2,1,0:T(2,128)(2,1)S(1)}, bf16[64,2,512]{2,1,0:T(2,128)(2,1)}, u32[]{:S(2)}) %copy-start.6) | copy-done | bytes 131096
  0.9 0.9 %copy-done.7 = bf16[8,8,2,512]{3,2,1,0:T(2,128)(2,1)S(1)} copy-done((bf16[8,8,2,512]{3,2,1,0:T(2,128)(2,1)S(1)}, bf16[8,8,2,512]{3,2,1,0:T(2,128)(2,1)}, u32[]{:S(2)}) %copy-start.7) | copy-done | bytes 131096
  1.8 0.7 %copy-done.8 = s32[32]{0:T(128)S(1)} copy-done((s32[32]{0:T(128)S(1)}, s32[32]{0:T(128)}, u32[]{:S(2)}) %copy-start.8) | copy-done | bytes 152
  2.5 1.5 %pack.1 = (bf16[32,1024]{1,0:T(8,128)(2,1)S(1)}, bf16[4,4,8,1024]{3,2,1,0:T(8,128)(2,1)}) custom-call(s32[32]{0:T(128)S(1)} %copy-done.8, bf16[64,2,512]{2,1,0:T(2,128)(2,1)S(1)} %copy-done.6, bf16[8,8,2,512]{3,2,1,0:T(2,128)(2,1)S(1)} %copy-done.7), custom_call_target="tpu_custom_call" | custom-call | tf_op jit(solution)/shard_map/pack/pallas_call | solution.py:157
  3.9 4.2 %all-to-all-start = ((bf16[4,4,8,1024]{3,2,1,0:T(8,128)(2,1)}), bf16[4,4,8,1024]{3,2,1,0:T(8,128)(2,1)S(1)}, u32[]{:S(2)}, u32[]{:S(2)}) async-start(bf16[4,4,8,1024]{3,2,1,0:T(8,128)(2,1)} %get-tuple-element.10), calls=%async_computation | async-start | bytes 524288 | tf_op jit(solution)/shard_map/all_to_all | solution.py:173
  8.2 2.2 %collective-permute-start.3 = (bf16[32,1024]{1,0:T(8,128)(2,1)S(1)}, bf16[32,1024]{1,0:T(8,128)(2,1)S(1)}, u32[]{:S(2)}, u32[]{:S(2)}) collective-permute-start(bf16[32,1024]{1,0:T(8,128)(2,1)S(1)} %get-tuple-element.11.refs_0_), channel_id=1, source_target_pairs={{0,1},{1,0},{2,3},{3,2},{4,5},{5,4},{6,7},{7,6},{8,9},{9,8},{10,11... | collective-permute-start | bytes 196616 | tf_op jit(solution)/shard_map/ppermute | solution.py:146
  10.4 3.6 %collective-permute-start.2 = (bf16[32,1024]{1,0:T(8,128)(2,1)S(1)}, bf16[32,1024]{1,0:T(8,128)(2,1)S(1)}, u32[]{:S(2)}, u32[]{:S(2)}) collective-permute-start(bf16[32,1024]{1,0:T(8,128)(2,1)S(1)} %get-tuple-element.11.refs_0_), channel_id=1, source_target_pairs={{0,6},{1,7},{2,4},{3,5},{4,2},{5,3},{6,0},{7,1},{8,14},{9,15},{10,... | collective-permute-start | bytes 196616 | tf_op jit(solution)/shard_map/ppermute | solution.py:146
  14.0 0.0 collective-permute-start.7
  14.0 0.0 collective-permute-start.1
  14.0 0.8 %collective-permute-start = (bf16[32,1024]{1,0:T(8,128)(2,1)S(1)}, bf16[32,1024]{1,0:T(8,128)(2,1)S(1)}, u32[]{:S(2)}, u32[]{:S(2)}) collective-permute-start(bf16[32,1024]{1,0:T(8,128)(2,1)S(1)} %get-tuple-element.11.refs_0_), channel_id=1, source_target_pairs={{0,2},{1,3},{2,0},{3,1},{4,6},{5,7},{6,4},{7,5},{8,10},{9,11},{10,... | collective-permute-start | bytes 196616 | tf_op jit(solution)/shard_map/ppermute | solution.py:146
  14.8 0.0 collective-permute-done.3.refs_4_
  14.8 0.0 collective-permute-start.11
  14.8 1.7 %collective-permute-done.2.refs_3_ = bf16[32,1024]{1,0:T(8,128)(2,1)S(1)} collective-permute-done((bf16[32,1024]{1,0:T(8,128)(2,1)S(1)}, bf16[32,1024]{1,0:T(8,128)(2,1)S(1)}, u32[]{:S(2)}, u32[]{:S(2)}) %collective-permute-start.2) | collective-permute-done | bytes 65568 | tf_op jit(solution)/shard_map/ppermute | solution.py:146
  16.5 0.0 collective-permute-start.10
  16.5 0.0 collective-permute-done.7.refs_8_
  16.5 0.5 collective-permute-start.6
  17.0 2.9 %collective-permute-done.1.refs_2_ = bf16[32,1024]{1,0:T(8,128)(2,1)S(1)} collective-permute-done((bf16[32,1024]{1,0:T(8,128)(2,1)S(1)}, bf16[32,1024]{1,0:T(8,128)(2,1)S(1)}, u32[]{:S(2)}, u32[]{:S(2)}) %collective-permute-start.1) | collective-permute-done | bytes 65568 | tf_op jit(solution)/shard_map/ppermute | solution.py:146
  19.9 0.5 collective-permute-start.5
  20.4 0.0 collective-permute-done.refs_1_
  20.4 1.5 %collective-permute-start.4 = (bf16[32,1024]{1,0:T(8,128)(2,1)S(1)}, bf16[32,1024]{1,0:T(8,128)(2,1)S(1)}, u32[]{:S(2)}, u32[]{:S(2)}) collective-permute-start(bf16[32,1024]{1,0:T(8,128)(2,1)S(1)} %collective-permute-done.refs_1_), channel_id=1, source_target_pairs={{0,1},{1,0},{2,3},{3,2},{4,5},{5,4},{6,7},{7,6},{8,9},{9,8},{10,11... | collective-permute-start | bytes 196616 | tf_op jit(solution)/shard_map/ppermute | solution.py:146
  21.9 0.7 %copy-done.9 = s32[32]{0:T(128)S(1)} copy-done((s32[32]{0:T(128)S(1)}, s32[32]{0:T(128)}, u32[]{:S(2)}) %copy-start.9) | copy-done | bytes 152
  22.6 1.2 %route.1 = bf16[8,8,1024]{2,1,0:T(8,128)(2,1)} custom-call(s32[32]{0:T(128)S(1)} %copy-done.9, bf16[4,4,8,1024]{3,2,1,0:T(8,128)(2,1)S(1)} %all-to-all-done.in_ref), custom_call_target="tpu_custom_call" | custom-call | tf_op jit(solution)/shard_map/route/pallas_call | solution.py:174
  23.8 4.0 %all-to-all-start.1 = ((bf16[8,8,1024]{2,1,0:T(8,128)(2,1)}), bf16[8,8,1024]{2,1,0:T(8,128)(2,1)S(1)}, u32[]{:S(2)}, u32[]{:S(2)}) async-start(bf16[8,8,1024]{2,1,0:T(8,128)(2,1)} %route.1), calls=%async_computation.1 | async-start | bytes 262144 | tf_op jit(solution)/shard_map/all_to_all | solution.py:182
  27.8 0.6 %copy-done.17 = bf16[32,1024]{1,0:T(8,128)(2,1)} copy-done((bf16[32,1024]{1,0:T(8,128)(2,1)}, bf16[32,1024]{1,0:T(8,128)(2,1)S(1)}, u32[]{:S(2)}) %copy-start.17) | copy-done | bytes 65560
  28.4 0.6 %copy-done.19 = bf16[32,1024]{1,0:T(8,128)(2,1)} copy-done((bf16[32,1024]{1,0:T(8,128)(2,1)}, bf16[32,1024]{1,0:T(8,128)(2,1)S(1)}, u32[]{:S(2)}) %copy-start.19) | copy-done | bytes 65560
  29.0 0.5 collective-permute-start.8
  29.6 0.0 collective-permute-start.14
  29.6 0.6 %copy-done.21 = bf16[32,1024]{1,0:T(8,128)(2,1)} copy-done((bf16[32,1024]{1,0:T(8,128)(2,1)}, bf16[32,1024]{1,0:T(8,128)(2,1)S(1)}, u32[]{:S(2)}) %copy-start.21) | copy-done | bytes 65560
  30.2 0.5 collective-permute-start.13
  30.7 0.6 %copy-done.23 = bf16[32,1024]{1,0:T(8,128)(2,1)} copy-done((bf16[32,1024]{1,0:T(8,128)(2,1)}, bf16[32,1024]{1,0:T(8,128)(2,1)S(1)}, u32[]{:S(2)}) %copy-start.23) | copy-done | bytes 65560
  31.3 0.0 collective-permute-start.12
  31.3 0.6 %copy-done.25 = bf16[32,1024]{1,0:T(8,128)(2,1)} copy-done((bf16[32,1024]{1,0:T(8,128)(2,1)}, bf16[32,1024]{1,0:T(8,128)(2,1)S(1)}, u32[]{:S(2)}) %copy-start.25) | copy-done | bytes 65560
  32.0 0.6 %collective-permute-done.12.refs_13_ = bf16[32,1024]{1,0:T(8,128)(2,1)S(1)} collective-permute-done((bf16[32,1024]{1,0:T(8,128)(2,1)S(1)}, bf16[32,1024]{1,0:T(8,128)(2,1)S(1)}, u32[]{:S(2)}, u32[]{:S(2)}) %collective-permute-start.12) | collective-permute-done | bytes 65568 | tf_op jit(solution)/shard_map/ppermute | solution.py:146
  32.6 1.2 %copy-done.4 = bf16[128,4096]{1,0:T(8,128)(2,1)S(1)} copy-done((bf16[128,4096]{1,0:T(8,128)(2,1)S(1)}, bf16[128,4096]{1,0:T(8,128)(2,1)}, u32[]{:S(2)}) %copy-start.4) | copy-done | bytes 1048600
  33.8 0.9 %copy-done.12 = bf16[128,2,512]{2,1,0:T(2,128)(2,1)S(1)} copy-done((bf16[128,2,512]{2,1,0:T(2,128)(2,1)S(1)}, bf16[128,2,512]{2,1,0:T(2,128)(2,1)}, u32[]{:S(2)}) %copy-start.12) | copy-done | bytes 262168
  34.8 0.8 %copy-done.14 = bf16[32,1024]{1,0:T(8,128)(2,1)S(1)} copy-done((bf16[32,1024]{1,0:T(8,128)(2,1)S(1)}, bf16[32,1024]{1,0:T(8,128)(2,1)}, u32[]{:S(2)}) %copy-start.14) | copy-done | bytes 65560
  35.6 0.8 %copy-done.16 = bf16[32,1024]{1,0:T(8,128)(2,1)S(1)} copy-done((bf16[32,1024]{1,0:T(8,128)(2,1)S(1)}, bf16[32,1024]{1,0:T(8,128)(2,1)}, u32[]{:S(2)}) %copy-start.16) | copy-done | bytes 65560
  36.4 0.8 %copy-done.18 = bf16[32,1024]{1,0:T(8,128)(2,1)S(1)} copy-done((bf16[32,1024]{1,0:T(8,128)(2,1)S(1)}, bf16[32,1024]{1,0:T(8,128)(2,1)}, u32[]{:S(2)}) %copy-start.18) | copy-done | bytes 65560
  37.3 0.8 %copy-done.20 = bf16[32,1024]{1,0:T(8,128)(2,1)S(1)} copy-done((bf16[32,1024]{1,0:T(8,128)(2,1)S(1)}, bf16[32,1024]{1,0:T(8,128)(2,1)}, u32[]{:S(2)}) %copy-start.20) | copy-done | bytes 65560
  38.1 0.8 %copy-done.22 = bf16[32,1024]{1,0:T(8,128)(2,1)S(1)} copy-done((bf16[32,1024]{1,0:T(8,128)(2,1)S(1)}, bf16[32,1024]{1,0:T(8,128)(2,1)}, u32[]{:S(2)}) %copy-start.22) | copy-done | bytes 65560
  39.0 0.8 %copy-done.24 = bf16[32,1024]{1,0:T(8,128)(2,1)S(1)} copy-done((bf16[32,1024]{1,0:T(8,128)(2,1)S(1)}, bf16[32,1024]{1,0:T(8,128)(2,1)}, u32[]{:S(2)}) %copy-start.24) | copy-done | bytes 65560
  39.8 0.8 %copy-done.26 = bf16[32,1024]{1,0:T(8,128)(2,1)S(1)} copy-done((bf16[32,1024]{1,0:T(8,128)(2,1)S(1)}, bf16[32,1024]{1,0:T(8,128)(2,1)}, u32[]{:S(2)}) %copy-start.26) | copy-done | bytes 65560
  40.6 4.1 %prompt_and_new.1 = (f32[128,4096]{1,0:T(8,128)S(1)}, f32[128,4096]{1,0:T(8,128)S(1)}, f32[128,4096]{1,0:T(8,128)S(1)}) custom-call(bf16[128,4096]{1,0:T(8,128)(2,1)S(1)} %copy-done.4, bf16[128,2,512]{2,1,0:T(2,128)(2,1)S(1)} %copy-done.12, bf16[32,1024]{1,0:T(8,128)(2,1)S(1)} %get-tuple-element.11.refs_0_, bf16[32,1024]{1,0:T(8,128)(2,1)S(1)} %copy-done.16, ...), custom_call_target="tpu_custom_call" | custom-call | flops 1342177280 | bytes 8388608 | tf_op jit(solution)/shard_map/prompt_and_new/pallas_call | solution.py:187
  44.7 1.3 %copy-done = f32[128,4096]{1,0:T(8,128)} copy-done((f32[128,4096]{1,0:T(8,128)}, f32[128,4096]{1,0:T(8,128)S(1)}, u32[]{:S(2)}) %copy-start) | copy-done | bytes 2097176
  46.1 1.3 %copy-done.2 = f32[128,4096]{1,0:T(8,128)} copy-done((f32[128,4096]{1,0:T(8,128)}, f32[128,4096]{1,0:T(8,128)S(1)}, u32[]{:S(2)}) %copy-start.2) | copy-done | bytes 2097176
  47.5 1.6 %copy-done.1 = f32[128,4096]{1,0:T(8,128)S(1)} copy-done((f32[128,4096]{1,0:T(8,128)S(1)}, f32[128,4096]{1,0:T(8,128)}, u32[]{:S(2)}) %copy-start.1) | copy-done | bytes 2097176
  49.0 1.6 %copy-done.3 = f32[128,4096]{1,0:T(8,128)S(1)} copy-done((f32[128,4096]{1,0:T(8,128)S(1)}, f32[128,4096]{1,0:T(8,128)}, u32[]{:S(2)}) %copy-start.3) | copy-done | bytes 2097176
  50.6 3.2 %cache_and_merge.1 = bf16[128,4096]{1,0:T(8,128)(2,1)} custom-call(s32[32]{0:T(128)S(1)} %copy-done.10, s32[32]{0:T(128)S(1)} %copy-done.11, bf16[128,4096]{1,0:T(8,128)(2,1)S(1)} %copy-done.5, bf16[64,1024]{1,0:T(8,128)(2,1)S(1)} %bitcast.1, f32[128,4096]{1,0:T(8,128)S(1)} %get-tuple-element.12.acc_ref, f32[128,4096]{1,0:T(8,128)S(1)} %copy-done.1, ...), custom_call_target="tpu_custom_call" | custom-call | tf_op jit(solution)/shard_map/cache_and_merge/pallas_call | solution.py:198
  (44 shorter events, 0.1 us)
Async XLA Ops:
  0.0 0.9 %copy-start.6 = (bf16[64,2,512]{2,1,0:T(2,128)(2,1)S(1)}, bf16[64,2,512]{2,1,0:T(2,128)(2,1)}, u32[]{:S(2)}) copy-start(bf16[64,2,512]{2,1,0:T(2,128)(2,1)} %prompt_ref.1) | copy-start | bytes 393220
  0.9 0.9 %copy-start.7 = (bf16[8,8,2,512]{3,2,1,0:T(2,128)(2,1)S(1)}, bf16[8,8,2,512]{3,2,1,0:T(2,128)(2,1)}, u32[]{:S(2)}) copy-start(bf16[8,8,2,512]{3,2,1,0:T(2,128)(2,1)} %cache_ref.1) | copy-start | bytes 393220
  1.8 0.7 %copy-start.8 = (s32[32]{0:T(128)S(1)}, s32[32]{0:T(128)}, u32[]{:S(2)}) copy-start(s32[32]{0:T(128)} %anc_ref.5) | copy-start | bytes 388
  3.9 18.0 %all-to-all-start = ((bf16[4,4,8,1024]{3,2,1,0:T(8,128)(2,1)}), bf16[4,4,8,1024]{3,2,1,0:T(8,128)(2,1)S(1)}, u32[]{:S(2)}, u32[]{:S(2)}) async-start(bf16[4,4,8,1024]{3,2,1,0:T(8,128)(2,1)} %get-tuple-element.10), calls=%async_computation | async-start | bytes 524288 | tf_op jit(solution)/shard_map/all_to_all | solution.py:173
  8.2 6.6 %collective-permute-start.3 = (bf16[32,1024]{1,0:T(8,128)(2,1)S(1)}, bf16[32,1024]{1,0:T(8,128)(2,1)S(1)}, u32[]{:S(2)}, u32[]{:S(2)}) collective-permute-start(bf16[32,1024]{1,0:T(8,128)(2,1)S(1)} %get-tuple-element.11.refs_0_), channel_id=1, source_target_pairs={{0,1},{1,0},{2,3},{3,2},{4,5},{5,4},{6,7},{7,6},{8,9},{9,8},{10,11... | collective-permute-start | bytes 196616 | tf_op jit(solution)/shard_map/ppermute | solution.py:146
  10.4 6.1 %collective-permute-start.2 = (bf16[32,1024]{1,0:T(8,128)(2,1)S(1)}, bf16[32,1024]{1,0:T(8,128)(2,1)S(1)}, u32[]{:S(2)}, u32[]{:S(2)}) collective-permute-start(bf16[32,1024]{1,0:T(8,128)(2,1)S(1)} %get-tuple-element.11.refs_0_), channel_id=1, source_target_pairs={{0,6},{1,7},{2,4},{3,5},{4,2},{5,3},{6,0},{7,1},{8,14},{9,15},{10,... | collective-permute-start | bytes 196616 | tf_op jit(solution)/shard_map/ppermute | solution.py:146
  14.0 2.5 %collective-permute-start.7 = (bf16[32,1024]{1,0:T(8,128)(2,1)S(1)}, bf16[32,1024]{1,0:T(8,128)(2,1)S(1)}, u32[]{:S(2)}, u32[]{:S(2)}) collective-permute-start(bf16[32,1024]{1,0:T(8,128)(2,1)S(1)} %get-tuple-element.11.refs_0_), channel_id=1, source_target_pairs={{0,8},{8,0},{16,24},{24,16},{1,9},{9,1},{17,25},{25,17},{2,10},{10... | collective-permute-start | bytes 196616 | tf_op jit(solution)/shard_map/ppermute | solution.py:146
  14.0 5.9 %collective-permute-start.1 = (bf16[32,1024]{1,0:T(8,128)(2,1)S(1)}, bf16[32,1024]{1,0:T(8,128)(2,1)S(1)}, u32[]{:S(2)}, u32[]{:S(2)}) collective-permute-start(bf16[32,1024]{1,0:T(8,128)(2,1)S(1)} %get-tuple-element.11.refs_0_), channel_id=1, source_target_pairs={{0,4},{1,5},{2,6},{3,7},{4,0},{5,1},{6,2},{7,3},{8,12},{9,13},{10,... | collective-permute-start | bytes 196616 | tf_op jit(solution)/shard_map/ppermute | solution.py:146
  14.0 6.4 %collective-permute-start = (bf16[32,1024]{1,0:T(8,128)(2,1)S(1)}, bf16[32,1024]{1,0:T(8,128)(2,1)S(1)}, u32[]{:S(2)}, u32[]{:S(2)}) collective-permute-start(bf16[32,1024]{1,0:T(8,128)(2,1)S(1)} %get-tuple-element.11.refs_0_), channel_id=1, source_target_pairs={{0,2},{1,3},{2,0},{3,1},{4,6},{5,7},{6,4},{7,5},{8,10},{9,11},{10,... | collective-permute-start | bytes 196616 | tf_op jit(solution)/shard_map/ppermute | solution.py:146
  14.8 13.0 %collective-permute-start.11 = (bf16[32,1024]{1,0:T(8,128)(2,1)S(1)}, bf16[32,1024]{1,0:T(8,128)(2,1)S(1)}, u32[]{:S(2)}, u32[]{:S(2)}) collective-permute-start(bf16[32,1024]{1,0:T(8,128)(2,1)S(1)} %collective-permute-done.3.refs_4_), channel_id=1, source_target_pairs={{0,8},{8,0},{16,24},{24,16},{1,9},{9,1},{17,25},{25,17},{2,10},{10... | collective-permute-start | bytes 196616 | tf_op jit(solution)/shard_map/ppermute | solution.py:146
  16.5 11.9 %collective-permute-start.10 = (bf16[32,1024]{1,0:T(8,128)(2,1)S(1)}, bf16[32,1024]{1,0:T(8,128)(2,1)S(1)}, u32[]{:S(2)}, u32[]{:S(2)}) collective-permute-start(bf16[32,1024]{1,0:T(8,128)(2,1)S(1)} %collective-permute-done.2.refs_3_), channel_id=1, source_target_pairs={{0,8},{8,0},{16,24},{24,16},{1,9},{9,1},{17,25},{25,17},{2,10},{10... | collective-permute-start | bytes 196616 | tf_op jit(solution)/shard_map/ppermute | solution.py:146
  16.5 13.0 %collective-permute-start.6 = (bf16[32,1024]{1,0:T(8,128)(2,1)S(1)}, bf16[32,1024]{1,0:T(8,128)(2,1)S(1)}, u32[]{:S(2)}, u32[]{:S(2)}) collective-permute-start(bf16[32,1024]{1,0:T(8,128)(2,1)S(1)} %collective-permute-done.2.refs_3_), channel_id=1, source_target_pairs={{0,1},{1,0},{2,3},{3,2},{4,5},{5,4},{6,7},{7,6},{8,9},{9,8},{10,11... | collective-permute-start | bytes 196616 | tf_op jit(solution)/shard_map/ppermute | solution.py:146
  19.9 12.1 %copy-start.13 = (bf16[32,1024]{1,0:T(8,128)(2,1)}, bf16[32,1024]{1,0:T(8,128)(2,1)S(1)}, u32[]{:S(2)}) copy-start(bf16[32,1024]{1,0:T(8,128)(2,1)S(1)} %collective-permute-done.1.refs_2_) | copy-start | bytes 196612
  19.9 10.3 %collective-permute-start.5 = (bf16[32,1024]{1,0:T(8,128)(2,1)S(1)}, bf16[32,1024]{1,0:T(8,128)(2,1)S(1)}, u32[]{:S(2)}, u32[]{:S(2)}) collective-permute-start(bf16[32,1024]{1,0:T(8,128)(2,1)S(1)} %collective-permute-done.1.refs_2_), channel_id=1, source_target_pairs={{0,1},{1,0},{2,3},{3,2},{4,5},{5,4},{6,7},{7,6},{8,9},{9,8},{10,11... | collective-permute-start | bytes 196616 | tf_op jit(solution)/shard_map/ppermute | solution.py:146
  20.4 11.6 %copy-start.15 = (bf16[32,1024]{1,0:T(8,128)(2,1)}, bf16[32,1024]{1,0:T(8,128)(2,1)S(1)}, u32[]{:S(2)}) copy-start(bf16[32,1024]{1,0:T(8,128)(2,1)S(1)} %collective-permute-done.refs_1_) | copy-start | bytes 196612
  20.4 10.9 %collective-permute-start.4 = (bf16[32,1024]{1,0:T(8,128)(2,1)S(1)}, bf16[32,1024]{1,0:T(8,128)(2,1)S(1)}, u32[]{:S(2)}, u32[]{:S(2)}) collective-permute-start(bf16[32,1024]{1,0:T(8,128)(2,1)S(1)} %collective-permute-done.refs_1_), channel_id=1, source_target_pairs={{0,1},{1,0},{2,3},{3,2},{4,5},{5,4},{6,7},{7,6},{8,9},{9,8},{10,11... | collective-permute-start | bytes 196616 | tf_op jit(solution)/shard_map/ppermute | solution.py:146
  21.9 0.7 %copy-start.9 = (s32[32]{0:T(128)S(1)}, s32[32]{0:T(128)}, u32[]{:S(2)}) copy-start(s32[32]{0:T(128)} %anc_ref.5) | copy-start | bytes 388
  23.8 23.6 %copy-start.10 = (s32[32]{0:T(128)S(1)}, s32[32]{0:T(128)}, u32[]{:S(2)}) copy-start(s32[32]{0:T(128)} %anc_ref.5) | copy-start | bytes 388
  23.8 23.6 %copy-start.11 = (s32[32]{0:T(128)S(1)}, s32[32]{0:T(128)}, u32[]{:S(2)}) copy-start(s32[32]{0:T(128)} %len_ref.1) | copy-start | bytes 388
  23.8 23.6 %all-to-all-start.1 = ((bf16[8,8,1024]{2,1,0:T(8,128)(2,1)}), bf16[8,8,1024]{2,1,0:T(8,128)(2,1)S(1)}, u32[]{:S(2)}, u32[]{:S(2)}) async-start(bf16[8,8,1024]{2,1,0:T(8,128)(2,1)} %route.1), calls=%async_computation.1 | async-start | bytes 262144 | tf_op jit(solution)/shard_map/all_to_all | solution.py:182
  27.8 0.6 %copy-start.17 = (bf16[32,1024]{1,0:T(8,128)(2,1)}, bf16[32,1024]{1,0:T(8,128)(2,1)S(1)}, u32[]{:S(2)}) copy-start(bf16[32,1024]{1,0:T(8,128)(2,1)S(1)} %collective-permute-done.11.refs_12_) | copy-start | bytes 196612
  28.4 3.5 %collective-permute-start.9 = (bf16[32,1024]{1,0:T(8,128)(2,1)S(1)}, bf16[32,1024]{1,0:T(8,128)(2,1)S(1)}, u32[]{:S(2)}, u32[]{:S(2)}) collective-permute-start(bf16[32,1024]{1,0:T(8,128)(2,1)S(1)} %collective-permute-done.1.refs_2_), channel_id=1, source_target_pairs={{0,8},{8,0},{16,24},{24,16},{1,9},{9,1},{17,25},{25,17},{2,10},{10... | collective-permute-start | bytes 196616 | tf_op jit(solution)/shard_map/ppermute | solution.py:146
  28.4 0.6 %copy-start.19 = (bf16[32,1024]{1,0:T(8,128)(2,1)}, bf16[32,1024]{1,0:T(8,128)(2,1)S(1)}, u32[]{:S(2)}) copy-start(bf16[32,1024]{1,0:T(8,128)(2,1)S(1)} %collective-permute-done.10.refs_11_) | copy-start | bytes 196612
  29.0 2.9 %collective-permute-start.8 = (bf16[32,1024]{1,0:T(8,128)(2,1)S(1)}, bf16[32,1024]{1,0:T(8,128)(2,1)S(1)}, u32[]{:S(2)}, u32[]{:S(2)}) collective-permute-start(bf16[32,1024]{1,0:T(8,128)(2,1)S(1)} %collective-permute-done.refs_1_), channel_id=1, source_target_pairs={{0,8},{8,0},{16,24},{24,16},{1,9},{9,1},{17,25},{25,17},{2,10},{10... | collective-permute-start | bytes 196616 | tf_op jit(solution)/shard_map/ppermute | solution.py:146
  29.6 2.4 %collective-permute-start.14 = (bf16[32,1024]{1,0:T(8,128)(2,1)S(1)}, bf16[32,1024]{1,0:T(8,128)(2,1)S(1)}, u32[]{:S(2)}, u32[]{:S(2)}) collective-permute-start(bf16[32,1024]{1,0:T(8,128)(2,1)S(1)} %collective-permute-done.6.refs_7_), channel_id=1, source_target_pairs={{0,8},{8,0},{16,24},{24,16},{1,9},{9,1},{17,25},{25,17},{2,10},{10... | collective-permute-start | bytes 196616 | tf_op jit(solution)/shard_map/ppermute | solution.py:146
  29.6 0.6 %copy-start.21 = (bf16[32,1024]{1,0:T(8,128)(2,1)}, bf16[32,1024]{1,0:T(8,128)(2,1)S(1)}, u32[]{:S(2)}) copy-start(bf16[32,1024]{1,0:T(8,128)(2,1)S(1)} %collective-permute-done.6.refs_7_) | copy-start | bytes 196612
  30.2 1.8 %collective-permute-start.13 = (bf16[32,1024]{1,0:T(8,128)(2,1)S(1)}, bf16[32,1024]{1,0:T(8,128)(2,1)S(1)}, u32[]{:S(2)}, u32[]{:S(2)}) collective-permute-start(bf16[32,1024]{1,0:T(8,128)(2,1)S(1)} %collective-permute-done.5.refs_6_), channel_id=1, source_target_pairs={{0,8},{8,0},{16,24},{24,16},{1,9},{9,1},{17,25},{25,17},{2,10},{10... | collective-permute-start | bytes 196616 | tf_op jit(solution)/shard_map/ppermute | solution.py:146
  30.7 0.6 %copy-start.23 = (bf16[32,1024]{1,0:T(8,128)(2,1)}, bf16[32,1024]{1,0:T(8,128)(2,1)S(1)}, u32[]{:S(2)}) copy-start(bf16[32,1024]{1,0:T(8,128)(2,1)S(1)} %collective-permute-done.5.refs_6_) | copy-start | bytes 196612
  31.3 1.3 %collective-permute-start.12 = (bf16[32,1024]{1,0:T(8,128)(2,1)S(1)}, bf16[32,1024]{1,0:T(8,128)(2,1)S(1)}, u32[]{:S(2)}, u32[]{:S(2)}) collective-permute-start(bf16[32,1024]{1,0:T(8,128)(2,1)S(1)} %collective-permute-done.4.refs_5_), channel_id=1, source_target_pairs={{0,8},{8,0},{16,24},{24,16},{1,9},{9,1},{17,25},{25,17},{2,10},{10... | collective-permute-start | bytes 196616 | tf_op jit(solution)/shard_map/ppermute | solution.py:146
  31.3 0.6 %copy-start.25 = (bf16[32,1024]{1,0:T(8,128)(2,1)}, bf16[32,1024]{1,0:T(8,128)(2,1)S(1)}, u32[]{:S(2)}) copy-start(bf16[32,1024]{1,0:T(8,128)(2,1)S(1)} %collective-permute-done.4.refs_5_) | copy-start | bytes 196612
  32.6 1.2 %copy-start.4 = (bf16[128,4096]{1,0:T(8,128)(2,1)S(1)}, bf16[128,4096]{1,0:T(8,128)(2,1)}, u32[]{:S(2)}) copy-start(bf16[128,4096]{1,0:T(8,128)(2,1)} %q_ref.3) | copy-start | bytes 3145732
  33.8 0.9 %copy-start.12 = (bf16[128,2,512]{2,1,0:T(2,128)(2,1)S(1)}, bf16[128,2,512]{2,1,0:T(2,128)(2,1)}, u32[]{:S(2)}) copy-start(bf16[128,2,512]{2,1,0:T(2,128)(2,1)} %new_ref.1) | copy-start | bytes 786436
  34.8 0.8 %copy-start.14 = (bf16[32,1024]{1,0:T(8,128)(2,1)S(1)}, bf16[32,1024]{1,0:T(8,128)(2,1)}, u32[]{:S(2)}) copy-start(bf16[32,1024]{1,0:T(8,128)(2,1)} %copy-done.13) | copy-start | bytes 196612
  35.6 0.8 %copy-start.16 = (bf16[32,1024]{1,0:T(8,128)(2,1)S(1)}, bf16[32,1024]{1,0:T(8,128)(2,1)}, u32[]{:S(2)}) copy-start(bf16[32,1024]{1,0:T(8,128)(2,1)} %copy-done.15) | copy-start | bytes 196612
  36.4 0.8 %copy-start.18 = (bf16[32,1024]{1,0:T(8,128)(2,1)S(1)}, bf16[32,1024]{1,0:T(8,128)(2,1)}, u32[]{:S(2)}) copy-start(bf16[32,1024]{1,0:T(8,128)(2,1)} %copy-done.17) | copy-start | bytes 196612
  37.3 0.8 %copy-start.20 = (bf16[32,1024]{1,0:T(8,128)(2,1)S(1)}, bf16[32,1024]{1,0:T(8,128)(2,1)}, u32[]{:S(2)}) copy-start(bf16[32,1024]{1,0:T(8,128)(2,1)} %copy-done.19) | copy-start | bytes 196612
  38.1 0.8 %copy-start.22 = (bf16[32,1024]{1,0:T(8,128)(2,1)S(1)}, bf16[32,1024]{1,0:T(8,128)(2,1)}, u32[]{:S(2)}) copy-start(bf16[32,1024]{1,0:T(8,128)(2,1)} %copy-done.21) | copy-start | bytes 196612
  39.0 0.8 %copy-start.24 = (bf16[32,1024]{1,0:T(8,128)(2,1)S(1)}, bf16[32,1024]{1,0:T(8,128)(2,1)}, u32[]{:S(2)}) copy-start(bf16[32,1024]{1,0:T(8,128)(2,1)} %copy-done.23) | copy-start | bytes 196612
  39.8 0.8 %copy-start.26 = (bf16[32,1024]{1,0:T(8,128)(2,1)S(1)}, bf16[32,1024]{1,0:T(8,128)(2,1)}, u32[]{:S(2)}) copy-start(bf16[32,1024]{1,0:T(8,128)(2,1)} %copy-done.25) | copy-start | bytes 196612
  40.6 6.8 %copy-start.5 = (bf16[128,4096]{1,0:T(8,128)(2,1)S(1)}, bf16[128,4096]{1,0:T(8,128)(2,1)}, u32[]{:S(2)}) copy-start(bf16[128,4096]{1,0:T(8,128)(2,1)} %q_ref.3) | copy-start | bytes 3145732
  44.7 1.3 %copy-start = (f32[128,4096]{1,0:T(8,128)}, f32[128,4096]{1,0:T(8,128)S(1)}, u32[]{:S(2)}) copy-start(f32[128,4096]{1,0:T(8,128)S(1)} %get-tuple-element.13.max_ref) | copy-start | bytes 6291460
  46.1 1.3 %copy-start.2 = (f32[128,4096]{1,0:T(8,128)}, f32[128,4096]{1,0:T(8,128)S(1)}, u32[]{:S(2)}) copy-start(f32[128,4096]{1,0:T(8,128)S(1)} %get-tuple-element.14.sum_ref) | copy-start | bytes 6291460
  47.4 1.6 %copy-start.1 = (f32[128,4096]{1,0:T(8,128)S(1)}, f32[128,4096]{1,0:T(8,128)}, u32[]{:S(2)}) copy-start(f32[128,4096]{1,0:T(8,128)} %copy-done) | copy-start | bytes 6291460
  49.0 1.6 %copy-start.3 = (f32[128,4096]{1,0:T(8,128)S(1)}, f32[128,4096]{1,0:T(8,128)}, u32[]{:S(2)}) copy-start(f32[128,4096]{1,0:T(8,128)} %copy-done.2) | copy-start | bytes 6291460

commit v2 on v1

v2 whole, which is shorter than its diff:
```python
import functools

import jax
import jax.numpy as jnp
from jax import lax
from jax.experimental import pallas as pl
from jax.experimental.pallas import tpu as pltpu
from jax.sharding import PartitionSpec as P

HD = 128
SPAN = 128
PAGE = 8
RUN = 4
NEGATIVE = -1e30
SCALE2 = HD ** (-0.5) * 1.4426950408889634
VMEM = pl.BlockSpec(memory_space=pltpu.VMEM)
HBM = pl.BlockSpec(memory_space=pltpu.HBM)


def params(mib):
    return pltpu.CompilerParams(vmem_limit_bytes=mib * 2**20)


def pack_kernel(dom_count, anc_hbm, len_hbm, prompt_hbm, cache_hbm, half_ref, out_ref, source_ref, limit_ref, anc_ref, len_ref, prompt_ref, cache_ref, sems):
    group = cache_ref.shape[0]
    dom = lax.axis_index("dom")
    copies_of, rows, width = half_ref.shape
    from_row = pl.multiple_of((dom % 2) * rows, rows)
    prompt_in = pltpu.make_async_copy(prompt_hbm.at[pl.ds(from_row, rows)], prompt_ref, sems.at[0])
    anc_in = pltpu.make_async_copy(anc_hbm, anc_ref, sems.at[1])
    len_in = pltpu.make_async_copy(len_hbm, len_ref, sems.at[2])
    cache_in = pltpu.make_async_copy(cache_hbm, cache_ref, sems.at[3])
    anc_in.start()
    len_in.start()
    prompt_in.start()
    cache_in.start()
    prompt_in.wait()
    half = prompt_ref[...].reshape(rows, width)
    for at in range(copies_of):
        half_ref[at] = half
    runs = group // RUN
    anc_in.wait()
    len_in.wait()
    for run in range(runs):
        source = anc_ref[dom * group + run * RUN] // group
        source_ref[run] = jnp.full(source_ref.shape[1:], source.astype(jnp.float32)).astype(jnp.bfloat16)
    particle = dom * group + lax.axis_index("ctx")
    limit_ref[...] = jnp.full(limit_ref.shape, len_ref[anc_ref[particle]] * PAGE)
    cache_in.wait()

    def one(step, carry):
        first = step * RUN
        anchor = anc_ref[first]

        @pl.when(anchor // group == dom)
        def _():
            for slot in range(RUN):
                local = anc_ref[first + slot] % group
                out_ref[step // runs, slot] = cache_ref[local].reshape(cache_ref.shape[1], width)

        return carry

    lax.fori_loop(0, dom_count * runs, one, 0)


def route_kernel(source_ref, in_ref, out_ref):
    dom_count, _, rows, width = in_ref.shape
    for run in range(source_ref.shape[0]):
        mask = source_ref[run]
        for slot in range(RUN):
            picked = in_ref[0, slot]
            for dom in range(1, dom_count):
                here = jnp.concatenate([mask == dom] * (width // mask.shape[1]), axis=1)
                picked = jnp.where(here, in_ref[dom, slot], picked)
            out_ref[run * RUN + slot] = picked


def head_rows(q_ref, g, gq):
    return jnp.concatenate(
        [q_ref[:, (g * gq + j) * HD : (g * gq + j + 1) * HD] for j in range(gq)], axis=0
    )


def dot_nt(a, b):
    return lax.dot_general(a, b, (((1,), (1,)), ((), ())), preferred_element_type=jnp.float32)


def dot_nn(a, b):
    return lax.dot_general(a, b, (((1,), (0,)), ((), ())), preferred_element_type=jnp.float32)


def row_top(parts):
    top = None
    for part in parts:
        for at in range(0, part.shape[1], HD):
            block = part[:, at : at + HD]
            if block.shape[1] < HD:
                continue
            top = block if top is None else jnp.maximum(top, block)
    top = jnp.max(top, axis=1, keepdims=True)
    for part in parts:
        if part.shape[1] % HD:
            top = jnp.maximum(top, jnp.max(part[:, part.shape[1] // HD * HD :], axis=1, keepdims=True))
    return top


def first_kernel(q_ref, new_ref, half_ref, acc_ref, max_ref, sum_ref):
    width = new_ref.shape[2]
    kvh = width // HD
    gq = q_ref.shape[1] // width
    new = new_ref[...].reshape(SPAN, 2 * width)
    ones = jnp.ones((SPAN + half_ref.shape[0], HD), jnp.bfloat16)
    token = lax.broadcasted_iota(jnp.int32, (SPAN, SPAN), 0)
    key = lax.broadcasted_iota(jnp.int32, (SPAN, SPAN), 1)
    causal = key <= token
    for g in range(kvh):
        k_at = slice(g * HD, (g + 1) * HD)
        v_at = slice(width + g * HD, width + (g + 1) * HD)
        keys = jnp.concatenate([new[:, k_at], half_ref[:, k_at]], axis=0)
        values = jnp.concatenate([new[:, v_at], half_ref[:, v_at]], axis=0)
        values = jnp.concatenate([values, ones], axis=1)
        scores = dot_nt(head_rows(q_ref, g, gq), keys)
        weights, tops = [], []
        for j in range(gq):
            s = scores[j * SPAN : (j + 1) * SPAN]
            s_new = jnp.where(causal, s[:, :SPAN], NEGATIVE)
            s_old = s[:, SPAN:]
            top = row_top([s_new, s_old])
            s = jnp.concatenate([s_new, s_old], axis=1)
            weights.append(jnp.exp2((s - top) * SCALE2).astype(jnp.bfloat16))
            tops.append(top)
        out = dot_nn(jnp.concatenate(weights, axis=0), values)
        for j in range(gq):
            at = slice((g * gq + j) * HD, (g * gq + j + 1) * HD)
            rows = slice(j * SPAN, (j + 1) * SPAN)
            acc_ref[:, at] = out[rows, :HD]
            sum_ref[:, at] = out[rows, HD:]
            max_ref[:, at] = jnp.broadcast_to(tops[j], (SPAN, HD))


def last_kernel(limit_ref, q_ref, half_ref, cache_ref, acc_ref, max_ref, sum_ref, out_ref, stage, sems):
    width = cache_ref.shape[1] // 2
    gen = cache_ref.shape[0]
    other = half_ref.shape[0]
    kvh = width // HD
    gq = q_ref.shape[1] // width
    visible = lax.broadcasted_iota(jnp.int32, (SPAN, gen), 1) < jnp.broadcast_to(limit_ref[:1], (SPAN, gen))
    ones = jnp.ones((other + gen, HD), jnp.bfloat16)
    copies = []
    for g in range(kvh):
        k_at = slice(g * HD, (g + 1) * HD)
        v_at = slice(width + g * HD, width + (g + 1) * HD)
        keys = jnp.concatenate([half_ref[:, k_at], cache_ref[:, k_at]], axis=0)
        values = jnp.concatenate([half_ref[:, v_at], cache_ref[:, v_at]], axis=0)
        values = jnp.concatenate([values, ones], axis=1)
        scores = dot_nt(head_rows(q_ref, g, gq), keys)
        weights, factors = [], []
        for j in range(gq):
            at = slice((g * gq + j) * HD, (g * gq + j + 1) * HD)
            s = scores[j * SPAN : (j + 1) * SPAN]
            s_cache = jnp.where(visible, s[:, other:], NEGATIVE)
            before = max_ref[:, at]
            top = jnp.maximum(before[:, :1], row_top([s[:, :other], s_cache]))
            s = jnp.concatenate([s[:, :other], s_cache], axis=1)
            weights.append(jnp.exp2((s - top) * SCALE2).astype(jnp.bfloat16))
            factors.append(jnp.exp2((before - top) * SCALE2))
        out = dot_nn(jnp.concatenate(weights, axis=0), values)
        for j in range(gq):
            at = slice((g * gq + j) * HD, (g * gq + j + 1) * HD)
            rows = slice(j * SPAN, (j + 1) * SPAN)
            total = sum_ref[:, at] * factors[j] + out[rows, HD:]
            value = acc_ref[:, at] * factors[j] + out[rows, :HD]
            stage[:, at] = (value / total).astype(jnp.bfloat16)
        columns = pl.ds(g * gq * HD, gq * HD)
        copy = pltpu.make_async_copy(stage.at[:, columns], out_ref.at[:, columns], sems.at[g])
        copy.start()
        copies.append(copy)
    for copy in copies:
        copy.wait()


def on_device(q_new, kv_new, prompt_kv, cache_kv, ancestors, lengths):
    dom_count = lax.axis_size("dom")
    ctx_count = lax.axis_size("ctx")
    group, page_rows, _, width = cache_kv.shape
    tokens, q_width = q_new.shape
    kvh = width // HD
    half_rows = prompt_kv.shape[0] // 2
    shape = jax.ShapeDtypeStruct
    halves, outgoing, sources, limit = pl.pallas_call(
        functools.partial(pack_kernel, dom_count),
        out_shape=(
            shape((ctx_count, half_rows, 2 * width), jnp.bfloat16),
            shape((dom_count, RUN, page_rows, 2 * width), jnp.bfloat16),
            shape((group // RUN, page_rows, HD), jnp.bfloat16),
            shape((8, ctx_count * page_rows), jnp.int32),
        ),
        in_specs=[HBM] * 4,
        out_specs=(VMEM,) * 4,
        scratch_shapes=[
            pltpu.SMEM(ancestors.shape, jnp.int32),
            pltpu.SMEM(lengths.shape, jnp.int32),
            pltpu.VMEM((half_rows, 2, width), jnp.bfloat16),
            pltpu.VMEM(cache_kv.shape, jnp.bfloat16),
            pltpu.SemaphoreType.DMA((4,)),
        ],
        compiler_params=params(16),
        name="pack",
    )(*(pltpu.with_memory_space_constraint(x, pltpu.HBM) for x in (ancestors, lengths, prompt_kv, cache_kv)))

    own_half = lax.all_to_all(halves, "ctx", split_axis=0, concat_axis=0, tiled=True)
    own_half = own_half.reshape(ctx_count * half_rows, 2 * width)
    other_half = lax.ppermute(own_half, "dom", [(i, i ^ 1) for i in range(dom_count)])

    incoming = lax.all_to_all(outgoing, "dom", split_axis=0, concat_axis=0, tiled=True)
    routed = pl.pallas_call(
        route_kernel,
        out_shape=shape((group, page_rows, 2 * width), jnp.bfloat16),
        in_specs=[VMEM, VMEM],
        out_specs=VMEM,
        compiler_params=params(12),
        name="route",
    )(sources, incoming)
    pages = lax.all_to_all(routed, "ctx", split_axis=0, concat_axis=0, tiled=True)
    pages = pages.reshape(ctx_count * page_rows, 2 * width)

    key_count = SPAN + own_half.shape[0]
    acc, top, total = pl.pallas_call(
        first_kernel,
        out_shape=(shape((tokens, q_width), jnp.float32),) * 3,
        in_specs=[VMEM] * 3,
        out_specs=(VMEM,) * 3,
        compiler_params=params(24),
        cost_estimate=pl.CostEstimate(
            flops=4 * tokens * q_width * key_count,
            bytes_accessed=2**23,
            transcendentals=tokens * q_width // HD * key_count,
        ),
        name="new_and_own_half",
    )(q_new, kv_new, own_half)
    return pl.pallas_call(
        last_kernel,
        out_shape=shape((tokens, q_width), jnp.bfloat16),
        in_specs=[VMEM] * 7,
        out_specs=HBM,
        scratch_shapes=[pltpu.VMEM((tokens, q_width), jnp.bfloat16), pltpu.SemaphoreType.DMA((kvh,))],
        compiler_params=params(24),
        name="other_half_and_cache",
    )(limit, q_new, other_half, pages, acc, top, total)


def solution(mesh):
    placed = (
        P(("dom", "ctx"), None),
        P(("dom", "ctx"), None, None),
        P("ctx", None, None),
        P("dom", "ctx", None, None),
        P(),
        P(),
    )
    return jax.shard_map(
        on_device, mesh=mesh, in_specs=placed, out_specs=P(("dom", "ctx"), None), check_vma=False
    )
```

time: 54.6 us -> 53.3 us (0.976)
  blocking collectives: 0 us -> 30.4 us
  starting transfers between devices: 18.4 us -> 3.59 us
  local copies, waits for them, and re-layouts: 20.1 us -> 5.84 us
  waiting for transfers between devices: 5.24 us -> 0.86 us
  Pallas kernels: 9.96 us -> 12 us
    all_to_all x0 -> x2, blocking collectives: none -> 30.4 us  [the longest x1 21.7 us: on_device(): lax.all_to_all(halves, 'ctx', split_axis=0, concat_axis=0, tiled=True)]
    unnamed x54 -> x12, local copies, waits for them, and re-layouts: 20.1 us -> 5.84 us
    ppermute x15 -> x1, starting transfers between devices: 10.2 us -> 0.01 us  [on_device(): lax.ppermute(own_half, 'dom', [(i, i ^ 1) for i in range(dom_count)])]
    ppermute x15 -> x1, waiting for transfers between devices: 5.23 us -> 0.01 us  [on_device(): lax.ppermute(own_half, 'dom', [(i, i ^ 1) for i in range(dom_count)])]
    all_to_all x1 -> x0, starting transfers between devices: 4.24 us -> none  [on_device(): lax.all_to_all(outgoing, 'dom', split_axis=0, concat_axis=0, tiled=True)]
    pallas_call x2, Pallas kernels: 7.27 us -> 10 us  [the longest x1 6.24 us: on_device(): pl.pallas_call(last_kernel, out_shape=shape((tokens, q_width), jnp.bfloat...]
    all_to_all x1, waiting for transfers between devices: 0.01 us -> 0.86 us  [on_device(): lax.all_to_all(routed, 'ctx', split_axis=0, concat_axis=0, tiled=True)]
  transfers between devices with their start and end apart: 17 -> 2, of which waited for: 3 -> 1; matrix products, arithmetic and copies ran while one was open for 0% -> 0% of each run, Pallas kernels for 10% -> 9%
where the time goes in v2:
time: 53.3 us; the launch traced here: 52.8 us
  blocking collectives  30.4 us (57%)
  Pallas kernels  12 us (23%)
  local copies, waits for them, and re-layouts  5.84 us (11%)
  starting transfers between devices  3.59 us (7%)
  waiting for transfers between devices  0.86 us (2%)
    all_to_all x1, blocking collectives, on_device(): lax.all_to_all(halves, 'ctx', split_axis=0, concat_axis=0, tiled=True)  21.7 us
    all_to_all x1, blocking collectives, on_device(): lax.all_to_all(outgoing, 'dom', split_axis=0, concat_axis=0, tiled=True)  8.7 us
    pallas_call x1, Pallas kernels, on_device(): pl.pallas_call(last_kernel, out_shape=shape((tokens, q_width), jnp.bfloat...  6.24 us
    unnamed x12, local copies, waits for them, and re-layouts  5.84 us
    pallas_call x1, Pallas kernels, on_device(): pl.pallas_call(first_kernel, out_shape=(shape((tokens, q_width), jnp.floa...  3.8 us
    all_to_all x1, starting transfers between devices, on_device(): lax.all_to_all(routed, 'ctx', split_axis=0, concat_axis=0, tiled=True)  3.59 us
    pallas_call x1, Pallas kernels, on_device(): pl.pallas_call(functools.partial(pack_kernel, dom_count), out_shape=(shap...  1.27 us
  transfers between devices with their start and end apart: 2, of which 1 were waited for; matrix products, arithmetic and copies ran while one was open for 0% of the time, Pallas kernels for 9%

profile of v2, /device:TPU:0, one launch (start us, length us, event | category | flops | bytes accessed | tf_op | source)
XLA Modules:
  0.0 52.8 jit_solution(15685899439623567704)
XLA Ops:
  0.0 0.0 copy-start.4
  0.0 0.0 copy-start.5
  0.0 1.3 %pack.1 = (bf16[8,32,1024]{2,1,0:T(8,128)(2,1)S(1)}, bf16[4,4,8,1024]{3,2,1,0:T(8,128)(2,1)S(1)}, bf16[2,8,128]{2,1,0:T(8,128)(2,1)S(1)}, s32[8,64]{1,0:T(8,128)S(1)}) custom-call(s32[32]{0:T(128)} %anc_hbm.1, s32[32]{0:T(128)} %len_hbm.1, bf16[64,2,512]{2,1,0:T(2,128)(2,1)} %prompt_hbm.1, bf16[8,8,2,512]{3,2,1,0:T(2,128)(2,1)} %cache_hbm.1), custom_call_target="tpu_custom_call" | custom-call | tf_op jit(solution)/shard_map/pack/pallas_call | solution.py:190
  1.3 21.7 %all_to_all.15 = bf16[8,32,1024]{2,1,0:T(8,128)(2,1)} all-to-all(bf16[8,32,1024]{2,1,0:T(8,128)(2,1)S(1)} %get-tuple-element.13), channel_id=1, replica_groups=mesh['dom'=4,'ctx'=8] {'ctx'}, dimensions={0} | all-to-all | bytes 1048576 | tf_op jit(solution)/shard_map/all_to_all | solution.py:211
  23.0 0.0 collective-permute-start
  23.0 8.7 %all_to_all.16.in_ref = bf16[4,4,8,1024]{3,2,1,0:T(8,128)(2,1)S(1)} all-to-all(bf16[4,4,8,1024]{3,2,1,0:T(8,128)(2,1)S(1)} %get-tuple-element.15), channel_id=1, replica_groups=mesh['dom'=4,'ctx'=8] {'dom'}, dimensions={0} | all-to-all | bytes 524288 | tf_op jit(solution)/shard_map/all_to_all | solution.py:215
  31.7 0.7 %route.1 = bf16[8,8,1024]{2,1,0:T(8,128)(2,1)} custom-call(bf16[2,8,128]{2,1,0:T(8,128)(2,1)S(1)} %get-tuple-element.14.source_ref, bf16[4,4,8,1024]{3,2,1,0:T(8,128)(2,1)S(1)} %all_to_all.16.in_ref), custom_call_target="tpu_custom_call" | custom-call | tf_op jit(solution)/shard_map/route/pallas_call | solution.py:216
  32.4 3.6 %all-to-all-start.2 = ((bf16[8,8,1024]{2,1,0:T(8,128)(2,1)}), bf16[8,8,1024]{2,1,0:T(8,128)(2,1)S(1)}, u32[]{:S(2)}, u32[]{:S(2)}) async-start(bf16[8,8,1024]{2,1,0:T(8,128)(2,1)} %route.1), calls=%async_computation.2 | async-start | bytes 262144 | tf_op jit(solution)/shard_map/all_to_all | solution.py:224
  36.0 0.0 copy-done.4
  36.0 0.0 copy-done.5
  36.0 3.8 %new_and_own_half.1 = (f32[128,4096]{1,0:T(8,128)S(1)}, f32[128,4096]{1,0:T(8,128)S(1)}, f32[128,4096]{1,0:T(8,128)S(1)}) custom-call(bf16[128,4096]{1,0:T(8,128)(2,1)S(1)} %copy-done.4, bf16[128,2,512]{2,1,0:T(2,128)(2,1)S(1)} %copy-done.5, bf16[256,1024]{1,0:T(8,128)(2,1)} %bitcast.half_ref), custom_call_target="tpu_custom_call" | custom-call | flops 805306368 | bytes 8388608 | tf_op jit(solution)/shard_map/new_and_own_half/pallas_call | solution.py:228
  39.8 0.0 copy-start
  39.9 1.3 %copy-done = f32[128,4096]{1,0:T(8,128)} copy-done((f32[128,4096]{1,0:T(8,128)}, f32[128,4096]{1,0:T(8,128)S(1)}, u32[]{:S(2)}) %copy-start) | copy-done | bytes 2097176
  41.2 0.0 copy-start.2
  41.2 1.3 %copy-done.2 = f32[128,4096]{1,0:T(8,128)} copy-done((f32[128,4096]{1,0:T(8,128)}, f32[128,4096]{1,0:T(8,128)S(1)}, u32[]{:S(2)}) %copy-start.2) | copy-done | bytes 2097176
  42.5 0.9 %all-to-all-done.2 = bf16[8,8,1024]{2,1,0:T(8,128)(2,1)S(1)} async-done(((bf16[8,8,1024]{2,1,0:T(8,128)(2,1)}), bf16[8,8,1024]{2,1,0:T(8,128)(2,1)S(1)}, u32[]{:S(2)}, u32[]{:S(2)}) %all-to-all-start.2) | async-done | bytes 131104 | tf_op jit(solution)/shard_map/all_to_all | solution.py:224
  43.4 0.0 collective-permute-done.half_ref
  43.4 0.0 copy-start.1
  43.4 1.6 %copy-done.1 = f32[128,4096]{1,0:T(8,128)S(1)} copy-done((f32[128,4096]{1,0:T(8,128)S(1)}, f32[128,4096]{1,0:T(8,128)}, u32[]{:S(2)}) %copy-start.1) | copy-done | bytes 2097176
  45.0 0.0 copy-start.3
  45.0 1.6 %copy-done.3 = f32[128,4096]{1,0:T(8,128)S(1)} copy-done((f32[128,4096]{1,0:T(8,128)S(1)}, f32[128,4096]{1,0:T(8,128)}, u32[]{:S(2)}) %copy-start.3) | copy-done | bytes 2097176
  46.5 6.2 %other_half_and_cache.1 = bf16[128,4096]{1,0:T(8,128)(2,1)} custom-call(s32[8,64]{1,0:T(8,128)S(1)} %get-tuple-element.12.limit_ref, bf16[128,4096]{1,0:T(8,128)(2,1)S(1)} %copy-done.4, bf16[256,1024]{1,0:T(8,128)(2,1)} %collective-permute-done.half_ref, bf16[64,1024]{1,0:T(8,128)(2,1)S(1)} %bitcast.2, f32[128,4096]{1,0:T(8,128)S(1)} %get-tuple-element.16.acc_ref, ...), custom_call_target="tpu_custom_call" | custom-call | tf_op jit(solution)/shard_map/other_half_and_cache/pallas_call | solution.py:241
Async XLA Ops:
  0.0 36.0 %copy-start.4 = (bf16[128,4096]{1,0:T(8,128)(2,1)S(1)}, bf16[128,4096]{1,0:T(8,128)(2,1)}, u32[]{:S(2)}) copy-start(bf16[128,4096]{1,0:T(8,128)(2,1)} %q_ref.3) | copy-start | bytes 3145732
  0.0 36.0 %copy-start.5 = (bf16[128,2,512]{2,1,0:T(2,128)(2,1)S(1)}, bf16[128,2,512]{2,1,0:T(2,128)(2,1)}, u32[]{:S(2)}) copy-start(bf16[128,2,512]{2,1,0:T(2,128)(2,1)} %new_ref.1) | copy-start | bytes 786436
  23.0 20.3 %collective-permute-start = (bf16[256,1024]{1,0:T(8,128)(2,1)}, bf16[256,1024]{1,0:T(8,128)(2,1)}, u32[]{:S(2)}, u32[]{:S(2)}) collective-permute-start(bf16[256,1024]{1,0:T(8,128)(2,1)} %bitcast.half_ref), channel_id=1, source_target_pairs={{0,8},{8,0},{16,24},{24,16},{1,9},{9,1},{17,25},{25,17},{2,10},{10... | collective-permute-start | bytes 1572872 | tf_op jit(solution)/shard_map/ppermute | solution.py:213
  32.4 10.9 %all-to-all-start.2 = ((bf16[8,8,1024]{2,1,0:T(8,128)(2,1)}), bf16[8,8,1024]{2,1,0:T(8,128)(2,1)S(1)}, u32[]{:S(2)}, u32[]{:S(2)}) async-start(bf16[8,8,1024]{2,1,0:T(8,128)(2,1)} %route.1), calls=%async_computation.2 | async-start | bytes 262144 | tf_op jit(solution)/shard_map/all_to_all | solution.py:224
  39.8 1.3 %copy-start = (f32[128,4096]{1,0:T(8,128)}, f32[128,4096]{1,0:T(8,128)S(1)}, u32[]{:S(2)}) copy-start(f32[128,4096]{1,0:T(8,128)S(1)} %get-tuple-element.17.max_ref) | copy-start | bytes 6291460
  41.2 1.3 %copy-start.2 = (f32[128,4096]{1,0:T(8,128)}, f32[128,4096]{1,0:T(8,128)S(1)}, u32[]{:S(2)}) copy-start(f32[128,4096]{1,0:T(8,128)S(1)} %get-tuple-element.18.sum_ref) | copy-start | bytes 6291460
  43.4 1.6 %copy-start.1 = (f32[128,4096]{1,0:T(8,128)S(1)}, f32[128,4096]{1,0:T(8,128)}, u32[]{:S(2)}) copy-start(f32[128,4096]{1,0:T(8,128)} %copy-done) | copy-start | bytes 6291460
  45.0 1.6 %copy-start.3 = (f32[128,4096]{1,0:T(8,128)S(1)}, f32[128,4096]{1,0:T(8,128)}, u32[]{:S(2)}) copy-start(f32[128,4096]{1,0:T(8,128)} %copy-done.2) | copy-start | bytes 6291460

commit v3 on v2

v3 whole, which is shorter than its diff:
```python
import functools

import jax
import jax.numpy as jnp
from jax import lax
from jax.experimental import pallas as pl
from jax.experimental.pallas import tpu as pltpu
from jax.sharding import PartitionSpec as P

HD = 128
SPAN = 128
PAGE = 8
RUN = 4
NEGATIVE = -1e30
SCALE2 = HD ** (-0.5) * 1.4426950408889634
VMEM = pl.BlockSpec(memory_space=pltpu.VMEM)
HBM = pl.BlockSpec(memory_space=pltpu.HBM)


def params(mib):
    return pltpu.CompilerParams(vmem_limit_bytes=mib * 2**20)


def pack_kernel(dom_count, anc_hbm, len_hbm, prompt_hbm, cache_hbm, halves_hbm, out_hbm, source_ref, limit_ref, anc_ref, len_ref, prompt_ref, half_ref, cache_ref, out_ref, sems):
    group = cache_ref.shape[0]
    dom = lax.axis_index("dom")
    rows, width = half_ref.shape
    from_row = pl.multiple_of((dom % 2) * rows, rows)
    prompt_in = pltpu.make_async_copy(prompt_hbm.at[pl.ds(from_row, rows)], prompt_ref, sems.at[0])
    anc_in = pltpu.make_async_copy(anc_hbm, anc_ref, sems.at[1])
    len_in = pltpu.make_async_copy(len_hbm, len_ref, sems.at[2])
    cache_in = pltpu.make_async_copy(cache_hbm, cache_ref, sems.at[3])
    anc_in.start()
    len_in.start()
    prompt_in.start()
    cache_in.start()
    prompt_in.wait()
    half_ref[...] = prompt_ref[...].reshape(rows, width)
    halves_out = [
        pltpu.make_async_copy(half_ref, halves_hbm.at[at], sems.at[5 + at]) for at in range(halves_hbm.shape[0])
    ]
    for copy in halves_out:
        copy.start()
    runs = group // RUN
    anc_in.wait()
    len_in.wait()
    for run in range(runs):
        source = anc_ref[dom * group + run * RUN] // group
        source_ref[run] = jnp.full(source_ref.shape[1:], source.astype(jnp.float32)).astype(jnp.bfloat16)
    particle = dom * group + lax.axis_index("ctx")
    limit_ref[...] = jnp.full(limit_ref.shape, len_ref[anc_ref[particle]] * PAGE)
    cache_in.wait()

    def one(step, carry):
        first = step * RUN
        anchor = anc_ref[first]

        @pl.when(anchor // group == dom)
        def _():
            for slot in range(RUN):
                local = anc_ref[first + slot] % group
                out_ref[step // runs, slot] = cache_ref[local].reshape(cache_ref.shape[1], width)

        return carry

    lax.fori_loop(0, dom_count * runs, one, 0)
    out = pltpu.make_async_copy(out_ref, out_hbm, sems.at[4])
    out.start()
    for copy in halves_out:
        copy.wait()
    out.wait()


def route_kernel(source_ref, in_ref, out_hbm, out_ref, sem):
    dom_count, _, rows, width = in_ref.shape
    for run in range(source_ref.shape[0]):
        mask = source_ref[run]
        for slot in range(RUN):
            picked = in_ref[0, slot]
            for dom in range(1, dom_count):
                here = jnp.concatenate([mask == dom] * (width // mask.shape[1]), axis=1)
                picked = jnp.where(here, in_ref[dom, slot], picked)
            out_ref[run * RUN + slot] = picked
    out = pltpu.make_async_copy(out_ref, out_hbm, sem)
    out.start()
    out.wait()


def head_rows(q_ref, g, gq):
    return jnp.concatenate(
        [q_ref[:, (g * gq + j) * HD : (g * gq + j + 1) * HD] for j in range(gq)], axis=0
    )


def dot(a, b, contract):
    return lax.dot_general(a, b, (contract, ((), ())), preferred_element_type=jnp.float32)


def first_kernel(q_ref, new_ref, half_ref, acc_ref, max_ref, sum_ref):
    width = new_ref.shape[2]
    kvh = width // HD
    gq = q_ref.shape[1] // width
    rows = gq * SPAN
    new = new_ref[...].reshape(SPAN, 2 * width)
    key = lax.broadcasted_iota(jnp.int32, (SPAN, rows), 0)
    token = lax.broadcasted_iota(jnp.int32, (SPAN, rows), 1) % SPAN
    causal = key <= token
    for g in range(kvh):
        k_at = slice(g * HD, (g + 1) * HD)
        v_at = slice(width + g * HD, width + (g + 1) * HD)
        at = slice(g * rows, (g + 1) * rows)
        keys = jnp.concatenate([new[:, k_at], half_ref[:, k_at]], axis=0)
        values = jnp.concatenate([new[:, v_at], half_ref[:, v_at]], axis=0)
        s = dot(keys, head_rows(q_ref, g, gq), ((1,), (1,)))
        s = jnp.concatenate([jnp.where(causal, s[:SPAN], NEGATIVE), s[SPAN:]], axis=0)
        top = jnp.max(s, axis=0, keepdims=True)
        weights = jnp.exp2((s - top) * SCALE2)
        acc_ref[:, at] = dot(values, weights.astype(jnp.bfloat16), ((0,), (0,)))
        sum_ref[:, at] = jnp.sum(weights, axis=0, keepdims=True)
        max_ref[:, at] = top


def last_kernel(limit_ref, q_ref, half_ref, cache_ref, acc_ref, max_ref, sum_ref, out_ref, stage, sems):
    width = cache_ref.shape[1] // 2
    gen = cache_ref.shape[0]
    other = half_ref.shape[0]
    kvh = width // HD
    gq = q_ref.shape[1] // width
    rows = gq * SPAN
    limit = jnp.concatenate([limit_ref[...]] * (rows // limit_ref.shape[1]), axis=1)
    visible = lax.broadcasted_iota(jnp.int32, (gen, rows), 0) < limit
    unit = lax.broadcasted_iota(jnp.int32, (HD, HD), 0) == lax.broadcasted_iota(jnp.int32, (HD, HD), 1)
    unit = unit.astype(jnp.float32).astype(jnp.bfloat16)
    copies = []
    for g in range(kvh):
        k_at = slice(g * HD, (g + 1) * HD)
        v_at = slice(width + g * HD, width + (g + 1) * HD)
        at = slice(g * rows, (g + 1) * rows)
        keys = jnp.concatenate([half_ref[:, k_at], cache_ref[:, k_at]], axis=0)
        values = jnp.concatenate([half_ref[:, v_at], cache_ref[:, v_at]], axis=0)
        s = dot(keys, head_rows(q_ref, g, gq), ((1,), (1,)))
        s = jnp.concatenate([s[:other], jnp.where(visible, s[other:], NEGATIVE)], axis=0)
        before = max_ref[:, at]
        top = jnp.maximum(before, jnp.max(s, axis=0, keepdims=True))
        weights = jnp.exp2((s - top) * SCALE2)
        factor = jnp.exp2((before - top) * SCALE2)
        value = acc_ref[:, at] * factor + dot(values, weights.astype(jnp.bfloat16), ((0,), (0,)))
        total = sum_ref[:, at] * factor + jnp.sum(weights, axis=0, keepdims=True)
        value = (value * (1.0 / total)).astype(jnp.bfloat16)
        for j in range(gq):
            turned = dot(unit, value[:, j * SPAN : (j + 1) * SPAN], ((1,), (1,)))
            stage[:, g * rows + j * HD : g * rows + (j + 1) * HD] = turned.astype(jnp.bfloat16)
        columns = pl.ds(g * gq * HD, gq * HD)
        copy = pltpu.make_async_copy(stage.at[:, columns], out_ref.at[:, columns], sems.at[g])
        copy.start()
        copies.append(copy)
    for copy in copies:
        copy.wait()


def on_device(q_new, kv_new, prompt_kv, cache_kv, ancestors, lengths):
    dom_count = lax.axis_size("dom")
    ctx_count = lax.axis_size("ctx")
    group, page_rows, _, width = cache_kv.shape
    tokens, q_width = q_new.shape
    kvh = width // HD
    q_rows = tokens * q_width // width
    half_rows = prompt_kv.shape[0] // 2
    shape = jax.ShapeDtypeStruct
    halves, outgoing, sources, limit = pl.pallas_call(
        functools.partial(pack_kernel, dom_count),
        out_shape=(
            pltpu.HBM((ctx_count, half_rows, 2 * width), jnp.bfloat16),
            pltpu.HBM((dom_count, RUN, page_rows, 2 * width), jnp.bfloat16),
            shape((group // RUN, page_rows, HD), jnp.bfloat16),
            shape((1, 128), jnp.int32),
        ),
        in_specs=[HBM] * 4,
        out_specs=(HBM, HBM, VMEM, VMEM),
        scratch_shapes=[
            pltpu.SMEM(ancestors.shape, jnp.int32),
            pltpu.SMEM(lengths.shape, jnp.int32),
            pltpu.VMEM((half_rows, 2, width), jnp.bfloat16),
            pltpu.VMEM((half_rows, 2 * width), jnp.bfloat16),
            pltpu.VMEM(cache_kv.shape, jnp.bfloat16),
            pltpu.VMEM((dom_count, RUN, page_rows, 2 * width), jnp.bfloat16),
            pltpu.SemaphoreType.DMA((5 + ctx_count,)),
        ],
        compiler_params=params(16),
        name="pack",
    )(*(pltpu.with_memory_space_constraint(x, pltpu.HBM) for x in (ancestors, lengths, prompt_kv, cache_kv)))

    own_half = lax.all_to_all(halves, "ctx", split_axis=0, concat_axis=0, tiled=True)
    own_half = own_half.reshape(ctx_count * half_rows, 2 * width)
    other_half = lax.ppermute(own_half, "dom", [(i, i ^ 1) for i in range(dom_count)])

    incoming = lax.all_to_all(outgoing, "dom", split_axis=0, concat_axis=0, tiled=True)
    routed = pl.pallas_call(
        route_kernel,
        out_shape=pltpu.HBM((group, page_rows, 2 * width), jnp.bfloat16),
        in_specs=[VMEM, VMEM],
        out_specs=HBM,
        scratch_shapes=[pltpu.VMEM((group, page_rows, 2 * width), jnp.bfloat16), pltpu.SemaphoreType.DMA],
        compiler_params=params(12),
        name="route",
    )(sources, incoming)
    pages = lax.all_to_all(routed, "ctx", split_axis=0, concat_axis=0, tiled=True)
    pages = pages.reshape(ctx_count * page_rows, 2 * width)

    key_count = SPAN + own_half.shape[0]
    acc, top, total = pl.pallas_call(
        first_kernel,
        out_shape=(
            shape((HD, kvh * q_rows), jnp.float32),
            shape((1, kvh * q_rows), jnp.float32),
            shape((1, kvh * q_rows), jnp.float32),
        ),
        in_specs=[VMEM] * 3,
        out_specs=(VMEM,) * 3,
        compiler_params=params(16),
        cost_estimate=pl.CostEstimate(
            flops=4 * tokens * q_width * key_count,
            bytes_accessed=2**23,
            transcendentals=tokens * q_width // HD * key_count,
        ),
        name="new_and_own_half",
    )(q_new, kv_new, own_half)
    return pl.pallas_call(
        last_kernel,
        out_shape=shape((tokens, q_width), jnp.bfloat16),
        in_specs=[VMEM] * 7,
        out_specs=HBM,
        scratch_shapes=[pltpu.VMEM((tokens, q_width), jnp.bfloat16), pltpu.SemaphoreType.DMA((kvh,))],
        compiler_params=params(16),
        name="other_half_and_cache",
    )(limit, q_new, other_half, pages, acc, top, total)


def solution(mesh):
    placed = (
        P(("dom", "ctx"), None),
        P(("dom", "ctx"), None, None),
        P("ctx", None, None),
        P("dom", "ctx", None, None),
        P(),
        P(),
    )
    return jax.shard_map(
        on_device, mesh=mesh, in_specs=placed, out_specs=P(("dom", "ctx"), None), check_vma=False
    )
```

time: 53.3 us -> 51.3 us (0.962)
  local copies, waits for them, and re-layouts: 5.84 us -> 0.95 us
  waiting for transfers between devices: 0.86 us -> 2.3 us
  blocking collectives: 30.4 us -> 31.3 us
  Pallas kernels: 12 us -> 12.6 us
    unnamed x12 -> x4, local copies, waits for them, and re-layouts: 5.84 us -> 0.95 us
    all_to_all x1, waiting for transfers between devices: 0.86 us -> 2.3 us  [on_device(): lax.all_to_all(routed, 'ctx', split_axis=0, concat_axis=0, tiled=True)]
    pallas_call x3, Pallas kernels: 5.79 us -> 6.83 us  [the longest x1 4.08 us: on_device(): pl.pallas_call(first_kernel, out_shape=(shape((HD, kvh * q_rows), jnp.flo...]
    all_to_all x1, blocking collectives: 8.7 us -> 9.41 us  [on_device(): lax.all_to_all(outgoing, 'dom', split_axis=0, concat_axis=0, tiled=True)]
where the time goes in v3:
time: 51.3 us; the launch traced here: 50.8 us
  blocking collectives  31.3 us (61%)
  Pallas kernels  12.6 us (25%)
  starting transfers between devices  3.6 us (7%)
  waiting for transfers between devices  2.3 us (4%)
  local copies, waits for them, and re-layouts  0.95 us (2%)
    all_to_all x1, blocking collectives, on_device(): lax.all_to_all(halves, 'ctx', split_axis=0, concat_axis=0, tiled=True)  21.9 us
    all_to_all x1, blocking collectives, on_device(): lax.all_to_all(outgoing, 'dom', split_axis=0, concat_axis=0, tiled=True)  9.41 us
    pallas_call x1, Pallas kernels, on_device(): pl.pallas_call(last_kernel, out_shape=shape((tokens, q_width), jnp.bfloat...  5.74 us
    pallas_call x1, Pallas kernels, on_device(): pl.pallas_call(first_kernel, out_shape=(shape((HD, kvh * q_rows), jnp.flo...  4.08 us
    all_to_all x1, starting transfers between devices, on_device(): lax.all_to_all(routed, 'ctx', split_axis=0, concat_axis=0, tiled=True)  3.6 us
    all_to_all x1, waiting for transfers between devices, on_device(): lax.all_to_all(routed, 'ctx', split_axis=0, concat_axis=0, tiled=True)  2.3 us
    pallas_call x1, Pallas kernels, on_device(): pl.pallas_call(functools.partial(pack_kernel, dom_count), out_shape=(pltp...  2.04 us
  transfers between devices with their start and end apart: 2, of which 1 were waited for; matrix products, arithmetic and copies ran while one was open for 0% of the time, Pallas kernels for 9%

profile of v3, /device:TPU:0, one launch (start us, length us, event | category | flops | bytes accessed | tf_op | source)
XLA Modules:
  0.0 50.8 jit_solution(11962269091985728607)
XLA Ops:
  0.0 0.0 copy-start
  0.0 2.0 %pack.1 = (bf16[8,32,1024]{2,1,0:T(8,128)(2,1)}, bf16[4,4,8,1024]{3,2,1,0:T(8,128)(2,1)}, bf16[2,8,128]{2,1,0:T(8,128)(2,1)S(1)}, s32[1,128]{1,0:T(1,128)S(1)}) custom-call(s32[32]{0:T(128)} %anc_hbm.1, s32[32]{0:T(128)} %len_hbm.1, bf16[64,2,512]{2,1,0:T(2,128)(2,1)} %prompt_hbm.1, bf16[8,8,2,512]{3,2,1,0:T(2,128)(2,1)} %cache_hbm.1), custom_call_target="tpu_custom_call" | custom-call | tf_op jit(solution)/shard_map/pack/pallas_call | solution.py:170
  2.0 21.9 %all_to_all.15 = bf16[8,32,1024]{2,1,0:T(8,128)(2,1)} all-to-all(bf16[8,32,1024]{2,1,0:T(8,128)(2,1)} %get-tuple-element.13), channel_id=1, replica_groups=mesh['dom'=4,'ctx'=8] {'ctx'}, dimensions={0} | all-to-all | bytes 1048576 | tf_op jit(solution)/shard_map/all_to_all | solution.py:193
  24.0 0.0 collective-permute-start
  24.0 9.4 %all_to_all.16.in_ref = bf16[4,4,8,1024]{3,2,1,0:T(8,128)(2,1)S(1)} all-to-all(bf16[4,4,8,1024]{3,2,1,0:T(8,128)(2,1)} %get-tuple-element.15), channel_id=1, replica_groups=mesh['dom'=4,'ctx'=8] {'dom'}, dimensions={0} | all-to-all | bytes 524288 | tf_op jit(solution)/shard_map/all_to_all | solution.py:197
  33.4 0.7 %route.1 = bf16[8,8,1024]{2,1,0:T(8,128)(2,1)} custom-call(bf16[2,8,128]{2,1,0:T(8,128)(2,1)S(1)} %get-tuple-element.14.source_ref, bf16[4,4,8,1024]{3,2,1,0:T(8,128)(2,1)S(1)} %all_to_all.16.in_ref), custom_call_target="tpu_custom_call" | custom-call | tf_op jit(solution)/shard_map/route/pallas_call | solution.py:198
  34.1 3.6 %all-to-all-start.2 = ((bf16[8,8,1024]{2,1,0:T(8,128)(2,1)}), bf16[8,8,1024]{2,1,0:T(8,128)(2,1)S(1)}, u32[]{:S(2)}, u32[]{:S(2)}) async-start(bf16[8,8,1024]{2,1,0:T(8,128)(2,1)} %route.1), calls=%async_computation.2 | async-start | bytes 262144 | tf_op jit(solution)/shard_map/all_to_all | solution.py:207
  37.7 0.0 copy-done
  37.7 0.0 copy-start.1
  37.7 0.9 %copy-done.1 = bf16[128,2,512]{2,1,0:T(2,128)(2,1)S(1)} copy-done((bf16[128,2,512]{2,1,0:T(2,128)(2,1)S(1)}, bf16[128,2,512]{2,1,0:T(2,128)(2,1)}, u32[]{:S(2)}) %copy-start.1) | copy-done | bytes 262168
  38.7 4.1 %new_and_own_half.1 = (f32[128,4096]{1,0:T(8,128)S(1)}, f32[1,4096]{1,0:T(1,128)S(1)}, f32[1,4096]{1,0:T(1,128)S(1)}) custom-call(bf16[128,4096]{1,0:T(8,128)(2,1)S(1)} %copy-done, bf16[128,2,512]{2,1,0:T(2,128)(2,1)S(1)} %copy-done.1, bf16[256,1024]{1,0:T(8,128)(2,1)} %bitcast.half_ref), custom_call_target="tpu_custom_call" | custom-call | flops 805306368 | bytes 8388608 | tf_op jit(solution)/shard_map/new_and_own_half/pallas_call | solution.py:211
  42.8 2.3 %all-to-all-done.2 = bf16[8,8,1024]{2,1,0:T(8,128)(2,1)S(1)} async-done(((bf16[8,8,1024]{2,1,0:T(8,128)(2,1)}), bf16[8,8,1024]{2,1,0:T(8,128)(2,1)S(1)}, u32[]{:S(2)}, u32[]{:S(2)}) %all-to-all-start.2) | async-done | bytes 131104 | tf_op jit(solution)/shard_map/all_to_all | solution.py:207
  45.1 0.0 collective-permute-done.half_ref
  45.1 5.7 %other_half_and_cache.1 = bf16[128,4096]{1,0:T(8,128)(2,1)} custom-call(s32[1,128]{1,0:T(1,128)S(1)} %get-tuple-element.12.limit_ref, bf16[128,4096]{1,0:T(8,128)(2,1)S(1)} %copy-done, bf16[256,1024]{1,0:T(8,128)(2,1)} %collective-permute-done.half_ref, bf16[64,1024]{1,0:T(8,128)(2,1)S(1)} %bitcast.2, f32[128,4096]{1,0:T(8,128)S(1)} %get-tuple-element.16.acc_ref, ...), custom_call_target="tpu_custom_call" | custom-call | tf_op jit(solution)/shard_map/other_half_and_cache/pallas_call | solution.py:228
Async XLA Ops:
  0.0 37.7 %copy-start = (bf16[128,4096]{1,0:T(8,128)(2,1)S(1)}, bf16[128,4096]{1,0:T(8,128)(2,1)}, u32[]{:S(2)}) copy-start(bf16[128,4096]{1,0:T(8,128)(2,1)} %q_ref.3) | copy-start | bytes 3145732
  24.0 21.1 %collective-permute-start = (bf16[256,1024]{1,0:T(8,128)(2,1)}, bf16[256,1024]{1,0:T(8,128)(2,1)}, u32[]{:S(2)}, u32[]{:S(2)}) collective-permute-start(bf16[256,1024]{1,0:T(8,128)(2,1)} %bitcast.half_ref), channel_id=1, source_target_pairs={{0,8},{8,0},{16,24},{24,16},{1,9},{9,1},{17,25},{25,17},{2,10},{10... | collective-permute-start | bytes 1572872 | tf_op jit(solution)/shard_map/ppermute | solution.py:195
  34.1 10.9 %all-to-all-start.2 = ((bf16[8,8,1024]{2,1,0:T(8,128)(2,1)}), bf16[8,8,1024]{2,1,0:T(8,128)(2,1)S(1)}, u32[]{:S(2)}, u32[]{:S(2)}) async-start(bf16[8,8,1024]{2,1,0:T(8,128)(2,1)} %route.1), calls=%async_computation.2 | async-start | bytes 262144 | tf_op jit(solution)/shard_map/all_to_all | solution.py:207
  37.7 1.0 %copy-start.1 = (bf16[128,2,512]{2,1,0:T(2,128)(2,1)S(1)}, bf16[128,2,512]{2,1,0:T(2,128)(2,1)}, u32[]{:S(2)}) copy-start(bf16[128,2,512]{2,1,0:T(2,128)(2,1)} %new_ref.1) | copy-start | bytes 786436

commit v4 on v2

v4 whole, which is shorter than its diff:
```python
import functools

import jax
import jax.numpy as jnp
from jax import lax
from jax.experimental import pallas as pl
from jax.experimental.pallas import tpu as pltpu
from jax.sharding import PartitionSpec as P

HD = 128
SPAN = 128
PAGE = 8
RUN = 4
Z = 4
NEGATIVE = -1e30
SCALE2 = HD ** (-0.5) * 1.4426950408889634
VMEM = pl.BlockSpec(memory_space=pltpu.VMEM)
HBM = pl.BlockSpec(memory_space=pltpu.HBM)


def params(mib):
    return pltpu.CompilerParams(vmem_limit_bytes=mib * 2**20)


def pack_kernel(dom_count, anc_hbm, len_hbm, prompt_hbm, cache_hbm, half_ref, *refs):
    out_refs = refs[:dom_count]
    far_ref, limit_ref, anc_ref, len_ref, prompt_ref, cache_ref, sems = refs[dom_count:]
    group = cache_ref.shape[0]
    dom = lax.axis_index("dom")
    rows, width = half_ref.shape
    from_row = pl.multiple_of((dom % 2) * rows, rows)
    prompt_in = pltpu.make_async_copy(prompt_hbm.at[pl.ds(from_row, rows)], prompt_ref, sems.at[0])
    anc_in = pltpu.make_async_copy(anc_hbm, anc_ref, sems.at[1])
    len_in = pltpu.make_async_copy(len_hbm, len_ref, sems.at[2])
    cache_in = pltpu.make_async_copy(cache_hbm, cache_ref, sems.at[3])
    prompt_in.start()
    anc_in.start()
    len_in.start()
    cache_in.start()
    runs = group // RUN
    anc_in.wait()
    len_in.wait()
    for run in range(runs):
        far = (anc_ref[dom * group + run * RUN] // group) ^ dom
        far_ref[run] = jnp.full(far_ref.shape[1:], far.astype(jnp.float32)).astype(jnp.bfloat16)
    particle = dom * group + lax.axis_index("ctx")
    limit_ref[...] = jnp.full(limit_ref.shape, len_ref[anc_ref[particle]] * PAGE)
    prompt_in.wait()
    half_ref[...] = prompt_ref[...].reshape(rows, width)
    cache_in.wait()
    for k, out_ref in enumerate(out_refs):
        for run in range(runs):
            first = (dom ^ k) * group + run * RUN

            @pl.when(anc_ref[first] // group == dom)
            def _(first=first, out_ref=out_ref):
                for slot in range(RUN):
                    local = anc_ref[first + slot] % group
                    out_ref[slot] = cache_ref[local].reshape(cache_ref.shape[1], width)


def route_kernel(far_ref, *refs):
    *in_refs, out_hbm, out_ref, sem = refs
    width = out_ref.shape[2]
    for run in range(far_ref.shape[0]):
        far = far_ref[run]
        for slot in range(RUN):
            picked = in_refs[0][slot]
            for k in range(1, len(in_refs)):
                here = jnp.concatenate([far == k] * (width // far.shape[1]), axis=1)
                picked = jnp.where(here, in_refs[k][slot], picked)
            out_ref[run * RUN + slot] = picked
    out = pltpu.make_async_copy(out_ref, out_hbm, sem)
    out.start()
    out.wait()


def head_rows(q_ref, g, gq):
    return jnp.concatenate(
        [q_ref[:, (g * gq + j) * HD : (g * gq + j + 1) * HD] for j in range(gq)], axis=0
    )


def dot_nt(a, b):
    return lax.dot_general(a, b, (((1,), (1,)), ((), ())), preferred_element_type=jnp.float32)


def dot_nn(a, b):
    return lax.dot_general(a, b, (((1,), (0,)), ((), ())), preferred_element_type=jnp.float32)


def attend_kernel(limit_ref, q_ref, new_ref, cache_ref, *refs):
    *pieces, out_ref, stage, sems = refs
    width = new_ref.shape[2]
    gen = cache_ref.shape[0]
    kvh = width // HD
    gq = q_ref.shape[1] // width
    new = new_ref[...].reshape(SPAN, 2 * width)
    old = sum(p.shape[0] for p in pieces)
    ones = jnp.ones((SPAN + old + gen, HD), jnp.bfloat16)
    token = lax.broadcasted_iota(jnp.int32, (SPAN, SPAN), 0)
    causal = lax.broadcasted_iota(jnp.int32, (SPAN, SPAN), 1) <= token
    visible = lax.broadcasted_iota(jnp.int32, (SPAN, gen), 1) < jnp.broadcast_to(limit_ref[:1], (SPAN, gen))
    copies = []
    for g in range(kvh):
        k_at = slice(g * HD, (g + 1) * HD)
        v_at = slice(width + g * HD, width + (g + 1) * HD)
        keys = jnp.concatenate([new[:, k_at]] + [p[:, k_at] for p in pieces] + [cache_ref[:, k_at]], axis=0)
        values = jnp.concatenate([new[:, v_at]] + [p[:, v_at] for p in pieces] + [cache_ref[:, v_at]], axis=0)
        values = jnp.concatenate([values, ones], axis=1)
        scores = dot_nt(head_rows(q_ref, g, gq), keys)
        weights = []
        for j in range(gq):
            s = scores[j * SPAN : (j + 1) * SPAN]
            s_new = jnp.where(causal, s[:, :SPAN], NEGATIVE)
            s_cache = jnp.where(visible, s[:, SPAN + old :], NEGATIVE)
            s = jnp.concatenate([s_new, s[:, SPAN : SPAN + old], s_cache], axis=1)
            top = jnp.max(s, axis=1, keepdims=True)
            weights.append(jnp.exp2((s - top) * SCALE2).astype(jnp.bfloat16))
        out = dot_nn(jnp.concatenate(weights, axis=0), values)
        out = (out[:, :HD] / out[:, HD:]).astype(jnp.bfloat16)
        for j in range(gq):
            stage[:, (g * gq + j) * HD : (g * gq + j + 1) * HD] = out[j * SPAN : (j + 1) * SPAN]
        columns = pl.ds(g * gq * HD, gq * HD)
        copy = pltpu.make_async_copy(stage.at[:, columns], out_ref.at[:, columns], sems.at[g])
        copy.start()
        copies.append(copy)
    for copy in copies:
        copy.wait()


def swap(x, axis, distance):
    return lax.ppermute(x, axis, [(i, i ^ distance) for i in range(lax.axis_size(axis))])


def on_device(q_new, kv_new, prompt_kv, cache_kv, ancestors, lengths):
    dom_count = lax.axis_size("dom")
    ctx_count = lax.axis_size("ctx")
    y_count = ctx_count // Z
    group, page_rows, _, width = cache_kv.shape
    tokens, q_width = q_new.shape
    kvh = width // HD
    half_rows = prompt_kv.shape[0] // 2
    shape = jax.ShapeDtypeStruct
    half, *rest = pl.pallas_call(
        functools.partial(pack_kernel, dom_count),
        out_shape=(
            shape((half_rows, 2 * width), jnp.bfloat16),
            *[shape((RUN, page_rows, 2 * width), jnp.bfloat16)] * dom_count,
            shape((group // RUN, page_rows, HD), jnp.bfloat16),
            shape((8, ctx_count * page_rows), jnp.int32),
        ),
        in_specs=[HBM] * 4,
        out_specs=(VMEM,) * (3 + dom_count),
        scratch_shapes=[
            pltpu.SMEM(ancestors.shape, jnp.int32),
            pltpu.SMEM(lengths.shape, jnp.int32),
            pltpu.VMEM((half_rows, 2, width), jnp.bfloat16),
            pltpu.VMEM(cache_kv.shape, jnp.bfloat16),
            pltpu.SemaphoreType.DMA((4,)),
        ],
        compiler_params=params(12),
        name="pack",
    )(*(pltpu.with_memory_space_constraint(x, pltpu.HBM) for x in (ancestors, lengths, prompt_kv, cache_kv)))
    outgoing, far, limit = rest[:dom_count], rest[dom_count], rest[dom_count + 1]

    pieces = [half] + [swap(half, "ctx", k * y_count) for k in range(1, Z)]
    pieces += [swap(p, "ctx", k) for k in range(1, y_count) for p in pieces[:Z]]
    pieces += [swap(p, "dom", 1) for p in pieces]

    incoming = outgoing[:1] + [swap(outgoing[k], "dom", k) for k in range(1, dom_count)]
    routed = pl.pallas_call(
        route_kernel,
        out_shape=pltpu.HBM((group, page_rows, 2 * width), jnp.bfloat16),
        in_specs=[VMEM] * (1 + dom_count),
        out_specs=HBM,
        scratch_shapes=[pltpu.VMEM((group, page_rows, 2 * width), jnp.bfloat16), pltpu.SemaphoreType.DMA],
        compiler_params=params(12),
        name="route",
    )(far, *incoming)
    pages = lax.all_to_all(routed, "ctx", split_axis=0, concat_axis=0, tiled=True)
    pages = pages.reshape(ctx_count * page_rows, 2 * width)

    return pl.pallas_call(
        attend_kernel,
        out_shape=shape((tokens, q_width), jnp.bfloat16),
        in_specs=[VMEM] * (4 + len(pieces)),
        out_specs=HBM,
        scratch_shapes=[pltpu.VMEM((tokens, q_width), jnp.bfloat16), pltpu.SemaphoreType.DMA((kvh,))],
        compiler_params=params(40 if prompt_kv.shape[0] * ctx_count > 1024 else 24),
        name="attend",
    )(limit, q_new, kv_new, pages, *pieces)


def solution(mesh):
    placed = (
        P(("dom", "ctx"), None),
        P(("dom", "ctx"), None, None),
        P("ctx", None, None),
        P("dom", "ctx", None, None),
        P(),
        P(),
    )
    return jax.shard_map(
        on_device, mesh=mesh, in_specs=placed, out_specs=P(("dom", "ctx"), None), check_vma=False
    )
```

time: 53.3 us -> 40.8 us (0.77)
  blocking collectives: 30.4 us -> 0 us
  starting transfers between devices: 3.59 us -> 19.8 us
  waiting for transfers between devices: 0.86 us -> 12.1 us
  Pallas kernels: 12 us -> 7.33 us
  local copies, waits for them, and re-layouts: 5.84 us -> 1.23 us
    all_to_all x2 -> x0, blocking collectives: 30.4 us -> none  [the longest x1 21.7 us: on_device(): lax.all_to_all(halves, 'ctx', split_axis=0, concat_axis=0, tiled=True)]
    ppermute x1 -> x18, starting transfers between devices: 0.01 us -> 13.9 us  [swap(): lax.ppermute(x, axis, [(i, i ^ distance) for i in range(lax.axis_size(axi...]
    ppermute x1 -> x18, waiting for transfers between devices: 0.01 us -> 12.1 us  [swap(): lax.ppermute(x, axis, [(i, i ^ distance) for i in range(lax.axis_size(axi...]
    unnamed x12 -> x4, local copies, waits for them, and re-layouts: 5.84 us -> 1.23 us
    pallas_call x3 -> x2, Pallas kernels: 10.8 us -> 6.17 us  [the longest x1 5.45 us: on_device(): pl.pallas_call(attend_kernel, out_shape=shape((tokens, q_width), jnp.bflo...]
    all_to_all x1, starting transfers between devices: 3.59 us -> 5.88 us  [on_device(): lax.all_to_all(routed, 'ctx', split_axis=0, concat_axis=0, tiled=True)]
    all_to_all x1, waiting for transfers between devices: 0.86 us -> 0.01 us  [on_device(): lax.all_to_all(routed, 'ctx', split_axis=0, concat_axis=0, tiled=True)]
  transfers between devices with their start and end apart: 2 -> 19, of which waited for: 1 -> 8; matrix products, arithmetic and copies ran while one was open for 0% -> 0% of each run, Pallas kernels for 9% -> 0%
where the time goes in v4:
time: 40.8 us; the launch traced here: 40.5 us
  starting transfers between devices  19.8 us (49%)
  waiting for transfers between devices  12.1 us (30%)
  Pallas kernels  7.33 us (18%)
  local copies, waits for them, and re-layouts  1.23 us (3%)
    ppermute x18, starting transfers between devices, swap(): lax.ppermute(x, axis, [(i, i ^ distance) for i in range(lax.axis_size(axi...  13.9 us
    ppermute x18, waiting for transfers between devices, swap(): lax.ppermute(x, axis, [(i, i ^ distance) for i in range(lax.axis_size(axi...  12.1 us
    all_to_all x1, starting transfers between devices, on_device(): lax.all_to_all(routed, 'ctx', split_axis=0, concat_axis=0, tiled=True)  5.88 us
    pallas_call x1, Pallas kernels, on_device(): pl.pallas_call(attend_kernel, out_shape=shape((tokens, q_width), jnp.bflo...  5.45 us
    unnamed x4, local copies, waits for them, and re-layouts  1.23 us
    pallas_call x1, Pallas kernels, on_device(): pl.pallas_call(functools.partial(pack_kernel, dom_count), out_shape=(shap...  1.16 us
  transfers between devices with their start and end apart: 19, of which 8 were waited for; matrix products, arithmetic and copies ran while one was open for 0% of the time, Pallas kernels for 0%

profile of v4, /device:TPU:0, one launch (start us, length us, event | category | flops | bytes accessed | tf_op | source)
XLA Modules:
  0.0 40.5 jit_solution(2560137940435229797)
XLA Ops:
  0.0 1.2 %pack.1 = (bf16[32,1024]{1,0:T(8,128)(2,1)S(1)}, bf16[4,8,1024]{2,1,0:T(8,128)(2,1)S(1)}, bf16[4,8,1024]{2,1,0:T(8,128)(2,1)S(1)}, bf16[4,8,1024]{2,1,0:T(8,128)...) custom-call(s32[32]{0:T(128)} %anc_hbm.1, s32[32]{0:T(128)} %len_hbm.1, ...), custom_call_target="tpu_custom_call" | custom-call | tf_op jit(solution)/shard_map/pack/pallas_call | solution.py:145
  1.2 0.4 collective-permute-start
  1.6 2.6 %collective-permute-start.1 = (bf16[4,8,1024]{2,1,0:T(8,128)(2,1)S(1)}, bf16[4,8,1024]{2,1,0:T(8,128)(2,1)S(1)}, u32[]{:S(2)}, u32[]{:S(2)}) collective-permute-start(bf16[4,8,1024]{2,1,0:T(8,128)(2,1)S(1)} %get-tuple-element.16), channel_id=1, source_target_pairs={{0,16},{8,24},{16,0},{24,8},{1,17},{9,25},{17,1},{25,9},{2,18},{10... | collective-permute-start | bytes 196616 | tf_op jit(solution)/shard_map/ppermute | solution.py:133
  4.2 0.1 collective-permute-start.2
  4.3 0.0 collective-permute-done.refs_1_
  4.3 2.6 %collective-permute-done.1.refs_2_ = bf16[4,8,1024]{2,1,0:T(8,128)(2,1)S(1)} collective-permute-done((bf16[4,8,1024]{2,1,0:T(8,128)(2,1)S(1)}, bf16[4,8,1024]{2,1,0:T(8,128)(2,1)S(1)}, u32[]{:S(2)}, u32[]{:S(2)}) %collective-permute-start.1) | collective-permute-done | bytes 65568 | tf_op jit(solution)/shard_map/ppermute | solution.py:133
  6.9 1.4 %collective-permute-done.2.refs_3_ = bf16[4,8,1024]{2,1,0:T(8,128)(2,1)S(1)} collective-permute-done((bf16[4,8,1024]{2,1,0:T(8,128)(2,1)S(1)}, bf16[4,8,1024]{2,1,0:T(8,128)(2,1)S(1)}, u32[]{:S(2)}, u32[]{:S(2)}) %collective-permute-start.2) | collective-permute-done | bytes 65568 | tf_op jit(solution)/shard_map/ppermute | solution.py:133
  8.2 0.0 copy-start.1
  8.2 0.7 %route.1 = bf16[8,8,1024]{2,1,0:T(8,128)(2,1)} custom-call(bf16[2,8,128]{2,1,0:T(8,128)(2,1)S(1)} %get-tuple-element.13.far_ref, bf16[4,8,1024]{2,1,0:T(8,128)(2,1)S(1)} %get-tuple-element.14.refs_0_, bf16[4,8,1024]{2,1,0:T(8,128)(2,1)S(1)} %collective-permute-done.refs_1_, bf16[4,8,1024]{2,1,0:T(8,128)(2,1)S(1)} %collective-permute-done.1.refs_2_, ...), custom_call_target="tpu_custom_call" | custom-call | tf_op jit(solution)/shard_map/route/pallas_call | solution.py:172
  9.0 5.9 %all-to-all-start = ((bf16[8,8,1024]{2,1,0:T(8,128)(2,1)}), bf16[8,8,1024]{2,1,0:T(8,128)(2,1)S(1)}, u32[]{:S(2)}, u32[]{:S(2)}) async-start(bf16[8,8,1024]{2,1,0:T(8,128)(2,1)} %route.1), calls=%async_computation | async-start | bytes 262144 | tf_op jit(solution)/shard_map/all_to_all | solution.py:181
  14.9 2.0 %collective-permute-start.6 = (bf16[32,1024]{1,0:T(8,128)(2,1)S(1)}, bf16[32,1024]{1,0:T(8,128)(2,1)S(1)}, u32[]{:S(2)}, u32[]{:S(2)}) collective-permute-start(bf16[32,1024]{1,0:T(8,128)(2,1)S(1)} %get-tuple-element.18.refs_0_), channel_id=1, source_target_pairs={{0,1},{1,0},{2,3},{3,2},{4,5},{5,4},{6,7},{7,6},{8,9},{9,8},{10,11... | collective-permute-start | bytes 196616 | tf_op jit(solution)/shard_map/ppermute | solution.py:133
  16.9 3.3 %collective-permute-start.5 = (bf16[32,1024]{1,0:T(8,128)(2,1)S(1)}, bf16[32,1024]{1,0:T(8,128)(2,1)S(1)}, u32[]{:S(2)}, u32[]{:S(2)}) collective-permute-start(bf16[32,1024]{1,0:T(8,128)(2,1)S(1)} %get-tuple-element.18.refs_0_), channel_id=1, source_target_pairs={{0,6},{1,7},{2,4},{3,5},{4,2},{5,3},{6,0},{7,1},{8,14},{9,15},{10,... | collective-permute-start | bytes 196616 | tf_op jit(solution)/shard_map/ppermute | solution.py:133
  20.1 0.0 collective-permute-start.10
  20.1 0.0 collective-permute-start.4
  20.1 1.1 %collective-permute-start.3 = (bf16[32,1024]{1,0:T(8,128)(2,1)S(1)}, bf16[32,1024]{1,0:T(8,128)(2,1)S(1)}, u32[]{:S(2)}, u32[]{:S(2)}) collective-permute-start(bf16[32,1024]{1,0:T(8,128)(2,1)S(1)} %get-tuple-element.18.refs_0_), channel_id=1, source_target_pairs={{0,2},{1,3},{2,0},{3,1},{4,6},{5,7},{6,4},{7,5},{8,10},{9,11},{10,... | collective-permute-start | bytes 196616 | tf_op jit(solution)/shard_map/ppermute | solution.py:133
  21.3 0.0 collective-permute-done.6.refs_4_
  21.3 0.0 collective-permute-start.14
  21.3 1.7 %collective-permute-done.5.refs_3_ = bf16[32,1024]{1,0:T(8,128)(2,1)S(1)} collective-permute-done((bf16[32,1024]{1,0:T(8,128)(2,1)S(1)}, bf16[32,1024]{1,0:T(8,128)(2,1)S(1)}, u32[]{:S(2)}, u32[]{:S(2)}) %collective-permute-start.5) | collective-permute-done | bytes 65568 | tf_op jit(solution)/shard_map/ppermute | solution.py:133
  23.0 0.0 collective-permute-start.13
  23.0 0.0 collective-permute-done.10.refs_8_
  23.0 1.8 %collective-permute-start.9 = (bf16[32,1024]{1,0:T(8,128)(2,1)S(1)}, bf16[32,1024]{1,0:T(8,128)(2,1)S(1)}, u32[]{:S(2)}, u32[]{:S(2)}) collective-permute-start(bf16[32,1024]{1,0:T(8,128)(2,1)S(1)} %collective-permute-done.5.refs_3_), channel_id=1, source_target_pairs={{0,1},{1,0},{2,3},{3,2},{4,5},{5,4},{6,7},{7,6},{8,9},{9,8},{10,11... | collective-permute-start | bytes 196616 | tf_op jit(solution)/shard_map/ppermute | solution.py:133
  24.8 2.4 %collective-permute-done.4.refs_2_ = bf16[32,1024]{1,0:T(8,128)(2,1)S(1)} collective-permute-done((bf16[32,1024]{1,0:T(8,128)(2,1)S(1)}, bf16[32,1024]{1,0:T(8,128)(2,1)S(1)}, u32[]{:S(2)}, u32[]{:S(2)}) %collective-permute-start.4) | collective-permute-done | bytes 65568 | tf_op jit(solution)/shard_map/ppermute | solution.py:133
  27.2 1.1 %collective-permute-start.8 = (bf16[32,1024]{1,0:T(8,128)(2,1)S(1)}, bf16[32,1024]{1,0:T(8,128)(2,1)S(1)}, u32[]{:S(2)}, u32[]{:S(2)}) collective-permute-start(bf16[32,1024]{1,0:T(8,128)(2,1)S(1)} %collective-permute-done.4.refs_2_), channel_id=1, source_target_pairs={{0,1},{1,0},{2,3},{3,2},{4,5},{5,4},{6,7},{7,6},{8,9},{9,8},{10,11... | collective-permute-start | bytes 196616 | tf_op jit(solution)/shard_map/ppermute | solution.py:133
  28.3 0.0 collective-permute-done.3.refs_1_
  28.3 0.9 %collective-permute-start.7 = (bf16[32,1024]{1,0:T(8,128)(2,1)S(1)}, bf16[32,1024]{1,0:T(8,128)(2,1)S(1)}, u32[]{:S(2)}, u32[]{:S(2)}) collective-permute-start(bf16[32,1024]{1,0:T(8,128)(2,1)S(1)} %collective-permute-done.3.refs_1_), channel_id=1, source_target_pairs={{0,1},{1,0},{2,3},{3,2},{4,5},{5,4},{6,7},{7,6},{8,9},{9,8},{10,11... | collective-permute-start | bytes 196616 | tf_op jit(solution)/shard_map/ppermute | solution.py:133
  29.2 0.0 collective-permute-done.14.refs_12_
  29.3 0.0 collective-permute-start.12
  29.3 0.0 collective-permute-done.13.refs_11_
  29.3 0.5 %collective-permute-start.11 = (bf16[32,1024]{1,0:T(8,128)(2,1)S(1)}, bf16[32,1024]{1,0:T(8,128)(2,1)S(1)}, u32[]{:S(2)}, u32[]{:S(2)}) collective-permute-start(bf16[32,1024]{1,0:T(8,128)(2,1)S(1)} %collective-permute-done.3.refs_1_), channel_id=1, source_target_pairs={{0,8},{8,0},{16,24},{24,16},{1,9},{9,1},{17,25},{25,17},{2,10},{10... | collective-permute-start | bytes 196616 | tf_op jit(solution)/shard_map/ppermute | solution.py:133
  29.8 0.0 collective-permute-done.9.refs_7_
  29.8 0.1 collective-permute-start.17
  29.8 1.6 %collective-permute-done.8.refs_6_ = bf16[32,1024]{1,0:T(8,128)(2,1)S(1)} collective-permute-done((bf16[32,1024]{1,0:T(8,128)(2,1)S(1)}, bf16[32,1024]{1,0:T(8,128)(2,1)S(1)}, u32[]{:S(2)}, u32[]{:S(2)}) %collective-permute-start.8) | collective-permute-done | bytes 65568 | tf_op jit(solution)/shard_map/ppermute | solution.py:133
  31.5 0.0 collective-permute-start.16
  31.5 1.1 %collective-permute-done.7.refs_5_ = bf16[32,1024]{1,0:T(8,128)(2,1)S(1)} collective-permute-done((bf16[32,1024]{1,0:T(8,128)(2,1)S(1)}, bf16[32,1024]{1,0:T(8,128)(2,1)S(1)}, u32[]{:S(2)}, u32[]{:S(2)}) %collective-permute-start.7) | collective-permute-done | bytes 65568 | tf_op jit(solution)/shard_map/ppermute | solution.py:133
  32.6 0.0 collective-permute-start.15
  32.6 0.0 collective-permute-done.12.refs_10_
  32.6 0.0 collective-permute-done.11.refs_9_
  32.6 0.0 collective-permute-done.17.refs_15_
  32.6 0.1 collective-permute-done.16.refs_14_
  32.7 1.1 %collective-permute-done.15.refs_13_ = bf16[32,1024]{1,0:T(8,128)(2,1)S(1)} collective-permute-done((bf16[32,1024]{1,0:T(8,128)(2,1)S(1)}, bf16[32,1024]{1,0:T(8,128)(2,1)S(1)}, u32[]{:S(2)}, u32[]{:S(2)}) %collective-permute-start.15) | collective-permute-done | bytes 65568 | tf_op jit(solution)/shard_map/ppermute | solution.py:133
  33.8 0.0 all-to-all-done
  33.8 0.0 copy-done.1
  33.8 0.0 copy-start
  33.8 1.2 %copy-done = bf16[128,4096]{1,0:T(8,128)(2,1)S(1)} copy-done((bf16[128,4096]{1,0:T(8,128)(2,1)S(1)}, bf16[128,4096]{1,0:T(8,128)(2,1)}, u32[]{:S(2)}) %copy-start) | copy-done | bytes 1048600
  35.1 5.5 %attend.1 = bf16[128,4096]{1,0:T(8,128)(2,1)} custom-call(s32[8,64]{1,0:T(8,128)S(1)} %get-tuple-element.12.limit_ref, bf16[128,4096]{1,0:T(8,128)(2,1)S(1)} %copy-done, bf16[128,2,512]{2,1,0:T(2,128)(2,1)S(1)} %copy-done.1, bf16[64,1024]{1,0:T(8,128)(2,1)S(1)} %bitcast.1, bf16[32,1024]{1,0:T(8,128)(2,1)S(1)} %get-tuple-element.18.refs_0_, ...), custom_call_target="tpu_custom_call" | custom-call | tf_op jit(solution)/shard_map/attend/pallas_call | solution.py:184
Async XLA Ops:
  1.2 3.1 %collective-permute-start = (bf16[4,8,1024]{2,1,0:T(8,128)(2,1)S(1)}, bf16[4,8,1024]{2,1,0:T(8,128)(2,1)S(1)}, u32[]{:S(2)}, u32[]{:S(2)}) collective-permute-start(bf16[4,8,1024]{2,1,0:T(8,128)(2,1)S(1)} %get-tuple-element.15), channel_id=1, source_target_pairs={{0,8},{8,0},{16,24},{24,16},{1,9},{9,1},{17,25},{25,17},{2,10},{10... | collective-permute-start | bytes 196616 | tf_op jit(solution)/shard_map/ppermute | solution.py:133
  1.6 5.3 %collective-permute-start.1 = (bf16[4,8,1024]{2,1,0:T(8,128)(2,1)S(1)}, bf16[4,8,1024]{2,1,0:T(8,128)(2,1)S(1)}, u32[]{:S(2)}, u32[]{:S(2)}) collective-permute-start(bf16[4,8,1024]{2,1,0:T(8,128)(2,1)S(1)} %get-tuple-element.16), channel_id=1, source_target_pairs={{0,16},{8,24},{16,0},{24,8},{1,17},{9,25},{17,1},{25,9},{2,18},{10... | collective-permute-start | bytes 196616 | tf_op jit(solution)/shard_map/ppermute | solution.py:133
  4.2 4.0 %collective-permute-start.2 = (bf16[4,8,1024]{2,1,0:T(8,128)(2,1)S(1)}, bf16[4,8,1024]{2,1,0:T(8,128)(2,1)S(1)}, u32[]{:S(2)}, u32[]{:S(2)}) collective-permute-start(bf16[4,8,1024]{2,1,0:T(8,128)(2,1)S(1)} %get-tuple-element.17), channel_id=1, source_target_pairs={{0,24},{8,16},{16,8},{24,0},{1,25},{9,17},{17,9},{25,1},{2,26},{10... | collective-permute-start | bytes 196616 | tf_op jit(solution)/shard_map/ppermute | solution.py:133
  8.2 25.6 %copy-start.1 = (bf16[128,2,512]{2,1,0:T(2,128)(2,1)S(1)}, bf16[128,2,512]{2,1,0:T(2,128)(2,1)}, u32[]{:S(2)}) copy-start(bf16[128,2,512]{2,1,0:T(2,128)(2,1)} %new_ref.1) | copy-start | bytes 786436
  9.0 24.9 %all-to-all-start = ((bf16[8,8,1024]{2,1,0:T(8,128)(2,1)}), bf16[8,8,1024]{2,1,0:T(8,128)(2,1)S(1)}, u32[]{:S(2)}, u32[]{:S(2)}) async-start(bf16[8,8,1024]{2,1,0:T(8,128)(2,1)} %route.1), calls=%async_computation | async-start | bytes 262144 | tf_op jit(solution)/shard_map/all_to_all | solution.py:181
  14.9 6.4 %collective-permute-start.6 = (bf16[32,1024]{1,0:T(8,128)(2,1)S(1)}, bf16[32,1024]{1,0:T(8,128)(2,1)S(1)}, u32[]{:S(2)}, u32[]{:S(2)}) collective-permute-start(bf16[32,1024]{1,0:T(8,128)(2,1)S(1)} %get-tuple-element.18.refs_0_), channel_id=1, source_target_pairs={{0,1},{1,0},{2,3},{3,2},{4,5},{5,4},{6,7},{7,6},{8,9},{9,8},{10,11... | collective-permute-start | bytes 196616 | tf_op jit(solution)/shard_map/ppermute | solution.py:133
  16.9 6.1 %collective-permute-start.5 = (bf16[32,1024]{1,0:T(8,128)(2,1)S(1)}, bf16[32,1024]{1,0:T(8,128)(2,1)S(1)}, u32[]{:S(2)}, u32[]{:S(2)}) collective-permute-start(bf16[32,1024]{1,0:T(8,128)(2,1)S(1)} %get-tuple-element.18.refs_0_), channel_id=1, source_target_pairs={{0,6},{1,7},{2,4},{3,5},{4,2},{5,3},{6,0},{7,1},{8,14},{9,15},{10,... | collective-permute-start | bytes 196616 | tf_op jit(solution)/shard_map/ppermute | solution.py:133
  20.1 2.9 %collective-permute-start.10 = (bf16[32,1024]{1,0:T(8,128)(2,1)S(1)}, bf16[32,1024]{1,0:T(8,128)(2,1)S(1)}, u32[]{:S(2)}, u32[]{:S(2)}) collective-permute-start(bf16[32,1024]{1,0:T(8,128)(2,1)S(1)} %get-tuple-element.18.refs_0_), channel_id=1, source_target_pairs={{0,8},{8,0},{16,24},{24,16},{1,9},{9,1},{17,25},{25,17},{2,10},{10... | collective-permute-start | bytes 196616 | tf_op jit(solution)/shard_map/ppermute | solution.py:133
  20.1 7.1 %collective-permute-start.4 = (bf16[32,1024]{1,0:T(8,128)(2,1)S(1)}, bf16[32,1024]{1,0:T(8,128)(2,1)S(1)}, u32[]{:S(2)}, u32[]{:S(2)}) collective-permute-start(bf16[32,1024]{1,0:T(8,128)(2,1)S(1)} %get-tuple-element.18.refs_0_), channel_id=1, source_target_pairs={{0,4},{1,5},{2,6},{3,7},{4,0},{5,1},{6,2},{7,3},{8,12},{9,13},{10,... | collective-permute-start | bytes 196616 | tf_op jit(solution)/shard_map/ppermute | solution.py:133
  20.1 8.2 %collective-permute-start.3 = (bf16[32,1024]{1,0:T(8,128)(2,1)S(1)}, bf16[32,1024]{1,0:T(8,128)(2,1)S(1)}, u32[]{:S(2)}, u32[]{:S(2)}) collective-permute-start(bf16[32,1024]{1,0:T(8,128)(2,1)S(1)} %get-tuple-element.18.refs_0_), channel_id=1, source_target_pairs={{0,2},{1,3},{2,0},{3,1},{4,6},{5,7},{6,4},{7,5},{8,10},{9,11},{10,... | collective-permute-start | bytes 196616 | tf_op jit(solution)/shard_map/ppermute | solution.py:133
  21.3 8.0 %collective-permute-start.14 = (bf16[32,1024]{1,0:T(8,128)(2,1)S(1)}, bf16[32,1024]{1,0:T(8,128)(2,1)S(1)}, u32[]{:S(2)}, u32[]{:S(2)}) collective-permute-start(bf16[32,1024]{1,0:T(8,128)(2,1)S(1)} %collective-permute-done.6.refs_4_), channel_id=1, source_target_pairs={{0,8},{8,0},{16,24},{24,16},{1,9},{9,1},{17,25},{25,17},{2,10},{10... | collective-permute-start | bytes 196616 | tf_op jit(solution)/shard_map/ppermute | solution.py:133
  23.0 6.3 %collective-permute-start.13 = (bf16[32,1024]{1,0:T(8,128)(2,1)S(1)}, bf16[32,1024]{1,0:T(8,128)(2,1)S(1)}, u32[]{:S(2)}, u32[]{:S(2)}) collective-permute-start(bf16[32,1024]{1,0:T(8,128)(2,1)S(1)} %collective-permute-done.5.refs_3_), channel_id=1, source_target_pairs={{0,8},{8,0},{16,24},{24,16},{1,9},{9,1},{17,25},{25,17},{2,10},{10... | collective-permute-start | bytes 196616 | tf_op jit(solution)/shard_map/ppermute | solution.py:133
  23.0 6.8 %collective-permute-start.9 = (bf16[32,1024]{1,0:T(8,128)(2,1)S(1)}, bf16[32,1024]{1,0:T(8,128)(2,1)S(1)}, u32[]{:S(2)}, u32[]{:S(2)}) collective-permute-start(bf16[32,1024]{1,0:T(8,128)(2,1)S(1)} %collective-permute-done.5.refs_3_), channel_id=1, source_target_pairs={{0,1},{1,0},{2,3},{3,2},{4,5},{5,4},{6,7},{7,6},{8,9},{9,8},{10,11... | collective-permute-start | bytes 196616 | tf_op jit(solution)/shard_map/ppermute | solution.py:133
  27.2 4.3 %collective-permute-start.8 = (bf16[32,1024]{1,0:T(8,128)(2,1)S(1)}, bf16[32,1024]{1,0:T(8,128)(2,1)S(1)}, u32[]{:S(2)}, u32[]{:S(2)}) collective-permute-start(bf16[32,1024]{1,0:T(8,128)(2,1)S(1)} %collective-permute-done.4.refs_2_), channel_id=1, source_target_pairs={{0,1},{1,0},{2,3},{3,2},{4,5},{5,4},{6,7},{7,6},{8,9},{9,8},{10,11... | collective-permute-start | bytes 196616 | tf_op jit(solution)/shard_map/ppermute | solution.py:133
  28.3 4.3 %collective-permute-start.7 = (bf16[32,1024]{1,0:T(8,128)(2,1)S(1)}, bf16[32,1024]{1,0:T(8,128)(2,1)S(1)}, u32[]{:S(2)}, u32[]{:S(2)}) collective-permute-start(bf16[32,1024]{1,0:T(8,128)(2,1)S(1)} %collective-permute-done.3.refs_1_), channel_id=1, source_target_pairs={{0,1},{1,0},{2,3},{3,2},{4,5},{5,4},{6,7},{7,6},{8,9},{9,8},{10,11... | collective-permute-start | bytes 196616 | tf_op jit(solution)/shard_map/ppermute | solution.py:133
  29.3 3.3 %collective-permute-start.12 = (bf16[32,1024]{1,0:T(8,128)(2,1)S(1)}, bf16[32,1024]{1,0:T(8,128)(2,1)S(1)}, u32[]{:S(2)}, u32[]{:S(2)}) collective-permute-start(bf16[32,1024]{1,0:T(8,128)(2,1)S(1)} %collective-permute-done.4.refs_2_), channel_id=1, source_target_pairs={{0,8},{8,0},{16,24},{24,16},{1,9},{9,1},{17,25},{25,17},{2,10},{10... | collective-permute-start | bytes 196616 | tf_op jit(solution)/shard_map/ppermute | solution.py:133
  29.3 3.3 %collective-permute-start.11 = (bf16[32,1024]{1,0:T(8,128)(2,1)S(1)}, bf16[32,1024]{1,0:T(8,128)(2,1)S(1)}, u32[]{:S(2)}, u32[]{:S(2)}) collective-permute-start(bf16[32,1024]{1,0:T(8,128)(2,1)S(1)} %collective-permute-done.3.refs_1_), channel_id=1, source_target_pairs={{0,8},{8,0},{16,24},{24,16},{1,9},{9,1},{17,25},{25,17},{2,10},{10... | collective-permute-start | bytes 196616 | tf_op jit(solution)/shard_map/ppermute | solution.py:133
  29.8 2.8 %collective-permute-start.17 = (bf16[32,1024]{1,0:T(8,128)(2,1)S(1)}, bf16[32,1024]{1,0:T(8,128)(2,1)S(1)}, u32[]{:S(2)}, u32[]{:S(2)}) collective-permute-start(bf16[32,1024]{1,0:T(8,128)(2,1)S(1)} %collective-permute-done.9.refs_7_), channel_id=1, source_target_pairs={{0,8},{8,0},{16,24},{24,16},{1,9},{9,1},{17,25},{25,17},{2,10},{10... | collective-permute-start | bytes 196616 | tf_op jit(solution)/shard_map/ppermute | solution.py:133
  31.5 1.3 %collective-permute-start.16 = (bf16[32,1024]{1,0:T(8,128)(2,1)S(1)}, bf16[32,1024]{1,0:T(8,128)(2,1)S(1)}, u32[]{:S(2)}, u32[]{:S(2)}) collective-permute-start(bf16[32,1024]{1,0:T(8,128)(2,1)S(1)} %collective-permute-done.8.refs_6_), channel_id=1, source_target_pairs={{0,8},{8,0},{16,24},{24,16},{1,9},{9,1},{17,25},{25,17},{2,10},{10... | collective-permute-start | bytes 196616 | tf_op jit(solution)/shard_map/ppermute | solution.py:133
  32.6 1.3 %collective-permute-start.15 = (bf16[32,1024]{1,0:T(8,128)(2,1)S(1)}, bf16[32,1024]{1,0:T(8,128)(2,1)S(1)}, u32[]{:S(2)}, u32[]{:S(2)}) collective-permute-start(bf16[32,1024]{1,0:T(8,128)(2,1)S(1)} %collective-permute-done.7.refs_5_), channel_id=1, source_target_pairs={{0,8},{8,0},{16,24},{24,16},{1,9},{9,1},{17,25},{25,17},{2,10},{10... | collective-permute-start | bytes 196616 | tf_op jit(solution)/shard_map/ppermute | solution.py:133
  33.8 1.2 %copy-start = (bf16[128,4096]{1,0:T(8,128)(2,1)S(1)}, bf16[128,4096]{1,0:T(8,128)(2,1)}, u32[]{:S(2)}) copy-start(bf16[128,4096]{1,0:T(8,128)(2,1)} %q_ref.1) | copy-start | bytes 3145732

commit v5 on v4

--- a/solution.py
+++ b/solution.py
@@ -59,20 +59,30 @@
                     out_ref[slot] = cache_ref[local].reshape(cache_ref.shape[1], width)
 
 
-def route_kernel(far_ref, *refs):
-    *in_refs, out_hbm, out_ref, sem = refs
-    width = out_ref.shape[2]
-    for run in range(far_ref.shape[0]):
-        far = far_ref[run]
-        for slot in range(RUN):
-            picked = in_refs[0][slot]
-            for k in range(1, len(in_refs)):
-                here = jnp.concatenate([far == k] * (width // far.shape[1]), axis=1)
-                picked = jnp.where(here, in_refs[k][slot], picked)
-            out_ref[run * RUN + slot] = picked
-    out = pltpu.make_async_copy(out_ref, out_hbm, sem)
-    out.start()
-    out.wait()
+def route_kernel(y_count, far_ref, *refs):
+    in_refs, out_refs = refs[:-Z], refs[-Z:]
+    own_z = lax.axis_index("ctx") // y_count
+    width = out_refs[0].shape[2]
+    for k, out_ref in enumerate(out_refs):
+        for y in range(y_count):
+            to = (own_z ^ k) * y_count + y
+            far = far_ref[to // RUN]
+            picked = in_refs[0][to % RUN]
+            for at in range(1, len(in_refs)):
+                here = jnp.concatenate([far == at] * (width // far.shape[1]), axis=1)
+                picked = jnp.where(here, in_refs[at][to % RUN], picked)
+            out_ref[y] = picked
+
+
+def turn_kernel(q_hbm, *refs):
+    in_refs, out_refs, (q_ref, sem) = refs[:Z], refs[Z:-2], refs[-2:]
+    q_in = pltpu.make_async_copy(q_hbm, q_ref, sem)
+    q_in.start()
+    own_y = lax.axis_index("ctx") % len(out_refs)
+    for j, out_ref in enumerate(out_refs):
+        for k, in_ref in enumerate(in_refs):
+            out_ref[k] = in_ref[own_y ^ j]
+    q_in.wait()
 
 
 def head_rows(q_ref, g, gq):
@@ -89,10 +99,11 @@
     return lax.dot_general(a, b, (((1,), (0,)), ((), ())), preferred_element_type=jnp.float32)
 
 
-def attend_kernel(limit_ref, q_ref, new_ref, cache_ref, *refs):
-    *pieces, out_ref, stage, sems = refs
+def attend_kernel(y_count, limit_ref, q_ref, new_ref, *refs):
+    pages, pieces, (out_ref, stage, sems) = refs[:y_count], refs[y_count:-3], refs[-3:]
     width = new_ref.shape[2]
-    gen = cache_ref.shape[0]
+    page_rows = pages[0].shape[0] // Z
+    gen = page_rows * Z * y_count
     kvh = width // HD
     gq = q_ref.shape[1] // width
     new = new_ref[...].reshape(SPAN, 2 * width)
@@ -100,13 +111,18 @@
     ones = jnp.ones((SPAN + old + gen, HD), jnp.bfloat16)
     token = lax.broadcasted_iota(jnp.int32, (SPAN, SPAN), 0)
     causal = lax.broadcasted_iota(jnp.int32, (SPAN, SPAN), 1) <= token
-    visible = lax.broadcasted_iota(jnp.int32, (SPAN, gen), 1) < jnp.broadcast_to(limit_ref[:1], (SPAN, gen))
+    at = lax.broadcasted_iota(jnp.int32, (SPAN, gen), 1)
+    ctx = lax.axis_index("ctx")
+    page_z = (at // page_rows % Z) ^ (ctx // y_count)
+    page_y = (at // (page_rows * Z)) ^ (ctx % y_count)
+    at = (page_z * y_count + page_y) * page_rows + at % page_rows
+    visible = at < jnp.broadcast_to(limit_ref[:1], (SPAN, gen))
     copies = []
     for g in range(kvh):
         k_at = slice(g * HD, (g + 1) * HD)
         v_at = slice(width + g * HD, width + (g + 1) * HD)
-        keys = jnp.concatenate([new[:, k_at]] + [p[:, k_at] for p in pieces] + [cache_ref[:, k_at]], axis=0)
-        values = jnp.concatenate([new[:, v_at]] + [p[:, v_at] for p in pieces] + [cache_ref[:, v_at]], axis=0)
+        keys = jnp.concatenate([new[:, k_at]] + [p[:, k_at] for p in (*pieces, *pages)], axis=0)
+        values = jnp.concatenate([new[:, v_at]] + [p[:, v_at] for p in (*pieces, *pages)], axis=0)
         values = jnp.concatenate([values, ones], axis=1)
         scores = dot_nt(head_rows(q_ref, g, gq), keys)
         weights = []
@@ -170,26 +186,35 @@
 
     incoming = outgoing[:1] + [swap(outgoing[k], "dom", k) for k in range(1, dom_count)]
     routed = pl.pallas_call(
-        route_kernel,
-        out_shape=pltpu.HBM((group, page_rows, 2 * width), jnp.bfloat16),
+        functools.partial(route_kernel, y_count),
+        out_shape=(shape((y_count, page_rows, 2 * width), jnp.bfloat16),) * Z,
         in_specs=[VMEM] * (1 + dom_count),
-        out_specs=HBM,
-        scratch_shapes=[pltpu.VMEM((group, page_rows, 2 * width), jnp.bfloat16), pltpu.SemaphoreType.DMA],
+        out_specs=(VMEM,) * Z,
         compiler_params=params(12),
         name="route",
     )(far, *incoming)
-    pages = lax.all_to_all(routed, "ctx", split_axis=0, concat_axis=0, tiled=True)
-    pages = pages.reshape(ctx_count * page_rows, 2 * width)
+    routed = routed[:1] + tuple(swap(routed[k], "ctx", k * y_count) for k in range(1, Z))
+    *pages, q_new = pl.pallas_call(
+        turn_kernel,
+        out_shape=(shape((Z, page_rows, 2 * width), jnp.bfloat16),) * y_count + (shape(q_new.shape, q_new.dtype),),
+        in_specs=[HBM] + [VMEM] * Z,
+        out_specs=(VMEM,) * (y_count + 1),
+        scratch_shapes=[pltpu.SemaphoreType.DMA],
+        compiler_params=params(12),
+        name="turn",
+    )(pltpu.with_memory_space_constraint(q_new, pltpu.HBM), *routed)
+    pages = pages[:1] + [swap(pages[j], "ctx", j) for j in range(1, y_count)]
+    pages = [page.reshape(Z * page_rows, 2 * width) for page in pages]
 
     return pl.pallas_call(
-        attend_kernel,
+        functools.partial(attend_kernel, y_count),
         out_shape=shape((tokens, q_width), jnp.bfloat16),
-        in_specs=[VMEM] * (4 + len(pieces)),
+        in_specs=[VMEM] * (3 + len(pages) + len(pieces)),
         out_specs=HBM,
         scratch_shapes=[pltpu.VMEM((tokens, q_width), jnp.bfloat16), pltpu.SemaphoreType.DMA((kvh,))],
         compiler_params=params(40 if prompt_kv.shape[0] * ctx_count > 1024 else 24),
         name="attend",
-    )(limit, q_new, kv_new, pages, *pieces)
+    )(limit, q_new, kv_new, *pages, *pieces)
 
 
 def solution(mesh):

time: 40.8 us -> 35.1 us (0.86)
  waiting for transfers between devices: 12.1 us -> 7.23 us
  local copies, waits for them, and re-layouts: 1.23 us -> 0.01 us
  Pallas kernels: 7.33 us -> 7.93 us
    all_to_all x1 -> x0, starting transfers between devices: 5.88 us -> none  [on_device(): lax.all_to_all(routed, 'ctx', split_axis=0, concat_axis=0, tiled=True)]
    ppermute x18 -> x22, starting transfers between devices: 13.9 us -> 19.7 us  [swap(): lax.ppermute(x, axis, [(i, i ^ distance) for i in range(lax.axis_size(axi...]
    ppermute x18 -> x22, waiting for transfers between devices: 12.1 us -> 7.23 us  [swap(): lax.ppermute(x, axis, [(i, i ^ distance) for i in range(lax.axis_size(axi...]
    unnamed x4 -> x2, local copies, waits for them, and re-layouts: 1.23 us -> 0.01 us
    pallas_call x2 -> x3, Pallas kernels: 6.17 us -> 6.82 us  [the longest x1 5.47 us: on_device(): pl.pallas_call(functools.partial(attend_kernel, y_count), out_shape=shape...]
  transfers between devices with their start and end apart: 19 -> 22, of which waited for: 8 -> 6; matrix products, arithmetic and copies ran while one was open for 0% -> 0% of each run, Pallas kernels for 0% -> 4%
where the time goes in v5:
time: 35.1 us; the launch traced here: 35 us
  starting transfers between devices  19.7 us (56%)
  Pallas kernels  7.93 us (23%)
  waiting for transfers between devices  7.23 us (21%)
    ppermute x22, starting transfers between devices, swap(): lax.ppermute(x, axis, [(i, i ^ distance) for i in range(lax.axis_size(axi...  19.7 us
    ppermute x22, waiting for transfers between devices, swap(): lax.ppermute(x, axis, [(i, i ^ distance) for i in range(lax.axis_size(axi...  7.23 us
    pallas_call x1, Pallas kernels, on_device(): pl.pallas_call(functools.partial(attend_kernel, y_count), out_shape=shape...  5.47 us
    pallas_call x1, Pallas kernels, on_device(): pl.pallas_call(turn_kernel, out_shape=(shape((Z, page_rows, 2 * width), j...  1.28 us
    pallas_call x1, Pallas kernels, on_device(): pl.pallas_call(functools.partial(pack_kernel, dom_count), out_shape=(shap...  1.12 us
  transfers between devices with their start and end apart: 22, of which 6 were waited for; matrix products, arithmetic and copies ran while one was open for 0% of the time, Pallas kernels for 4%

profile of v5, /device:TPU:0, one launch (start us, length us, event | category | flops | bytes accessed | tf_op | source)
XLA Modules:
  0.0 35.0 jit_solution(10176310843457656283)
XLA Ops:
  0.0 1.1 %pack.1 = (bf16[32,1024]{1,0:T(8,128)(2,1)S(1)}, bf16[4,8,1024]{2,1,0:T(8,128)(2,1)S(1)}, bf16[4,8,1024]{2,1,0:T(8,128)(2,1)S(1)}, bf16[4,8,1024]{2,1,0:T(8,128)...) custom-call(s32[32]{0:T(128)} %anc_hbm.1, s32[32]{0:T(128)} %len_hbm.1, ...), custom_call_target="tpu_custom_call" | custom-call | tf_op jit(solution)/shard_map/pack/pallas_call | solution.py:161
  1.1 0.5 %collective-permute-start = (bf16[4,8,1024]{2,1,0:T(8,128)(2,1)S(1)}, bf16[4,8,1024]{2,1,0:T(8,128)(2,1)S(1)}, u32[]{:S(2)}, u32[]{:S(2)}) collective-permute-start(bf16[4,8,1024]{2,1,0:T(8,128)(2,1)S(1)} %get-tuple-element.22), channel_id=1, source_target_pairs={{0,8},{8,0},{16,24},{24,16},{1,9},{9,1},{17,25},{25,17},{2,10},{10... | collective-permute-start | bytes 196616 | tf_op jit(solution)/shard_map/ppermute | solution.py:149
  1.6 2.6 %collective-permute-start.1 = (bf16[4,8,1024]{2,1,0:T(8,128)(2,1)S(1)}, bf16[4,8,1024]{2,1,0:T(8,128)(2,1)S(1)}, u32[]{:S(2)}, u32[]{:S(2)}) collective-permute-start(bf16[4,8,1024]{2,1,0:T(8,128)(2,1)S(1)} %get-tuple-element.23), channel_id=1, source_target_pairs={{0,16},{8,24},{16,0},{24,8},{1,17},{9,25},{17,1},{25,9},{2,18},{10... | collective-permute-start | bytes 196616 | tf_op jit(solution)/shard_map/ppermute | solution.py:149
  4.2 0.1 collective-permute-start.2
  4.3 1.8 %collective-permute-start.10 = (bf16[32,1024]{1,0:T(8,128)(2,1)S(1)}, bf16[32,1024]{1,0:T(8,128)(2,1)S(1)}, u32[]{:S(2)}, u32[]{:S(2)}) collective-permute-start(bf16[32,1024]{1,0:T(8,128)(2,1)S(1)} %get-tuple-element.32.refs_2_), channel_id=1, source_target_pairs={{0,1},{1,0},{2,3},{3,2},{4,5},{5,4},{6,7},{7,6},{8,9},{9,8},{10,11... | collective-permute-start | bytes 196616 | tf_op jit(solution)/shard_map/ppermute | solution.py:149
  6.0 0.1 collective-permute-start.14
  6.1 0.0 collective-permute-done.refs_1_
  6.1 3.6 %collective-permute-start.9 = (bf16[32,1024]{1,0:T(8,128)(2,1)S(1)}, bf16[32,1024]{1,0:T(8,128)(2,1)S(1)}, u32[]{:S(2)}, u32[]{:S(2)}) collective-permute-start(bf16[32,1024]{1,0:T(8,128)(2,1)S(1)} %get-tuple-element.32.refs_2_), channel_id=1, source_target_pairs={{0,6},{1,7},{2,4},{3,5},{4,2},{5,3},{6,0},{7,1},{8,14},{9,15},{10,... | collective-permute-start | bytes 196616 | tf_op jit(solution)/shard_map/ppermute | solution.py:149
  9.7 0.0 collective-permute-done.1.refs_2_
  9.7 0.0 collective-permute-start.8
  9.7 0.0 collective-permute-done.2.refs_3_
  9.8 1.6 %collective-permute-start.7 = (bf16[32,1024]{1,0:T(8,128)(2,1)S(1)}, bf16[32,1024]{1,0:T(8,128)(2,1)S(1)}, u32[]{:S(2)}, u32[]{:S(2)}) collective-permute-start(bf16[32,1024]{1,0:T(8,128)(2,1)S(1)} %get-tuple-element.32.refs_2_), channel_id=1, source_target_pairs={{0,2},{1,3},{2,0},{3,1},{4,6},{5,7},{6,4},{7,5},{8,10},{9,11},{10,... | collective-permute-start | bytes 196616 | tf_op jit(solution)/shard_map/ppermute | solution.py:149
  11.3 0.0 collective-permute-done.10.refs_6_
  11.3 0.0 collective-permute-start.18
  11.3 0.1 route.1
  11.4 0.0 collective-permute-done.14.refs_10_
  11.4 0.5 %collective-permute-start.3 = (bf16[2,8,1024]{2,1,0:T(8,128)(2,1)S(1)}, bf16[2,8,1024]{2,1,0:T(8,128)(2,1)S(1)}, u32[]{:S(2)}, u32[]{:S(2)}) collective-permute-start(bf16[2,8,1024]{2,1,0:T(8,128)(2,1)S(1)} %get-tuple-element.26), channel_id=1, source_target_pairs={{0,2},{1,3},{2,0},{3,1},{4,6},{5,7},{6,4},{7,5},{8,10},{9,11},{10,... | collective-permute-start | bytes 98312 | tf_op jit(solution)/shard_map/ppermute | solution.py:149
  12.0 0.7 %collective-permute-done.9.refs_5_ = bf16[32,1024]{1,0:T(8,128)(2,1)S(1)} collective-permute-done((bf16[32,1024]{1,0:T(8,128)(2,1)S(1)}, bf16[32,1024]{1,0:T(8,128)(2,1)S(1)}, u32[]{:S(2)}, u32[]{:S(2)}) %collective-permute-start.9) | collective-permute-done | bytes 65568 | tf_op jit(solution)/shard_map/ppermute | solution.py:149
  12.6 2.2 %collective-permute-start.4 = (bf16[2,8,1024]{2,1,0:T(8,128)(2,1)S(1)}, bf16[2,8,1024]{2,1,0:T(8,128)(2,1)S(1)}, u32[]{:S(2)}, u32[]{:S(2)}) collective-permute-start(bf16[2,8,1024]{2,1,0:T(8,128)(2,1)S(1)} %get-tuple-element.27), channel_id=1, source_target_pairs={{0,4},{1,5},{2,6},{3,7},{4,0},{5,1},{6,2},{7,3},{8,12},{9,13},{10,... | collective-permute-start | bytes 98312 | tf_op jit(solution)/shard_map/ppermute | solution.py:149
  14.8 1.0 %collective-permute-done.8.refs_4_ = bf16[32,1024]{1,0:T(8,128)(2,1)S(1)} collective-permute-done((bf16[32,1024]{1,0:T(8,128)(2,1)S(1)}, bf16[32,1024]{1,0:T(8,128)(2,1)S(1)}, u32[]{:S(2)}, u32[]{:S(2)}) %collective-permute-start.8) | collective-permute-done | bytes 65568 | tf_op jit(solution)/shard_map/ppermute | solution.py:149
  15.9 2.5 %collective-permute-start.5 = (bf16[2,8,1024]{2,1,0:T(8,128)(2,1)S(1)}, bf16[2,8,1024]{2,1,0:T(8,128)(2,1)S(1)}, u32[]{:S(2)}, u32[]{:S(2)}) collective-permute-start(bf16[2,8,1024]{2,1,0:T(8,128)(2,1)S(1)} %get-tuple-element.28), channel_id=1, source_target_pairs={{0,6},{1,7},{2,4},{3,5},{4,2},{5,3},{6,0},{7,1},{8,14},{9,15},{10,... | collective-permute-start | bytes 98312 | tf_op jit(solution)/shard_map/ppermute | solution.py:149
  18.4 0.0 collective-permute-done.7.refs_3_
  18.4 0.0 collective-permute-start.17
  18.4 0.0 collective-permute-done.3.refs_1_
  18.4 1.1 %collective-permute-start.13 = (bf16[32,1024]{1,0:T(8,128)(2,1)S(1)}, bf16[32,1024]{1,0:T(8,128)(2,1)S(1)}, u32[]{:S(2)}, u32[]{:S(2)}) collective-permute-start(bf16[32,1024]{1,0:T(8,128)(2,1)S(1)} %collective-permute-done.9.refs_5_), channel_id=1, source_target_pairs={{0,1},{1,0},{2,3},{3,2},{4,5},{5,4},{6,7},{7,6},{8,9},{9,8},{10,11... | collective-permute-start | bytes 196616 | tf_op jit(solution)/shard_map/ppermute | solution.py:149
  19.4 0.0 collective-permute-done.4.refs_2_
  19.4 0.2 collective-permute-start.16
  19.6 2.0 %collective-permute-done.5.refs_3_ = bf16[2,8,1024]{2,1,0:T(8,128)(2,1)S(1)} collective-permute-done((bf16[2,8,1024]{2,1,0:T(8,128)(2,1)S(1)}, bf16[2,8,1024]{2,1,0:T(8,128)(2,1)S(1)}, u32[]{:S(2)}, u32[]{:S(2)}) %collective-permute-start.5) | collective-permute-done | bytes 32800 | tf_op jit(solution)/shard_map/ppermute | solution.py:149
  21.6 0.5 %collective-permute-start.12 = (bf16[32,1024]{1,0:T(8,128)(2,1)S(1)}, bf16[32,1024]{1,0:T(8,128)(2,1)S(1)}, u32[]{:S(2)}, u32[]{:S(2)}) collective-permute-start(bf16[32,1024]{1,0:T(8,128)(2,1)S(1)} %collective-permute-done.8.refs_4_), channel_id=1, source_target_pairs={{0,1},{1,0},{2,3},{3,2},{4,5},{5,4},{6,7},{7,6},{8,9},{9,8},{10,11... | collective-permute-start | bytes 196616 | tf_op jit(solution)/shard_map/ppermute | solution.py:149
  22.1 0.0 collective-permute-done.18.refs_14_
  22.1 1.5 %collective-permute-start.11 = (bf16[32,1024]{1,0:T(8,128)(2,1)S(1)}, bf16[32,1024]{1,0:T(8,128)(2,1)S(1)}, u32[]{:S(2)}, u32[]{:S(2)}) collective-permute-start(bf16[32,1024]{1,0:T(8,128)(2,1)S(1)} %collective-permute-done.7.refs_3_), channel_id=1, source_target_pairs={{0,1},{1,0},{2,3},{3,2},{4,5},{5,4},{6,7},{7,6},{8,9},{9,8},{10,11... | collective-permute-start | bytes 196616 | tf_op jit(solution)/shard_map/ppermute | solution.py:149
  23.6 1.3 %turn.1 = (bf16[4,8,1024]{2,1,0:T(8,128)(2,1)S(1)}, bf16[4,8,1024]{2,1,0:T(8,128)(2,1)S(1)}, bf16[128,4096]{1,0:T(8,128)(2,1)S(1)}) custom-call(bf16[128,4096]{1,0:T(8,128)(2,1)} %q_hbm.1, bf16[2,8,1024]{2,1,0:T(8,128)(2,1)S(1)} %get-tuple-element.25.refs_0_, bf16[2,8,1024]{2,1,0:T(8,128)(2,1)S(1)} %collective-permute-done.3.refs_1_, ...), custom_call_target="tpu_custom_call" | custom-call | tf_op jit(solution)/shard_map/turn/pallas_call | solution.py:197
  24.9 0.0 collective-permute-done.17.refs_13_
  24.9 0.1 collective-permute-start.15
  25.0 0.0 collective-permute-done.13.refs_9_
  25.0 0.6 %collective-permute-start.6 = (bf16[4,8,1024]{2,1,0:T(8,128)(2,1)S(1)}, bf16[4,8,1024]{2,1,0:T(8,128)(2,1)S(1)}, u32[]{:S(2)}, u32[]{:S(2)}) collective-permute-start(bf16[4,8,1024]{2,1,0:T(8,128)(2,1)S(1)} %get-tuple-element.31), channel_id=1, source_target_pairs={{0,1},{1,0},{2,3},{3,2},{4,5},{5,4},{6,7},{7,6},{8,9},{9,8},{10,11... | collective-permute-start | bytes 196616 | tf_op jit(solution)/shard_map/ppermute | solution.py:149
  25.6 0.0 collective-permute-done.16.refs_12_
  25.6 0.2 collective-permute-start.21
  25.7 0.1 collective-permute-done.12.refs_8_
  25.9 0.2 collective-permute-start.20
  26.1 0.5 %collective-permute-done.11.refs_7_ = bf16[32,1024]{1,0:T(8,128)(2,1)S(1)} collective-permute-done((bf16[32,1024]{1,0:T(8,128)(2,1)S(1)}, bf16[32,1024]{1,0:T(8,128)(2,1)S(1)}, u32[]{:S(2)}, u32[]{:S(2)}) %collective-permute-start.11) | collective-permute-done | bytes 65568 | tf_op jit(solution)/shard_map/ppermute | solution.py:149
  26.6 0.0 collective-permute-start.19
  26.6 0.0 collective-permute-done.15.refs_11_
  26.6 2.9 %collective-permute-done.6 = bf16[4,8,1024]{2,1,0:T(8,128)(2,1)S(1)} collective-permute-done((bf16[4,8,1024]{2,1,0:T(8,128)(2,1)S(1)}, bf16[4,8,1024]{2,1,0:T(8,128)(2,1)S(1)}, u32[]{:S(2)}, u32[]{:S(2)}) %collective-permute-start.6) | collective-permute-done | bytes 65568 | tf_op jit(solution)/shard_map/ppermute | solution.py:149
  29.5 0.0 collective-permute-done.21.refs_17_
  29.5 0.0 collective-permute-done.20.refs_16_
  29.5 0.0 collective-permute-done.19.refs_15_
  29.5 5.5 %attend.1 = bf16[128,4096]{1,0:T(8,128)(2,1)} custom-call(s32[8,64]{1,0:T(8,128)S(1)} %get-tuple-element.19.limit_ref, bf16[128,4096]{1,0:T(8,128)(2,1)S(1)} %get-tuple-element.29.q_ref, bf16[128,2,512]{2,1,0:T(2,128)(2,1)S(1)} %copy-done, bf16[32,1024]{1,0:T(8,128)(2,1)S(1)} %bitcast.2, bf16[32,1024]{1,0:T(8,128)(2,1)S(1)} %bitcast.3, ...), custom_call_target="tpu_custom_call" | custom-call | tf_op jit(solution)/shard_map/attend/pallas_call | solution.py:209
  (2 shorter events, 0.0 us)
Async XLA Ops:
  1.1 5.0 %collective-permute-start = (bf16[4,8,1024]{2,1,0:T(8,128)(2,1)S(1)}, bf16[4,8,1024]{2,1,0:T(8,128)(2,1)S(1)}, u32[]{:S(2)}, u32[]{:S(2)}) collective-permute-start(bf16[4,8,1024]{2,1,0:T(8,128)(2,1)S(1)} %get-tuple-element.22), channel_id=1, source_target_pairs={{0,8},{8,0},{16,24},{24,16},{1,9},{9,1},{17,25},{25,17},{2,10},{10... | collective-permute-start | bytes 196616 | tf_op jit(solution)/shard_map/ppermute | solution.py:149
  1.6 8.1 %collective-permute-start.1 = (bf16[4,8,1024]{2,1,0:T(8,128)(2,1)S(1)}, bf16[4,8,1024]{2,1,0:T(8,128)(2,1)S(1)}, u32[]{:S(2)}, u32[]{:S(2)}) collective-permute-start(bf16[4,8,1024]{2,1,0:T(8,128)(2,1)S(1)} %get-tuple-element.23), channel_id=1, source_target_pairs={{0,16},{8,24},{16,0},{24,8},{1,17},{9,25},{17,1},{25,9},{2,18},{10... | collective-permute-start | bytes 196616 | tf_op jit(solution)/shard_map/ppermute | solution.py:149
  4.2 5.6 %collective-permute-start.2 = (bf16[4,8,1024]{2,1,0:T(8,128)(2,1)S(1)}, bf16[4,8,1024]{2,1,0:T(8,128)(2,1)S(1)}, u32[]{:S(2)}, u32[]{:S(2)}) collective-permute-start(bf16[4,8,1024]{2,1,0:T(8,128)(2,1)S(1)} %get-tuple-element.24), channel_id=1, source_target_pairs={{0,24},{8,16},{16,8},{24,0},{1,25},{9,17},{17,9},{25,1},{2,26},{10... | collective-permute-start | bytes 196616 | tf_op jit(solution)/shard_map/ppermute | solution.py:149
  4.3 7.1 %collective-permute-start.10 = (bf16[32,1024]{1,0:T(8,128)(2,1)S(1)}, bf16[32,1024]{1,0:T(8,128)(2,1)S(1)}, u32[]{:S(2)}, u32[]{:S(2)}) collective-permute-start(bf16[32,1024]{1,0:T(8,128)(2,1)S(1)} %get-tuple-element.32.refs_2_), channel_id=1, source_target_pairs={{0,1},{1,0},{2,3},{3,2},{4,5},{5,4},{6,7},{7,6},{8,9},{9,8},{10,11... | collective-permute-start | bytes 196616 | tf_op jit(solution)/shard_map/ppermute | solution.py:149
  6.0 5.4 %collective-permute-start.14 = (bf16[32,1024]{1,0:T(8,128)(2,1)S(1)}, bf16[32,1024]{1,0:T(8,128)(2,1)S(1)}, u32[]{:S(2)}, u32[]{:S(2)}) collective-permute-start(bf16[32,1024]{1,0:T(8,128)(2,1)S(1)} %get-tuple-element.32.refs_2_), channel_id=1, source_target_pairs={{0,8},{8,0},{16,24},{24,16},{1,9},{9,1},{17,25},{25,17},{2,10},{10... | collective-permute-start | bytes 196616 | tf_op jit(solution)/shard_map/ppermute | solution.py:149
  6.1 6.5 %collective-permute-start.9 = (bf16[32,1024]{1,0:T(8,128)(2,1)S(1)}, bf16[32,1024]{1,0:T(8,128)(2,1)S(1)}, u32[]{:S(2)}, u32[]{:S(2)}) collective-permute-start(bf16[32,1024]{1,0:T(8,128)(2,1)S(1)} %get-tuple-element.32.refs_2_), channel_id=1, source_target_pairs={{0,6},{1,7},{2,4},{3,5},{4,2},{5,3},{6,0},{7,1},{8,14},{9,15},{10,... | collective-permute-start | bytes 196616 | tf_op jit(solution)/shard_map/ppermute | solution.py:149
  9.7 6.2 %collective-permute-start.8 = (bf16[32,1024]{1,0:T(8,128)(2,1)S(1)}, bf16[32,1024]{1,0:T(8,128)(2,1)S(1)}, u32[]{:S(2)}, u32[]{:S(2)}) collective-permute-start(bf16[32,1024]{1,0:T(8,128)(2,1)S(1)} %get-tuple-element.32.refs_2_), channel_id=1, source_target_pairs={{0,4},{1,5},{2,6},{3,7},{4,0},{5,1},{6,2},{7,3},{8,12},{9,13},{10,... | collective-permute-start | bytes 196616 | tf_op jit(solution)/shard_map/ppermute | solution.py:149
  9.8 8.6 %collective-permute-start.7 = (bf16[32,1024]{1,0:T(8,128)(2,1)S(1)}, bf16[32,1024]{1,0:T(8,128)(2,1)S(1)}, u32[]{:S(2)}, u32[]{:S(2)}) collective-permute-start(bf16[32,1024]{1,0:T(8,128)(2,1)S(1)} %get-tuple-element.32.refs_2_), channel_id=1, source_target_pairs={{0,2},{1,3},{2,0},{3,1},{4,6},{5,7},{6,4},{7,5},{8,10},{9,11},{10,... | collective-permute-start | bytes 196616 | tf_op jit(solution)/shard_map/ppermute | solution.py:149
  11.3 10.8 %collective-permute-start.18 = (bf16[32,1024]{1,0:T(8,128)(2,1)S(1)}, bf16[32,1024]{1,0:T(8,128)(2,1)S(1)}, u32[]{:S(2)}, u32[]{:S(2)}) collective-permute-start(bf16[32,1024]{1,0:T(8,128)(2,1)S(1)} %collective-permute-done.10.refs_6_), channel_id=1, source_target_pairs={{0,8},{8,0},{16,24},{24,16},{1,9},{9,1},{17,25},{25,17},{2,10},{10... | collective-permute-start | bytes 196616 | tf_op jit(solution)/shard_map/ppermute | solution.py:149
  11.4 6.9 %collective-permute-start.3 = (bf16[2,8,1024]{2,1,0:T(8,128)(2,1)S(1)}, bf16[2,8,1024]{2,1,0:T(8,128)(2,1)S(1)}, u32[]{:S(2)}, u32[]{:S(2)}) collective-permute-start(bf16[2,8,1024]{2,1,0:T(8,128)(2,1)S(1)} %get-tuple-element.26), channel_id=1, source_target_pairs={{0,2},{1,3},{2,0},{3,1},{4,6},{5,7},{6,4},{7,5},{8,10},{9,11},{10,... | collective-permute-start | bytes 98312 | tf_op jit(solution)/shard_map/ppermute | solution.py:149
  12.6 6.8 %collective-permute-start.4 = (bf16[2,8,1024]{2,1,0:T(8,128)(2,1)S(1)}, bf16[2,8,1024]{2,1,0:T(8,128)(2,1)S(1)}, u32[]{:S(2)}, u32[]{:S(2)}) collective-permute-start(bf16[2,8,1024]{2,1,0:T(8,128)(2,1)S(1)} %get-tuple-element.27), channel_id=1, source_target_pairs={{0,4},{1,5},{2,6},{3,7},{4,0},{5,1},{6,2},{7,3},{8,12},{9,13},{10,... | collective-permute-start | bytes 98312 | tf_op jit(solution)/shard_map/ppermute | solution.py:149
  15.9 5.7 %collective-permute-start.5 = (bf16[2,8,1024]{2,1,0:T(8,128)(2,1)S(1)}, bf16[2,8,1024]{2,1,0:T(8,128)(2,1)S(1)}, u32[]{:S(2)}, u32[]{:S(2)}) collective-permute-start(bf16[2,8,1024]{2,1,0:T(8,128)(2,1)S(1)} %get-tuple-element.28), channel_id=1, source_target_pairs={{0,6},{1,7},{2,4},{3,5},{4,2},{5,3},{6,0},{7,1},{8,14},{9,15},{10,... | collective-permute-start | bytes 98312 | tf_op jit(solution)/shard_map/ppermute | solution.py:149
  18.4 6.6 %collective-permute-start.17 = (bf16[32,1024]{1,0:T(8,128)(2,1)S(1)}, bf16[32,1024]{1,0:T(8,128)(2,1)S(1)}, u32[]{:S(2)}, u32[]{:S(2)}) collective-permute-start(bf16[32,1024]{1,0:T(8,128)(2,1)S(1)} %collective-permute-done.9.refs_5_), channel_id=1, source_target_pairs={{0,8},{8,0},{16,24},{24,16},{1,9},{9,1},{17,25},{25,17},{2,10},{10... | collective-permute-start | bytes 196616 | tf_op jit(solution)/shard_map/ppermute | solution.py:149
  18.4 6.6 %collective-permute-start.13 = (bf16[32,1024]{1,0:T(8,128)(2,1)S(1)}, bf16[32,1024]{1,0:T(8,128)(2,1)S(1)}, u32[]{:S(2)}, u32[]{:S(2)}) collective-permute-start(bf16[32,1024]{1,0:T(8,128)(2,1)S(1)} %collective-permute-done.9.refs_5_), channel_id=1, source_target_pairs={{0,1},{1,0},{2,3},{3,2},{4,5},{5,4},{6,7},{7,6},{8,9},{9,8},{10,11... | collective-permute-start | bytes 196616 | tf_op jit(solution)/shard_map/ppermute | solution.py:149
  19.4 6.1 %collective-permute-start.16 = (bf16[32,1024]{1,0:T(8,128)(2,1)S(1)}, bf16[32,1024]{1,0:T(8,128)(2,1)S(1)}, u32[]{:S(2)}, u32[]{:S(2)}) collective-permute-start(bf16[32,1024]{1,0:T(8,128)(2,1)S(1)} %collective-permute-done.8.refs_4_), channel_id=1, source_target_pairs={{0,8},{8,0},{16,24},{24,16},{1,9},{9,1},{17,25},{25,17},{2,10},{10... | collective-permute-start | bytes 196616 | tf_op jit(solution)/shard_map/ppermute | solution.py:149
  21.6 4.3 %collective-permute-start.12 = (bf16[32,1024]{1,0:T(8,128)(2,1)S(1)}, bf16[32,1024]{1,0:T(8,128)(2,1)S(1)}, u32[]{:S(2)}, u32[]{:S(2)}) collective-permute-start(bf16[32,1024]{1,0:T(8,128)(2,1)S(1)} %collective-permute-done.8.refs_4_), channel_id=1, source_target_pairs={{0,1},{1,0},{2,3},{3,2},{4,5},{5,4},{6,7},{7,6},{8,9},{9,8},{10,11... | collective-permute-start | bytes 196616 | tf_op jit(solution)/shard_map/ppermute | solution.py:149
  22.1 4.5 %collective-permute-start.11 = (bf16[32,1024]{1,0:T(8,128)(2,1)S(1)}, bf16[32,1024]{1,0:T(8,128)(2,1)S(1)}, u32[]{:S(2)}, u32[]{:S(2)}) collective-permute-start(bf16[32,1024]{1,0:T(8,128)(2,1)S(1)} %collective-permute-done.7.refs_3_), channel_id=1, source_target_pairs={{0,1},{1,0},{2,3},{3,2},{4,5},{5,4},{6,7},{7,6},{8,9},{9,8},{10,11... | collective-permute-start | bytes 196616 | tf_op jit(solution)/shard_map/ppermute | solution.py:149
  23.6 5.9 %copy-start = (bf16[128,2,512]{2,1,0:T(2,128)(2,1)S(1)}, bf16[128,2,512]{2,1,0:T(2,128)(2,1)}, u32[]{:S(2)}) copy-start(bf16[128,2,512]{2,1,0:T(2,128)(2,1)} %new_ref.1) | copy-start | bytes 786436
  24.9 1.6 %collective-permute-start.15 = (bf16[32,1024]{1,0:T(8,128)(2,1)S(1)}, bf16[32,1024]{1,0:T(8,128)(2,1)S(1)}, u32[]{:S(2)}, u32[]{:S(2)}) collective-permute-start(bf16[32,1024]{1,0:T(8,128)(2,1)S(1)} %collective-permute-done.7.refs_3_), channel_id=1, source_target_pairs={{0,8},{8,0},{16,24},{24,16},{1,9},{9,1},{17,25},{25,17},{2,10},{10... | collective-permute-start | bytes 196616 | tf_op jit(solution)/shard_map/ppermute | solution.py:149
  25.0 4.5 %collective-permute-start.6 = (bf16[4,8,1024]{2,1,0:T(8,128)(2,1)S(1)}, bf16[4,8,1024]{2,1,0:T(8,128)(2,1)S(1)}, u32[]{:S(2)}, u32[]{:S(2)}) collective-permute-start(bf16[4,8,1024]{2,1,0:T(8,128)(2,1)S(1)} %get-tuple-element.31), channel_id=1, source_target_pairs={{0,1},{1,0},{2,3},{3,2},{4,5},{5,4},{6,7},{7,6},{8,9},{9,8},{10,11... | collective-permute-start | bytes 196616 | tf_op jit(solution)/shard_map/ppermute | solution.py:149
  25.6 3.9 %collective-permute-start.21 = (bf16[32,1024]{1,0:T(8,128)(2,1)S(1)}, bf16[32,1024]{1,0:T(8,128)(2,1)S(1)}, u32[]{:S(2)}, u32[]{:S(2)}) collective-permute-start(bf16[32,1024]{1,0:T(8,128)(2,1)S(1)} %collective-permute-done.13.refs_9_), channel_id=1, source_target_pairs={{0,8},{8,0},{16,24},{24,16},{1,9},{9,1},{17,25},{25,17},{2,10},{10... | collective-permute-start | bytes 196616 | tf_op jit(solution)/shard_map/ppermute | solution.py:149
  25.9 3.7 %collective-permute-start.20 = (bf16[32,1024]{1,0:T(8,128)(2,1)S(1)}, bf16[32,1024]{1,0:T(8,128)(2,1)S(1)}, u32[]{:S(2)}, u32[]{:S(2)}) collective-permute-start(bf16[32,1024]{1,0:T(8,128)(2,1)S(1)} %collective-permute-done.12.refs_8_), channel_id=1, source_target_pairs={{0,8},{8,0},{16,24},{24,16},{1,9},{9,1},{17,25},{25,17},{2,10},{10... | collective-permute-start | bytes 196616 | tf_op jit(solution)/shard_map/ppermute | solution.py:149
  26.6 3.0 %collective-permute-start.19 = (bf16[32,1024]{1,0:T(8,128)(2,1)S(1)}, bf16[32,1024]{1,0:T(8,128)(2,1)S(1)}, u32[]{:S(2)}, u32[]{:S(2)}) collective-permute-start(bf16[32,1024]{1,0:T(8,128)(2,1)S(1)} %collective-permute-done.11.refs_7_), channel_id=1, source_target_pairs={{0,8},{8,0},{16,24},{24,16},{1,9},{9,1},{17,25},{25,17},{2,10},{10... | collective-permute-start | bytes 196616 | tf_op jit(solution)/shard_map/ppermute | solution.py:149

commit v6 on v5

--- a/solution.py
+++ b/solution.py
@@ -27,7 +27,7 @@
     far_ref, limit_ref, anc_ref, len_ref, prompt_ref, cache_ref, sems = refs[dom_count:]
     group = cache_ref.shape[0]
     dom = lax.axis_index("dom")
-    rows, width = half_ref.shape
+    _, rows, width = half_ref.shape
     from_row = pl.multiple_of((dom % 2) * rows, rows)
     prompt_in = pltpu.make_async_copy(prompt_hbm.at[pl.ds(from_row, rows)], prompt_ref, sems.at[0])
     anc_in = pltpu.make_async_copy(anc_hbm, anc_ref, sems.at[1])
@@ -46,7 +46,9 @@
     particle = dom * group + lax.axis_index("ctx")
     limit_ref[...] = jnp.full(limit_ref.shape, len_ref[anc_ref[particle]] * PAGE)
     prompt_in.wait()
-    half_ref[...] = prompt_ref[...].reshape(rows, width)
+    half = prompt_ref[...].reshape(rows, width)
+    for to in range(half_ref.shape[0]):
+        half_ref[to] = half
     cache_in.wait()
     for k, out_ref in enumerate(out_refs):
         for run in range(runs):
@@ -161,7 +163,7 @@
     half, *rest = pl.pallas_call(
         functools.partial(pack_kernel, dom_count),
         out_shape=(
-            shape((half_rows, 2 * width), jnp.bfloat16),
+            shape((ctx_count, half_rows, 2 * width), jnp.bfloat16),
             *[shape((RUN, page_rows, 2 * width), jnp.bfloat16)] * dom_count,
             shape((group // RUN, page_rows, HD), jnp.bfloat16),
             shape((8, ctx_count * page_rows), jnp.int32),
@@ -180,9 +182,8 @@
     )(*(pltpu.with_memory_space_constraint(x, pltpu.HBM) for x in (ancestors, lengths, prompt_kv, cache_kv)))
     outgoing, far, limit = rest[:dom_count], rest[dom_count], rest[dom_count + 1]
 
-    pieces = [half] + [swap(half, "ctx", k * y_count) for k in range(1, Z)]
-    pieces += [swap(p, "ctx", k) for k in range(1, y_count) for p in pieces[:Z]]
-    pieces += [swap(p, "dom", 1) for p in pieces]
+    own_half = lax.all_to_all(half, "ctx", split_axis=0, concat_axis=0, tiled=True)
+    own_half = own_half.reshape(ctx_count * half_rows, 2 * width)
 
     incoming = outgoing[:1] + [swap(outgoing[k], "dom", k) for k in range(1, dom_count)]
     routed = pl.pallas_call(
@@ -203,6 +204,8 @@
         compiler_params=params(12),
         name="turn",
     )(pltpu.with_memory_space_constraint(q_new, pltpu.HBM), *routed)
+    own_half, pages[0] = lax.optimization_barrier((own_half, pages[0]))
+    pieces = [own_half, swap(own_half, "dom", 1)]
     pages = pages[:1] + [swap(pages[j], "ctx", j) for j in range(1, y_count)]
     pages = [page.reshape(Z * page_rows, 2 * width) for page in pages]
 

time: 35.1 us -> 37.7 us (1.074)
  waiting for transfers between devices: 7.23 us -> 13.4 us
  starting transfers between devices: 19.7 us -> 15.3 us
  Pallas kernels: 7.93 us -> 8.7 us
    ppermute x22 -> x8, starting transfers between devices: 19.7 us -> 7.98 us  [swap(): lax.ppermute(x, axis, [(i, i ^ distance) for i in range(lax.axis_size(axi...]
    all_to_all x0 -> x1, starting transfers between devices: none -> 7.29 us  [on_device(): lax.all_to_all(half, 'ctx', split_axis=0, concat_axis=0, tiled=True)]
    ppermute x22 -> x8, waiting for transfers between devices: 7.23 us -> 13.4 us  [swap(): lax.ppermute(x, axis, [(i, i ^ distance) for i in range(lax.axis_size(axi...]
    pallas_call x1, Pallas kernels: 1.12 us -> 1.94 us  [on_device(): pl.pallas_call(functools.partial(pack_kernel, dom_count), out_shape=(shap...]
  transfers between devices with their start and end apart: 22 -> 9, of which waited for: 6 -> 4; matrix products, arithmetic and copies ran while one was open for 0% -> 0% of each run, Pallas kernels for 4% -> 4%
where the time goes in v6:
time: 37.7 us; the launch traced here: 37.5 us
  starting transfers between devices  15.3 us (41%)
  waiting for transfers between devices  13.4 us (36%)
  Pallas kernels  8.7 us (23%)
    ppermute x8, waiting for transfers between devices, swap(): lax.ppermute(x, axis, [(i, i ^ distance) for i in range(lax.axis_size(axi...  13.4 us
    ppermute x8, starting transfers between devices, swap(): lax.ppermute(x, axis, [(i, i ^ distance) for i in range(lax.axis_size(axi...  7.98 us
    all_to_all x1, starting transfers between devices, on_device(): lax.all_to_all(half, 'ctx', split_axis=0, concat_axis=0, tiled=True)  7.29 us
    pallas_call x1, Pallas kernels, on_device(): pl.pallas_call(functools.partial(attend_kernel, y_count), out_shape=shape...  5.42 us
    pallas_call x1, Pallas kernels, on_device(): pl.pallas_call(functools.partial(pack_kernel, dom_count), out_shape=(shap...  1.94 us
    pallas_call x1, Pallas kernels, on_device(): pl.pallas_call(turn_kernel, out_shape=(shape((Z, page_rows, 2 * width), j...  1.28 us
  transfers between devices with their start and end apart: 9, of which 4 were waited for; matrix products, arithmetic and copies ran while one was open for 0% of the time, Pallas kernels for 4%

profile of v6, /device:TPU:0, one launch (start us, length us, event | category | flops | bytes accessed | tf_op | source)
XLA Modules:
  0.0 37.5 jit_solution(4416335176763665956)
XLA Ops:
  0.0 1.9 %pack.1 = (bf16[8,32,1024]{2,1,0:T(8,128)(2,1)}, bf16[4,8,1024]{2,1,0:T(8,128)(2,1)S(1)}, bf16[4,8,1024]{2,1,0:T(8,128)(2,1)S(1)}, bf16[4,8,1024]{2,1,0:T(8,128)...) custom-call(s32[32]{0:T(128)} %anc_hbm.1, s32[32]{0:T(128)} %len_hbm.1, ...), custom_call_target="tpu_custom_call" | custom-call | tf_op jit(solution)/shard_map/pack/pallas_call | solution.py:163
  1.9 7.3 %all-to-all-start = ((bf16[8,32,1024]{2,1,0:T(8,128)(2,1)}), bf16[8,32,1024]{2,1,0:T(8,128)(2,1)S(1)}, u32[]{:S(2)}, u32[]{:S(2)}) async-start(bf16[8,32,1024]{2,1,0:T(8,128)(2,1)} %get-tuple-element.32), calls=%async_computation | async-start | bytes 1048576 | tf_op jit(solution)/shard_map/all_to_all | solution.py:185
  9.2 0.0 collective-permute-start
  9.2 1.5 %collective-permute-start.1 = (bf16[4,8,1024]{2,1,0:T(8,128)(2,1)S(1)}, bf16[4,8,1024]{2,1,0:T(8,128)(2,1)S(1)}, u32[]{:S(2)}, u32[]{:S(2)}) collective-permute-start(bf16[4,8,1024]{2,1,0:T(8,128)(2,1)S(1)} %get-tuple-element.25), channel_id=1, source_target_pairs={{0,16},{8,24},{16,0},{24,8},{1,17},{9,25},{17,1},{25,9},{2,18},{10... | collective-permute-start | bytes 196616 | tf_op jit(solution)/shard_map/ppermute | solution.py:151
  10.7 0.4 collective-permute-start.2
  11.1 0.0 collective-permute-done.refs_1_
  11.1 2.7 %collective-permute-done.1.refs_2_ = bf16[4,8,1024]{2,1,0:T(8,128)(2,1)S(1)} collective-permute-done((bf16[4,8,1024]{2,1,0:T(8,128)(2,1)S(1)}, bf16[4,8,1024]{2,1,0:T(8,128)(2,1)S(1)}, u32[]{:S(2)}, u32[]{:S(2)}) %collective-permute-start.1) | collective-permute-done | bytes 65568 | tf_op jit(solution)/shard_map/ppermute | solution.py:151
  13.8 1.0 %collective-permute-done.2.refs_3_ = bf16[4,8,1024]{2,1,0:T(8,128)(2,1)S(1)} collective-permute-done((bf16[4,8,1024]{2,1,0:T(8,128)(2,1)S(1)}, bf16[4,8,1024]{2,1,0:T(8,128)(2,1)S(1)}, u32[]{:S(2)}, u32[]{:S(2)}) %collective-permute-start.2) | collective-permute-done | bytes 65568 | tf_op jit(solution)/shard_map/ppermute | solution.py:151
  14.8 0.1 route.1
  14.9 2.1 %collective-permute-start.3 = (bf16[2,8,1024]{2,1,0:T(8,128)(2,1)S(1)}, bf16[2,8,1024]{2,1,0:T(8,128)(2,1)S(1)}, u32[]{:S(2)}, u32[]{:S(2)}) collective-permute-start(bf16[2,8,1024]{2,1,0:T(8,128)(2,1)S(1)} %get-tuple-element.28), channel_id=1, source_target_pairs={{0,2},{1,3},{2,0},{3,1},{4,6},{5,7},{6,4},{7,5},{8,10},{9,11},{10,... | collective-permute-start | bytes 98312 | tf_op jit(solution)/shard_map/ppermute | solution.py:151
  17.0 2.4 %collective-permute-start.4 = (bf16[2,8,1024]{2,1,0:T(8,128)(2,1)S(1)}, bf16[2,8,1024]{2,1,0:T(8,128)(2,1)S(1)}, u32[]{:S(2)}, u32[]{:S(2)}) collective-permute-start(bf16[2,8,1024]{2,1,0:T(8,128)(2,1)S(1)} %get-tuple-element.29), channel_id=1, source_target_pairs={{0,4},{1,5},{2,6},{3,7},{4,0},{5,1},{6,2},{7,3},{8,12},{9,13},{10,... | collective-permute-start | bytes 98312 | tf_op jit(solution)/shard_map/ppermute | solution.py:151
  19.4 0.1 collective-permute-start.5
  19.4 0.0 collective-permute-done.3.refs_1_
  19.4 6.7 %collective-permute-done.4.refs_2_ = bf16[2,8,1024]{2,1,0:T(8,128)(2,1)S(1)} collective-permute-done((bf16[2,8,1024]{2,1,0:T(8,128)(2,1)S(1)}, bf16[2,8,1024]{2,1,0:T(8,128)(2,1)S(1)}, u32[]{:S(2)}, u32[]{:S(2)}) %collective-permute-start.4) | collective-permute-done | bytes 32800 | tf_op jit(solution)/shard_map/ppermute | solution.py:151
  26.2 0.0 collective-permute-done.5.refs_3_
  26.2 0.0 copy-start
  26.2 1.3 %turn.1 = (bf16[4,8,1024]{2,1,0:T(8,128)(2,1)S(1)}, bf16[4,8,1024]{2,1,0:T(8,128)(2,1)S(1)}, bf16[128,4096]{1,0:T(8,128)(2,1)S(1)}) custom-call(bf16[128,4096]{1,0:T(8,128)(2,1)} %q_hbm.1, bf16[2,8,1024]{2,1,0:T(8,128)(2,1)S(1)} %get-tuple-element.27.refs_0_, bf16[2,8,1024]{2,1,0:T(8,128)(2,1)S(1)} %collective-permute-done.3.refs_1_, ...), custom_call_target="tpu_custom_call" | custom-call | tf_op jit(solution)/shard_map/turn/pallas_call | solution.py:198
  27.5 0.0 all-to-all-done
  27.5 0.1 collective-permute-start.7
  27.5 1.5 %collective-permute-start.6 = (bf16[4,8,1024]{2,1,0:T(8,128)(2,1)S(1)}, bf16[4,8,1024]{2,1,0:T(8,128)(2,1)S(1)}, u32[]{:S(2)}, u32[]{:S(2)}) collective-permute-start(bf16[4,8,1024]{2,1,0:T(8,128)(2,1)S(1)} %get-tuple-element.35), channel_id=1, source_target_pairs={{0,1},{1,0},{2,3},{3,2},{4,5},{5,4},{6,7},{7,6},{8,9},{9,8},{10,11... | collective-permute-start | bytes 196616 | tf_op jit(solution)/shard_map/ppermute | solution.py:151
  29.1 3.0 %collective-permute-done.6 = bf16[4,8,1024]{2,1,0:T(8,128)(2,1)S(1)} collective-permute-done((bf16[4,8,1024]{2,1,0:T(8,128)(2,1)S(1)}, bf16[4,8,1024]{2,1,0:T(8,128)(2,1)S(1)}, u32[]{:S(2)}, u32[]{:S(2)}) %collective-permute-start.6) | collective-permute-done | bytes 65568 | tf_op jit(solution)/shard_map/ppermute | solution.py:151
  32.1 0.0 collective-permute-done.7.refs_3_
  32.1 0.0 copy-done
  32.1 5.4 %attend.1 = bf16[128,4096]{1,0:T(8,128)(2,1)} custom-call(s32[8,64]{1,0:T(8,128)S(1)} %get-tuple-element.21.limit_ref, bf16[128,4096]{1,0:T(8,128)(2,1)S(1)} %get-tuple-element.31.q_ref, bf16[128,2,512]{2,1,0:T(2,128)(2,1)S(1)} %copy-done, bf16[32,1024]{1,0:T(8,128)(2,1)S(1)} %bitcast.5, bf16[32,1024]{1,0:T(8,128)(2,1)S(1)} %bitcast.6, ...), custom_call_target="tpu_custom_call" | custom-call | tf_op jit(solution)/shard_map/attend/pallas_call | solution.py:212
Async XLA Ops:
  1.9 25.5 %all-to-all-start = ((bf16[8,32,1024]{2,1,0:T(8,128)(2,1)}), bf16[8,32,1024]{2,1,0:T(8,128)(2,1)S(1)}, u32[]{:S(2)}, u32[]{:S(2)}) async-start(bf16[8,32,1024]{2,1,0:T(8,128)(2,1)} %get-tuple-element.32), calls=%async_computation | async-start | bytes 1048576 | tf_op jit(solution)/shard_map/all_to_all | solution.py:185
  9.2 1.9 %collective-permute-start = (bf16[4,8,1024]{2,1,0:T(8,128)(2,1)S(1)}, bf16[4,8,1024]{2,1,0:T(8,128)(2,1)S(1)}, u32[]{:S(2)}, u32[]{:S(2)}) collective-permute-start(bf16[4,8,1024]{2,1,0:T(8,128)(2,1)S(1)} %get-tuple-element.24), channel_id=1, source_target_pairs={{0,8},{8,0},{16,24},{24,16},{1,9},{9,1},{17,25},{25,17},{2,10},{10... | collective-permute-start | bytes 196616 | tf_op jit(solution)/shard_map/ppermute | solution.py:151
  9.2 4.5 %collective-permute-start.1 = (bf16[4,8,1024]{2,1,0:T(8,128)(2,1)S(1)}, bf16[4,8,1024]{2,1,0:T(8,128)(2,1)S(1)}, u32[]{:S(2)}, u32[]{:S(2)}) collective-permute-start(bf16[4,8,1024]{2,1,0:T(8,128)(2,1)S(1)} %get-tuple-element.25), channel_id=1, source_target_pairs={{0,16},{8,24},{16,0},{24,8},{1,17},{9,25},{17,1},{25,9},{2,18},{10... | collective-permute-start | bytes 196616 | tf_op jit(solution)/shard_map/ppermute | solution.py:151
  10.7 4.1 %collective-permute-start.2 = (bf16[4,8,1024]{2,1,0:T(8,128)(2,1)S(1)}, bf16[4,8,1024]{2,1,0:T(8,128)(2,1)S(1)}, u32[]{:S(2)}, u32[]{:S(2)}) collective-permute-start(bf16[4,8,1024]{2,1,0:T(8,128)(2,1)S(1)} %get-tuple-element.26), channel_id=1, source_target_pairs={{0,24},{8,16},{16,8},{24,0},{1,25},{9,17},{17,9},{25,1},{2,26},{10... | collective-permute-start | bytes 196616 | tf_op jit(solution)/shard_map/ppermute | solution.py:151
  14.9 4.5 %collective-permute-start.3 = (bf16[2,8,1024]{2,1,0:T(8,128)(2,1)S(1)}, bf16[2,8,1024]{2,1,0:T(8,128)(2,1)S(1)}, u32[]{:S(2)}, u32[]{:S(2)}) collective-permute-start(bf16[2,8,1024]{2,1,0:T(8,128)(2,1)S(1)} %get-tuple-element.28), channel_id=1, source_target_pairs={{0,2},{1,3},{2,0},{3,1},{4,6},{5,7},{6,4},{7,5},{8,10},{9,11},{10,... | collective-permute-start | bytes 98312 | tf_op jit(solution)/shard_map/ppermute | solution.py:151
  17.0 9.2 %collective-permute-start.4 = (bf16[2,8,1024]{2,1,0:T(8,128)(2,1)S(1)}, bf16[2,8,1024]{2,1,0:T(8,128)(2,1)S(1)}, u32[]{:S(2)}, u32[]{:S(2)}) collective-permute-start(bf16[2,8,1024]{2,1,0:T(8,128)(2,1)S(1)} %get-tuple-element.29), channel_id=1, source_target_pairs={{0,4},{1,5},{2,6},{3,7},{4,0},{5,1},{6,2},{7,3},{8,12},{9,13},{10,... | collective-permute-start | bytes 98312 | tf_op jit(solution)/shard_map/ppermute | solution.py:151
  19.4 6.8 %collective-permute-start.5 = (bf16[2,8,1024]{2,1,0:T(8,128)(2,1)S(1)}, bf16[2,8,1024]{2,1,0:T(8,128)(2,1)S(1)}, u32[]{:S(2)}, u32[]{:S(2)}) collective-permute-start(bf16[2,8,1024]{2,1,0:T(8,128)(2,1)S(1)} %get-tuple-element.30), channel_id=1, source_target_pairs={{0,6},{1,7},{2,4},{3,5},{4,2},{5,3},{6,0},{7,1},{8,14},{9,15},{10,... | collective-permute-start | bytes 98312 | tf_op jit(solution)/shard_map/ppermute | solution.py:151
  26.2 5.9 %copy-start = (bf16[128,2,512]{2,1,0:T(2,128)(2,1)S(1)}, bf16[128,2,512]{2,1,0:T(2,128)(2,1)}, u32[]{:S(2)}) copy-start(bf16[128,2,512]{2,1,0:T(2,128)(2,1)} %new_ref.1) | copy-start | bytes 786436
  27.5 4.6 %collective-permute-start.7 = (bf16[256,1024]{1,0:T(8,128)(2,1)S(1)}, bf16[256,1024]{1,0:T(8,128)(2,1)S(1)}, u32[]{:S(2)}, u32[]{:S(2)}) collective-permute-start(bf16[256,1024]{1,0:T(8,128)(2,1)S(1)} %bitcast.3), channel_id=1, source_target_pairs={{0,8},{8,0},{16,24},{24,16},{1,9},{9,1},{17,25},{25,17},{2,10},{10... | collective-permute-start | bytes 1572872 | tf_op jit(solution)/shard_map/ppermute | solution.py:151
  27.5 4.5 %collective-permute-start.6 = (bf16[4,8,1024]{2,1,0:T(8,128)(2,1)S(1)}, bf16[4,8,1024]{2,1,0:T(8,128)(2,1)S(1)}, u32[]{:S(2)}, u32[]{:S(2)}) collective-permute-start(bf16[4,8,1024]{2,1,0:T(8,128)(2,1)S(1)} %get-tuple-element.35), channel_id=1, source_target_pairs={{0,1},{1,0},{2,3},{3,2},{4,5},{5,4},{6,7},{7,6},{8,9},{9,8},{10,11... | collective-permute-start | bytes 196616 | tf_op jit(solution)/shard_map/ppermute | solution.py:151

commit v7 on v5

--- a/solution.py
+++ b/solution.py
@@ -11,7 +11,9 @@
 SPAN = 128
 PAGE = 8
 RUN = 4
+PARTS = 4
 Z = 4
+CHUNK = 4
 NEGATIVE = -1e30
 SCALE2 = HD ** (-0.5) * 1.4426950408889634
 VMEM = pl.BlockSpec(memory_space=pltpu.VMEM)
@@ -22,13 +24,13 @@
     return pltpu.CompilerParams(vmem_limit_bytes=mib * 2**20)
 
 
-def pack_kernel(dom_count, anc_hbm, len_hbm, prompt_hbm, cache_hbm, half_ref, *refs):
+def pack_kernel(dom_count, anc_hbm, len_hbm, prompt_hbm, cache_hbm, part_ref, *refs):
     out_refs = refs[:dom_count]
     far_ref, limit_ref, anc_ref, len_ref, prompt_ref, cache_ref, sems = refs[dom_count:]
     group = cache_ref.shape[0]
     dom = lax.axis_index("dom")
-    rows, width = half_ref.shape
-    from_row = pl.multiple_of((dom % 2) * rows, rows)
+    _, rows, width = part_ref.shape
+    from_row = pl.multiple_of((dom % PARTS) * rows, rows)
     prompt_in = pltpu.make_async_copy(prompt_hbm.at[pl.ds(from_row, rows)], prompt_ref, sems.at[0])
     anc_in = pltpu.make_async_copy(anc_hbm, anc_ref, sems.at[1])
     len_in = pltpu.make_async_copy(len_hbm, len_ref, sems.at[2])
@@ -46,7 +48,9 @@
     particle = dom * group + lax.axis_index("ctx")
     limit_ref[...] = jnp.full(limit_ref.shape, len_ref[anc_ref[particle]] * PAGE)
     prompt_in.wait()
-    half_ref[...] = prompt_ref[...].reshape(rows, width)
+    part = prompt_ref[...].reshape(rows, width)
+    for to in range(part_ref.shape[0]):
+        part_ref[to] = part
     cache_in.wait()
     for k, out_ref in enumerate(out_refs):
         for run in range(runs):
@@ -117,28 +121,40 @@
     page_y = (at // (page_rows * Z)) ^ (ctx % y_count)
     at = (page_z * y_count + page_y) * page_rows + at % page_rows
     visible = at < jnp.broadcast_to(limit_ref[:1], (SPAN, gen))
-    copies = []
+    keys, values = [], []
     for g in range(kvh):
         k_at = slice(g * HD, (g + 1) * HD)
         v_at = slice(width + g * HD, width + (g + 1) * HD)
-        keys = jnp.concatenate([new[:, k_at]] + [p[:, k_at] for p in (*pieces, *pages)], axis=0)
-        values = jnp.concatenate([new[:, v_at]] + [p[:, v_at] for p in (*pieces, *pages)], axis=0)
-        values = jnp.concatenate([values, ones], axis=1)
-        scores = dot_nt(head_rows(q_ref, g, gq), keys)
+        keys.append(jnp.concatenate([new[:, k_at]] + [p[:, k_at] for p in (*pieces, *pages)], axis=0))
+        value = jnp.concatenate([new[:, v_at]] + [p[:, v_at] for p in (*pieces, *pages)], axis=0)
+        values.append(jnp.concatenate([value, ones], axis=1))
+    chunk = CHUNK * HD
+    per_group = gq // CHUNK
+    count = q_ref.shape[1] // chunk
+
+    def scores_of(c):
+        return dot_nt(head_rows(q_ref, c, CHUNK), keys[c // per_group])
+
+    copies = []
+    ahead = scores_of(0)
+    for c in range(count):
+        scores = ahead
+        if c + 1 < count:
+            ahead = scores_of(c + 1)
         weights = []
-        for j in range(gq):
+        for j in range(CHUNK):
             s = scores[j * SPAN : (j + 1) * SPAN]
             s_new = jnp.where(causal, s[:, :SPAN], NEGATIVE)
             s_cache = jnp.where(visible, s[:, SPAN + old :], NEGATIVE)
             s = jnp.concatenate([s_new, s[:, SPAN : SPAN + old], s_cache], axis=1)
             top = jnp.max(s, axis=1, keepdims=True)
             weights.append(jnp.exp2((s - top) * SCALE2).astype(jnp.bfloat16))
-        out = dot_nn(jnp.concatenate(weights, axis=0), values)
+        out = dot_nn(jnp.concatenate(weights, axis=0), values[c // per_group])
         out = (out[:, :HD] / out[:, HD:]).astype(jnp.bfloat16)
-        for j in range(gq):
-            stage[:, (g * gq + j) * HD : (g * gq + j + 1) * HD] = out[j * SPAN : (j + 1) * SPAN]
-        columns = pl.ds(g * gq * HD, gq * HD)
-        copy = pltpu.make_async_copy(stage.at[:, columns], out_ref.at[:, columns], sems.at[g])
+        for j in range(CHUNK):
+            stage[:, (c * CHUNK + j) * HD : (c * CHUNK + j + 1) * HD] = out[j * SPAN : (j + 1) * SPAN]
+        columns = pl.ds(c * chunk, chunk)
+        copy = pltpu.make_async_copy(stage.at[:, columns], out_ref.at[:, columns], sems.at[c])
         copy.start()
         copies.append(copy)
     for copy in copies:
@@ -156,12 +172,12 @@
     group, page_rows, _, width = cache_kv.shape
     tokens, q_width = q_new.shape
     kvh = width // HD
-    half_rows = prompt_kv.shape[0] // 2
+    part_rows = prompt_kv.shape[0] // PARTS
     shape = jax.ShapeDtypeStruct
-    half, *rest = pl.pallas_call(
+    parts, *rest = pl.pallas_call(
         functools.partial(pack_kernel, dom_count),
         out_shape=(
-            shape((half_rows, 2 * width), jnp.bfloat16),
+            shape((ctx_count, part_rows, 2 * width), jnp.bfloat16),
             *[shape((RUN, page_rows, 2 * width), jnp.bfloat16)] * dom_count,
             shape((group // RUN, page_rows, HD), jnp.bfloat16),
             shape((8, ctx_count * page_rows), jnp.int32),
@@ -171,7 +187,7 @@
         scratch_shapes=[
             pltpu.SMEM(ancestors.shape, jnp.int32),
             pltpu.SMEM(lengths.shape, jnp.int32),
-            pltpu.VMEM((half_rows, 2, width), jnp.bfloat16),
+            pltpu.VMEM((part_rows, 2, width), jnp.bfloat16),
             pltpu.VMEM(cache_kv.shape, jnp.bfloat16),
             pltpu.SemaphoreType.DMA((4,)),
         ],
@@ -180,9 +196,8 @@
     )(*(pltpu.with_memory_space_constraint(x, pltpu.HBM) for x in (ancestors, lengths, prompt_kv, cache_kv)))
     outgoing, far, limit = rest[:dom_count], rest[dom_count], rest[dom_count + 1]
 
-    pieces = [half] + [swap(half, "ctx", k * y_count) for k in range(1, Z)]
-    pieces += [swap(p, "ctx", k) for k in range(1, y_count) for p in pieces[:Z]]
-    pieces += [swap(p, "dom", 1) for p in pieces]
+    own_part = lax.all_to_all(parts, "ctx", split_axis=0, concat_axis=0, tiled=True)
+    own_part = own_part.reshape(ctx_count * part_rows, 2 * width)
 
     incoming = outgoing[:1] + [swap(outgoing[k], "dom", k) for k in range(1, dom_count)]
     routed = pl.pallas_call(
@@ -193,6 +208,9 @@
         compiler_params=params(12),
         name="route",
     )(far, *incoming)
+    own_part, own_route = lax.optimization_barrier((own_part, routed[0]))
+    routed = (own_route,) + tuple(routed[1:])
+    pieces = [own_part, swap(own_part, "dom", 2)]
     routed = routed[:1] + tuple(swap(routed[k], "ctx", k * y_count) for k in range(1, Z))
     *pages, q_new = pl.pallas_call(
         turn_kernel,
@@ -203,6 +221,8 @@
         compiler_params=params(12),
         name="turn",
     )(pltpu.with_memory_space_constraint(q_new, pltpu.HBM), *routed)
+    pieces[1], pages[0] = lax.optimization_barrier((pieces[1], pages[0]))
+    pieces += [swap(piece, "dom", 1) for piece in pieces]
     pages = pages[:1] + [swap(pages[j], "ctx", j) for j in range(1, y_count)]
     pages = [page.reshape(Z * page_rows, 2 * width) for page in pages]
 
@@ -211,7 +231,7 @@
         out_shape=shape((tokens, q_width), jnp.bfloat16),
         in_specs=[VMEM] * (3 + len(pages) + len(pieces)),
         out_specs=HBM,
-        scratch_shapes=[pltpu.VMEM((tokens, q_width), jnp.bfloat16), pltpu.SemaphoreType.DMA((kvh,))],
+        scratch_shapes=[pltpu.VMEM((tokens, q_width), jnp.bfloat16), pltpu.SemaphoreType.DMA((q_width // (CHUNK * HD),))],
         compiler_params=params(40 if prompt_kv.shape[0] * ctx_count > 1024 else 24),
         name="attend",
     )(limit, q_new, kv_new, *pages, *pieces)

time: 35.1 us -> 38 us (1.083)
  waiting for transfers between devices: 7.23 us -> 12.7 us
  starting transfers between devices: 19.7 us -> 16.8 us
    ppermute x22 -> x10, starting transfers between devices: 19.7 us -> 9.49 us  [swap(): lax.ppermute(x, axis, [(i, i ^ distance) for i in range(lax.axis_size(axi...]
    all_to_all x0 -> x1, starting transfers between devices: none -> 7.29 us  [on_device(): lax.all_to_all(parts, 'ctx', split_axis=0, concat_axis=0, tiled=True)]
    all_to_all x0 -> x1, waiting for transfers between devices: none -> 3.22 us  [on_device(): lax.all_to_all(parts, 'ctx', split_axis=0, concat_axis=0, tiled=True)]
    ppermute x22 -> x10, waiting for transfers between devices: 7.23 us -> 9.5 us  [swap(): lax.ppermute(x, axis, [(i, i ^ distance) for i in range(lax.axis_size(axi...]
    pallas_call x1, Pallas kernels: 1.12 us -> 1.81 us  [on_device(): pl.pallas_call(functools.partial(pack_kernel, dom_count), out_shape=(shap...]
    pallas_call x1, Pallas kernels: 5.47 us -> 4.97 us  [on_device(): pl.pallas_call(functools.partial(attend_kernel, y_count), out_shape=shape...]
  transfers between devices with their start and end apart: 22 -> 11, of which waited for: 6 -> 6; matrix products, arithmetic and copies ran while one was open for 0% -> 0% of each run, Pallas kernels for 4% -> 3%
where the time goes in v7:
time: 38 us; the launch traced here: 37.6 us
  starting transfers between devices  16.8 us (44%)
  waiting for transfers between devices  12.7 us (33%)
  Pallas kernels  8.08 us (21%)
    ppermute x10, waiting for transfers between devices, swap(): lax.ppermute(x, axis, [(i, i ^ distance) for i in range(lax.axis_size(axi...  9.5 us
    ppermute x10, starting transfers between devices, swap(): lax.ppermute(x, axis, [(i, i ^ distance) for i in range(lax.axis_size(axi...  9.49 us
    all_to_all x1, starting transfers between devices, on_device(): lax.all_to_all(parts, 'ctx', split_axis=0, concat_axis=0, tiled=True)  7.29 us
    pallas_call x1, Pallas kernels, on_device(): pl.pallas_call(functools.partial(attend_kernel, y_count), out_shape=shape...  4.97 us
    all_to_all x1, waiting for transfers between devices, on_device(): lax.all_to_all(parts, 'ctx', split_axis=0, concat_axis=0, tiled=True)  3.22 us
    pallas_call x1, Pallas kernels, on_device(): pl.pallas_call(functools.partial(pack_kernel, dom_count), out_shape=(shap...  1.81 us
    pallas_call x1, Pallas kernels, on_device(): pl.pallas_call(turn_kernel, out_shape=(shape((Z, page_rows, 2 * width), j...  1.23 us
  transfers between devices with their start and end apart: 11, of which 6 were waited for; matrix products, arithmetic and copies ran while one was open for 0% of the time, Pallas kernels for 3%

profile of v7, /device:TPU:0, one launch (start us, length us, event | category | flops | bytes accessed | tf_op | source)
XLA Modules:
  0.0 37.6 jit_solution(377974552079685919)
XLA Ops:
  0.0 1.8 %pack.1 = (bf16[8,16,1024]{2,1,0:T(8,128)(2,1)}, bf16[4,8,1024]{2,1,0:T(8,128)(2,1)S(1)}, bf16[4,8,1024]{2,1,0:T(8,128)(2,1)S(1)}, bf16[4,8,1024]{2,1,0:T(8,128)...) custom-call(s32[32]{0:T(128)} %anc_hbm.1, s32[32]{0:T(128)} %len_hbm.1, ...), custom_call_target="tpu_custom_call" | custom-call | tf_op jit(solution)/shard_map/pack/pallas_call | solution.py:177
  1.8 7.3 %all-to-all-start = ((bf16[8,16,1024]{2,1,0:T(8,128)(2,1)}), bf16[8,16,1024]{2,1,0:T(8,128)(2,1)S(1)}, u32[]{:S(2)}, u32[]{:S(2)}) async-start(bf16[8,16,1024]{2,1,0:T(8,128)(2,1)} %get-tuple-element.24), calls=%async_computation | async-start | bytes 524288 | tf_op jit(solution)/shard_map/all_to_all | solution.py:199
  9.1 0.0 collective-permute-start
  9.1 1.6 %collective-permute-start.1 = (bf16[4,8,1024]{2,1,0:T(8,128)(2,1)S(1)}, bf16[4,8,1024]{2,1,0:T(8,128)(2,1)S(1)}, u32[]{:S(2)}, u32[]{:S(2)}) collective-permute-start(bf16[4,8,1024]{2,1,0:T(8,128)(2,1)S(1)} %get-tuple-element.28), channel_id=1, source_target_pairs={{0,16},{8,24},{16,0},{24,8},{1,17},{9,25},{17,1},{25,9},{2,18},{10... | collective-permute-start | bytes 196616 | tf_op jit(solution)/shard_map/ppermute | solution.py:165
  10.7 0.3 collective-permute-start.2
  11.0 0.0 collective-permute-done.refs_1_
  11.0 2.6 %collective-permute-done.1.refs_2_ = bf16[4,8,1024]{2,1,0:T(8,128)(2,1)S(1)} collective-permute-done((bf16[4,8,1024]{2,1,0:T(8,128)(2,1)S(1)}, bf16[4,8,1024]{2,1,0:T(8,128)(2,1)S(1)}, u32[]{:S(2)}, u32[]{:S(2)}) %collective-permute-start.1) | collective-permute-done | bytes 65568 | tf_op jit(solution)/shard_map/ppermute | solution.py:165
  13.6 1.1 %collective-permute-done.2.refs_3_ = bf16[4,8,1024]{2,1,0:T(8,128)(2,1)S(1)} collective-permute-done((bf16[4,8,1024]{2,1,0:T(8,128)(2,1)S(1)}, bf16[4,8,1024]{2,1,0:T(8,128)(2,1)S(1)}, u32[]{:S(2)}, u32[]{:S(2)}) %collective-permute-start.2) | collective-permute-done | bytes 65568 | tf_op jit(solution)/shard_map/ppermute | solution.py:165
  14.7 0.1 route.1
  14.8 3.2 %all-to-all-done = bf16[8,16,1024]{2,1,0:T(8,128)(2,1)S(1)} async-done(((bf16[8,16,1024]{2,1,0:T(8,128)(2,1)}), bf16[8,16,1024]{2,1,0:T(8,128)(2,1)S(1)}, u32[]{:S(2)}, u32[]{:S(2)}) %all-to-all-start) | async-done | bytes 262176 | tf_op jit(solution)/shard_map/all_to_all | solution.py:199
  18.0 1.4 %collective-permute-start.6 = (bf16[128,1024]{1,0:T(8,128)(2,1)S(1)}, bf16[128,1024]{1,0:T(8,128)(2,1)S(1)}, u32[]{:S(2)}, u32[]{:S(2)}) collective-permute-start(bf16[128,1024]{1,0:T(8,128)(2,1)S(1)} %bitcast.3), channel_id=1, source_target_pairs={{0,16},{8,24},{16,0},{24,8},{1,17},{9,25},{17,1},{25,9},{2,18},{10... | collective-permute-start | bytes 786440 | tf_op jit(solution)/shard_map/ppermute | solution.py:165
  19.4 1.1 %collective-permute-start.3 = (bf16[2,8,1024]{2,1,0:T(8,128)(2,1)S(1)}, bf16[2,8,1024]{2,1,0:T(8,128)(2,1)S(1)}, u32[]{:S(2)}, u32[]{:S(2)}) collective-permute-start(bf16[2,8,1024]{2,1,0:T(8,128)(2,1)S(1)} %get-tuple-element.32), channel_id=1, source_target_pairs={{0,2},{1,3},{2,0},{3,1},{4,6},{5,7},{6,4},{7,5},{8,10},{9,11},{10,... | collective-permute-start | bytes 98312 | tf_op jit(solution)/shard_map/ppermute | solution.py:165
  20.5 0.6 %collective-permute-start.4 = (bf16[2,8,1024]{2,1,0:T(8,128)(2,1)S(1)}, bf16[2,8,1024]{2,1,0:T(8,128)(2,1)S(1)}, u32[]{:S(2)}, u32[]{:S(2)}) collective-permute-start(bf16[2,8,1024]{2,1,0:T(8,128)(2,1)S(1)} %get-tuple-element.33), channel_id=1, source_target_pairs={{0,4},{1,5},{2,6},{3,7},{4,0},{5,1},{6,2},{7,3},{8,12},{9,13},{10,... | collective-permute-start | bytes 98312 | tf_op jit(solution)/shard_map/ppermute | solution.py:165
  21.1 0.0 copy-start
  21.1 2.7 %collective-permute-start.5 = (bf16[2,8,1024]{2,1,0:T(8,128)(2,1)S(1)}, bf16[2,8,1024]{2,1,0:T(8,128)(2,1)S(1)}, u32[]{:S(2)}, u32[]{:S(2)}) collective-permute-start(bf16[2,8,1024]{2,1,0:T(8,128)(2,1)S(1)} %get-tuple-element.34), channel_id=1, source_target_pairs={{0,6},{1,7},{2,4},{3,5},{4,2},{5,3},{6,0},{7,1},{8,14},{9,15},{10,... | collective-permute-start | bytes 98312 | tf_op jit(solution)/shard_map/ppermute | solution.py:165
  23.8 0.0 collective-permute-start.8
  23.8 0.0 collective-permute-done.3.refs_1_
  23.8 2.0 %collective-permute-done.4.refs_2_ = bf16[2,8,1024]{2,1,0:T(8,128)(2,1)S(1)} collective-permute-done((bf16[2,8,1024]{2,1,0:T(8,128)(2,1)S(1)}, bf16[2,8,1024]{2,1,0:T(8,128)(2,1)S(1)}, u32[]{:S(2)}, u32[]{:S(2)}) %collective-permute-start.4) | collective-permute-done | bytes 32800 | tf_op jit(solution)/shard_map/ppermute | solution.py:165
  25.8 1.0 %collective-permute-done.5.refs_3_ = bf16[2,8,1024]{2,1,0:T(8,128)(2,1)S(1)} collective-permute-done((bf16[2,8,1024]{2,1,0:T(8,128)(2,1)S(1)}, bf16[2,8,1024]{2,1,0:T(8,128)(2,1)S(1)}, u32[]{:S(2)}, u32[]{:S(2)}) %collective-permute-start.5) | collective-permute-done | bytes 32800 | tf_op jit(solution)/shard_map/ppermute | solution.py:165
  26.8 1.2 %turn.1 = (bf16[4,8,1024]{2,1,0:T(8,128)(2,1)S(1)}, bf16[4,8,1024]{2,1,0:T(8,128)(2,1)S(1)}, bf16[128,4096]{1,0:T(8,128)(2,1)S(1)}) custom-call(bf16[128,4096]{1,0:T(8,128)(2,1)} %q_hbm.1, bf16[2,8,1024]{2,1,0:T(8,128)(2,1)S(1)} %get-tuple-element.31.refs_0_, bf16[2,8,1024]{2,1,0:T(8,128)(2,1)S(1)} %collective-permute-done.3.refs_1_, ...), custom_call_target="tpu_custom_call" | custom-call | tf_op jit(solution)/shard_map/turn/pallas_call | solution.py:215
  28.1 0.0 collective-permute-done.6.refs_3_
  28.1 0.1 collective-permute-start.9
  28.2 1.8 %collective-permute-start.7 = (bf16[4,8,1024]{2,1,0:T(8,128)(2,1)S(1)}, bf16[4,8,1024]{2,1,0:T(8,128)(2,1)S(1)}, u32[]{:S(2)}, u32[]{:S(2)}) collective-permute-start(bf16[4,8,1024]{2,1,0:T(8,128)(2,1)S(1)} %get-tuple-element.39), channel_id=1, source_target_pairs={{0,1},{1,0},{2,3},{3,2},{4,5},{5,4},{6,7},{7,6},{8,9},{9,8},{10,11... | collective-permute-start | bytes 196616 | tf_op jit(solution)/shard_map/ppermute | solution.py:165
  30.0 2.7 %collective-permute-done.7 = bf16[4,8,1024]{2,1,0:T(8,128)(2,1)S(1)} collective-permute-done((bf16[4,8,1024]{2,1,0:T(8,128)(2,1)S(1)}, bf16[4,8,1024]{2,1,0:T(8,128)(2,1)S(1)}, u32[]{:S(2)}, u32[]{:S(2)}) %collective-permute-start.7) | collective-permute-done | bytes 65568 | tf_op jit(solution)/shard_map/ppermute | solution.py:165
  32.7 0.0 collective-permute-done.8.refs_4_
  32.7 0.0 collective-permute-done.9.refs_5_
  32.7 0.0 copy-done
  32.7 5.0 %attend.1 = bf16[128,4096]{1,0:T(8,128)(2,1)} custom-call(s32[8,64]{1,0:T(8,128)S(1)} %get-tuple-element.23.limit_ref, bf16[128,4096]{1,0:T(8,128)(2,1)S(1)} %get-tuple-element.35.q_ref, bf16[128,2,512]{2,1,0:T(2,128)(2,1)S(1)} %copy-done, bf16[32,1024]{1,0:T(8,128)(2,1)S(1)} %bitcast.6, bf16[32,1024]{1,0:T(8,128)(2,1)S(1)} %bitcast.7, ...), custom_call_target="tpu_custom_call" | custom-call | tf_op jit(solution)/shard_map/attend/pallas_call | solution.py:229
Async XLA Ops:
  1.8 16.2 %all-to-all-start = ((bf16[8,16,1024]{2,1,0:T(8,128)(2,1)}), bf16[8,16,1024]{2,1,0:T(8,128)(2,1)S(1)}, u32[]{:S(2)}, u32[]{:S(2)}) async-start(bf16[8,16,1024]{2,1,0:T(8,128)(2,1)} %get-tuple-element.24), calls=%async_computation | async-start | bytes 524288 | tf_op jit(solution)/shard_map/all_to_all | solution.py:199
  9.1 1.9 %collective-permute-start = (bf16[4,8,1024]{2,1,0:T(8,128)(2,1)S(1)}, bf16[4,8,1024]{2,1,0:T(8,128)(2,1)S(1)}, u32[]{:S(2)}, u32[]{:S(2)}) collective-permute-start(bf16[4,8,1024]{2,1,0:T(8,128)(2,1)S(1)} %get-tuple-element.27), channel_id=1, source_target_pairs={{0,8},{8,0},{16,24},{24,16},{1,9},{9,1},{17,25},{25,17},{2,10},{10... | collective-permute-start | bytes 196616 | tf_op jit(solution)/shard_map/ppermute | solution.py:165
  9.1 4.5 %collective-permute-start.1 = (bf16[4,8,1024]{2,1,0:T(8,128)(2,1)S(1)}, bf16[4,8,1024]{2,1,0:T(8,128)(2,1)S(1)}, u32[]{:S(2)}, u32[]{:S(2)}) collective-permute-start(bf16[4,8,1024]{2,1,0:T(8,128)(2,1)S(1)} %get-tuple-element.28), channel_id=1, source_target_pairs={{0,16},{8,24},{16,0},{24,8},{1,17},{9,25},{17,1},{25,9},{2,18},{10... | collective-permute-start | bytes 196616 | tf_op jit(solution)/shard_map/ppermute | solution.py:165
  10.7 4.1 %collective-permute-start.2 = (bf16[4,8,1024]{2,1,0:T(8,128)(2,1)S(1)}, bf16[4,8,1024]{2,1,0:T(8,128)(2,1)S(1)}, u32[]{:S(2)}, u32[]{:S(2)}) collective-permute-start(bf16[4,8,1024]{2,1,0:T(8,128)(2,1)S(1)} %get-tuple-element.29), channel_id=1, source_target_pairs={{0,24},{8,16},{16,8},{24,0},{1,25},{9,17},{17,9},{25,1},{2,26},{10... | collective-permute-start | bytes 196616 | tf_op jit(solution)/shard_map/ppermute | solution.py:165
  18.0 10.0 %collective-permute-start.6 = (bf16[128,1024]{1,0:T(8,128)(2,1)S(1)}, bf16[128,1024]{1,0:T(8,128)(2,1)S(1)}, u32[]{:S(2)}, u32[]{:S(2)}) collective-permute-start(bf16[128,1024]{1,0:T(8,128)(2,1)S(1)} %bitcast.3), channel_id=1, source_target_pairs={{0,16},{8,24},{16,0},{24,8},{1,17},{9,25},{17,1},{25,9},{2,18},{10... | collective-permute-start | bytes 786440 | tf_op jit(solution)/shard_map/ppermute | solution.py:165
  19.4 4.4 %collective-permute-start.3 = (bf16[2,8,1024]{2,1,0:T(8,128)(2,1)S(1)}, bf16[2,8,1024]{2,1,0:T(8,128)(2,1)S(1)}, u32[]{:S(2)}, u32[]{:S(2)}) collective-permute-start(bf16[2,8,1024]{2,1,0:T(8,128)(2,1)S(1)} %get-tuple-element.32), channel_id=1, source_target_pairs={{0,2},{1,3},{2,0},{3,1},{4,6},{5,7},{6,4},{7,5},{8,10},{9,11},{10,... | collective-permute-start | bytes 98312 | tf_op jit(solution)/shard_map/ppermute | solution.py:165
  20.5 5.3 %collective-permute-start.4 = (bf16[2,8,1024]{2,1,0:T(8,128)(2,1)S(1)}, bf16[2,8,1024]{2,1,0:T(8,128)(2,1)S(1)}, u32[]{:S(2)}, u32[]{:S(2)}) collective-permute-start(bf16[2,8,1024]{2,1,0:T(8,128)(2,1)S(1)} %get-tuple-element.33), channel_id=1, source_target_pairs={{0,4},{1,5},{2,6},{3,7},{4,0},{5,1},{6,2},{7,3},{8,12},{9,13},{10,... | collective-permute-start | bytes 98312 | tf_op jit(solution)/shard_map/ppermute | solution.py:165
  21.1 11.6 %copy-start = (bf16[128,2,512]{2,1,0:T(2,128)(2,1)S(1)}, bf16[128,2,512]{2,1,0:T(2,128)(2,1)}, u32[]{:S(2)}) copy-start(bf16[128,2,512]{2,1,0:T(2,128)(2,1)} %new_ref.1) | copy-start | bytes 786436
  21.1 5.7 %collective-permute-start.5 = (bf16[2,8,1024]{2,1,0:T(8,128)(2,1)S(1)}, bf16[2,8,1024]{2,1,0:T(8,128)(2,1)S(1)}, u32[]{:S(2)}, u32[]{:S(2)}) collective-permute-start(bf16[2,8,1024]{2,1,0:T(8,128)(2,1)S(1)} %get-tuple-element.34), channel_id=1, source_target_pairs={{0,6},{1,7},{2,4},{3,5},{4,2},{5,3},{6,0},{7,1},{8,14},{9,15},{10,... | collective-permute-start | bytes 98312 | tf_op jit(solution)/shard_map/ppermute | solution.py:165
  23.8 8.9 %collective-permute-start.8 = (bf16[128,1024]{1,0:T(8,128)(2,1)S(1)}, bf16[128,1024]{1,0:T(8,128)(2,1)S(1)}, u32[]{:S(2)}, u32[]{:S(2)}) collective-permute-start(bf16[128,1024]{1,0:T(8,128)(2,1)S(1)} %bitcast.4), channel_id=1, source_target_pairs={{0,8},{8,0},{16,24},{24,16},{1,9},{9,1},{17,25},{25,17},{2,10},{10... | collective-permute-start | bytes 786440 | tf_op jit(solution)/shard_map/ppermute | solution.py:165
  28.1 4.6 %collective-permute-start.9 = (bf16[128,1024]{1,0:T(8,128)(2,1)S(1)}, bf16[128,1024]{1,0:T(8,128)(2,1)S(1)}, u32[]{:S(2)}, u32[]{:S(2)}) collective-permute-start(bf16[128,1024]{1,0:T(8,128)(2,1)S(1)} %collective-permute-done.6.refs_3_), channel_id=1, source_target_pairs={{0,8},{8,0},{16,24},{24,16},{1,9},{9,1},{17,25},{25,17},{2,10},{10... | collective-permute-start | bytes 786440 | tf_op jit(solution)/shard_map/ppermute | solution.py:165
  28.2 4.5 %collective-permute-start.7 = (bf16[4,8,1024]{2,1,0:T(8,128)(2,1)S(1)}, bf16[4,8,1024]{2,1,0:T(8,128)(2,1)S(1)}, u32[]{:S(2)}, u32[]{:S(2)}) collective-permute-start(bf16[4,8,1024]{2,1,0:T(8,128)(2,1)S(1)} %get-tuple-element.39), channel_id=1, source_target_pairs={{0,1},{1,0},{2,3},{3,2},{4,5},{5,4},{6,7},{7,6},{8,9},{9,8},{10,11... | collective-permute-start | bytes 196616 | tf_op jit(solution)/shard_map/ppermute | solution.py:165

commit v8 on v4

--- a/solution.py
+++ b/solution.py
@@ -12,6 +12,7 @@
 PAGE = 8
 RUN = 4
 Z = 4
+CHUNK = 4
 NEGATIVE = -1e30
 SCALE2 = HD ** (-0.5) * 1.4426950408889634
 VMEM = pl.BlockSpec(memory_space=pltpu.VMEM)
@@ -59,8 +60,8 @@
                     out_ref[slot] = cache_ref[local].reshape(cache_ref.shape[1], width)
 
 
-def route_kernel(far_ref, *refs):
-    *in_refs, out_hbm, out_ref, sem = refs
+def route_kernel(dom_count, far_ref, *refs):
+    in_refs, (out_hbm, out_ref, sem) = refs[:dom_count], refs[-3:]
     width = out_ref.shape[2]
     for run in range(far_ref.shape[0]):
         far = far_ref[run]
@@ -89,8 +90,15 @@
     return lax.dot_general(a, b, (((1,), (0,)), ((), ())), preferred_element_type=jnp.float32)
 
 
-def attend_kernel(limit_ref, q_ref, new_ref, cache_ref, *refs):
-    *pieces, out_ref, stage, sems = refs
+def attend_kernel(limit_ref, q_hbm, new_ref, cache_ref, *refs):
+    pieces, (out_ref, q_ref, stage, sems) = refs[:-4], refs[-4:]
+    chunk = CHUNK * HD
+    count = q_ref.shape[1] // chunk
+    q_copies = []
+    for c in range(count):
+        columns = pl.ds(c * chunk, chunk)
+        q_copies.append(pltpu.make_async_copy(q_hbm.at[:, columns], q_ref.at[:, columns], sems.at[count + c]))
+        q_copies[c].start()
     width = new_ref.shape[2]
     gen = cache_ref.shape[0]
     kvh = width // HD
@@ -101,28 +109,39 @@
     token = lax.broadcasted_iota(jnp.int32, (SPAN, SPAN), 0)
     causal = lax.broadcasted_iota(jnp.int32, (SPAN, SPAN), 1) <= token
     visible = lax.broadcasted_iota(jnp.int32, (SPAN, gen), 1) < jnp.broadcast_to(limit_ref[:1], (SPAN, gen))
-    copies = []
+    keys, values = [], []
     for g in range(kvh):
         k_at = slice(g * HD, (g + 1) * HD)
         v_at = slice(width + g * HD, width + (g + 1) * HD)
-        keys = jnp.concatenate([new[:, k_at]] + [p[:, k_at] for p in pieces] + [cache_ref[:, k_at]], axis=0)
-        values = jnp.concatenate([new[:, v_at]] + [p[:, v_at] for p in pieces] + [cache_ref[:, v_at]], axis=0)
-        values = jnp.concatenate([values, ones], axis=1)
-        scores = dot_nt(head_rows(q_ref, g, gq), keys)
+        keys.append(jnp.concatenate([new[:, k_at]] + [p[:, k_at] for p in (*pieces, cache_ref)], axis=0))
+        value = jnp.concatenate([new[:, v_at]] + [p[:, v_at] for p in (*pieces, cache_ref)], axis=0)
+        values.append(jnp.concatenate([value, ones], axis=1))
+    per_group = gq // CHUNK
+
+    def scores_of(c):
+        q_copies[c].wait()
+        return dot_nt(head_rows(q_ref, c, CHUNK), keys[c // per_group])
+
+    copies = []
+    ahead = scores_of(0)
+    for c in range(count):
+        scores = ahead
+        if c + 1 < count:
+            ahead = scores_of(c + 1)
         weights = []
-        for j in range(gq):
+        for j in range(CHUNK):
             s = scores[j * SPAN : (j + 1) * SPAN]
             s_new = jnp.where(causal, s[:, :SPAN], NEGATIVE)
             s_cache = jnp.where(visible, s[:, SPAN + old :], NEGATIVE)
             s = jnp.concatenate([s_new, s[:, SPAN : SPAN + old], s_cache], axis=1)
             top = jnp.max(s, axis=1, keepdims=True)
             weights.append(jnp.exp2((s - top) * SCALE2).astype(jnp.bfloat16))
-        out = dot_nn(jnp.concatenate(weights, axis=0), values)
+        out = dot_nn(jnp.concatenate(weights, axis=0), values[c // per_group])
         out = (out[:, :HD] / out[:, HD:]).astype(jnp.bfloat16)
-        for j in range(gq):
-            stage[:, (g * gq + j) * HD : (g * gq + j + 1) * HD] = out[j * SPAN : (j + 1) * SPAN]
-        columns = pl.ds(g * gq * HD, gq * HD)
-        copy = pltpu.make_async_copy(stage.at[:, columns], out_ref.at[:, columns], sems.at[g])
+        for j in range(CHUNK):
+            stage[:, (c * CHUNK + j) * HD : (c * CHUNK + j + 1) * HD] = out[j * SPAN : (j + 1) * SPAN]
+        columns = pl.ds(c * chunk, chunk)
+        copy = pltpu.make_async_copy(stage.at[:, columns], out_ref.at[:, columns], sems.at[c])
         copy.start()
         copies.append(copy)
     for copy in copies:
@@ -139,7 +158,6 @@
     y_count = ctx_count // Z
     group, page_rows, _, width = cache_kv.shape
     tokens, q_width = q_new.shape
-    kvh = width // HD
     half_rows = prompt_kv.shape[0] // 2
     shape = jax.ShapeDtypeStruct
     half, *rest = pl.pallas_call(
@@ -166,30 +184,35 @@
 
     pieces = [half] + [swap(half, "ctx", k * y_count) for k in range(1, Z)]
     pieces += [swap(p, "ctx", k) for k in range(1, y_count) for p in pieces[:Z]]
+    underway = pieces[1 : Z + 2]
     pieces += [swap(p, "dom", 1) for p in pieces]
 
     incoming = outgoing[:1] + [swap(outgoing[k], "dom", k) for k in range(1, dom_count)]
     routed = pl.pallas_call(
-        route_kernel,
+        functools.partial(route_kernel, dom_count),
         out_shape=pltpu.HBM((group, page_rows, 2 * width), jnp.bfloat16),
-        in_specs=[VMEM] * (1 + dom_count),
+        in_specs=[VMEM] * (1 + dom_count) + [pl.BlockSpec(memory_space=pl.ANY)] * len(underway),
         out_specs=HBM,
         scratch_shapes=[pltpu.VMEM((group, page_rows, 2 * width), jnp.bfloat16), pltpu.SemaphoreType.DMA],
         compiler_params=params(12),
         name="route",
-    )(far, *incoming)
+    )(far, *incoming, *underway)
     pages = lax.all_to_all(routed, "ctx", split_axis=0, concat_axis=0, tiled=True)
     pages = pages.reshape(ctx_count * page_rows, 2 * width)
 
     return pl.pallas_call(
         attend_kernel,
         out_shape=shape((tokens, q_width), jnp.bfloat16),
-        in_specs=[VMEM] * (4 + len(pieces)),
+        in_specs=[VMEM, HBM] + [VMEM] * (2 + len(pieces)),
         out_specs=HBM,
-        scratch_shapes=[pltpu.VMEM((tokens, q_width), jnp.bfloat16), pltpu.SemaphoreType.DMA((kvh,))],
+        scratch_shapes=[
+            pltpu.VMEM((tokens, q_width), jnp.bfloat16),
+            pltpu.VMEM((tokens, q_width), jnp.bfloat16),
+            pltpu.SemaphoreType.DMA((2 * q_width // (CHUNK * HD),)),
+        ],
         compiler_params=params(40 if prompt_kv.shape[0] * ctx_count > 1024 else 24),
         name="attend",
-    )(limit, q_new, kv_new, pages, *pieces)
+    )(limit, pltpu.with_memory_space_constraint(q_new, pltpu.HBM), kv_new, pages, *pieces)
 
 
 def solution(mesh):

time: 40.8 us -> 37.4 us (0.917)
  starting transfers between devices: 19.8 us -> 17.3 us
  Pallas kernels: 7.33 us -> 9.36 us
  waiting for transfers between devices: 12.1 us -> 10.4 us
  local copies, waits for them, and re-layouts: 1.23 us -> 0.01 us
    all_to_all x1, starting transfers between devices: 5.88 us -> 3.52 us  [on_device(): lax.all_to_all(routed, 'ctx', split_axis=0, concat_axis=0, tiled=True)]
    pallas_call x1, Pallas kernels: 5.45 us -> 7.6 us  [on_device(): pl.pallas_call(attend_kernel, out_shape=shape((tokens, q_width), jnp.bflo...]
    ppermute x18, waiting for transfers between devices: 12.1 us -> 10.4 us  [swap(): lax.ppermute(x, axis, [(i, i ^ distance) for i in range(lax.axis_size(axi...]
    unnamed x4 -> x2, local copies, waits for them, and re-layouts: 1.23 us -> 0.01 us
  transfers between devices with their start and end apart: 19 -> 19, of which waited for: 8 -> 6; matrix products, arithmetic and copies ran while one was open for 0% -> 0% of each run, Pallas kernels for 0% -> 0%
where the time goes in v8:
time: 37.4 us; the launch traced here: 37.1 us
  starting transfers between devices  17.3 us (46%)
  waiting for transfers between devices  10.4 us (28%)
  Pallas kernels  9.36 us (25%)
    ppermute x18, starting transfers between devices, swap(): lax.ppermute(x, axis, [(i, i ^ distance) for i in range(lax.axis_size(axi...  13.8 us
    ppermute x18, waiting for transfers between devices, swap(): lax.ppermute(x, axis, [(i, i ^ distance) for i in range(lax.axis_size(axi...  10.4 us
    pallas_call x1, Pallas kernels, on_device(): pl.pallas_call(attend_kernel, out_shape=shape((tokens, q_width), jnp.bflo...  7.6 us
    all_to_all x1, starting transfers between devices, on_device(): lax.all_to_all(routed, 'ctx', split_axis=0, concat_axis=0, tiled=True)  3.52 us
    pallas_call x1, Pallas kernels, on_device(): pl.pallas_call(functools.partial(pack_kernel, dom_count), out_shape=(shap...  1.04 us
  transfers between devices with their start and end apart: 19, of which 6 were waited for; matrix products, arithmetic and copies ran while one was open for 0% of the time, Pallas kernels for 0%

profile of v8, /device:TPU:0, one launch (start us, length us, event | category | flops | bytes accessed | tf_op | source)
XLA Modules:
  0.0 37.1 jit_solution(11376263468693145925)
XLA Ops:
  0.0 1.0 %pack.1 = (bf16[32,1024]{1,0:T(8,128)(2,1)S(1)}, bf16[4,8,1024]{2,1,0:T(8,128)(2,1)S(1)}, bf16[4,8,1024]{2,1,0:T(8,128)(2,1)S(1)}, bf16[4,8,1024]{2,1,0:T(8,128)...) custom-call(s32[32]{0:T(128)} %anc_hbm.1, s32[32]{0:T(128)} %len_hbm.1, ...), custom_call_target="tpu_custom_call" | custom-call | tf_op jit(solution)/shard_map/pack/pallas_call | solution.py:163
  1.1 0.5 %collective-permute-start = (bf16[4,8,1024]{2,1,0:T(8,128)(2,1)S(1)}, bf16[4,8,1024]{2,1,0:T(8,128)(2,1)S(1)}, u32[]{:S(2)}, u32[]{:S(2)}) collective-permute-start(bf16[4,8,1024]{2,1,0:T(8,128)(2,1)S(1)} %get-tuple-element.15), channel_id=1, source_target_pairs={{0,8},{8,0},{16,24},{24,16},{1,9},{9,1},{17,25},{25,17},{2,10},{10... | collective-permute-start | bytes 196616 | tf_op jit(solution)/shard_map/ppermute | solution.py:152
  1.6 2.6 %collective-permute-start.1 = (bf16[4,8,1024]{2,1,0:T(8,128)(2,1)S(1)}, bf16[4,8,1024]{2,1,0:T(8,128)(2,1)S(1)}, u32[]{:S(2)}, u32[]{:S(2)}) collective-permute-start(bf16[4,8,1024]{2,1,0:T(8,128)(2,1)S(1)} %get-tuple-element.16), channel_id=1, source_target_pairs={{0,16},{8,24},{16,0},{24,8},{1,17},{9,25},{17,1},{25,9},{2,18},{10... | collective-permute-start | bytes 196616 | tf_op jit(solution)/shard_map/ppermute | solution.py:152
  4.2 1.6 %collective-permute-start.3 = (bf16[32,1024]{1,0:T(8,128)(2,1)S(1)}, bf16[32,1024]{1,0:T(8,128)(2,1)S(1)}, u32[]{:S(2)}, u32[]{:S(2)}) collective-permute-start(bf16[32,1024]{1,0:T(8,128)(2,1)S(1)} %get-tuple-element.18.refs_0_), channel_id=1, source_target_pairs={{0,2},{1,3},{2,0},{3,1},{4,6},{5,7},{6,4},{7,5},{8,10},{9,11},{10,... | collective-permute-start | bytes 196616 | tf_op jit(solution)/shard_map/ppermute | solution.py:152
  5.8 1.5 %collective-permute-start.6 = (bf16[32,1024]{1,0:T(8,128)(2,1)S(1)}, bf16[32,1024]{1,0:T(8,128)(2,1)S(1)}, u32[]{:S(2)}, u32[]{:S(2)}) collective-permute-start(bf16[32,1024]{1,0:T(8,128)(2,1)S(1)} %get-tuple-element.18.refs_0_), channel_id=1, source_target_pairs={{0,1},{1,0},{2,3},{3,2},{4,5},{5,4},{6,7},{7,6},{8,9},{9,8},{10,11... | collective-permute-start | bytes 196616 | tf_op jit(solution)/shard_map/ppermute | solution.py:152
  7.3 2.5 %collective-permute-start.5 = (bf16[32,1024]{1,0:T(8,128)(2,1)S(1)}, bf16[32,1024]{1,0:T(8,128)(2,1)S(1)}, u32[]{:S(2)}, u32[]{:S(2)}) collective-permute-start(bf16[32,1024]{1,0:T(8,128)(2,1)S(1)} %get-tuple-element.18.refs_0_), channel_id=1, source_target_pairs={{0,6},{1,7},{2,4},{3,5},{4,2},{5,3},{6,0},{7,1},{8,14},{9,15},{10,... | collective-permute-start | bytes 196616 | tf_op jit(solution)/shard_map/ppermute | solution.py:152
  9.8 0.0 collective-permute-done.refs_1_
  9.8 0.0 collective-permute-start.2
  9.8 0.0 collective-permute-done.1.refs_2_
  9.8 0.2 collective-permute-start.4
  10.0 0.0 collective-permute-done.3.refs_4_.refs_1_
  10.0 1.2 %collective-permute-start.7 = (bf16[32,1024]{1,0:T(8,128)(2,1)S(1)}, bf16[32,1024]{1,0:T(8,128)(2,1)S(1)}, u32[]{:S(2)}, u32[]{:S(2)}) collective-permute-start(bf16[32,1024]{1,0:T(8,128)(2,1)S(1)} %collective-permute-done.3.refs_4_.refs_1_), channel_id=1, source_target_pairs={{0,1},{1,0},{2,3},{3,2},{4,5},{5,4},{6,7},{7,6},{8,9},{9,8},{10,11... | collective-permute-start | bytes 196616 | tf_op jit(solution)/shard_map/ppermute | solution.py:152
  11.2 2.5 %collective-permute-done.2.refs_3_ = bf16[4,8,1024]{2,1,0:T(8,128)(2,1)S(1)} collective-permute-done((bf16[4,8,1024]{2,1,0:T(8,128)(2,1)S(1)}, bf16[4,8,1024]{2,1,0:T(8,128)(2,1)S(1)}, u32[]{:S(2)}, u32[]{:S(2)}) %collective-permute-start.2) | collective-permute-done | bytes 65568 | tf_op jit(solution)/shard_map/ppermute | solution.py:152
  13.7 0.0 collective-permute-done.6.refs_7_.refs_4_
  13.7 0.0 collective-permute-done.5.refs_6_.refs_3_
  13.7 3.0 %collective-permute-done.4.refs_5_.refs_2_ = bf16[32,1024]{1,0:T(8,128)(2,1)S(1)} collective-permute-done((bf16[32,1024]{1,0:T(8,128)(2,1)S(1)}, bf16[32,1024]{1,0:T(8,128)(2,1)S(1)}, u32[]{:S(2)}, u32[]{:S(2)}) %collective-permute-start.4) | collective-permute-done | bytes 65568 | tf_op jit(solution)/shard_map/ppermute | solution.py:152
  16.7 0.0 collective-permute-done.7.refs_8_.refs_5_
  16.7 0.7 %route.1 = bf16[8,8,1024]{2,1,0:T(8,128)(2,1)} custom-call(bf16[2,8,128]{2,1,0:T(8,128)(2,1)S(1)} %get-tuple-element.13.far_ref, bf16[4,8,1024]{2,1,0:T(8,128)(2,1)S(1)} %get-tuple-element.14.refs_0_, bf16[4,8,1024]{2,1,0:T(8,128)(2,1)S(1)} %collective-permute-done.refs_1_, bf16[4,8,1024]{2,1,0:T(8,128)(2,1)S(1)} %collective-permute-done.1.refs_2_, ...), custom_call_target="tpu_custom_call" | custom-call | tf_op jit(solution)/shard_map/route/pallas_call | solution.py:191
  17.4 0.0 copy-start
  17.4 3.5 %all-to-all-start = ((bf16[8,8,1024]{2,1,0:T(8,128)(2,1)}), bf16[8,8,1024]{2,1,0:T(8,128)(2,1)S(1)}, u32[]{:S(2)}, u32[]{:S(2)}) async-start(bf16[8,8,1024]{2,1,0:T(8,128)(2,1)} %route.1), calls=%async_computation | async-start | bytes 262144 | tf_op jit(solution)/shard_map/all_to_all | solution.py:200
  20.9 0.1 collective-permute-start.10
  21.0 0.5 %collective-permute-start.14 = (bf16[32,1024]{1,0:T(8,128)(2,1)S(1)}, bf16[32,1024]{1,0:T(8,128)(2,1)S(1)}, u32[]{:S(2)}, u32[]{:S(2)}) collective-permute-start(bf16[32,1024]{1,0:T(8,128)(2,1)S(1)} %collective-permute-done.6.refs_7_.refs_4_), channel_id=1, source_target_pairs={{0,8},{8,0},{16,24},{24,16},{1,9},{9,1},{17,25},{25,17},{2,10},{10... | collective-permute-start | bytes 196616 | tf_op jit(solution)/shard_map/ppermute | solution.py:152
  21.5 1.9 %collective-permute-start.9 = (bf16[32,1024]{1,0:T(8,128)(2,1)S(1)}, bf16[32,1024]{1,0:T(8,128)(2,1)S(1)}, u32[]{:S(2)}, u32[]{:S(2)}) collective-permute-start(bf16[32,1024]{1,0:T(8,128)(2,1)S(1)} %collective-permute-done.5.refs_6_.refs_3_), channel_id=1, source_target_pairs={{0,1},{1,0},{2,3},{3,2},{4,5},{5,4},{6,7},{7,6},{8,9},{9,8},{10,11... | collective-permute-start | bytes 196616 | tf_op jit(solution)/shard_map/ppermute | solution.py:152
  23.4 0.1 collective-permute-start.8
  23.5 0.0 collective-permute-start.13
  23.5 0.0 collective-permute-done.10.refs_8_
  23.5 0.5 %collective-permute-start.12 = (bf16[32,1024]{1,0:T(8,128)(2,1)S(1)}, bf16[32,1024]{1,0:T(8,128)(2,1)S(1)}, u32[]{:S(2)}, u32[]{:S(2)}) collective-permute-start(bf16[32,1024]{1,0:T(8,128)(2,1)S(1)} %collective-permute-done.4.refs_5_.refs_2_), channel_id=1, source_target_pairs={{0,8},{8,0},{16,24},{24,16},{1,9},{9,1},{17,25},{25,17},{2,10},{10... | collective-permute-start | bytes 196616 | tf_op jit(solution)/shard_map/ppermute | solution.py:152
  24.0 0.0 collective-permute-done.14.refs_12_
  24.1 0.1 collective-permute-start.11
  24.1 2.8 %collective-permute-done.9.refs_7_ = bf16[32,1024]{1,0:T(8,128)(2,1)S(1)} collective-permute-done((bf16[32,1024]{1,0:T(8,128)(2,1)S(1)}, bf16[32,1024]{1,0:T(8,128)(2,1)S(1)}, u32[]{:S(2)}, u32[]{:S(2)}) %collective-permute-start.9) | collective-permute-done | bytes 65568 | tf_op jit(solution)/shard_map/ppermute | solution.py:152
  27.0 0.0 collective-permute-start.17
  27.0 1.1 %collective-permute-done.8.refs_6_ = bf16[32,1024]{1,0:T(8,128)(2,1)S(1)} collective-permute-done((bf16[32,1024]{1,0:T(8,128)(2,1)S(1)}, bf16[32,1024]{1,0:T(8,128)(2,1)S(1)}, u32[]{:S(2)}, u32[]{:S(2)}) %collective-permute-start.8) | collective-permute-done | bytes 65568 | tf_op jit(solution)/shard_map/ppermute | solution.py:152
  28.1 0.0 collective-permute-start.16
  28.1 0.0 collective-permute-done.13.refs_11_
  28.1 0.5 %collective-permute-start.15 = (bf16[32,1024]{1,0:T(8,128)(2,1)S(1)}, bf16[32,1024]{1,0:T(8,128)(2,1)S(1)}, u32[]{:S(2)}, u32[]{:S(2)}) collective-permute-start(bf16[32,1024]{1,0:T(8,128)(2,1)S(1)} %collective-permute-done.7.refs_8_.refs_5_), channel_id=1, source_target_pairs={{0,8},{8,0},{16,24},{24,16},{1,9},{9,1},{17,25},{25,17},{2,10},{10... | collective-permute-start | bytes 196616 | tf_op jit(solution)/shard_map/ppermute | solution.py:152
  28.6 0.0 collective-permute-done.12.refs_10_
  28.6 0.0 collective-permute-done.11.refs_9_
  28.6 0.0 collective-permute-done.17.refs_15_
  28.6 0.7 %collective-permute-done.16.refs_14_ = bf16[32,1024]{1,0:T(8,128)(2,1)S(1)} collective-permute-done((bf16[32,1024]{1,0:T(8,128)(2,1)S(1)}, bf16[32,1024]{1,0:T(8,128)(2,1)S(1)}, u32[]{:S(2)}, u32[]{:S(2)}) %collective-permute-start.16) | collective-permute-done | bytes 65568 | tf_op jit(solution)/shard_map/ppermute | solution.py:152
  29.4 0.2 collective-permute-done.15.refs_13_
  29.5 0.0 all-to-all-done
  29.5 0.0 copy-done
  29.5 7.6 %attend.1 = bf16[128,4096]{1,0:T(8,128)(2,1)} custom-call(s32[8,64]{1,0:T(8,128)S(1)} %get-tuple-element.12.limit_ref, bf16[128,4096]{1,0:T(8,128)(2,1)} %q_hbm.1, bf16[128,2,512]{2,1,0:T(2,128)(2,1)S(1)} %copy-done, bf16[64,1024]{1,0:T(8,128)(2,1)S(1)} %bitcast.1, bf16[32,1024]{1,0:T(8,128)(2,1)S(1)} %get-tuple-element.18.refs_0_, ...), custom_call_target="tpu_custom_call" | custom-call | tf_op jit(solution)/shard_map/attend/pallas_call | solution.py:203
Async XLA Ops:
  1.1 8.7 %collective-permute-start = (bf16[4,8,1024]{2,1,0:T(8,128)(2,1)S(1)}, bf16[4,8,1024]{2,1,0:T(8,128)(2,1)S(1)}, u32[]{:S(2)}, u32[]{:S(2)}) collective-permute-start(bf16[4,8,1024]{2,1,0:T(8,128)(2,1)S(1)} %get-tuple-element.15), channel_id=1, source_target_pairs={{0,8},{8,0},{16,24},{24,16},{1,9},{9,1},{17,25},{25,17},{2,10},{10... | collective-permute-start | bytes 196616 | tf_op jit(solution)/shard_map/ppermute | solution.py:152
  1.6 8.2 %collective-permute-start.1 = (bf16[4,8,1024]{2,1,0:T(8,128)(2,1)S(1)}, bf16[4,8,1024]{2,1,0:T(8,128)(2,1)S(1)}, u32[]{:S(2)}, u32[]{:S(2)}) collective-permute-start(bf16[4,8,1024]{2,1,0:T(8,128)(2,1)S(1)} %get-tuple-element.16), channel_id=1, source_target_pairs={{0,16},{8,24},{16,0},{24,8},{1,17},{9,25},{17,1},{25,9},{2,18},{10... | collective-permute-start | bytes 196616 | tf_op jit(solution)/shard_map/ppermute | solution.py:152
  4.2 5.8 %collective-permute-start.3 = (bf16[32,1024]{1,0:T(8,128)(2,1)S(1)}, bf16[32,1024]{1,0:T(8,128)(2,1)S(1)}, u32[]{:S(2)}, u32[]{:S(2)}) collective-permute-start(bf16[32,1024]{1,0:T(8,128)(2,1)S(1)} %get-tuple-element.18.refs_0_), channel_id=1, source_target_pairs={{0,2},{1,3},{2,0},{3,1},{4,6},{5,7},{6,4},{7,5},{8,10},{9,11},{10,... | collective-permute-start | bytes 196616 | tf_op jit(solution)/shard_map/ppermute | solution.py:152
  5.8 7.9 %collective-permute-start.6 = (bf16[32,1024]{1,0:T(8,128)(2,1)S(1)}, bf16[32,1024]{1,0:T(8,128)(2,1)S(1)}, u32[]{:S(2)}, u32[]{:S(2)}) collective-permute-start(bf16[32,1024]{1,0:T(8,128)(2,1)S(1)} %get-tuple-element.18.refs_0_), channel_id=1, source_target_pairs={{0,1},{1,0},{2,3},{3,2},{4,5},{5,4},{6,7},{7,6},{8,9},{9,8},{10,11... | collective-permute-start | bytes 196616 | tf_op jit(solution)/shard_map/ppermute | solution.py:152
  7.3 6.4 %collective-permute-start.5 = (bf16[32,1024]{1,0:T(8,128)(2,1)S(1)}, bf16[32,1024]{1,0:T(8,128)(2,1)S(1)}, u32[]{:S(2)}, u32[]{:S(2)}) collective-permute-start(bf16[32,1024]{1,0:T(8,128)(2,1)S(1)} %get-tuple-element.18.refs_0_), channel_id=1, source_target_pairs={{0,6},{1,7},{2,4},{3,5},{4,2},{5,3},{6,0},{7,1},{8,14},{9,15},{10,... | collective-permute-start | bytes 196616 | tf_op jit(solution)/shard_map/ppermute | solution.py:152
  9.8 3.9 %collective-permute-start.2 = (bf16[4,8,1024]{2,1,0:T(8,128)(2,1)S(1)}, bf16[4,8,1024]{2,1,0:T(8,128)(2,1)S(1)}, u32[]{:S(2)}, u32[]{:S(2)}) collective-permute-start(bf16[4,8,1024]{2,1,0:T(8,128)(2,1)S(1)} %get-tuple-element.17), channel_id=1, source_target_pairs={{0,24},{8,16},{16,8},{24,0},{1,25},{9,17},{17,9},{25,1},{2,26},{10... | collective-permute-start | bytes 196616 | tf_op jit(solution)/shard_map/ppermute | solution.py:152
  9.8 6.9 %collective-permute-start.4 = (bf16[32,1024]{1,0:T(8,128)(2,1)S(1)}, bf16[32,1024]{1,0:T(8,128)(2,1)S(1)}, u32[]{:S(2)}, u32[]{:S(2)}) collective-permute-start(bf16[32,1024]{1,0:T(8,128)(2,1)S(1)} %get-tuple-element.18.refs_0_), channel_id=1, source_target_pairs={{0,4},{1,5},{2,6},{3,7},{4,0},{5,1},{6,2},{7,3},{8,12},{9,13},{10,... | collective-permute-start | bytes 196616 | tf_op jit(solution)/shard_map/ppermute | solution.py:152
  10.0 6.7 %collective-permute-start.7 = (bf16[32,1024]{1,0:T(8,128)(2,1)S(1)}, bf16[32,1024]{1,0:T(8,128)(2,1)S(1)}, u32[]{:S(2)}, u32[]{:S(2)}) collective-permute-start(bf16[32,1024]{1,0:T(8,128)(2,1)S(1)} %collective-permute-done.3.refs_4_.refs_1_), channel_id=1, source_target_pairs={{0,1},{1,0},{2,3},{3,2},{4,5},{5,4},{6,7},{7,6},{8,9},{9,8},{10,11... | collective-permute-start | bytes 196616 | tf_op jit(solution)/shard_map/ppermute | solution.py:152
  17.4 12.1 %copy-start = (bf16[128,2,512]{2,1,0:T(2,128)(2,1)S(1)}, bf16[128,2,512]{2,1,0:T(2,128)(2,1)}, u32[]{:S(2)}) copy-start(bf16[128,2,512]{2,1,0:T(2,128)(2,1)} %new_ref.1) | copy-start | bytes 786436
  17.4 12.1 %all-to-all-start = ((bf16[8,8,1024]{2,1,0:T(8,128)(2,1)}), bf16[8,8,1024]{2,1,0:T(8,128)(2,1)S(1)}, u32[]{:S(2)}, u32[]{:S(2)}) async-start(bf16[8,8,1024]{2,1,0:T(8,128)(2,1)} %route.1), calls=%async_computation | async-start | bytes 262144 | tf_op jit(solution)/shard_map/all_to_all | solution.py:200
  20.9 2.6 %collective-permute-start.10 = (bf16[32,1024]{1,0:T(8,128)(2,1)S(1)}, bf16[32,1024]{1,0:T(8,128)(2,1)S(1)}, u32[]{:S(2)}, u32[]{:S(2)}) collective-permute-start(bf16[32,1024]{1,0:T(8,128)(2,1)S(1)} %get-tuple-element.18.refs_0_), channel_id=1, source_target_pairs={{0,8},{8,0},{16,24},{24,16},{1,9},{9,1},{17,25},{25,17},{2,10},{10... | collective-permute-start | bytes 196616 | tf_op jit(solution)/shard_map/ppermute | solution.py:152
  21.0 3.0 %collective-permute-start.14 = (bf16[32,1024]{1,0:T(8,128)(2,1)S(1)}, bf16[32,1024]{1,0:T(8,128)(2,1)S(1)}, u32[]{:S(2)}, u32[]{:S(2)}) collective-permute-start(bf16[32,1024]{1,0:T(8,128)(2,1)S(1)} %collective-permute-done.6.refs_7_.refs_4_), channel_id=1, source_target_pairs={{0,8},{8,0},{16,24},{24,16},{1,9},{9,1},{17,25},{25,17},{2,10},{10... | collective-permute-start | bytes 196616 | tf_op jit(solution)/shard_map/ppermute | solution.py:152
  21.5 5.5 %collective-permute-start.9 = (bf16[32,1024]{1,0:T(8,128)(2,1)S(1)}, bf16[32,1024]{1,0:T(8,128)(2,1)S(1)}, u32[]{:S(2)}, u32[]{:S(2)}) collective-permute-start(bf16[32,1024]{1,0:T(8,128)(2,1)S(1)} %collective-permute-done.5.refs_6_.refs_3_), channel_id=1, source_target_pairs={{0,1},{1,0},{2,3},{3,2},{4,5},{5,4},{6,7},{7,6},{8,9},{9,8},{10,11... | collective-permute-start | bytes 196616 | tf_op jit(solution)/shard_map/ppermute | solution.py:152
  23.4 4.7 %collective-permute-start.8 = (bf16[32,1024]{1,0:T(8,128)(2,1)S(1)}, bf16[32,1024]{1,0:T(8,128)(2,1)S(1)}, u32[]{:S(2)}, u32[]{:S(2)}) collective-permute-start(bf16[32,1024]{1,0:T(8,128)(2,1)S(1)} %collective-permute-done.4.refs_5_.refs_2_), channel_id=1, source_target_pairs={{0,1},{1,0},{2,3},{3,2},{4,5},{5,4},{6,7},{7,6},{8,9},{9,8},{10,11... | collective-permute-start | bytes 196616 | tf_op jit(solution)/shard_map/ppermute | solution.py:152
  23.5 4.6 %collective-permute-start.13 = (bf16[32,1024]{1,0:T(8,128)(2,1)S(1)}, bf16[32,1024]{1,0:T(8,128)(2,1)S(1)}, u32[]{:S(2)}, u32[]{:S(2)}) collective-permute-start(bf16[32,1024]{1,0:T(8,128)(2,1)S(1)} %collective-permute-done.5.refs_6_.refs_3_), channel_id=1, source_target_pairs={{0,8},{8,0},{16,24},{24,16},{1,9},{9,1},{17,25},{25,17},{2,10},{10... | collective-permute-start | bytes 196616 | tf_op jit(solution)/shard_map/ppermute | solution.py:152
  23.5 5.1 %collective-permute-start.12 = (bf16[32,1024]{1,0:T(8,128)(2,1)S(1)}, bf16[32,1024]{1,0:T(8,128)(2,1)S(1)}, u32[]{:S(2)}, u32[]{:S(2)}) collective-permute-start(bf16[32,1024]{1,0:T(8,128)(2,1)S(1)} %collective-permute-done.4.refs_5_.refs_2_), channel_id=1, source_target_pairs={{0,8},{8,0},{16,24},{24,16},{1,9},{9,1},{17,25},{25,17},{2,10},{10... | collective-permute-start | bytes 196616 | tf_op jit(solution)/shard_map/ppermute | solution.py:152
  24.1 4.6 %collective-permute-start.11 = (bf16[32,1024]{1,0:T(8,128)(2,1)S(1)}, bf16[32,1024]{1,0:T(8,128)(2,1)S(1)}, u32[]{:S(2)}, u32[]{:S(2)}) collective-permute-start(bf16[32,1024]{1,0:T(8,128)(2,1)S(1)} %collective-permute-done.3.refs_4_.refs_1_), channel_id=1, source_target_pairs={{0,8},{8,0},{16,24},{24,16},{1,9},{9,1},{17,25},{25,17},{2,10},{10... | collective-permute-start | bytes 196616 | tf_op jit(solution)/shard_map/ppermute | solution.py:152
  27.0 1.7 %collective-permute-start.17 = (bf16[32,1024]{1,0:T(8,128)(2,1)S(1)}, bf16[32,1024]{1,0:T(8,128)(2,1)S(1)}, u32[]{:S(2)}, u32[]{:S(2)}) collective-permute-start(bf16[32,1024]{1,0:T(8,128)(2,1)S(1)} %collective-permute-done.9.refs_7_), channel_id=1, source_target_pairs={{0,8},{8,0},{16,24},{24,16},{1,9},{9,1},{17,25},{25,17},{2,10},{10... | collective-permute-start | bytes 196616 | tf_op jit(solution)/shard_map/ppermute | solution.py:152
  28.1 1.3 %collective-permute-start.16 = (bf16[32,1024]{1,0:T(8,128)(2,1)S(1)}, bf16[32,1024]{1,0:T(8,128)(2,1)S(1)}, u32[]{:S(2)}, u32[]{:S(2)}) collective-permute-start(bf16[32,1024]{1,0:T(8,128)(2,1)S(1)} %collective-permute-done.8.refs_6_), channel_id=1, source_target_pairs={{0,8},{8,0},{16,24},{24,16},{1,9},{9,1},{17,25},{25,17},{2,10},{10... | collective-permute-start | bytes 196616 | tf_op jit(solution)/shard_map/ppermute | solution.py:152
  28.1 1.4 %collective-permute-start.15 = (bf16[32,1024]{1,0:T(8,128)(2,1)S(1)}, bf16[32,1024]{1,0:T(8,128)(2,1)S(1)}, u32[]{:S(2)}, u32[]{:S(2)}) collective-permute-start(bf16[32,1024]{1,0:T(8,128)(2,1)S(1)} %collective-permute-done.7.refs_8_.refs_5_), channel_id=1, source_target_pairs={{0,8},{8,0},{16,24},{24,16},{1,9},{9,1},{17,25},{25,17},{2,10},{10... | collective-permute-start | bytes 196616 | tf_op jit(solution)/shard_map/ppermute | solution.py:152

commit v9 on v8

--- a/solution.py
+++ b/solution.py
@@ -13,6 +13,7 @@
 RUN = 4
 Z = 4
 CHUNK = 4
+Q_COPIES = 4
 NEGATIVE = -1e30
 SCALE2 = HD ** (-0.5) * 1.4426950408889634
 VMEM = pl.BlockSpec(memory_space=pltpu.VMEM)
@@ -23,9 +24,9 @@
     return pltpu.CompilerParams(vmem_limit_bytes=mib * 2**20)
 
 
-def pack_kernel(dom_count, anc_hbm, len_hbm, prompt_hbm, cache_hbm, half_ref, *refs):
+def pack_kernel(dom_count, anc_hbm, len_hbm, prompt_hbm, cache_hbm, q_hbm, half_ref, *refs):
     out_refs = refs[:dom_count]
-    far_ref, limit_ref, anc_ref, len_ref, prompt_ref, cache_ref, sems = refs[dom_count:]
+    far_ref, limit_ref, q_ref, anc_ref, len_ref, prompt_ref, cache_ref, sems = refs[dom_count:]
     group = cache_ref.shape[0]
     dom = lax.axis_index("dom")
     rows, width = half_ref.shape
@@ -38,6 +39,12 @@
     anc_in.start()
     len_in.start()
     cache_in.start()
+    q_rows = q_ref.shape[0] // Q_COPIES
+    q_in = []
+    for at in range(Q_COPIES):
+        rows_at = pl.ds(at * q_rows, q_rows)
+        q_in.append(pltpu.make_async_copy(q_hbm.at[rows_at], q_ref.at[rows_at], sems.at[4 + at]))
+        q_in[at].start()
     runs = group // RUN
     anc_in.wait()
     len_in.wait()
@@ -59,21 +66,22 @@
                     local = anc_ref[first + slot] % group
                     out_ref[slot] = cache_ref[local].reshape(cache_ref.shape[1], width)
 
+    for copy in q_in:
+        copy.wait()
+
 
 def route_kernel(dom_count, far_ref, *refs):
-    in_refs, (out_hbm, out_ref, sem) = refs[:dom_count], refs[-3:]
-    width = out_ref.shape[2]
-    for run in range(far_ref.shape[0]):
-        far = far_ref[run]
-        for slot in range(RUN):
-            picked = in_refs[0][slot]
-            for k in range(1, len(in_refs)):
-                here = jnp.concatenate([far == k] * (width // far.shape[1]), axis=1)
-                picked = jnp.where(here, in_refs[k][slot], picked)
-            out_ref[run * RUN + slot] = picked
-    out = pltpu.make_async_copy(out_ref, out_hbm, sem)
-    out.start()
-    out.wait()
+    in_refs, out_refs = refs[:dom_count], refs[dom_count:]
+    ctx = lax.axis_index("ctx")
+    width = out_refs[0].shape[1]
+    for k, out_ref in enumerate(out_refs):
+        to = ctx ^ k
+        far = far_ref[to // RUN]
+        picked = in_refs[0][to % RUN]
+        for at in range(1, dom_count):
+            here = jnp.concatenate([far == at] * (width // far.shape[1]), axis=1)
+            picked = jnp.where(here, in_refs[at][to % RUN], picked)
+        out_ref[...] = picked
 
 
 def head_rows(q_ref, g, gq):
@@ -90,36 +98,45 @@
     return lax.dot_general(a, b, (((1,), (0,)), ((), ())), preferred_element_type=jnp.float32)
 
 
-def attend_kernel(limit_ref, q_hbm, new_ref, cache_ref, *refs):
-    pieces, (out_ref, q_ref, stage, sems) = refs[:-4], refs[-4:]
-    chunk = CHUNK * HD
-    count = q_ref.shape[1] // chunk
-    q_copies = []
-    for c in range(count):
-        columns = pl.ds(c * chunk, chunk)
-        q_copies.append(pltpu.make_async_copy(q_hbm.at[:, columns], q_ref.at[:, columns], sems.at[count + c]))
-        q_copies[c].start()
+def gather_kernel(new_ref, *refs):
+    pieces, (key_ref, value_ref) = refs[:-2], refs[-2:]
     width = new_ref.shape[2]
-    gen = cache_ref.shape[0]
+    new = new_ref[...].reshape(SPAN, 2 * width)
+    at = 0
+    for piece in (new, *pieces):
+        rows = slice(at, at + piece.shape[0])
+        at += piece.shape[0]
+        key_ref[rows, :] = piece[:, :width]
+        for g in range(width // HD):
+            value_ref[rows, 2 * g * HD : (2 * g + 1) * HD] = piece[:, width + g * HD : width + (g + 1) * HD]
+            value_ref[rows, (2 * g + 1) * HD : (2 * g + 2) * HD] = jnp.ones((piece.shape[0], HD), jnp.bfloat16)
+
+
+def attend_kernel(limit_ref, q_ref, key_ref, value_ref, *refs):
+    pages, (out_ref, stage, sems) = refs[:-3], refs[-3:]
+    width = key_ref.shape[1]
+    page_rows = pages[0].shape[0]
+    gen = page_rows * len(pages)
     kvh = width // HD
     gq = q_ref.shape[1] // width
-    new = new_ref[...].reshape(SPAN, 2 * width)
-    old = sum(p.shape[0] for p in pieces)
-    ones = jnp.ones((SPAN + old + gen, HD), jnp.bfloat16)
+    old = key_ref.shape[0] - SPAN
     token = lax.broadcasted_iota(jnp.int32, (SPAN, SPAN), 0)
     causal = lax.broadcasted_iota(jnp.int32, (SPAN, SPAN), 1) <= token
-    visible = lax.broadcasted_iota(jnp.int32, (SPAN, gen), 1) < jnp.broadcast_to(limit_ref[:1], (SPAN, gen))
+    at = lax.broadcasted_iota(jnp.int32, (SPAN, gen), 1)
+    at = ((at // page_rows) ^ lax.axis_index("ctx")) * page_rows + at % page_rows
+    visible = at < jnp.broadcast_to(limit_ref[:1], (SPAN, gen))
+    pages = jnp.concatenate([page[...] for page in pages], axis=0)
+    ones = jnp.ones((gen, HD), jnp.bfloat16)
     keys, values = [], []
     for g in range(kvh):
-        k_at = slice(g * HD, (g + 1) * HD)
-        v_at = slice(width + g * HD, width + (g + 1) * HD)
-        keys.append(jnp.concatenate([new[:, k_at]] + [p[:, k_at] for p in (*pieces, cache_ref)], axis=0))
-        value = jnp.concatenate([new[:, v_at]] + [p[:, v_at] for p in (*pieces, cache_ref)], axis=0)
-        values.append(jnp.concatenate([value, ones], axis=1))
+        keys.append(jnp.concatenate([key_ref[:, g * HD : (g + 1) * HD], pages[:, g * HD : (g + 1) * HD]], axis=0))
+        value = jnp.concatenate([pages[:, width + g * HD : width + (g + 1) * HD], ones], axis=1)
+        values.append(jnp.concatenate([value_ref[:, 2 * g * HD : (2 * g + 2) * HD], value], axis=0))
+    chunk = CHUNK * HD
     per_group = gq // CHUNK
+    count = q_ref.shape[1] // chunk
 
     def scores_of(c):
-        q_copies[c].wait()
         return dot_nt(head_rows(q_ref, c, CHUNK), keys[c // per_group])
 
     copies = []
@@ -167,52 +184,56 @@
             *[shape((RUN, page_rows, 2 * width), jnp.bfloat16)] * dom_count,
             shape((group // RUN, page_rows, HD), jnp.bfloat16),
             shape((8, ctx_count * page_rows), jnp.int32),
+            shape(q_new.shape, q_new.dtype),
         ),
-        in_specs=[HBM] * 4,
-        out_specs=(VMEM,) * (3 + dom_count),
+        in_specs=[HBM] * 5,
+        out_specs=(VMEM,) * (4 + dom_count),
         scratch_shapes=[
             pltpu.SMEM(ancestors.shape, jnp.int32),
             pltpu.SMEM(lengths.shape, jnp.int32),
             pltpu.VMEM((half_rows, 2, width), jnp.bfloat16),
             pltpu.VMEM(cache_kv.shape, jnp.bfloat16),
-            pltpu.SemaphoreType.DMA((4,)),
+            pltpu.SemaphoreType.DMA((4 + Q_COPIES,)),
         ],
         compiler_params=params(12),
         name="pack",
-    )(*(pltpu.with_memory_space_constraint(x, pltpu.HBM) for x in (ancestors, lengths, prompt_kv, cache_kv)))
-    outgoing, far, limit = rest[:dom_count], rest[dom_count], rest[dom_count + 1]
+    )(*(pltpu.with_memory_space_constraint(x, pltpu.HBM) for x in (ancestors, lengths, prompt_kv, cache_kv, q_new)))
+    outgoing, (far, limit, queries) = rest[:dom_count], rest[dom_count:]
 
     pieces = [half] + [swap(half, "ctx", k * y_count) for k in range(1, Z)]
     pieces += [swap(p, "ctx", k) for k in range(1, y_count) for p in pieces[:Z]]
-    underway = pieces[1 : Z + 2]
     pieces += [swap(p, "dom", 1) for p in pieces]
 
     incoming = outgoing[:1] + [swap(outgoing[k], "dom", k) for k in range(1, dom_count)]
     routed = pl.pallas_call(
         functools.partial(route_kernel, dom_count),
-        out_shape=pltpu.HBM((group, page_rows, 2 * width), jnp.bfloat16),
-        in_specs=[VMEM] * (1 + dom_count) + [pl.BlockSpec(memory_space=pl.ANY)] * len(underway),
-        out_specs=HBM,
-        scratch_shapes=[pltpu.VMEM((group, page_rows, 2 * width), jnp.bfloat16), pltpu.SemaphoreType.DMA],
+        out_shape=(shape((page_rows, 2 * width), jnp.bfloat16),) * ctx_count,
+        in_specs=[VMEM] * (1 + dom_count),
+        out_specs=(VMEM,) * ctx_count,
         compiler_params=params(12),
         name="route",
-    )(far, *incoming, *underway)
-    pages = lax.all_to_all(routed, "ctx", split_axis=0, concat_axis=0, tiled=True)
-    pages = pages.reshape(ctx_count * page_rows, 2 * width)
-
+    )(far, *incoming)
+    pages = [routed[0]] + [swap(routed[k], "ctx", k) for k in range(1, ctx_count)]
+
+    key_count = SPAN + sum(piece.shape[0] for piece in pieces)
+    keys, values = pl.pallas_call(
+        gather_kernel,
+        out_shape=(shape((key_count, width), jnp.bfloat16), shape((key_count, 2 * width), jnp.bfloat16)),
+        in_specs=[VMEM] * (1 + len(pieces)),
+        out_specs=(VMEM, VMEM),
+        compiler_params=params(16),
+        cost_estimate=pl.CostEstimate(flops=10**10, bytes_accessed=2**22, transcendentals=0),
+        name="gather",
+    )(kv_new, *pieces)
     return pl.pallas_call(
         attend_kernel,
         out_shape=shape((tokens, q_width), jnp.bfloat16),
-        in_specs=[VMEM, HBM] + [VMEM] * (2 + len(pieces)),
+        in_specs=[VMEM] * (4 + len(pages)),
         out_specs=HBM,
-        scratch_shapes=[
-            pltpu.VMEM((tokens, q_width), jnp.bfloat16),
-            pltpu.VMEM((tokens, q_width), jnp.bfloat16),
-            pltpu.SemaphoreType.DMA((2 * q_width // (CHUNK * HD),)),
-        ],
+        scratch_shapes=[pltpu.VMEM((tokens, q_width), jnp.bfloat16), pltpu.SemaphoreType.DMA((q_width // (CHUNK * HD),))],
         compiler_params=params(40 if prompt_kv.shape[0] * ctx_count > 1024 else 24),
         name="attend",
-    )(limit, pltpu.with_memory_space_constraint(q_new, pltpu.HBM), kv_new, pages, *pieces)
+    )(limit, queries, keys, values, *pages)
 
 
 def solution(mesh):

time: 37.4 us -> 41.6 us (1.11)
  starting transfers between devices: 17.3 us -> 24.3 us
  Pallas kernels: 9.36 us -> 6.71 us
    ppermute x18 -> x25, starting transfers between devices: 13.8 us -> 24.3 us  [swap(): lax.ppermute(x, axis, [(i, i ^ distance) for i in range(lax.axis_size(axi...]
    all_to_all x1 -> x0, starting transfers between devices: 3.52 us -> none  [on_device(): lax.all_to_all(routed, 'ctx', split_axis=0, concat_axis=0, tiled=True)]
    pallas_call x1, Pallas kernels: 7.6 us -> 4.96 us  [on_device(): pl.pallas_call(attend_kernel, out_shape=shape((tokens, q_width), jnp.bflo...]
    ppermute x18 -> x25, waiting for transfers between devices: 10.4 us -> 10.3 us  [swap(): lax.ppermute(x, axis, [(i, i ^ distance) for i in range(lax.axis_size(axi...]
  transfers between devices with their start and end apart: 19 -> 25, of which waited for: 6 -> 7; matrix products, arithmetic and copies ran while one was open for 0% -> 0% of each run, Pallas kernels for 0% -> 1%
where the time goes in v9:
time: 41.6 us; the launch traced here: 41.4 us
  starting transfers between devices  24.3 us (58%)
  waiting for transfers between devices  10.3 us (25%)
  Pallas kernels  6.71 us (16%)
    ppermute x25, starting transfers between devices, swap(): lax.ppermute(x, axis, [(i, i ^ distance) for i in range(lax.axis_size(axi...  24.3 us
    ppermute x25, waiting for transfers between devices, swap(): lax.ppermute(x, axis, [(i, i ^ distance) for i in range(lax.axis_size(axi...  10.3 us
    pallas_call x1, Pallas kernels, on_device(): pl.pallas_call(attend_kernel, out_shape=shape((tokens, q_width), jnp.bflo...  4.96 us
    pallas_call x1, Pallas kernels, on_device(): pl.pallas_call(functools.partial(pack_kernel, dom_count), out_shape=(shap...  1.4 us
  transfers between devices with their start and end apart: 25, of which 7 were waited for; matrix products, arithmetic and copies ran while one was open for 0% of the time, Pallas kernels for 1%

profile of v9, /device:TPU:0, one launch (start us, length us, event | category | flops | bytes accessed | tf_op | source)
XLA Modules:
  0.0 41.4 jit_solution(12681594760514773729)
XLA Ops:
  0.0 1.4 %pack.1 = (bf16[32,1024]{1,0:T(8,128)(2,1)S(1)}, bf16[4,8,1024]{2,1,0:T(8,128)(2,1)S(1)}, bf16[4,8,1024]{2,1,0:T(8,128)(2,1)S(1)}, bf16[4,8,1024]{2,1,0:T(8,128)...) custom-call(s32[32]{0:T(128)} %anc_hbm.1, ...), custom_call_target="tpu_custom_call" | custom-call | tf_op jit(solution)/shard_map/pack/pallas_call | solution.py:180
  1.4 0.5 %collective-permute-start.15 = (bf16[4,8,1024]{2,1,0:T(8,128)(2,1)S(1)}, bf16[4,8,1024]{2,1,0:T(8,128)(2,1)S(1)}, u32[]{:S(2)}, u32[]{:S(2)}) collective-permute-start(bf16[4,8,1024]{2,1,0:T(8,128)(2,1)S(1)} %get-tuple-element.30), channel_id=1, source_target_pairs={{0,8},{8,0},{16,24},{24,16},{1,9},{9,1},{17,25},{25,17},{2,10},{10... | collective-permute-start | bytes 196616 | tf_op jit(solution)/shard_map/ppermute | solution.py:169
  1.9 2.6 %collective-permute-start.16 = (bf16[4,8,1024]{2,1,0:T(8,128)(2,1)S(1)}, bf16[4,8,1024]{2,1,0:T(8,128)(2,1)S(1)}, u32[]{:S(2)}, u32[]{:S(2)}) collective-permute-start(bf16[4,8,1024]{2,1,0:T(8,128)(2,1)S(1)} %get-tuple-element.31), channel_id=1, source_target_pairs={{0,16},{8,24},{16,0},{24,8},{1,17},{9,25},{17,1},{25,9},{2,18},{10... | collective-permute-start | bytes 196616 | tf_op jit(solution)/shard_map/ppermute | solution.py:169
  4.5 0.1 collective-permute-start.17
  4.6 0.1 collective-permute-start.7
  4.7 2.0 %collective-permute-start.3 = (bf16[32,1024]{1,0:T(8,128)(2,1)S(1)}, bf16[32,1024]{1,0:T(8,128)(2,1)S(1)}, u32[]{:S(2)}, u32[]{:S(2)}) collective-permute-start(bf16[32,1024]{1,0:T(8,128)(2,1)S(1)} %get-tuple-element.25.refs_0_), channel_id=1, source_target_pairs={{0,1},{1,0},{2,3},{3,2},{4,5},{5,4},{6,7},{7,6},{8,9},{9,8},{10,11... | collective-permute-start | bytes 196616 | tf_op jit(solution)/shard_map/ppermute | solution.py:169
  6.7 0.0 collective-permute-done.15.refs_1_
  6.7 3.6 %collective-permute-start.2 = (bf16[32,1024]{1,0:T(8,128)(2,1)S(1)}, bf16[32,1024]{1,0:T(8,128)(2,1)S(1)}, u32[]{:S(2)}, u32[]{:S(2)}) collective-permute-start(bf16[32,1024]{1,0:T(8,128)(2,1)S(1)} %get-tuple-element.25.refs_0_), channel_id=1, source_target_pairs={{0,6},{1,7},{2,4},{3,5},{4,2},{5,3},{6,0},{7,1},{8,14},{9,15},{10,... | collective-permute-start | bytes 196616 | tf_op jit(solution)/shard_map/ppermute | solution.py:169
  10.3 0.0 collective-permute-done.16.refs_2_
  10.3 0.0 collective-permute-start.1
  10.3 0.0 collective-permute-done.17.refs_3_
  10.3 1.3 %collective-permute-start = (bf16[32,1024]{1,0:T(8,128)(2,1)S(1)}, bf16[32,1024]{1,0:T(8,128)(2,1)S(1)}, u32[]{:S(2)}, u32[]{:S(2)}) collective-permute-start(bf16[32,1024]{1,0:T(8,128)(2,1)S(1)} %get-tuple-element.25.refs_0_), channel_id=1, source_target_pairs={{0,2},{1,3},{2,0},{3,1},{4,6},{5,7},{6,4},{7,5},{8,10},{9,11},{10,... | collective-permute-start | bytes 196616 | tf_op jit(solution)/shard_map/ppermute | solution.py:169
  11.6 0.1 route.1
  11.7 0.0 collective-permute-done.7.refs_8_
  11.7 1.6 %collective-permute-start.18 = (bf16[8,1024]{1,0:T(8,128)(2,1)S(1)}, bf16[8,1024]{1,0:T(8,128)(2,1)S(1)}, u32[]{:S(2)}, u32[]{:S(2)}) collective-permute-start(bf16[8,1024]{1,0:T(8,128)(2,1)S(1)} %get-tuple-element.34), channel_id=1, source_target_pairs={{0,1},{1,0},{2,3},{3,2},{4,5},{5,4},{6,7},{7,6},{8,9},{9,8},{10,11... | collective-permute-start | bytes 49160 | tf_op jit(solution)/shard_map/ppermute | solution.py:169
  13.3 0.0 collective-permute-done.3.refs_4_
  13.3 0.5 %collective-permute-start.19 = (bf16[8,1024]{1,0:T(8,128)(2,1)S(1)}, bf16[8,1024]{1,0:T(8,128)(2,1)S(1)}, u32[]{:S(2)}, u32[]{:S(2)}) collective-permute-start(bf16[8,1024]{1,0:T(8,128)(2,1)S(1)} %get-tuple-element.35), channel_id=1, source_target_pairs={{0,2},{1,3},{2,0},{3,1},{4,6},{5,7},{6,4},{7,5},{8,10},{9,11},{10,... | collective-permute-start | bytes 49160 | tf_op jit(solution)/shard_map/ppermute | solution.py:169
  13.7 0.0 collective-permute-done.2.refs_3_
  13.7 0.0 collective-permute-start.11
  13.7 2.3 %collective-permute-done.1.refs_2_ = bf16[32,1024]{1,0:T(8,128)(2,1)S(1)} collective-permute-done((bf16[32,1024]{1,0:T(8,128)(2,1)S(1)}, bf16[32,1024]{1,0:T(8,128)(2,1)S(1)}, u32[]{:S(2)}, u32[]{:S(2)}) %collective-permute-start.1) | collective-permute-done | bytes 65568 | tf_op jit(solution)/shard_map/ppermute | solution.py:169
  16.0 0.0 collective-permute-start.10
  16.0 0.0 collective-permute-done.refs_1_
  16.0 1.0 %collective-permute-start.6 = (bf16[32,1024]{1,0:T(8,128)(2,1)S(1)}, bf16[32,1024]{1,0:T(8,128)(2,1)S(1)}, u32[]{:S(2)}, u32[]{:S(2)}) collective-permute-start(bf16[32,1024]{1,0:T(8,128)(2,1)S(1)} %collective-permute-done.2.refs_3_), channel_id=1, source_target_pairs={{0,1},{1,0},{2,3},{3,2},{4,5},{5,4},{6,7},{7,6},{8,9},{9,8},{10,11... | collective-permute-start | bytes 196616 | tf_op jit(solution)/shard_map/ppermute | solution.py:169
  17.1 0.0 collective-permute-done.18.refs_1_
  17.1 1.0 %collective-permute-start.5 = (bf16[32,1024]{1,0:T(8,128)(2,1)S(1)}, bf16[32,1024]{1,0:T(8,128)(2,1)S(1)}, u32[]{:S(2)}, u32[]{:S(2)}) collective-permute-start(bf16[32,1024]{1,0:T(8,128)(2,1)S(1)} %collective-permute-done.1.refs_2_), channel_id=1, source_target_pairs={{0,1},{1,0},{2,3},{3,2},{4,5},{5,4},{6,7},{7,6},{8,9},{9,8},{10,11... | collective-permute-start | bytes 196616 | tf_op jit(solution)/shard_map/ppermute | solution.py:169
  18.1 0.0 collective-permute-done.19.refs_2_
  18.1 1.0 %collective-permute-start.4 = (bf16[32,1024]{1,0:T(8,128)(2,1)S(1)}, bf16[32,1024]{1,0:T(8,128)(2,1)S(1)}, u32[]{:S(2)}, u32[]{:S(2)}) collective-permute-start(bf16[32,1024]{1,0:T(8,128)(2,1)S(1)} %collective-permute-done.refs_1_), channel_id=1, source_target_pairs={{0,1},{1,0},{2,3},{3,2},{4,5},{5,4},{6,7},{7,6},{8,9},{9,8},{10,11... | collective-permute-start | bytes 196616 | tf_op jit(solution)/shard_map/ppermute | solution.py:169
  19.1 0.0 collective-permute-done.11.refs_12_
  19.1 0.0 collective-permute-done.10.refs_11_
  19.1 0.5 %collective-permute-start.8 = (bf16[32,1024]{1,0:T(8,128)(2,1)S(1)}, bf16[32,1024]{1,0:T(8,128)(2,1)S(1)}, u32[]{:S(2)}, u32[]{:S(2)}) collective-permute-start(bf16[32,1024]{1,0:T(8,128)(2,1)S(1)} %collective-permute-done.refs_1_), channel_id=1, source_target_pairs={{0,8},{8,0},{16,24},{24,16},{1,9},{9,1},{17,25},{25,17},{2,10},{10... | collective-permute-start | bytes 196616 | tf_op jit(solution)/shard_map/ppermute | solution.py:169
  19.6 1.3 %collective-permute-done.6.refs_7_ = bf16[32,1024]{1,0:T(8,128)(2,1)S(1)} collective-permute-done((bf16[32,1024]{1,0:T(8,128)(2,1)S(1)}, bf16[32,1024]{1,0:T(8,128)(2,1)S(1)}, u32[]{:S(2)}, u32[]{:S(2)}) %collective-permute-start.6) | collective-permute-done | bytes 65568 | tf_op jit(solution)/shard_map/ppermute | solution.py:169
  20.9 0.0 collective-permute-start.14
  20.9 1.4 %collective-permute-done.5.refs_6_ = bf16[32,1024]{1,0:T(8,128)(2,1)S(1)} collective-permute-done((bf16[32,1024]{1,0:T(8,128)(2,1)S(1)}, bf16[32,1024]{1,0:T(8,128)(2,1)S(1)}, u32[]{:S(2)}, u32[]{:S(2)}) %collective-permute-start.5) | collective-permute-done | bytes 65568 | tf_op jit(solution)/shard_map/ppermute | solution.py:169
  22.3 1.0 %collective-permute-done.4.refs_5_ = bf16[32,1024]{1,0:T(8,128)(2,1)S(1)} collective-permute-done((bf16[32,1024]{1,0:T(8,128)(2,1)S(1)}, bf16[32,1024]{1,0:T(8,128)(2,1)S(1)}, u32[]{:S(2)}, u32[]{:S(2)}) %collective-permute-start.4) | collective-permute-done | bytes 65568 | tf_op jit(solution)/shard_map/ppermute | solution.py:169
  23.3 0.0 collective-permute-start.12
  23.4 0.3 collective-permute-start.20
  23.7 0.0 collective-permute-done.8.refs_9_
  23.7 3.4 %collective-permute-start.21 = (bf16[8,1024]{1,0:T(8,128)(2,1)S(1)}, bf16[8,1024]{1,0:T(8,128)(2,1)S(1)}, u32[]{:S(2)}, u32[]{:S(2)}) collective-permute-start(bf16[8,1024]{1,0:T(8,128)(2,1)S(1)} %get-tuple-element.37), channel_id=1, source_target_pairs={{0,4},{1,5},{2,6},{3,7},{4,0},{5,1},{6,2},{7,3},{8,12},{9,13},{10,... | collective-permute-start | bytes 49160 | tf_op jit(solution)/shard_map/ppermute | solution.py:169
  27.1 0.5 %collective-permute-start.22 = (bf16[8,1024]{1,0:T(8,128)(2,1)S(1)}, bf16[8,1024]{1,0:T(8,128)(2,1)S(1)}, u32[]{:S(2)}, u32[]{:S(2)}) collective-permute-start(bf16[8,1024]{1,0:T(8,128)(2,1)S(1)} %get-tuple-element.38), channel_id=1, source_target_pairs={{0,5},{1,4},{2,7},{3,6},{4,1},{5,0},{6,3},{7,2},{8,13},{9,12},{10,... | collective-permute-start | bytes 49160 | tf_op jit(solution)/shard_map/ppermute | solution.py:169
  27.6 2.4 %collective-permute-start.23 = (bf16[8,1024]{1,0:T(8,128)(2,1)S(1)}, bf16[8,1024]{1,0:T(8,128)(2,1)S(1)}, u32[]{:S(2)}, u32[]{:S(2)}) collective-permute-start(bf16[8,1024]{1,0:T(8,128)(2,1)S(1)} %get-tuple-element.39), channel_id=1, source_target_pairs={{0,6},{1,7},{2,4},{3,5},{4,2},{5,3},{6,0},{7,1},{8,14},{9,15},{10,... | collective-permute-start | bytes 49160 | tf_op jit(solution)/shard_map/ppermute | solution.py:169
  30.0 0.0 collective-permute-done.12.refs_13_
  30.0 1.9 %collective-permute-start.24 = (bf16[8,1024]{1,0:T(8,128)(2,1)S(1)}, bf16[8,1024]{1,0:T(8,128)(2,1)S(1)}, u32[]{:S(2)}, u32[]{:S(2)}) collective-permute-start(bf16[8,1024]{1,0:T(8,128)(2,1)S(1)} %get-tuple-element.40), channel_id=1, source_target_pairs={{0,7},{1,6},{2,5},{3,4},{4,3},{5,2},{6,1},{7,0},{8,15},{9,14},{10,... | collective-permute-start | bytes 49160 | tf_op jit(solution)/shard_map/ppermute | solution.py:169
  31.9 0.3 gather.1
  32.2 0.0 collective-permute-done.20.refs_3_
  32.2 0.5 %collective-permute-done.22.refs_5_ = bf16[8,1024]{1,0:T(8,128)(2,1)S(1)} collective-permute-done((bf16[8,1024]{1,0:T(8,128)(2,1)S(1)}, bf16[8,1024]{1,0:T(8,128)(2,1)S(1)}, u32[]{:S(2)}, u32[]{:S(2)}) %collective-permute-start.22) | collective-permute-done | bytes 16416 | tf_op jit(solution)/shard_map/ppermute | solution.py:169
  32.7 0.5 %collective-permute-done.23.refs_6_ = bf16[8,1024]{1,0:T(8,128)(2,1)S(1)} collective-permute-done((bf16[8,1024]{1,0:T(8,128)(2,1)S(1)}, bf16[8,1024]{1,0:T(8,128)(2,1)S(1)}, u32[]{:S(2)}, u32[]{:S(2)}) %collective-permute-start.23) | collective-permute-done | bytes 16416 | tf_op jit(solution)/shard_map/ppermute | solution.py:169
  33.2 3.2 %collective-permute-done.24.refs_7_ = bf16[8,1024]{1,0:T(8,128)(2,1)S(1)} collective-permute-done((bf16[8,1024]{1,0:T(8,128)(2,1)S(1)}, bf16[8,1024]{1,0:T(8,128)(2,1)S(1)}, u32[]{:S(2)}, u32[]{:S(2)}) %collective-permute-start.24) | collective-permute-done | bytes 16416 | tf_op jit(solution)/shard_map/ppermute | solution.py:169
  36.4 5.0 %attend.1 = bf16[128,4096]{1,0:T(8,128)(2,1)} custom-call(s32[8,64]{1,0:T(8,128)S(1)} %get-tuple-element.23.limit_ref, bf16[128,4096]{1,0:T(8,128)(2,1)S(1)} %get-tuple-element.24.q_ref, bf16[640,512]{1,0:T(8,128)(2,1)S(1)} %get-tuple-element.26.key_ref, bf16[640,1024]{1,0:T(8,128)(2,1)S(1)} %get-tuple-element.27.value_ref, ...), custom_call_target="tpu_custom_call" | custom-call | tf_op jit(solution)/shard_map/attend/pallas_call | solution.py:228
  (8 shorter events, 0.0 us)
Async XLA Ops:
  0.0 31.9 %copy-start = (bf16[128,2,512]{2,1,0:T(2,128)(2,1)S(1)}, bf16[128,2,512]{2,1,0:T(2,128)(2,1)}, u32[]{:S(2)}) copy-start(bf16[128,2,512]{2,1,0:T(2,128)(2,1)} %new_ref.1) | copy-start | bytes 786436
  1.4 5.3 %collective-permute-start.15 = (bf16[4,8,1024]{2,1,0:T(8,128)(2,1)S(1)}, bf16[4,8,1024]{2,1,0:T(8,128)(2,1)S(1)}, u32[]{:S(2)}, u32[]{:S(2)}) collective-permute-start(bf16[4,8,1024]{2,1,0:T(8,128)(2,1)S(1)} %get-tuple-element.30), channel_id=1, source_target_pairs={{0,8},{8,0},{16,24},{24,16},{1,9},{9,1},{17,25},{25,17},{2,10},{10... | collective-permute-start | bytes 196616 | tf_op jit(solution)/shard_map/ppermute | solution.py:169
  1.9 8.3 %collective-permute-start.16 = (bf16[4,8,1024]{2,1,0:T(8,128)(2,1)S(1)}, bf16[4,8,1024]{2,1,0:T(8,128)(2,1)S(1)}, u32[]{:S(2)}, u32[]{:S(2)}) collective-permute-start(bf16[4,8,1024]{2,1,0:T(8,128)(2,1)S(1)} %get-tuple-element.31), channel_id=1, source_target_pairs={{0,16},{8,24},{16,0},{24,8},{1,17},{9,25},{17,1},{25,9},{2,18},{10... | collective-permute-start | bytes 196616 | tf_op jit(solution)/shard_map/ppermute | solution.py:169
  4.5 5.8 %collective-permute-start.17 = (bf16[4,8,1024]{2,1,0:T(8,128)(2,1)S(1)}, bf16[4,8,1024]{2,1,0:T(8,128)(2,1)S(1)}, u32[]{:S(2)}, u32[]{:S(2)}) collective-permute-start(bf16[4,8,1024]{2,1,0:T(8,128)(2,1)S(1)} %get-tuple-element.32), channel_id=1, source_target_pairs={{0,24},{8,16},{16,8},{24,0},{1,25},{9,17},{17,9},{25,1},{2,26},{10... | collective-permute-start | bytes 196616 | tf_op jit(solution)/shard_map/ppermute | solution.py:169
  4.6 7.1 %collective-permute-start.7 = (bf16[32,1024]{1,0:T(8,128)(2,1)S(1)}, bf16[32,1024]{1,0:T(8,128)(2,1)S(1)}, u32[]{:S(2)}, u32[]{:S(2)}) collective-permute-start(bf16[32,1024]{1,0:T(8,128)(2,1)S(1)} %get-tuple-element.25.refs_0_), channel_id=1, source_target_pairs={{0,8},{8,0},{16,24},{24,16},{1,9},{9,1},{17,25},{25,17},{2,10},{10... | collective-permute-start | bytes 196616 | tf_op jit(solution)/shard_map/ppermute | solution.py:169
  4.7 8.6 %collective-permute-start.3 = (bf16[32,1024]{1,0:T(8,128)(2,1)S(1)}, bf16[32,1024]{1,0:T(8,128)(2,1)S(1)}, u32[]{:S(2)}, u32[]{:S(2)}) collective-permute-start(bf16[32,1024]{1,0:T(8,128)(2,1)S(1)} %get-tuple-element.25.refs_0_), channel_id=1, source_target_pairs={{0,1},{1,0},{2,3},{3,2},{4,5},{5,4},{6,7},{7,6},{8,9},{9,8},{10,11... | collective-permute-start | bytes 196616 | tf_op jit(solution)/shard_map/ppermute | solution.py:169
  6.7 7.1 %collective-permute-start.2 = (bf16[32,1024]{1,0:T(8,128)(2,1)S(1)}, bf16[32,1024]{1,0:T(8,128)(2,1)S(1)}, u32[]{:S(2)}, u32[]{:S(2)}) collective-permute-start(bf16[32,1024]{1,0:T(8,128)(2,1)S(1)} %get-tuple-element.25.refs_0_), channel_id=1, source_target_pairs={{0,6},{1,7},{2,4},{3,5},{4,2},{5,3},{6,0},{7,1},{8,14},{9,15},{10,... | collective-permute-start | bytes 196616 | tf_op jit(solution)/shard_map/ppermute | solution.py:169
  10.3 5.8 %collective-permute-start.1 = (bf16[32,1024]{1,0:T(8,128)(2,1)S(1)}, bf16[32,1024]{1,0:T(8,128)(2,1)S(1)}, u32[]{:S(2)}, u32[]{:S(2)}) collective-permute-start(bf16[32,1024]{1,0:T(8,128)(2,1)S(1)} %get-tuple-element.25.refs_0_), channel_id=1, source_target_pairs={{0,4},{1,5},{2,6},{3,7},{4,0},{5,1},{6,2},{7,3},{8,12},{9,13},{10,... | collective-permute-start | bytes 196616 | tf_op jit(solution)/shard_map/ppermute | solution.py:169
  10.3 5.8 %collective-permute-start = (bf16[32,1024]{1,0:T(8,128)(2,1)S(1)}, bf16[32,1024]{1,0:T(8,128)(2,1)S(1)}, u32[]{:S(2)}, u32[]{:S(2)}) collective-permute-start(bf16[32,1024]{1,0:T(8,128)(2,1)S(1)} %get-tuple-element.25.refs_0_), channel_id=1, source_target_pairs={{0,2},{1,3},{2,0},{3,1},{4,6},{5,7},{6,4},{7,5},{8,10},{9,11},{10,... | collective-permute-start | bytes 196616 | tf_op jit(solution)/shard_map/ppermute | solution.py:169
  11.7 5.4 %collective-permute-start.18 = (bf16[8,1024]{1,0:T(8,128)(2,1)S(1)}, bf16[8,1024]{1,0:T(8,128)(2,1)S(1)}, u32[]{:S(2)}, u32[]{:S(2)}) collective-permute-start(bf16[8,1024]{1,0:T(8,128)(2,1)S(1)} %get-tuple-element.34), channel_id=1, source_target_pairs={{0,1},{1,0},{2,3},{3,2},{4,5},{5,4},{6,7},{7,6},{8,9},{9,8},{10,11... | collective-permute-start | bytes 49160 | tf_op jit(solution)/shard_map/ppermute | solution.py:169
  13.3 4.8 %collective-permute-start.19 = (bf16[8,1024]{1,0:T(8,128)(2,1)S(1)}, bf16[8,1024]{1,0:T(8,128)(2,1)S(1)}, u32[]{:S(2)}, u32[]{:S(2)}) collective-permute-start(bf16[8,1024]{1,0:T(8,128)(2,1)S(1)} %get-tuple-element.35), channel_id=1, source_target_pairs={{0,2},{1,3},{2,0},{3,1},{4,6},{5,7},{6,4},{7,5},{8,10},{9,11},{10,... | collective-permute-start | bytes 49160 | tf_op jit(solution)/shard_map/ppermute | solution.py:169
  13.7 5.4 %collective-permute-start.11 = (bf16[32,1024]{1,0:T(8,128)(2,1)S(1)}, bf16[32,1024]{1,0:T(8,128)(2,1)S(1)}, u32[]{:S(2)}, u32[]{:S(2)}) collective-permute-start(bf16[32,1024]{1,0:T(8,128)(2,1)S(1)} %collective-permute-done.3.refs_4_), channel_id=1, source_target_pairs={{0,8},{8,0},{16,24},{24,16},{1,9},{9,1},{17,25},{25,17},{2,10},{10... | collective-permute-start | bytes 196616 | tf_op jit(solution)/shard_map/ppermute | solution.py:169
  16.0 3.1 %collective-permute-start.10 = (bf16[32,1024]{1,0:T(8,128)(2,1)S(1)}, bf16[32,1024]{1,0:T(8,128)(2,1)S(1)}, u32[]{:S(2)}, u32[]{:S(2)}) collective-permute-start(bf16[32,1024]{1,0:T(8,128)(2,1)S(1)} %collective-permute-done.2.refs_3_), channel_id=1, source_target_pairs={{0,8},{8,0},{16,24},{24,16},{1,9},{9,1},{17,25},{25,17},{2,10},{10... | collective-permute-start | bytes 196616 | tf_op jit(solution)/shard_map/ppermute | solution.py:169
  16.0 4.9 %collective-permute-start.6 = (bf16[32,1024]{1,0:T(8,128)(2,1)S(1)}, bf16[32,1024]{1,0:T(8,128)(2,1)S(1)}, u32[]{:S(2)}, u32[]{:S(2)}) collective-permute-start(bf16[32,1024]{1,0:T(8,128)(2,1)S(1)} %collective-permute-done.2.refs_3_), channel_id=1, source_target_pairs={{0,1},{1,0},{2,3},{3,2},{4,5},{5,4},{6,7},{7,6},{8,9},{9,8},{10,11... | collective-permute-start | bytes 196616 | tf_op jit(solution)/shard_map/ppermute | solution.py:169
  17.1 5.3 %collective-permute-start.5 = (bf16[32,1024]{1,0:T(8,128)(2,1)S(1)}, bf16[32,1024]{1,0:T(8,128)(2,1)S(1)}, u32[]{:S(2)}, u32[]{:S(2)}) collective-permute-start(bf16[32,1024]{1,0:T(8,128)(2,1)S(1)} %collective-permute-done.1.refs_2_), channel_id=1, source_target_pairs={{0,1},{1,0},{2,3},{3,2},{4,5},{5,4},{6,7},{7,6},{8,9},{9,8},{10,11... | collective-permute-start | bytes 196616 | tf_op jit(solution)/shard_map/ppermute | solution.py:169
  18.1 5.3 %collective-permute-start.4 = (bf16[32,1024]{1,0:T(8,128)(2,1)S(1)}, bf16[32,1024]{1,0:T(8,128)(2,1)S(1)}, u32[]{:S(2)}, u32[]{:S(2)}) collective-permute-start(bf16[32,1024]{1,0:T(8,128)(2,1)S(1)} %collective-permute-done.refs_1_), channel_id=1, source_target_pairs={{0,1},{1,0},{2,3},{3,2},{4,5},{5,4},{6,7},{7,6},{8,9},{9,8},{10,11... | collective-permute-start | bytes 196616 | tf_op jit(solution)/shard_map/ppermute | solution.py:169
  19.1 4.2 %collective-permute-start.9 = (bf16[32,1024]{1,0:T(8,128)(2,1)S(1)}, bf16[32,1024]{1,0:T(8,128)(2,1)S(1)}, u32[]{:S(2)}, u32[]{:S(2)}) collective-permute-start(bf16[32,1024]{1,0:T(8,128)(2,1)S(1)} %collective-permute-done.1.refs_2_), channel_id=1, source_target_pairs={{0,8},{8,0},{16,24},{24,16},{1,9},{9,1},{17,25},{25,17},{2,10},{10... | collective-permute-start | bytes 196616 | tf_op jit(solution)/shard_map/ppermute | solution.py:169
  19.1 4.5 %collective-permute-start.8 = (bf16[32,1024]{1,0:T(8,128)(2,1)S(1)}, bf16[32,1024]{1,0:T(8,128)(2,1)S(1)}, u32[]{:S(2)}, u32[]{:S(2)}) collective-permute-start(bf16[32,1024]{1,0:T(8,128)(2,1)S(1)} %collective-permute-done.refs_1_), channel_id=1, source_target_pairs={{0,8},{8,0},{16,24},{24,16},{1,9},{9,1},{17,25},{25,17},{2,10},{10... | collective-permute-start | bytes 196616 | tf_op jit(solution)/shard_map/ppermute | solution.py:169
  20.9 6.1 %collective-permute-start.14 = (bf16[32,1024]{1,0:T(8,128)(2,1)S(1)}, bf16[32,1024]{1,0:T(8,128)(2,1)S(1)}, u32[]{:S(2)}, u32[]{:S(2)}) collective-permute-start(bf16[32,1024]{1,0:T(8,128)(2,1)S(1)} %collective-permute-done.6.refs_7_), channel_id=1, source_target_pairs={{0,8},{8,0},{16,24},{24,16},{1,9},{9,1},{17,25},{25,17},{2,10},{10... | collective-permute-start | bytes 196616 | tf_op jit(solution)/shard_map/ppermute | solution.py:169
  22.3 5.2 %collective-permute-start.13 = (bf16[32,1024]{1,0:T(8,128)(2,1)S(1)}, bf16[32,1024]{1,0:T(8,128)(2,1)S(1)}, u32[]{:S(2)}, u32[]{:S(2)}) collective-permute-start(bf16[32,1024]{1,0:T(8,128)(2,1)S(1)} %collective-permute-done.5.refs_6_), channel_id=1, source_target_pairs={{0,8},{8,0},{16,24},{24,16},{1,9},{9,1},{17,25},{25,17},{2,10},{10... | collective-permute-start | bytes 196616 | tf_op jit(solution)/shard_map/ppermute | solution.py:169
  23.3 6.7 %collective-permute-start.12 = (bf16[32,1024]{1,0:T(8,128)(2,1)S(1)}, bf16[32,1024]{1,0:T(8,128)(2,1)S(1)}, u32[]{:S(2)}, u32[]{:S(2)}) collective-permute-start(bf16[32,1024]{1,0:T(8,128)(2,1)S(1)} %collective-permute-done.4.refs_5_), channel_id=1, source_target_pairs={{0,8},{8,0},{16,24},{24,16},{1,9},{9,1},{17,25},{25,17},{2,10},{10... | collective-permute-start | bytes 196616 | tf_op jit(solution)/shard_map/ppermute | solution.py:169
  23.4 8.8 %collective-permute-start.20 = (bf16[8,1024]{1,0:T(8,128)(2,1)S(1)}, bf16[8,1024]{1,0:T(8,128)(2,1)S(1)}, u32[]{:S(2)}, u32[]{:S(2)}) collective-permute-start(bf16[8,1024]{1,0:T(8,128)(2,1)S(1)} %get-tuple-element.36), channel_id=1, source_target_pairs={{0,3},{1,2},{2,1},{3,0},{4,7},{5,6},{6,5},{7,4},{8,11},{9,10},{10,... | collective-permute-start | bytes 49160 | tf_op jit(solution)/shard_map/ppermute | solution.py:169
  23.7 8.5 %collective-permute-start.21 = (bf16[8,1024]{1,0:T(8,128)(2,1)S(1)}, bf16[8,1024]{1,0:T(8,128)(2,1)S(1)}, u32[]{:S(2)}, u32[]{:S(2)}) collective-permute-start(bf16[8,1024]{1,0:T(8,128)(2,1)S(1)} %get-tuple-element.37), channel_id=1, source_target_pairs={{0,4},{1,5},{2,6},{3,7},{4,0},{5,1},{6,2},{7,3},{8,12},{9,13},{10,... | collective-permute-start | bytes 49160 | tf_op jit(solution)/shard_map/ppermute | solution.py:169
  27.1 5.7 %collective-permute-start.22 = (bf16[8,1024]{1,0:T(8,128)(2,1)S(1)}, bf16[8,1024]{1,0:T(8,128)(2,1)S(1)}, u32[]{:S(2)}, u32[]{:S(2)}) collective-permute-start(bf16[8,1024]{1,0:T(8,128)(2,1)S(1)} %get-tuple-element.38), channel_id=1, source_target_pairs={{0,5},{1,4},{2,7},{3,6},{4,1},{5,0},{6,3},{7,2},{8,13},{9,12},{10,... | collective-permute-start | bytes 49160 | tf_op jit(solution)/shard_map/ppermute | solution.py:169
  27.6 5.6 %collective-permute-start.23 = (bf16[8,1024]{1,0:T(8,128)(2,1)S(1)}, bf16[8,1024]{1,0:T(8,128)(2,1)S(1)}, u32[]{:S(2)}, u32[]{:S(2)}) collective-permute-start(bf16[8,1024]{1,0:T(8,128)(2,1)S(1)} %get-tuple-element.39), channel_id=1, source_target_pairs={{0,6},{1,7},{2,4},{3,5},{4,2},{5,3},{6,0},{7,1},{8,14},{9,15},{10,... | collective-permute-start | bytes 49160 | tf_op jit(solution)/shard_map/ppermute | solution.py:169
  30.0 6.4 %collective-permute-start.24 = (bf16[8,1024]{1,0:T(8,128)(2,1)S(1)}, bf16[8,1024]{1,0:T(8,128)(2,1)S(1)}, u32[]{:S(2)}, u32[]{:S(2)}) collective-permute-start(bf16[8,1024]{1,0:T(8,128)(2,1)S(1)} %get-tuple-element.40), channel_id=1, source_target_pairs={{0,7},{1,6},{2,5},{3,4},{4,3},{5,2},{6,1},{7,0},{8,15},{9,14},{10,... | collective-permute-start | bytes 49160 | tf_op jit(solution)/shard_map/ppermute | solution.py:169

commit v10 on v9

--- a/solution.py
+++ b/solution.py
@@ -70,18 +70,20 @@
         copy.wait()
 
 
-def route_kernel(dom_count, far_ref, *refs):
-    in_refs, out_refs = refs[:dom_count], refs[dom_count:]
-    ctx = lax.axis_index("ctx")
-    width = out_refs[0].shape[1]
-    for k, out_ref in enumerate(out_refs):
-        to = ctx ^ k
-        far = far_ref[to // RUN]
-        picked = in_refs[0][to % RUN]
-        for at in range(1, dom_count):
-            here = jnp.concatenate([far == at] * (width // far.shape[1]), axis=1)
-            picked = jnp.where(here, in_refs[at][to % RUN], picked)
-        out_ref[...] = picked
+def route_kernel(far_ref, *refs):
+    *in_refs, out_hbm, out_ref, sem = refs
+    width = out_ref.shape[2]
+    for run in range(far_ref.shape[0]):
+        far = far_ref[run]
+        for slot in range(RUN):
+            picked = in_refs[0][slot]
+            for k in range(1, len(in_refs)):
+                here = jnp.concatenate([far == k] * (width // far.shape[1]), axis=1)
+                picked = jnp.where(here, in_refs[k][slot], picked)
+            out_ref[run * RUN + slot] = picked
+    out = pltpu.make_async_copy(out_ref, out_hbm, sem)
+    out.start()
+    out.wait()
 
 
 def head_rows(q_ref, g, gq):
@@ -112,25 +114,20 @@
             value_ref[rows, (2 * g + 1) * HD : (2 * g + 2) * HD] = jnp.ones((piece.shape[0], HD), jnp.bfloat16)
 
 
-def attend_kernel(limit_ref, q_ref, key_ref, value_ref, *refs):
-    pages, (out_ref, stage, sems) = refs[:-3], refs[-3:]
+def attend_kernel(limit_ref, q_ref, key_ref, value_ref, cache_ref, out_ref, stage, sems):
     width = key_ref.shape[1]
-    page_rows = pages[0].shape[0]
-    gen = page_rows * len(pages)
+    gen = cache_ref.shape[0]
     kvh = width // HD
     gq = q_ref.shape[1] // width
     old = key_ref.shape[0] - SPAN
     token = lax.broadcasted_iota(jnp.int32, (SPAN, SPAN), 0)
     causal = lax.broadcasted_iota(jnp.int32, (SPAN, SPAN), 1) <= token
-    at = lax.broadcasted_iota(jnp.int32, (SPAN, gen), 1)
-    at = ((at // page_rows) ^ lax.axis_index("ctx")) * page_rows + at % page_rows
-    visible = at < jnp.broadcast_to(limit_ref[:1], (SPAN, gen))
-    pages = jnp.concatenate([page[...] for page in pages], axis=0)
+    visible = lax.broadcasted_iota(jnp.int32, (SPAN, gen), 1) < jnp.broadcast_to(limit_ref[:1], (SPAN, gen))
     ones = jnp.ones((gen, HD), jnp.bfloat16)
     keys, values = [], []
     for g in range(kvh):
-        keys.append(jnp.concatenate([key_ref[:, g * HD : (g + 1) * HD], pages[:, g * HD : (g + 1) * HD]], axis=0))
-        value = jnp.concatenate([pages[:, width + g * HD : width + (g + 1) * HD], ones], axis=1)
+        keys.append(jnp.concatenate([key_ref[:, g * HD : (g + 1) * HD], cache_ref[:, g * HD : (g + 1) * HD]], axis=0))
+        value = jnp.concatenate([cache_ref[:, width + g * HD : width + (g + 1) * HD], ones], axis=1)
         values.append(jnp.concatenate([value_ref[:, 2 * g * HD : (2 * g + 2) * HD], value], axis=0))
     chunk = CHUNK * HD
     per_group = gq // CHUNK
@@ -206,14 +203,16 @@
 
     incoming = outgoing[:1] + [swap(outgoing[k], "dom", k) for k in range(1, dom_count)]
     routed = pl.pallas_call(
-        functools.partial(route_kernel, dom_count),
-        out_shape=(shape((page_rows, 2 * width), jnp.bfloat16),) * ctx_count,
+        route_kernel,
+        out_shape=pltpu.HBM((group, page_rows, 2 * width), jnp.bfloat16),
         in_specs=[VMEM] * (1 + dom_count),
-        out_specs=(VMEM,) * ctx_count,
+        out_specs=HBM,
+        scratch_shapes=[pltpu.VMEM((group, page_rows, 2 * width), jnp.bfloat16), pltpu.SemaphoreType.DMA],
         compiler_params=params(12),
         name="route",
     )(far, *incoming)
-    pages = [routed[0]] + [swap(routed[k], "ctx", k) for k in range(1, ctx_count)]
+    pages = lax.all_to_all(routed, "ctx", split_axis=0, concat_axis=0, tiled=True)
+    pages = pages.reshape(ctx_count * page_rows, 2 * width)
 
     key_count = SPAN + sum(piece.shape[0] for piece in pieces)
     keys, values = pl.pallas_call(
@@ -228,12 +227,12 @@
     return pl.pallas_call(
         attend_kernel,
         out_shape=shape((tokens, q_width), jnp.bfloat16),
-        in_specs=[VMEM] * (4 + len(pages)),
+        in_specs=[VMEM] * 5,
         out_specs=HBM,
         scratch_shapes=[pltpu.VMEM((tokens, q_width), jnp.bfloat16), pltpu.SemaphoreType.DMA((q_width // (CHUNK * HD),))],
         compiler_params=params(40 if prompt_kv.shape[0] * ctx_count > 1024 else 24),
         name="attend",
-    )(limit, queries, keys, values, *pages)
+    )(limit, queries, keys, values, pages)
 
 
 def solution(mesh):

time: 41.6 us -> 48.1 us (1.16); the launches traced: 41.4 us -> 47.3 us
  local copies, waits for them, and re-layouts: 0.01 us -> 16.1 us
  waiting for transfers between devices: 10.3 us -> 4.49 us
  starting transfers between devices: 24.3 us -> 19.3 us
  Pallas kernels: 6.71 us -> 7.23 us
    unnamed x2 -> x58, local copies, waits for them, and re-layouts: 0.01 us -> 16.1 us
    ppermute x25 -> x18, starting transfers between devices: 24.3 us -> 14 us  [swap(): lax.ppermute(x, axis, [(i, i ^ distance) for i in range(lax.axis_size(axi...]
    ppermute x25 -> x18, waiting for transfers between devices: 10.3 us -> 4.49 us  [swap(): lax.ppermute(x, axis, [(i, i ^ distance) for i in range(lax.axis_size(axi...]
    all_to_all x0 -> x1, starting transfers between devices: none -> 5.24 us  [on_device(): lax.all_to_all(routed, 'ctx', split_axis=0, concat_axis=0, tiled=True)]
    pallas_call x1, Pallas kernels: 0.07 us -> 0.72 us  [on_device(): pl.pallas_call(route_kernel, out_shape=pltpu.HBM((group, page_rows, 2 * w...]
  transfers between devices with their start and end apart: 25 -> 19, of which waited for: 7 -> 4; matrix products, arithmetic and copies ran while one was open for 0% -> 0% of each run, Pallas kernels for 1% -> 2%
where the time goes in v10:
time: 48.1 us; the launch traced here: 47.3 us
  starting transfers between devices  19.3 us (40%)
  local copies, waits for them, and re-layouts  16.1 us (33%)
  Pallas kernels  7.23 us (15%)
  waiting for transfers between devices  4.49 us (9%)
    unnamed x58, local copies, waits for them, and re-layouts  16.1 us
    ppermute x18, starting transfers between devices, swap(): lax.ppermute(x, axis, [(i, i ^ distance) for i in range(lax.axis_size(axi...  14 us
    all_to_all x1, starting transfers between devices, on_device(): lax.all_to_all(routed, 'ctx', split_axis=0, concat_axis=0, tiled=True)  5.24 us
    pallas_call x1, Pallas kernels, on_device(): pl.pallas_call(attend_kernel, out_shape=shape((tokens, q_width), jnp.bflo...  4.82 us
    ppermute x18, waiting for transfers between devices, swap(): lax.ppermute(x, axis, [(i, i ^ distance) for i in range(lax.axis_size(axi...  4.49 us
    pallas_call x1, Pallas kernels, on_device(): pl.pallas_call(functools.partial(pack_kernel, dom_count), out_shape=(shap...  1.4 us
  transfers between devices with their start and end apart: 19, of which 4 were waited for; matrix products, arithmetic and copies ran while one was open for 0% of the time, Pallas kernels for 2%

profile of v10, /device:TPU:0, one launch (start us, length us, event | category | flops | bytes accessed | tf_op | source)
XLA Modules:
  0.0 47.3 jit_solution(17587296704257540826)
XLA Ops:
  0.0 1.4 %pack.1 = (bf16[32,1024]{1,0:T(8,128)(2,1)S(1)}, bf16[4,8,1024]{2,1,0:T(8,128)(2,1)S(1)}, bf16[4,8,1024]{2,1,0:T(8,128)(2,1)S(1)}, bf16[4,8,1024]{2,1,0:T(8,128)...) custom-call(s32[32]{0:T(128)} %anc_hbm.1, ...), custom_call_target="tpu_custom_call" | custom-call | tf_op jit(solution)/shard_map/pack/pallas_call | solution.py:177
  1.4 0.5 %collective-permute-start.15 = (bf16[4,8,1024]{2,1,0:T(8,128)(2,1)S(1)}, bf16[4,8,1024]{2,1,0:T(8,128)(2,1)S(1)}, u32[]{:S(2)}, u32[]{:S(2)}) collective-permute-start(bf16[4,8,1024]{2,1,0:T(8,128)(2,1)S(1)} %get-tuple-element.22), channel_id=1, source_target_pairs={{0,8},{8,0},{16,24},{24,16},{1,9},{9,1},{17,25},{25,17},{2,10},{10... | collective-permute-start | bytes 196616 | tf_op jit(solution)/shard_map/ppermute | solution.py:166
  1.9 2.6 %collective-permute-start.16 = (bf16[4,8,1024]{2,1,0:T(8,128)(2,1)S(1)}, bf16[4,8,1024]{2,1,0:T(8,128)(2,1)S(1)}, u32[]{:S(2)}, u32[]{:S(2)}) collective-permute-start(bf16[4,8,1024]{2,1,0:T(8,128)(2,1)S(1)} %get-tuple-element.23), channel_id=1, source_target_pairs={{0,16},{8,24},{16,0},{24,8},{1,17},{9,25},{17,1},{25,9},{2,18},{10... | collective-permute-start | bytes 196616 | tf_op jit(solution)/shard_map/ppermute | solution.py:166
  4.5 0.1 collective-permute-start.17
  4.6 1.8 %collective-permute-start.3 = (bf16[32,1024]{1,0:T(8,128)(2,1)S(1)}, bf16[32,1024]{1,0:T(8,128)(2,1)S(1)}, u32[]{:S(2)}, u32[]{:S(2)}) collective-permute-start(bf16[32,1024]{1,0:T(8,128)(2,1)S(1)} %get-tuple-element.17.refs_0_), channel_id=1, source_target_pairs={{0,1},{1,0},{2,3},{3,2},{4,5},{5,4},{6,7},{7,6},{8,9},{9,8},{10,11... | collective-permute-start | bytes 196616 | tf_op jit(solution)/shard_map/ppermute | solution.py:166
  6.3 3.6 %collective-permute-start.2 = (bf16[32,1024]{1,0:T(8,128)(2,1)S(1)}, bf16[32,1024]{1,0:T(8,128)(2,1)S(1)}, u32[]{:S(2)}, u32[]{:S(2)}) collective-permute-start(bf16[32,1024]{1,0:T(8,128)(2,1)S(1)} %get-tuple-element.17.refs_0_), channel_id=1, source_target_pairs={{0,6},{1,7},{2,4},{3,5},{4,2},{5,3},{6,0},{7,1},{8,14},{9,15},{10,... | collective-permute-start | bytes 196616 | tf_op jit(solution)/shard_map/ppermute | solution.py:166
  9.9 0.0 collective-permute-done.16.refs_2_
  9.9 0.1 collective-permute-start.1
  10.0 0.0 collective-permute-done.17.refs_3_
  10.0 1.6 %collective-permute-start = (bf16[32,1024]{1,0:T(8,128)(2,1)S(1)}, bf16[32,1024]{1,0:T(8,128)(2,1)S(1)}, u32[]{:S(2)}, u32[]{:S(2)}) collective-permute-start(bf16[32,1024]{1,0:T(8,128)(2,1)S(1)} %get-tuple-element.17.refs_0_), channel_id=1, source_target_pairs={{0,2},{1,3},{2,0},{3,1},{4,6},{5,7},{6,4},{7,5},{8,10},{9,11},{10,... | collective-permute-start | bytes 196616 | tf_op jit(solution)/shard_map/ppermute | solution.py:166
  11.6 0.0 collective-permute-done.3.refs_4_
  11.6 0.0 collective-permute-start.11
  11.6 0.8 %collective-permute-done.2.refs_3_ = bf16[32,1024]{1,0:T(8,128)(2,1)S(1)} collective-permute-done((bf16[32,1024]{1,0:T(8,128)(2,1)S(1)}, bf16[32,1024]{1,0:T(8,128)(2,1)S(1)}, u32[]{:S(2)}, u32[]{:S(2)}) %collective-permute-start.2) | collective-permute-done | bytes 65568 | tf_op jit(solution)/shard_map/ppermute | solution.py:166
  12.4 0.6 %copy-done.3 = bf16[32,1024]{1,0:T(8,128)(2,1)} copy-done((bf16[32,1024]{1,0:T(8,128)(2,1)}, bf16[32,1024]{1,0:T(8,128)(2,1)S(1)}, u32[]{:S(2)}) %copy-start.3) | copy-done | bytes 65560
  13.1 1.2 %collective-permute-start.6 = (bf16[32,1024]{1,0:T(8,128)(2,1)S(1)}, bf16[32,1024]{1,0:T(8,128)(2,1)S(1)}, u32[]{:S(2)}, u32[]{:S(2)}) collective-permute-start(bf16[32,1024]{1,0:T(8,128)(2,1)S(1)} %collective-permute-done.2.refs_3_), channel_id=1, source_target_pairs={{0,1},{1,0},{2,3},{3,2},{4,5},{5,4},{6,7},{7,6},{8,9},{9,8},{10,11... | collective-permute-start | bytes 196616 | tf_op jit(solution)/shard_map/ppermute | solution.py:166
  14.3 0.6 %copy-done.1 = bf16[32,1024]{1,0:T(8,128)(2,1)} copy-done((bf16[32,1024]{1,0:T(8,128)(2,1)}, bf16[32,1024]{1,0:T(8,128)(2,1)S(1)}, u32[]{:S(2)}) %copy-start.1) | copy-done | bytes 65560
  14.9 0.9 %collective-permute-done.1.refs_2_ = bf16[32,1024]{1,0:T(8,128)(2,1)S(1)} collective-permute-done((bf16[32,1024]{1,0:T(8,128)(2,1)S(1)}, bf16[32,1024]{1,0:T(8,128)(2,1)S(1)}, u32[]{:S(2)}, u32[]{:S(2)}) %collective-permute-start.1) | collective-permute-done | bytes 65568 | tf_op jit(solution)/shard_map/ppermute | solution.py:166
  15.9 0.8 %collective-permute-start.5 = (bf16[32,1024]{1,0:T(8,128)(2,1)S(1)}, bf16[32,1024]{1,0:T(8,128)(2,1)S(1)}, u32[]{:S(2)}, u32[]{:S(2)}) collective-permute-start(bf16[32,1024]{1,0:T(8,128)(2,1)S(1)} %collective-permute-done.1.refs_2_), channel_id=1, source_target_pairs={{0,1},{1,0},{2,3},{3,2},{4,5},{5,4},{6,7},{7,6},{8,9},{9,8},{10,11... | collective-permute-start | bytes 196616 | tf_op jit(solution)/shard_map/ppermute | solution.py:166
  16.7 0.0 collective-permute-done.refs_1_
  16.7 1.2 %collective-permute-start.4 = (bf16[32,1024]{1,0:T(8,128)(2,1)S(1)}, bf16[32,1024]{1,0:T(8,128)(2,1)S(1)}, u32[]{:S(2)}, u32[]{:S(2)}) collective-permute-start(bf16[32,1024]{1,0:T(8,128)(2,1)S(1)} %collective-permute-done.refs_1_), channel_id=1, source_target_pairs={{0,1},{1,0},{2,3},{3,2},{4,5},{5,4},{6,7},{7,6},{8,9},{9,8},{10,11... | collective-permute-start | bytes 196616 | tf_op jit(solution)/shard_map/ppermute | solution.py:166
  17.9 0.0 collective-permute-start.9
  17.9 0.5 %collective-permute-start.8 = (bf16[32,1024]{1,0:T(8,128)(2,1)S(1)}, bf16[32,1024]{1,0:T(8,128)(2,1)S(1)}, u32[]{:S(2)}, u32[]{:S(2)}) collective-permute-start(bf16[32,1024]{1,0:T(8,128)(2,1)S(1)} %collective-permute-done.refs_1_), channel_id=1, source_target_pairs={{0,8},{8,0},{16,24},{24,16},{1,9},{9,1},{17,25},{25,17},{2,10},{10... | collective-permute-start | bytes 196616 | tf_op jit(solution)/shard_map/ppermute | solution.py:166
  18.4 0.1 collective-permute-start.14
  18.5 2.0 %collective-permute-done.5.refs_6_ = bf16[32,1024]{1,0:T(8,128)(2,1)S(1)} collective-permute-done((bf16[32,1024]{1,0:T(8,128)(2,1)S(1)}, bf16[32,1024]{1,0:T(8,128)(2,1)S(1)}, u32[]{:S(2)}, u32[]{:S(2)}) %collective-permute-start.5) | collective-permute-done | bytes 65568 | tf_op jit(solution)/shard_map/ppermute | solution.py:166
  20.5 0.7 %collective-permute-done.4.refs_5_ = bf16[32,1024]{1,0:T(8,128)(2,1)S(1)} collective-permute-done((bf16[32,1024]{1,0:T(8,128)(2,1)S(1)}, bf16[32,1024]{1,0:T(8,128)(2,1)S(1)}, u32[]{:S(2)}, u32[]{:S(2)}) %collective-permute-start.4) | collective-permute-done | bytes 65568 | tf_op jit(solution)/shard_map/ppermute | solution.py:166
  21.2 0.7 %route.1 = bf16[8,8,1024]{2,1,0:T(8,128)(2,1)} custom-call(bf16[2,8,128]{2,1,0:T(8,128)(2,1)S(1)} %get-tuple-element.20.far_ref, bf16[4,8,1024]{2,1,0:T(8,128)(2,1)S(1)} %get-tuple-element.21.refs_0_, bf16[4,8,1024]{2,1,0:T(8,128)(2,1)S(1)} %collective-permute-done.15.refs_1_, bf16[4,8,1024]{2,1,0:T(8,128)(2,1)S(1)} %collective-permute-done.16.refs_2_, ...), custom_call_target="tpu_custom_call" | custom-call | tf_op jit(solution)/shard_map/route/pallas_call | solution.py:205
  21.9 5.2 %all-to-all-start = ((bf16[8,8,1024]{2,1,0:T(8,128)(2,1)}), bf16[8,8,1024]{2,1,0:T(8,128)(2,1)S(1)}, u32[]{:S(2)}, u32[]{:S(2)}) async-start(bf16[8,8,1024]{2,1,0:T(8,128)(2,1)} %route.1), calls=%async_computation | async-start | bytes 262144 | tf_op jit(solution)/shard_map/all_to_all | solution.py:214
  27.2 0.6 %copy-done.19 = bf16[32,1024]{1,0:T(8,128)(2,1)} copy-done((bf16[32,1024]{1,0:T(8,128)(2,1)}, bf16[32,1024]{1,0:T(8,128)(2,1)S(1)}, u32[]{:S(2)}) %copy-start.19) | copy-done | bytes 65560
  27.8 0.6 %copy-done.21 = bf16[32,1024]{1,0:T(8,128)(2,1)} copy-done((bf16[32,1024]{1,0:T(8,128)(2,1)}, bf16[32,1024]{1,0:T(8,128)(2,1)S(1)}, u32[]{:S(2)}) %copy-start.21) | copy-done | bytes 65560
  28.4 0.6 %copy-done.23 = bf16[32,1024]{1,0:T(8,128)(2,1)} copy-done((bf16[32,1024]{1,0:T(8,128)(2,1)}, bf16[32,1024]{1,0:T(8,128)(2,1)S(1)}, u32[]{:S(2)}) %copy-start.23) | copy-done | bytes 65560
  29.1 0.6 %copy-done.25 = bf16[32,1024]{1,0:T(8,128)(2,1)} copy-done((bf16[32,1024]{1,0:T(8,128)(2,1)}, bf16[32,1024]{1,0:T(8,128)(2,1)S(1)}, u32[]{:S(2)}) %copy-start.25) | copy-done | bytes 65560
  29.7 0.6 %copy-done.27 = bf16[32,1024]{1,0:T(8,128)(2,1)} copy-done((bf16[32,1024]{1,0:T(8,128)(2,1)}, bf16[32,1024]{1,0:T(8,128)(2,1)S(1)}, u32[]{:S(2)}) %copy-start.27) | copy-done | bytes 65560
  30.4 0.8 %copy-done.2 = bf16[32,1024]{1,0:T(8,128)(2,1)S(1)} copy-done((bf16[32,1024]{1,0:T(8,128)(2,1)S(1)}, bf16[32,1024]{1,0:T(8,128)(2,1)}, u32[]{:S(2)}) %copy-start.2) | copy-done | bytes 65560
  31.2 0.8 %copy-done.4 = bf16[32,1024]{1,0:T(8,128)(2,1)S(1)} copy-done((bf16[32,1024]{1,0:T(8,128)(2,1)S(1)}, bf16[32,1024]{1,0:T(8,128)(2,1)}, u32[]{:S(2)}) %copy-start.4) | copy-done | bytes 65560
  32.1 0.8 %copy-done.6 = bf16[32,1024]{1,0:T(8,128)(2,1)S(1)} copy-done((bf16[32,1024]{1,0:T(8,128)(2,1)S(1)}, bf16[32,1024]{1,0:T(8,128)(2,1)}, u32[]{:S(2)}) %copy-start.6) | copy-done | bytes 65560
  32.9 0.8 %copy-done.8 = bf16[32,1024]{1,0:T(8,128)(2,1)S(1)} copy-done((bf16[32,1024]{1,0:T(8,128)(2,1)S(1)}, bf16[32,1024]{1,0:T(8,128)(2,1)}, u32[]{:S(2)}) %copy-start.8) | copy-done | bytes 65560
  33.7 0.8 %copy-done.10 = bf16[32,1024]{1,0:T(8,128)(2,1)S(1)} copy-done((bf16[32,1024]{1,0:T(8,128)(2,1)S(1)}, bf16[32,1024]{1,0:T(8,128)(2,1)}, u32[]{:S(2)}) %copy-start.10) | copy-done | bytes 65560
  34.6 0.8 %copy-done.12 = bf16[32,1024]{1,0:T(8,128)(2,1)S(1)} copy-done((bf16[32,1024]{1,0:T(8,128)(2,1)S(1)}, bf16[32,1024]{1,0:T(8,128)(2,1)}, u32[]{:S(2)}) %copy-start.12) | copy-done | bytes 65560
  35.4 0.8 %copy-done.14 = bf16[32,1024]{1,0:T(8,128)(2,1)S(1)} copy-done((bf16[32,1024]{1,0:T(8,128)(2,1)S(1)}, bf16[32,1024]{1,0:T(8,128)(2,1)}, u32[]{:S(2)}) %copy-start.14) | copy-done | bytes 65560
  36.3 0.8 %copy-done.16 = bf16[32,1024]{1,0:T(8,128)(2,1)S(1)} copy-done((bf16[32,1024]{1,0:T(8,128)(2,1)S(1)}, bf16[32,1024]{1,0:T(8,128)(2,1)}, u32[]{:S(2)}) %copy-start.16) | copy-done | bytes 65560
  37.1 0.8 %copy-done.18 = bf16[32,1024]{1,0:T(8,128)(2,1)S(1)} copy-done((bf16[32,1024]{1,0:T(8,128)(2,1)S(1)}, bf16[32,1024]{1,0:T(8,128)(2,1)}, u32[]{:S(2)}) %copy-start.18) | copy-done | bytes 65560
  37.9 0.8 %copy-done.20 = bf16[32,1024]{1,0:T(8,128)(2,1)S(1)} copy-done((bf16[32,1024]{1,0:T(8,128)(2,1)S(1)}, bf16[32,1024]{1,0:T(8,128)(2,1)}, u32[]{:S(2)}) %copy-start.20) | copy-done | bytes 65560
  38.8 0.8 %copy-done.22 = bf16[32,1024]{1,0:T(8,128)(2,1)S(1)} copy-done((bf16[32,1024]{1,0:T(8,128)(2,1)S(1)}, bf16[32,1024]{1,0:T(8,128)(2,1)}, u32[]{:S(2)}) %copy-start.22) | copy-done | bytes 65560
  39.6 0.8 %copy-done.24 = bf16[32,1024]{1,0:T(8,128)(2,1)S(1)} copy-done((bf16[32,1024]{1,0:T(8,128)(2,1)S(1)}, bf16[32,1024]{1,0:T(8,128)(2,1)}, u32[]{:S(2)}) %copy-start.24) | copy-done | bytes 65560
  40.5 0.8 %copy-done.26 = bf16[32,1024]{1,0:T(8,128)(2,1)S(1)} copy-done((bf16[32,1024]{1,0:T(8,128)(2,1)S(1)}, bf16[32,1024]{1,0:T(8,128)(2,1)}, u32[]{:S(2)}) %copy-start.26) | copy-done | bytes 65560
  41.3 0.8 %copy-done.28 = bf16[32,1024]{1,0:T(8,128)(2,1)S(1)} copy-done((bf16[32,1024]{1,0:T(8,128)(2,1)S(1)}, bf16[32,1024]{1,0:T(8,128)(2,1)}, u32[]{:S(2)}) %copy-start.28) | copy-done | bytes 65560
  42.1 0.3 gather.1
  42.5 4.8 %attend.1 = bf16[128,4096]{1,0:T(8,128)(2,1)} custom-call(s32[8,64]{1,0:T(8,128)S(1)} %get-tuple-element.15.limit_ref, bf16[128,4096]{1,0:T(8,128)(2,1)S(1)} %get-tuple-element.16.q_ref, bf16[640,512]{1,0:T(8,128)(2,1)S(1)} %get-tuple-element.18.key_ref, bf16[640,1024]{1,0:T(8,128)(2,1)S(1)} %get-tuple-element.19.value_ref, bf16[64,1024]{1,0:T(8,128)(2,1)S(1)} %bitcast.1), custom_call_target="tpu_custom_call" | custom-call | tf_op jit(solution)/shard_map/attend/pallas_call | solution.py:227
  (52 shorter events, 0.1 us)
Async XLA Ops:
  0.0 30.4 %copy-start = (bf16[128,2,512]{2,1,0:T(2,128)(2,1)S(1)}, bf16[128,2,512]{2,1,0:T(2,128)(2,1)}, u32[]{:S(2)}) copy-start(bf16[128,2,512]{2,1,0:T(2,128)(2,1)} %new_ref.1) | copy-start | bytes 786436
  1.4 8.5 %collective-permute-start.15 = (bf16[4,8,1024]{2,1,0:T(8,128)(2,1)S(1)}, bf16[4,8,1024]{2,1,0:T(8,128)(2,1)S(1)}, u32[]{:S(2)}, u32[]{:S(2)}) collective-permute-start(bf16[4,8,1024]{2,1,0:T(8,128)(2,1)S(1)} %get-tuple-element.22), channel_id=1, source_target_pairs={{0,8},{8,0},{16,24},{24,16},{1,9},{9,1},{17,25},{25,17},{2,10},{10... | collective-permute-start | bytes 196616 | tf_op jit(solution)/shard_map/ppermute | solution.py:166
  1.9 8.0 %collective-permute-start.16 = (bf16[4,8,1024]{2,1,0:T(8,128)(2,1)S(1)}, bf16[4,8,1024]{2,1,0:T(8,128)(2,1)S(1)}, u32[]{:S(2)}, u32[]{:S(2)}) collective-permute-start(bf16[4,8,1024]{2,1,0:T(8,128)(2,1)S(1)} %get-tuple-element.23), channel_id=1, source_target_pairs={{0,16},{8,24},{16,0},{24,8},{1,17},{9,25},{17,1},{25,9},{2,18},{10... | collective-permute-start | bytes 196616 | tf_op jit(solution)/shard_map/ppermute | solution.py:166
  4.5 5.5 %collective-permute-start.17 = (bf16[4,8,1024]{2,1,0:T(8,128)(2,1)S(1)}, bf16[4,8,1024]{2,1,0:T(8,128)(2,1)S(1)}, u32[]{:S(2)}, u32[]{:S(2)}) collective-permute-start(bf16[4,8,1024]{2,1,0:T(8,128)(2,1)S(1)} %get-tuple-element.24), channel_id=1, source_target_pairs={{0,24},{8,16},{16,8},{24,0},{1,25},{9,17},{17,9},{25,1},{2,26},{10... | collective-permute-start | bytes 196616 | tf_op jit(solution)/shard_map/ppermute | solution.py:166
  4.6 7.1 %collective-permute-start.3 = (bf16[32,1024]{1,0:T(8,128)(2,1)S(1)}, bf16[32,1024]{1,0:T(8,128)(2,1)S(1)}, u32[]{:S(2)}, u32[]{:S(2)}) collective-permute-start(bf16[32,1024]{1,0:T(8,128)(2,1)S(1)} %get-tuple-element.17.refs_0_), channel_id=1, source_target_pairs={{0,1},{1,0},{2,3},{3,2},{4,5},{5,4},{6,7},{7,6},{8,9},{9,8},{10,11... | collective-permute-start | bytes 196616 | tf_op jit(solution)/shard_map/ppermute | solution.py:166
  6.3 6.1 %collective-permute-start.2 = (bf16[32,1024]{1,0:T(8,128)(2,1)S(1)}, bf16[32,1024]{1,0:T(8,128)(2,1)S(1)}, u32[]{:S(2)}, u32[]{:S(2)}) collective-permute-start(bf16[32,1024]{1,0:T(8,128)(2,1)S(1)} %get-tuple-element.17.refs_0_), channel_id=1, source_target_pairs={{0,6},{1,7},{2,4},{3,5},{4,2},{5,3},{6,0},{7,1},{8,14},{9,15},{10,... | collective-permute-start | bytes 196616 | tf_op jit(solution)/shard_map/ppermute | solution.py:166
  9.9 2.5 %collective-permute-start.7 = (bf16[32,1024]{1,0:T(8,128)(2,1)S(1)}, bf16[32,1024]{1,0:T(8,128)(2,1)S(1)}, u32[]{:S(2)}, u32[]{:S(2)}) collective-permute-start(bf16[32,1024]{1,0:T(8,128)(2,1)S(1)} %get-tuple-element.17.refs_0_), channel_id=1, source_target_pairs={{0,8},{8,0},{16,24},{24,16},{1,9},{9,1},{17,25},{25,17},{2,10},{10... | collective-permute-start | bytes 196616 | tf_op jit(solution)/shard_map/ppermute | solution.py:166
  9.9 5.9 %collective-permute-start.1 = (bf16[32,1024]{1,0:T(8,128)(2,1)S(1)}, bf16[32,1024]{1,0:T(8,128)(2,1)S(1)}, u32[]{:S(2)}, u32[]{:S(2)}) collective-permute-start(bf16[32,1024]{1,0:T(8,128)(2,1)S(1)} %get-tuple-element.17.refs_0_), channel_id=1, source_target_pairs={{0,4},{1,5},{2,6},{3,7},{4,0},{5,1},{6,2},{7,3},{8,12},{9,13},{10,... | collective-permute-start | bytes 196616 | tf_op jit(solution)/shard_map/ppermute | solution.py:166
  10.0 6.6 %collective-permute-start = (bf16[32,1024]{1,0:T(8,128)(2,1)S(1)}, bf16[32,1024]{1,0:T(8,128)(2,1)S(1)}, u32[]{:S(2)}, u32[]{:S(2)}) collective-permute-start(bf16[32,1024]{1,0:T(8,128)(2,1)S(1)} %get-tuple-element.17.refs_0_), channel_id=1, source_target_pairs={{0,2},{1,3},{2,0},{3,1},{4,6},{5,7},{6,4},{7,5},{8,10},{9,11},{10,... | collective-permute-start | bytes 196616 | tf_op jit(solution)/shard_map/ppermute | solution.py:166
  11.6 6.3 %collective-permute-start.11 = (bf16[32,1024]{1,0:T(8,128)(2,1)S(1)}, bf16[32,1024]{1,0:T(8,128)(2,1)S(1)}, u32[]{:S(2)}, u32[]{:S(2)}) collective-permute-start(bf16[32,1024]{1,0:T(8,128)(2,1)S(1)} %collective-permute-done.3.refs_4_), channel_id=1, source_target_pairs={{0,8},{8,0},{16,24},{24,16},{1,9},{9,1},{17,25},{25,17},{2,10},{10... | collective-permute-start | bytes 196616 | tf_op jit(solution)/shard_map/ppermute | solution.py:166
  12.4 5.5 %collective-permute-start.10 = (bf16[32,1024]{1,0:T(8,128)(2,1)S(1)}, bf16[32,1024]{1,0:T(8,128)(2,1)S(1)}, u32[]{:S(2)}, u32[]{:S(2)}) collective-permute-start(bf16[32,1024]{1,0:T(8,128)(2,1)S(1)} %collective-permute-done.2.refs_3_), channel_id=1, source_target_pairs={{0,8},{8,0},{16,24},{24,16},{1,9},{9,1},{17,25},{25,17},{2,10},{10... | collective-permute-start | bytes 196616 | tf_op jit(solution)/shard_map/ppermute | solution.py:166
  12.4 0.6 %copy-start.3 = (bf16[32,1024]{1,0:T(8,128)(2,1)}, bf16[32,1024]{1,0:T(8,128)(2,1)S(1)}, u32[]{:S(2)}) copy-start(bf16[32,1024]{1,0:T(8,128)(2,1)S(1)} %collective-permute-done.7.refs_8_) | copy-start | bytes 196612
  13.1 5.3 %collective-permute-start.6 = (bf16[32,1024]{1,0:T(8,128)(2,1)S(1)}, bf16[32,1024]{1,0:T(8,128)(2,1)S(1)}, u32[]{:S(2)}, u32[]{:S(2)}) collective-permute-start(bf16[32,1024]{1,0:T(8,128)(2,1)S(1)} %collective-permute-done.2.refs_3_), channel_id=1, source_target_pairs={{0,1},{1,0},{2,3},{3,2},{4,5},{5,4},{6,7},{7,6},{8,9},{9,8},{10,11... | collective-permute-start | bytes 196616 | tf_op jit(solution)/shard_map/ppermute | solution.py:166
  14.3 0.6 %copy-start.1 = (bf16[32,1024]{1,0:T(8,128)(2,1)}, bf16[32,1024]{1,0:T(8,128)(2,1)S(1)}, u32[]{:S(2)}) copy-start(bf16[32,1024]{1,0:T(8,128)(2,1)S(1)} %collective-permute-done.2.refs_3_) | copy-start | bytes 196612
  15.9 13.2 %copy-start.5 = (bf16[32,1024]{1,0:T(8,128)(2,1)}, bf16[32,1024]{1,0:T(8,128)(2,1)S(1)}, u32[]{:S(2)}) copy-start(bf16[32,1024]{1,0:T(8,128)(2,1)S(1)} %collective-permute-done.1.refs_2_) | copy-start | bytes 196612
  15.9 4.6 %collective-permute-start.5 = (bf16[32,1024]{1,0:T(8,128)(2,1)S(1)}, bf16[32,1024]{1,0:T(8,128)(2,1)S(1)}, u32[]{:S(2)}, u32[]{:S(2)}) collective-permute-start(bf16[32,1024]{1,0:T(8,128)(2,1)S(1)} %collective-permute-done.1.refs_2_), channel_id=1, source_target_pairs={{0,1},{1,0},{2,3},{3,2},{4,5},{5,4},{6,7},{7,6},{8,9},{9,8},{10,11... | collective-permute-start | bytes 196616 | tf_op jit(solution)/shard_map/ppermute | solution.py:166
  16.7 12.4 %copy-start.7 = (bf16[32,1024]{1,0:T(8,128)(2,1)}, bf16[32,1024]{1,0:T(8,128)(2,1)S(1)}, u32[]{:S(2)}) copy-start(bf16[32,1024]{1,0:T(8,128)(2,1)S(1)} %collective-permute-done.refs_1_) | copy-start | bytes 196612
  16.7 4.5 %collective-permute-start.4 = (bf16[32,1024]{1,0:T(8,128)(2,1)S(1)}, bf16[32,1024]{1,0:T(8,128)(2,1)S(1)}, u32[]{:S(2)}, u32[]{:S(2)}) collective-permute-start(bf16[32,1024]{1,0:T(8,128)(2,1)S(1)} %collective-permute-done.refs_1_), channel_id=1, source_target_pairs={{0,1},{1,0},{2,3},{3,2},{4,5},{5,4},{6,7},{7,6},{8,9},{9,8},{10,11... | collective-permute-start | bytes 196616 | tf_op jit(solution)/shard_map/ppermute | solution.py:166
  17.9 11.2 %copy-start.9 = (bf16[32,1024]{1,0:T(8,128)(2,1)}, bf16[32,1024]{1,0:T(8,128)(2,1)S(1)}, u32[]{:S(2)}) copy-start(bf16[32,1024]{1,0:T(8,128)(2,1)S(1)} %collective-permute-done.11.refs_12_) | copy-start | bytes 196612
  17.9 9.3 %collective-permute-start.9 = (bf16[32,1024]{1,0:T(8,128)(2,1)S(1)}, bf16[32,1024]{1,0:T(8,128)(2,1)S(1)}, u32[]{:S(2)}, u32[]{:S(2)}) collective-permute-start(bf16[32,1024]{1,0:T(8,128)(2,1)S(1)} %collective-permute-done.1.refs_2_), channel_id=1, source_target_pairs={{0,8},{8,0},{16,24},{24,16},{1,9},{9,1},{17,25},{25,17},{2,10},{10... | collective-permute-start | bytes 196616 | tf_op jit(solution)/shard_map/ppermute | solution.py:166
  17.9 11.2 %copy-start.11 = (bf16[32,1024]{1,0:T(8,128)(2,1)}, bf16[32,1024]{1,0:T(8,128)(2,1)S(1)}, u32[]{:S(2)}) copy-start(bf16[32,1024]{1,0:T(8,128)(2,1)S(1)} %collective-permute-done.10.refs_11_) | copy-start | bytes 196612
  17.9 9.9 %collective-permute-start.8 = (bf16[32,1024]{1,0:T(8,128)(2,1)S(1)}, bf16[32,1024]{1,0:T(8,128)(2,1)S(1)}, u32[]{:S(2)}, u32[]{:S(2)}) collective-permute-start(bf16[32,1024]{1,0:T(8,128)(2,1)S(1)} %collective-permute-done.refs_1_), channel_id=1, source_target_pairs={{0,8},{8,0},{16,24},{24,16},{1,9},{9,1},{17,25},{25,17},{2,10},{10... | collective-permute-start | bytes 196616 | tf_op jit(solution)/shard_map/ppermute | solution.py:166
  18.4 10.7 %copy-start.13 = (bf16[32,1024]{1,0:T(8,128)(2,1)}, bf16[32,1024]{1,0:T(8,128)(2,1)S(1)}, u32[]{:S(2)}) copy-start(bf16[32,1024]{1,0:T(8,128)(2,1)S(1)} %collective-permute-done.6.refs_7_) | copy-start | bytes 196612
  18.4 10.0 %collective-permute-start.14 = (bf16[32,1024]{1,0:T(8,128)(2,1)S(1)}, bf16[32,1024]{1,0:T(8,128)(2,1)S(1)}, u32[]{:S(2)}, u32[]{:S(2)}) collective-permute-start(bf16[32,1024]{1,0:T(8,128)(2,1)S(1)} %collective-permute-done.6.refs_7_), channel_id=1, source_target_pairs={{0,8},{8,0},{16,24},{24,16},{1,9},{9,1},{17,25},{25,17},{2,10},{10... | collective-permute-start | bytes 196616 | tf_op jit(solution)/shard_map/ppermute | solution.py:166
  20.5 8.6 %copy-start.15 = (bf16[32,1024]{1,0:T(8,128)(2,1)}, bf16[32,1024]{1,0:T(8,128)(2,1)S(1)}, u32[]{:S(2)}) copy-start(bf16[32,1024]{1,0:T(8,128)(2,1)S(1)} %collective-permute-done.5.refs_6_) | copy-start | bytes 196612
  20.5 8.6 %collective-permute-start.13 = (bf16[32,1024]{1,0:T(8,128)(2,1)S(1)}, bf16[32,1024]{1,0:T(8,128)(2,1)S(1)}, u32[]{:S(2)}, u32[]{:S(2)}) collective-permute-start(bf16[32,1024]{1,0:T(8,128)(2,1)S(1)} %collective-permute-done.5.refs_6_), channel_id=1, source_target_pairs={{0,8},{8,0},{16,24},{24,16},{1,9},{9,1},{17,25},{25,17},{2,10},{10... | collective-permute-start | bytes 196616 | tf_op jit(solution)/shard_map/ppermute | solution.py:166
  21.2 7.9 %copy-start.17 = (bf16[32,1024]{1,0:T(8,128)(2,1)}, bf16[32,1024]{1,0:T(8,128)(2,1)S(1)}, u32[]{:S(2)}) copy-start(bf16[32,1024]{1,0:T(8,128)(2,1)S(1)} %collective-permute-done.4.refs_5_) | copy-start | bytes 196612
  21.2 8.5 %collective-permute-start.12 = (bf16[32,1024]{1,0:T(8,128)(2,1)S(1)}, bf16[32,1024]{1,0:T(8,128)(2,1)S(1)}, u32[]{:S(2)}, u32[]{:S(2)}) collective-permute-start(bf16[32,1024]{1,0:T(8,128)(2,1)S(1)} %collective-permute-done.4.refs_5_), channel_id=1, source_target_pairs={{0,8},{8,0},{16,24},{24,16},{1,9},{9,1},{17,25},{25,17},{2,10},{10... | collective-permute-start | bytes 196616 | tf_op jit(solution)/shard_map/ppermute | solution.py:166
  21.9 20.5 %all-to-all-start = ((bf16[8,8,1024]{2,1,0:T(8,128)(2,1)}), bf16[8,8,1024]{2,1,0:T(8,128)(2,1)S(1)}, u32[]{:S(2)}, u32[]{:S(2)}) async-start(bf16[8,8,1024]{2,1,0:T(8,128)(2,1)} %route.1), calls=%async_computation | async-start | bytes 262144 | tf_op jit(solution)/shard_map/all_to_all | solution.py:214
  27.2 0.6 %copy-start.19 = (bf16[32,1024]{1,0:T(8,128)(2,1)}, bf16[32,1024]{1,0:T(8,128)(2,1)S(1)}, u32[]{:S(2)}) copy-start(bf16[32,1024]{1,0:T(8,128)(2,1)S(1)} %collective-permute-done.9.refs_10_) | copy-start | bytes 196612
  27.8 0.6 %copy-start.21 = (bf16[32,1024]{1,0:T(8,128)(2,1)}, bf16[32,1024]{1,0:T(8,128)(2,1)S(1)}, u32[]{:S(2)}) copy-start(bf16[32,1024]{1,0:T(8,128)(2,1)S(1)} %collective-permute-done.8.refs_9_) | copy-start | bytes 196612
  28.4 0.6 %copy-start.23 = (bf16[32,1024]{1,0:T(8,128)(2,1)}, bf16[32,1024]{1,0:T(8,128)(2,1)S(1)}, u32[]{:S(2)}) copy-start(bf16[32,1024]{1,0:T(8,128)(2,1)S(1)} %collective-permute-done.14.refs_15_) | copy-start | bytes 196612
  29.1 0.6 %copy-start.25 = (bf16[32,1024]{1,0:T(8,128)(2,1)}, bf16[32,1024]{1,0:T(8,128)(2,1)S(1)}, u32[]{:S(2)}) copy-start(bf16[32,1024]{1,0:T(8,128)(2,1)S(1)} %collective-permute-done.13.refs_14_) | copy-start | bytes 196612
  29.7 0.6 %copy-start.27 = (bf16[32,1024]{1,0:T(8,128)(2,1)}, bf16[32,1024]{1,0:T(8,128)(2,1)S(1)}, u32[]{:S(2)}) copy-start(bf16[32,1024]{1,0:T(8,128)(2,1)S(1)} %collective-permute-done.12.refs_13_) | copy-start | bytes 196612
  30.4 0.8 %copy-start.2 = (bf16[32,1024]{1,0:T(8,128)(2,1)S(1)}, bf16[32,1024]{1,0:T(8,128)(2,1)}, u32[]{:S(2)}) copy-start(bf16[32,1024]{1,0:T(8,128)(2,1)} %copy-done.1) | copy-start | bytes 196612
  31.2 0.8 %copy-start.4 = (bf16[32,1024]{1,0:T(8,128)(2,1)S(1)}, bf16[32,1024]{1,0:T(8,128)(2,1)}, u32[]{:S(2)}) copy-start(bf16[32,1024]{1,0:T(8,128)(2,1)} %copy-done.3) | copy-start | bytes 196612
  32.1 0.8 %copy-start.6 = (bf16[32,1024]{1,0:T(8,128)(2,1)S(1)}, bf16[32,1024]{1,0:T(8,128)(2,1)}, u32[]{:S(2)}) copy-start(bf16[32,1024]{1,0:T(8,128)(2,1)} %copy-done.5) | copy-start | bytes 196612
  32.9 0.8 %copy-start.8 = (bf16[32,1024]{1,0:T(8,128)(2,1)S(1)}, bf16[32,1024]{1,0:T(8,128)(2,1)}, u32[]{:S(2)}) copy-start(bf16[32,1024]{1,0:T(8,128)(2,1)} %copy-done.7) | copy-start | bytes 196612
  33.7 0.8 %copy-start.10 = (bf16[32,1024]{1,0:T(8,128)(2,1)S(1)}, bf16[32,1024]{1,0:T(8,128)(2,1)}, u32[]{:S(2)}) copy-start(bf16[32,1024]{1,0:T(8,128)(2,1)} %copy-done.9) | copy-start | bytes 196612
  34.6 0.8 %copy-start.12 = (bf16[32,1024]{1,0:T(8,128)(2,1)S(1)}, bf16[32,1024]{1,0:T(8,128)(2,1)}, u32[]{:S(2)}) copy-start(bf16[32,1024]{1,0:T(8,128)(2,1)} %copy-done.11) | copy-start | bytes 196612
  35.4 0.8 %copy-start.14 = (bf16[32,1024]{1,0:T(8,128)(2,1)S(1)}, bf16[32,1024]{1,0:T(8,128)(2,1)}, u32[]{:S(2)}) copy-start(bf16[32,1024]{1,0:T(8,128)(2,1)} %copy-done.13) | copy-start | bytes 196612
  36.3 0.8 %copy-start.16 = (bf16[32,1024]{1,0:T(8,128)(2,1)S(1)}, bf16[32,1024]{1,0:T(8,128)(2,1)}, u32[]{:S(2)}) copy-start(bf16[32,1024]{1,0:T(8,128)(2,1)} %copy-done.15) | copy-start | bytes 196612
  37.1 0.8 %copy-start.18 = (bf16[32,1024]{1,0:T(8,128)(2,1)S(1)}, bf16[32,1024]{1,0:T(8,128)(2,1)}, u32[]{:S(2)}) copy-start(bf16[32,1024]{1,0:T(8,128)(2,1)} %copy-done.17) | copy-start | bytes 196612
  37.9 0.8 %copy-start.20 = (bf16[32,1024]{1,0:T(8,128)(2,1)S(1)}, bf16[32,1024]{1,0:T(8,128)(2,1)}, u32[]{:S(2)}) copy-start(bf16[32,1024]{1,0:T(8,128)(2,1)} %copy-done.19) | copy-start | bytes 196612
  38.8 0.8 %copy-start.22 = (bf16[32,1024]{1,0:T(8,128)(2,1)S(1)}, bf16[32,1024]{1,0:T(8,128)(2,1)}, u32[]{:S(2)}) copy-start(bf16[32,1024]{1,0:T(8,128)(2,1)} %copy-done.21) | copy-start | bytes 196612
  39.6 0.8 %copy-start.24 = (bf16[32,1024]{1,0:T(8,128)(2,1)S(1)}, bf16[32,1024]{1,0:T(8,128)(2,1)}, u32[]{:S(2)}) copy-start(bf16[32,1024]{1,0:T(8,128)(2,1)} %copy-done.23) | copy-start | bytes 196612
  40.5 0.8 %copy-start.26 = (bf16[32,1024]{1,0:T(8,128)(2,1)S(1)}, bf16[32,1024]{1,0:T(8,128)(2,1)}, u32[]{:S(2)}) copy-start(bf16[32,1024]{1,0:T(8,128)(2,1)} %copy-done.25) | copy-start | bytes 196612
  41.3 0.8 %copy-start.28 = (bf16[32,1024]{1,0:T(8,128)(2,1)S(1)}, bf16[32,1024]{1,0:T(8,128)(2,1)}, u32[]{:S(2)}) copy-start(bf16[32,1024]{1,0:T(8,128)(2,1)} %copy-done.27) | copy-start | bytes 196612

commit v11 on v8

--- a/solution.py
+++ b/solution.py
@@ -13,6 +13,7 @@
 RUN = 4
 Z = 4
 CHUNK = 4
+Q_COPIES = 4
 NEGATIVE = -1e30
 SCALE2 = HD ** (-0.5) * 1.4426950408889634
 VMEM = pl.BlockSpec(memory_space=pltpu.VMEM)
@@ -60,8 +61,8 @@
                     out_ref[slot] = cache_ref[local].reshape(cache_ref.shape[1], width)
 
 
-def route_kernel(dom_count, far_ref, *refs):
-    in_refs, (out_hbm, out_ref, sem) = refs[:dom_count], refs[-3:]
+def route_kernel(far_ref, *refs):
+    *in_refs, out_hbm, out_ref, sem = refs
     width = out_ref.shape[2]
     for run in range(far_ref.shape[0]):
         far = far_ref[run]
@@ -90,36 +91,46 @@
     return lax.dot_general(a, b, (((1,), (0,)), ((), ())), preferred_element_type=jnp.float32)
 
 
-def attend_kernel(limit_ref, q_hbm, new_ref, cache_ref, *refs):
-    pieces, (out_ref, q_ref, stage, sems) = refs[:-4], refs[-4:]
-    chunk = CHUNK * HD
-    count = q_ref.shape[1] // chunk
-    q_copies = []
-    for c in range(count):
-        columns = pl.ds(c * chunk, chunk)
-        q_copies.append(pltpu.make_async_copy(q_hbm.at[:, columns], q_ref.at[:, columns], sems.at[count + c]))
-        q_copies[c].start()
-    width = new_ref.shape[2]
+def gather_kernel(q_hbm, new_ref, *refs):
+    pieces, (kv_ref, q_ref, sems) = refs[:-3], refs[-3:]
+    q_rows = q_ref.shape[0] // Q_COPIES
+    copies = []
+    for number in range(Q_COPIES):
+        rows_at = pl.ds(number * q_rows, q_rows)
+        copies.append(pltpu.make_async_copy(q_hbm.at[rows_at], q_ref.at[rows_at], sems.at[number]))
+        copies[number].start()
+    kv_ref[:SPAN, :] = new_ref[...].reshape(SPAN, kv_ref.shape[1])
+    at = SPAN
+    for piece in pieces:
+        kv_ref[at : at + piece.shape[0], :] = piece[...]
+        at += piece.shape[0]
+    for copy in copies:
+        copy.wait()
+
+
+def attend_kernel(limit_ref, q_ref, kv_ref, *refs):
+    late, (cache_ref, out_ref, stage, sems) = refs[:-4], refs[-4:]
+    width = kv_ref.shape[1] // 2
     gen = cache_ref.shape[0]
     kvh = width // HD
     gq = q_ref.shape[1] // width
-    new = new_ref[...].reshape(SPAN, 2 * width)
-    old = sum(p.shape[0] for p in pieces)
-    ones = jnp.ones((SPAN + old + gen, HD), jnp.bfloat16)
+    old = kv_ref.shape[0] - SPAN + sum(piece.shape[0] for piece in late)
     token = lax.broadcasted_iota(jnp.int32, (SPAN, SPAN), 0)
     causal = lax.broadcasted_iota(jnp.int32, (SPAN, SPAN), 1) <= token
     visible = lax.broadcasted_iota(jnp.int32, (SPAN, gen), 1) < jnp.broadcast_to(limit_ref[:1], (SPAN, gen))
+    ones = jnp.ones((SPAN + old + gen, HD), jnp.bfloat16)
     keys, values = [], []
     for g in range(kvh):
         k_at = slice(g * HD, (g + 1) * HD)
         v_at = slice(width + g * HD, width + (g + 1) * HD)
-        keys.append(jnp.concatenate([new[:, k_at]] + [p[:, k_at] for p in (*pieces, cache_ref)], axis=0))
-        value = jnp.concatenate([new[:, v_at]] + [p[:, v_at] for p in (*pieces, cache_ref)], axis=0)
+        keys.append(jnp.concatenate([ref[:, k_at] for ref in (kv_ref, *late, cache_ref)], axis=0))
+        value = jnp.concatenate([ref[:, v_at] for ref in (kv_ref, *late, cache_ref)], axis=0)
         values.append(jnp.concatenate([value, ones], axis=1))
+    chunk = CHUNK * HD
     per_group = gq // CHUNK
+    count = q_ref.shape[1] // chunk
 
     def scores_of(c):
-        q_copies[c].wait()
         return dot_nt(head_rows(q_ref, c, CHUNK), keys[c // per_group])
 
     copies = []
@@ -180,39 +191,46 @@
         compiler_params=params(12),
         name="pack",
     )(*(pltpu.with_memory_space_constraint(x, pltpu.HBM) for x in (ancestors, lengths, prompt_kv, cache_kv)))
-    outgoing, far, limit = rest[:dom_count], rest[dom_count], rest[dom_count + 1]
+    outgoing, (far, limit) = rest[:dom_count], rest[dom_count:]
 
     pieces = [half] + [swap(half, "ctx", k * y_count) for k in range(1, Z)]
     pieces += [swap(p, "ctx", k) for k in range(1, y_count) for p in pieces[:Z]]
-    underway = pieces[1 : Z + 2]
     pieces += [swap(p, "dom", 1) for p in pieces]
 
     incoming = outgoing[:1] + [swap(outgoing[k], "dom", k) for k in range(1, dom_count)]
     routed = pl.pallas_call(
-        functools.partial(route_kernel, dom_count),
+        route_kernel,
         out_shape=pltpu.HBM((group, page_rows, 2 * width), jnp.bfloat16),
-        in_specs=[VMEM] * (1 + dom_count) + [pl.BlockSpec(memory_space=pl.ANY)] * len(underway),
+        in_specs=[VMEM] * (1 + dom_count),
         out_specs=HBM,
         scratch_shapes=[pltpu.VMEM((group, page_rows, 2 * width), jnp.bfloat16), pltpu.SemaphoreType.DMA],
         compiler_params=params(12),
         name="route",
-    )(far, *incoming, *underway)
+    )(far, *incoming)
     pages = lax.all_to_all(routed, "ctx", split_axis=0, concat_axis=0, tiled=True)
     pages = pages.reshape(ctx_count * page_rows, 2 * width)
 
+    late = [pieces.pop(at) for at in sorted((*range(Z + 2, 2 * Z), *range(len(pieces) - Z + 2, len(pieces))), reverse=True)]
+    key_count = SPAN + sum(piece.shape[0] for piece in pieces)
+    kv, queries = pl.pallas_call(
+        gather_kernel,
+        out_shape=(shape((key_count, 2 * width), jnp.bfloat16), shape(q_new.shape, q_new.dtype)),
+        in_specs=[HBM] + [VMEM] * (1 + len(pieces)),
+        out_specs=(VMEM, VMEM),
+        scratch_shapes=[pltpu.SemaphoreType.DMA((Q_COPIES,))],
+        compiler_params=params(16),
+        cost_estimate=pl.CostEstimate(flops=10**9, bytes_accessed=2**22, transcendentals=0),
+        name="gather",
+    )(pltpu.with_memory_space_constraint(q_new, pltpu.HBM), kv_new, *pieces)
     return pl.pallas_call(
         attend_kernel,
         out_shape=shape((tokens, q_width), jnp.bfloat16),
-        in_specs=[VMEM, HBM] + [VMEM] * (2 + len(pieces)),
+        in_specs=[VMEM] * (4 + len(late)),
         out_specs=HBM,
-        scratch_shapes=[
-            pltpu.VMEM((tokens, q_width), jnp.bfloat16),
-            pltpu.VMEM((tokens, q_width), jnp.bfloat16),
-            pltpu.SemaphoreType.DMA((2 * q_width // (CHUNK * HD),)),
-        ],
+        scratch_shapes=[pltpu.VMEM((tokens, q_width), jnp.bfloat16), pltpu.SemaphoreType.DMA((q_width // (CHUNK * HD),))],
         compiler_params=params(40 if prompt_kv.shape[0] * ctx_count > 1024 else 24),
         name="attend",
-    )(limit, pltpu.with_memory_space_constraint(q_new, pltpu.HBM), kv_new, pages, *pieces)
+    )(limit, queries, kv, *late, pages)
 
 
 def solution(mesh):

time: 37.4 us -> 35.1 us (0.939)
  waiting for transfers between devices: 10.4 us -> 5.93 us
  starting transfers between devices: 17.3 us -> 20.8 us
  Pallas kernels: 9.36 us -> 7.99 us
    ppermute x18, waiting for transfers between devices: 10.4 us -> 5.92 us  [swap(): lax.ppermute(x, axis, [(i, i ^ distance) for i in range(lax.axis_size(axi...]
    pallas_call x1, Pallas kernels: 7.6 us -> 4.93 us  [on_device(): pl.pallas_call(attend_kernel, out_shape=shape((tokens, q_width), jnp.bflo...]
    ppermute x18, starting transfers between devices: 13.8 us -> 16.3 us  [swap(): lax.ppermute(x, axis, [(i, i ^ distance) for i in range(lax.axis_size(axi...]
    pallas_call x1 -> x2, Pallas kernels: 0.72 us -> 1.95 us  [the longest x1 1.23 us: on_device(): pl.pallas_call(gather_kernel, out_shape=(shape((key_count, 2 * width), jn...]
    all_to_all x1, starting transfers between devices: 3.52 us -> 4.49 us  [on_device(): lax.all_to_all(routed, 'ctx', split_axis=0, concat_axis=0, tiled=True)]
  transfers between devices with their start and end apart: 19 -> 19, of which waited for: 6 -> 2; matrix products, arithmetic and copies ran while one was open for 0% -> 0% of each run, Pallas kernels for 0% -> 6%
where the time goes in v11:
time: 35.1 us; the launch traced here: 34.8 us
  starting transfers between devices  20.8 us (59%)
  Pallas kernels  7.99 us (23%)
  waiting for transfers between devices  5.93 us (17%)
    ppermute x18, starting transfers between devices, swap(): lax.ppermute(x, axis, [(i, i ^ distance) for i in range(lax.axis_size(axi...  16.3 us
    ppermute x18, waiting for transfers between devices, swap(): lax.ppermute(x, axis, [(i, i ^ distance) for i in range(lax.axis_size(axi...  5.92 us
    pallas_call x1, Pallas kernels, on_device(): pl.pallas_call(attend_kernel, out_shape=shape((tokens, q_width), jnp.bflo...  4.93 us
    all_to_all x1, starting transfers between devices, on_device(): lax.all_to_all(routed, 'ctx', split_axis=0, concat_axis=0, tiled=True)  4.49 us
    pallas_call x1, Pallas kernels, on_device(): pl.pallas_call(gather_kernel, out_shape=(shape((key_count, 2 * width), jn...  1.23 us
    pallas_call x1, Pallas kernels, on_device(): pl.pallas_call(functools.partial(pack_kernel, dom_count), out_shape=(shap...  1.12 us
    pallas_call x1, Pallas kernels, on_device(): pl.pallas_call(route_kernel, out_shape=pltpu.HBM((group, page_rows, 2 * w...  0.72 us
  transfers between devices with their start and end apart: 19, of which 2 were waited for; matrix products, arithmetic and copies ran while one was open for 0% of the time, Pallas kernels for 6%

profile of v11, /device:TPU:0, one launch (start us, length us, event | category | flops | bytes accessed | tf_op | source)
XLA Modules:
  0.0 34.8 jit_solution(1370996922692515193)
XLA Ops:
  0.0 1.1 %pack.1 = (bf16[32,1024]{1,0:T(8,128)(2,1)S(1)}, bf16[4,8,1024]{2,1,0:T(8,128)(2,1)S(1)}, bf16[4,8,1024]{2,1,0:T(8,128)(2,1)S(1)}, bf16[4,8,1024]{2,1,0:T(8,128)...) custom-call(s32[32]{0:T(128)} %anc_hbm.1, s32[32]{0:T(128)} %len_hbm.1, ...), custom_call_target="tpu_custom_call" | custom-call | tf_op jit(solution)/shard_map/pack/pallas_call | solution.py:174
  1.1 0.6 %collective-permute-start.15 = (bf16[4,8,1024]{2,1,0:T(8,128)(2,1)S(1)}, bf16[4,8,1024]{2,1,0:T(8,128)(2,1)S(1)}, u32[]{:S(2)}, u32[]{:S(2)}) collective-permute-start(bf16[4,8,1024]{2,1,0:T(8,128)(2,1)S(1)} %get-tuple-element.20), channel_id=1, source_target_pairs={{0,8},{8,0},{16,24},{24,16},{1,9},{9,1},{17,25},{25,17},{2,10},{10... | collective-permute-start | bytes 196616 | tf_op jit(solution)/shard_map/ppermute | solution.py:163
  1.7 2.4 %collective-permute-start.16 = (bf16[4,8,1024]{2,1,0:T(8,128)(2,1)S(1)}, bf16[4,8,1024]{2,1,0:T(8,128)(2,1)S(1)}, u32[]{:S(2)}, u32[]{:S(2)}) collective-permute-start(bf16[4,8,1024]{2,1,0:T(8,128)(2,1)S(1)} %get-tuple-element.21), channel_id=1, source_target_pairs={{0,16},{8,24},{16,0},{24,8},{1,17},{9,25},{17,1},{25,9},{2,18},{10... | collective-permute-start | bytes 196616 | tf_op jit(solution)/shard_map/ppermute | solution.py:163
  4.1 0.1 collective-permute-start.17
  4.2 1.9 %collective-permute-start.3 = (bf16[32,1024]{1,0:T(8,128)(2,1)S(1)}, bf16[32,1024]{1,0:T(8,128)(2,1)S(1)}, u32[]{:S(2)}, u32[]{:S(2)}) collective-permute-start(bf16[32,1024]{1,0:T(8,128)(2,1)S(1)} %get-tuple-element.15.refs_0_), channel_id=1, source_target_pairs={{0,1},{1,0},{2,3},{3,2},{4,5},{5,4},{6,7},{7,6},{8,9},{9,8},{10,11... | collective-permute-start | bytes 196616 | tf_op jit(solution)/shard_map/ppermute | solution.py:163
  6.0 3.6 %collective-permute-start.2 = (bf16[32,1024]{1,0:T(8,128)(2,1)S(1)}, bf16[32,1024]{1,0:T(8,128)(2,1)S(1)}, u32[]{:S(2)}, u32[]{:S(2)}) collective-permute-start(bf16[32,1024]{1,0:T(8,128)(2,1)S(1)} %get-tuple-element.15.refs_0_), channel_id=1, source_target_pairs={{0,6},{1,7},{2,4},{3,5},{4,2},{5,3},{6,0},{7,1},{8,14},{9,15},{10,... | collective-permute-start | bytes 196616 | tf_op jit(solution)/shard_map/ppermute | solution.py:163
  9.6 0.0 collective-permute-done.15.refs_1_
  9.6 0.0 collective-permute-start
  9.6 0.0 collective-permute-done.16.refs_2_
  9.6 0.0 collective-permute-done.17.refs_3_
  9.7 0.0 copy-start
  9.7 0.7 %route.1 = bf16[8,8,1024]{2,1,0:T(8,128)(2,1)} custom-call(bf16[2,8,128]{2,1,0:T(8,128)(2,1)S(1)} %get-tuple-element.18.far_ref, bf16[4,8,1024]{2,1,0:T(8,128)(2,1)S(1)} %get-tuple-element.19.refs_0_, bf16[4,8,1024]{2,1,0:T(8,128)(2,1)S(1)} %collective-permute-done.15.refs_1_, bf16[4,8,1024]{2,1,0:T(8,128)(2,1)S(1)} %collective-permute-done.16.refs_2_, ...), custom_call_target="tpu_custom_call" | custom-call | tf_op jit(solution)/shard_map/route/pallas_call | solution.py:201
  10.4 4.5 %all-to-all-start = ((bf16[8,8,1024]{2,1,0:T(8,128)(2,1)}), bf16[8,8,1024]{2,1,0:T(8,128)(2,1)S(1)}, u32[]{:S(2)}, u32[]{:S(2)}) async-start(bf16[8,8,1024]{2,1,0:T(8,128)(2,1)} %route.1), calls=%async_computation | async-start | bytes 262144 | tf_op jit(solution)/shard_map/all_to_all | solution.py:210
  14.9 0.1 collective-permute-start.5
  15.0 2.8 %collective-permute-start.1 = (bf16[32,1024]{1,0:T(8,128)(2,1)S(1)}, bf16[32,1024]{1,0:T(8,128)(2,1)S(1)}, u32[]{:S(2)}, u32[]{:S(2)}) collective-permute-start(bf16[32,1024]{1,0:T(8,128)(2,1)S(1)} %get-tuple-element.15.refs_0_), channel_id=1, source_target_pairs={{0,4},{1,5},{2,6},{3,7},{4,0},{5,1},{6,2},{7,3},{8,12},{9,13},{10,... | collective-permute-start | bytes 196616 | tf_op jit(solution)/shard_map/ppermute | solution.py:163
  17.8 0.0 collective-permute-done.3.refs_4_
  17.8 0.2 collective-permute-start.9
  18.0 0.0 collective-permute-done.2.refs_3_
  18.1 1.5 %collective-permute-start.11 = (bf16[32,1024]{1,0:T(8,128)(2,1)S(1)}, bf16[32,1024]{1,0:T(8,128)(2,1)S(1)}, u32[]{:S(2)}, u32[]{:S(2)}) collective-permute-start(bf16[32,1024]{1,0:T(8,128)(2,1)S(1)} %collective-permute-done.2.refs_3_), channel_id=1, source_target_pairs={{0,1},{1,0},{2,3},{3,2},{4,5},{5,4},{6,7},{7,6},{8,9},{9,8},{10,11... | collective-permute-start | bytes 196616 | tf_op jit(solution)/shard_map/ppermute | solution.py:163
  19.5 0.0 collective-permute-done.refs_1_
  19.5 0.6 %collective-permute-start.4 = (bf16[32,1024]{1,0:T(8,128)(2,1)S(1)}, bf16[32,1024]{1,0:T(8,128)(2,1)S(1)}, u32[]{:S(2)}, u32[]{:S(2)}) collective-permute-start(bf16[32,1024]{1,0:T(8,128)(2,1)S(1)} %collective-permute-done.refs_1_), channel_id=1, source_target_pairs={{0,1},{1,0},{2,3},{3,2},{4,5},{5,4},{6,7},{7,6},{8,9},{9,8},{10,11... | collective-permute-start | bytes 196616 | tf_op jit(solution)/shard_map/ppermute | solution.py:163
  20.1 0.0 collective-permute-done.5.refs_6_
  20.1 0.0 collective-permute-start.8
  20.1 4.2 %collective-permute-done.1.refs_2_ = bf16[32,1024]{1,0:T(8,128)(2,1)S(1)} collective-permute-done((bf16[32,1024]{1,0:T(8,128)(2,1)S(1)}, bf16[32,1024]{1,0:T(8,128)(2,1)S(1)}, u32[]{:S(2)}, u32[]{:S(2)}) %collective-permute-start.1) | collective-permute-done | bytes 65568 | tf_op jit(solution)/shard_map/ppermute | solution.py:163
  24.3 1.5 %collective-permute-start.13 = (bf16[32,1024]{1,0:T(8,128)(2,1)S(1)}, bf16[32,1024]{1,0:T(8,128)(2,1)S(1)}, u32[]{:S(2)}, u32[]{:S(2)}) collective-permute-start(bf16[32,1024]{1,0:T(8,128)(2,1)S(1)} %collective-permute-done.1.refs_2_), channel_id=1, source_target_pairs={{0,1},{1,0},{2,3},{3,2},{4,5},{5,4},{6,7},{7,6},{8,9},{9,8},{10,11... | collective-permute-start | bytes 196616 | tf_op jit(solution)/shard_map/ppermute | solution.py:163
  25.8 0.0 collective-permute-done.9.refs_10_
  25.8 0.0 collective-permute-start.7
  25.8 0.0 collective-permute-done.11.refs_2_
  25.8 0.5 %collective-permute-start.6 = (bf16[32,1024]{1,0:T(8,128)(2,1)S(1)}, bf16[32,1024]{1,0:T(8,128)(2,1)S(1)}, u32[]{:S(2)}, u32[]{:S(2)}) collective-permute-start(bf16[32,1024]{1,0:T(8,128)(2,1)S(1)} %collective-permute-done.refs_1_), channel_id=1, source_target_pairs={{0,8},{8,0},{16,24},{24,16},{1,9},{9,1},{17,25},{25,17},{2,10},{10... | collective-permute-start | bytes 196616 | tf_op jit(solution)/shard_map/ppermute | solution.py:163
  26.4 0.0 collective-permute-done.4.refs_5_
  26.4 0.1 collective-permute-start.10
  26.4 0.0 collective-permute-done.8.refs_9_
  26.4 0.4 %collective-permute-start.12 = (bf16[32,1024]{1,0:T(8,128)(2,1)S(1)}, bf16[32,1024]{1,0:T(8,128)(2,1)S(1)}, u32[]{:S(2)}, u32[]{:S(2)}) collective-permute-start(bf16[32,1024]{1,0:T(8,128)(2,1)S(1)} %collective-permute-done.11.refs_2_), channel_id=1, source_target_pairs={{0,8},{8,0},{16,24},{24,16},{1,9},{9,1},{17,25},{25,17},{2,10},{10... | collective-permute-start | bytes 196616 | tf_op jit(solution)/shard_map/ppermute | solution.py:163
  26.9 1.7 %collective-permute-done.13.refs_3_ = bf16[32,1024]{1,0:T(8,128)(2,1)S(1)} collective-permute-done((bf16[32,1024]{1,0:T(8,128)(2,1)S(1)}, bf16[32,1024]{1,0:T(8,128)(2,1)S(1)}, u32[]{:S(2)}, u32[]{:S(2)}) %collective-permute-start.13) | collective-permute-done | bytes 65568 | tf_op jit(solution)/shard_map/ppermute | solution.py:163
  28.6 0.0 collective-permute-start.14
  28.6 0.0 collective-permute-done.7.refs_8_
  28.6 0.0 collective-permute-done.6.refs_7_
  28.6 0.0 collective-permute-done.10.refs_11_
  28.6 0.0 copy-done
  28.6 1.2 %gather.1 = (bf16[512,1024]{1,0:T(8,128)(2,1)S(1)}, bf16[128,4096]{1,0:T(8,128)(2,1)S(1)}) custom-call(bf16[128,4096]{1,0:T(8,128)(2,1)} %q_hbm.1, bf16[128,2,512]{2,1,0:T(2,128)(2,1)S(1)} %copy-done, bf16[32,1024]{1,0:T(8,128)(2,1)S(1)} %get-tuple-element.15.refs_0_, bf16[32,1024]{1,0:T(8,128)(2,1)S(1)} %collective-permute-done.refs_1_, ...), custom_call_target="tpu_custom_call" | custom-call | flops 1000000000 | bytes 4194304 | tf_op jit(solution)/shard_map/gather/pallas_call | solution.py:215
  29.8 0.0 collective-permute-done.12.refs_0_
  29.8 0.0 collective-permute-done.14.refs_1_
  29.8 0.0 all-to-all-done
  29.9 4.9 %attend.1 = bf16[128,4096]{1,0:T(8,128)(2,1)} custom-call(s32[8,64]{1,0:T(8,128)S(1)} %get-tuple-element.14.limit_ref, bf16[128,4096]{1,0:T(8,128)(2,1)S(1)} %get-tuple-element.16.q_ref, bf16[512,1024]{1,0:T(8,128)(2,1)S(1)} %get-tuple-element.17.kv_ref, bf16[32,1024]{1,0:T(8,128)(2,1)S(1)} %collective-permute-done.12.refs_0_, ...), custom_call_target="tpu_custom_call" | custom-call | tf_op jit(solution)/shard_map/attend/pallas_call | solution.py:225
Async XLA Ops:
  1.1 8.5 %collective-permute-start.15 = (bf16[4,8,1024]{2,1,0:T(8,128)(2,1)S(1)}, bf16[4,8,1024]{2,1,0:T(8,128)(2,1)S(1)}, u32[]{:S(2)}, u32[]{:S(2)}) collective-permute-start(bf16[4,8,1024]{2,1,0:T(8,128)(2,1)S(1)} %get-tuple-element.20), channel_id=1, source_target_pairs={{0,8},{8,0},{16,24},{24,16},{1,9},{9,1},{17,25},{25,17},{2,10},{10... | collective-permute-start | bytes 196616 | tf_op jit(solution)/shard_map/ppermute | solution.py:163
  1.7 7.9 %collective-permute-start.16 = (bf16[4,8,1024]{2,1,0:T(8,128)(2,1)S(1)}, bf16[4,8,1024]{2,1,0:T(8,128)(2,1)S(1)}, u32[]{:S(2)}, u32[]{:S(2)}) collective-permute-start(bf16[4,8,1024]{2,1,0:T(8,128)(2,1)S(1)} %get-tuple-element.21), channel_id=1, source_target_pairs={{0,16},{8,24},{16,0},{24,8},{1,17},{9,25},{17,1},{25,9},{2,18},{10... | collective-permute-start | bytes 196616 | tf_op jit(solution)/shard_map/ppermute | solution.py:163
  4.1 5.5 %collective-permute-start.17 = (bf16[4,8,1024]{2,1,0:T(8,128)(2,1)S(1)}, bf16[4,8,1024]{2,1,0:T(8,128)(2,1)S(1)}, u32[]{:S(2)}, u32[]{:S(2)}) collective-permute-start(bf16[4,8,1024]{2,1,0:T(8,128)(2,1)S(1)} %get-tuple-element.22), channel_id=1, source_target_pairs={{0,24},{8,16},{16,8},{24,0},{1,25},{9,17},{17,9},{25,1},{2,26},{10... | collective-permute-start | bytes 196616 | tf_op jit(solution)/shard_map/ppermute | solution.py:163
  4.2 13.6 %collective-permute-start.3 = (bf16[32,1024]{1,0:T(8,128)(2,1)S(1)}, bf16[32,1024]{1,0:T(8,128)(2,1)S(1)}, u32[]{:S(2)}, u32[]{:S(2)}) collective-permute-start(bf16[32,1024]{1,0:T(8,128)(2,1)S(1)} %get-tuple-element.15.refs_0_), channel_id=1, source_target_pairs={{0,1},{1,0},{2,3},{3,2},{4,5},{5,4},{6,7},{7,6},{8,9},{9,8},{10,11... | collective-permute-start | bytes 196616 | tf_op jit(solution)/shard_map/ppermute | solution.py:163
  6.0 12.0 %collective-permute-start.2 = (bf16[32,1024]{1,0:T(8,128)(2,1)S(1)}, bf16[32,1024]{1,0:T(8,128)(2,1)S(1)}, u32[]{:S(2)}, u32[]{:S(2)}) collective-permute-start(bf16[32,1024]{1,0:T(8,128)(2,1)S(1)} %get-tuple-element.15.refs_0_), channel_id=1, source_target_pairs={{0,6},{1,7},{2,4},{3,5},{4,2},{5,3},{6,0},{7,1},{8,14},{9,15},{10,... | collective-permute-start | bytes 196616 | tf_op jit(solution)/shard_map/ppermute | solution.py:163
  9.6 9.9 %collective-permute-start = (bf16[32,1024]{1,0:T(8,128)(2,1)S(1)}, bf16[32,1024]{1,0:T(8,128)(2,1)S(1)}, u32[]{:S(2)}, u32[]{:S(2)}) collective-permute-start(bf16[32,1024]{1,0:T(8,128)(2,1)S(1)} %get-tuple-element.15.refs_0_), channel_id=1, source_target_pairs={{0,2},{1,3},{2,0},{3,1},{4,6},{5,7},{6,4},{7,5},{8,10},{9,11},{10,... | collective-permute-start | bytes 196616 | tf_op jit(solution)/shard_map/ppermute | solution.py:163
  9.7 18.9 %copy-start = (bf16[128,2,512]{2,1,0:T(2,128)(2,1)S(1)}, bf16[128,2,512]{2,1,0:T(2,128)(2,1)}, u32[]{:S(2)}) copy-start(bf16[128,2,512]{2,1,0:T(2,128)(2,1)} %new_ref.1) | copy-start | bytes 786436
  10.4 19.4 %all-to-all-start = ((bf16[8,8,1024]{2,1,0:T(8,128)(2,1)}), bf16[8,8,1024]{2,1,0:T(8,128)(2,1)S(1)}, u32[]{:S(2)}, u32[]{:S(2)}) async-start(bf16[8,8,1024]{2,1,0:T(8,128)(2,1)} %route.1), calls=%async_computation | async-start | bytes 262144 | tf_op jit(solution)/shard_map/all_to_all | solution.py:210
  14.9 5.2 %collective-permute-start.5 = (bf16[32,1024]{1,0:T(8,128)(2,1)S(1)}, bf16[32,1024]{1,0:T(8,128)(2,1)S(1)}, u32[]{:S(2)}, u32[]{:S(2)}) collective-permute-start(bf16[32,1024]{1,0:T(8,128)(2,1)S(1)} %get-tuple-element.15.refs_0_), channel_id=1, source_target_pairs={{0,8},{8,0},{16,24},{24,16},{1,9},{9,1},{17,25},{25,17},{2,10},{10... | collective-permute-start | bytes 196616 | tf_op jit(solution)/shard_map/ppermute | solution.py:163
  15.0 9.3 %collective-permute-start.1 = (bf16[32,1024]{1,0:T(8,128)(2,1)S(1)}, bf16[32,1024]{1,0:T(8,128)(2,1)S(1)}, u32[]{:S(2)}, u32[]{:S(2)}) collective-permute-start(bf16[32,1024]{1,0:T(8,128)(2,1)S(1)} %get-tuple-element.15.refs_0_), channel_id=1, source_target_pairs={{0,4},{1,5},{2,6},{3,7},{4,0},{5,1},{6,2},{7,3},{8,12},{9,13},{10,... | collective-permute-start | bytes 196616 | tf_op jit(solution)/shard_map/ppermute | solution.py:163
  17.8 8.0 %collective-permute-start.9 = (bf16[32,1024]{1,0:T(8,128)(2,1)S(1)}, bf16[32,1024]{1,0:T(8,128)(2,1)S(1)}, u32[]{:S(2)}, u32[]{:S(2)}) collective-permute-start(bf16[32,1024]{1,0:T(8,128)(2,1)S(1)} %collective-permute-done.3.refs_4_), channel_id=1, source_target_pairs={{0,8},{8,0},{16,24},{24,16},{1,9},{9,1},{17,25},{25,17},{2,10},{10... | collective-permute-start | bytes 196616 | tf_op jit(solution)/shard_map/ppermute | solution.py:163
  18.1 7.8 %collective-permute-start.11 = (bf16[32,1024]{1,0:T(8,128)(2,1)S(1)}, bf16[32,1024]{1,0:T(8,128)(2,1)S(1)}, u32[]{:S(2)}, u32[]{:S(2)}) collective-permute-start(bf16[32,1024]{1,0:T(8,128)(2,1)S(1)} %collective-permute-done.2.refs_3_), channel_id=1, source_target_pairs={{0,1},{1,0},{2,3},{3,2},{4,5},{5,4},{6,7},{7,6},{8,9},{9,8},{10,11... | collective-permute-start | bytes 196616 | tf_op jit(solution)/shard_map/ppermute | solution.py:163
  19.5 6.8 %collective-permute-start.4 = (bf16[32,1024]{1,0:T(8,128)(2,1)S(1)}, bf16[32,1024]{1,0:T(8,128)(2,1)S(1)}, u32[]{:S(2)}, u32[]{:S(2)}) collective-permute-start(bf16[32,1024]{1,0:T(8,128)(2,1)S(1)} %collective-permute-done.refs_1_), channel_id=1, source_target_pairs={{0,1},{1,0},{2,3},{3,2},{4,5},{5,4},{6,7},{7,6},{8,9},{9,8},{10,11... | collective-permute-start | bytes 196616 | tf_op jit(solution)/shard_map/ppermute | solution.py:163
  20.1 6.3 %collective-permute-start.8 = (bf16[32,1024]{1,0:T(8,128)(2,1)S(1)}, bf16[32,1024]{1,0:T(8,128)(2,1)S(1)}, u32[]{:S(2)}, u32[]{:S(2)}) collective-permute-start(bf16[32,1024]{1,0:T(8,128)(2,1)S(1)} %collective-permute-done.2.refs_3_), channel_id=1, source_target_pairs={{0,8},{8,0},{16,24},{24,16},{1,9},{9,1},{17,25},{25,17},{2,10},{10... | collective-permute-start | bytes 196616 | tf_op jit(solution)/shard_map/ppermute | solution.py:163
  24.3 4.3 %collective-permute-start.13 = (bf16[32,1024]{1,0:T(8,128)(2,1)S(1)}, bf16[32,1024]{1,0:T(8,128)(2,1)S(1)}, u32[]{:S(2)}, u32[]{:S(2)}) collective-permute-start(bf16[32,1024]{1,0:T(8,128)(2,1)S(1)} %collective-permute-done.1.refs_2_), channel_id=1, source_target_pairs={{0,1},{1,0},{2,3},{3,2},{4,5},{5,4},{6,7},{7,6},{8,9},{9,8},{10,11... | collective-permute-start | bytes 196616 | tf_op jit(solution)/shard_map/ppermute | solution.py:163
  25.8 2.7 %collective-permute-start.7 = (bf16[32,1024]{1,0:T(8,128)(2,1)S(1)}, bf16[32,1024]{1,0:T(8,128)(2,1)S(1)}, u32[]{:S(2)}, u32[]{:S(2)}) collective-permute-start(bf16[32,1024]{1,0:T(8,128)(2,1)S(1)} %collective-permute-done.1.refs_2_), channel_id=1, source_target_pairs={{0,8},{8,0},{16,24},{24,16},{1,9},{9,1},{17,25},{25,17},{2,10},{10... | collective-permute-start | bytes 196616 | tf_op jit(solution)/shard_map/ppermute | solution.py:163
  25.8 2.7 %collective-permute-start.6 = (bf16[32,1024]{1,0:T(8,128)(2,1)S(1)}, bf16[32,1024]{1,0:T(8,128)(2,1)S(1)}, u32[]{:S(2)}, u32[]{:S(2)}) collective-permute-start(bf16[32,1024]{1,0:T(8,128)(2,1)S(1)} %collective-permute-done.refs_1_), channel_id=1, source_target_pairs={{0,8},{8,0},{16,24},{24,16},{1,9},{9,1},{17,25},{25,17},{2,10},{10... | collective-permute-start | bytes 196616 | tf_op jit(solution)/shard_map/ppermute | solution.py:163
  26.4 2.2 %collective-permute-start.10 = (bf16[32,1024]{1,0:T(8,128)(2,1)S(1)}, bf16[32,1024]{1,0:T(8,128)(2,1)S(1)}, u32[]{:S(2)}, u32[]{:S(2)}) collective-permute-start(bf16[32,1024]{1,0:T(8,128)(2,1)S(1)} %collective-permute-done.4.refs_5_), channel_id=1, source_target_pairs={{0,8},{8,0},{16,24},{24,16},{1,9},{9,1},{17,25},{25,17},{2,10},{10... | collective-permute-start | bytes 196616 | tf_op jit(solution)/shard_map/ppermute | solution.py:163
  26.4 3.4 %collective-permute-start.12 = (bf16[32,1024]{1,0:T(8,128)(2,1)S(1)}, bf16[32,1024]{1,0:T(8,128)(2,1)S(1)}, u32[]{:S(2)}, u32[]{:S(2)}) collective-permute-start(bf16[32,1024]{1,0:T(8,128)(2,1)S(1)} %collective-permute-done.11.refs_2_), channel_id=1, source_target_pairs={{0,8},{8,0},{16,24},{24,16},{1,9},{9,1},{17,25},{25,17},{2,10},{10... | collective-permute-start | bytes 196616 | tf_op jit(solution)/shard_map/ppermute | solution.py:163
  28.6 1.3 %collective-permute-start.14 = (bf16[32,1024]{1,0:T(8,128)(2,1)S(1)}, bf16[32,1024]{1,0:T(8,128)(2,1)S(1)}, u32[]{:S(2)}, u32[]{:S(2)}) collective-permute-start(bf16[32,1024]{1,0:T(8,128)(2,1)S(1)} %collective-permute-done.13.refs_3_), channel_id=1, source_target_pairs={{0,8},{8,0},{16,24},{24,16},{1,9},{9,1},{17,25},{25,17},{2,10},{10... | collective-permute-start | bytes 196616 | tf_op jit(solution)/shard_map/ppermute | solution.py:163

commit v12 on v11

--- a/solution.py
+++ b/solution.py
@@ -210,7 +210,7 @@
     pages = lax.all_to_all(routed, "ctx", split_axis=0, concat_axis=0, tiled=True)
     pages = pages.reshape(ctx_count * page_rows, 2 * width)
 
-    late = [pieces.pop(at) for at in sorted((*range(Z + 2, 2 * Z), *range(len(pieces) - Z + 2, len(pieces))), reverse=True)]
+    late = [pieces.pop(at) for at in sorted((Z, *range(Z + 2, 2 * Z), len(pieces) - Z, *range(len(pieces) - Z + 2, len(pieces))), reverse=True)]
     key_count = SPAN + sum(piece.shape[0] for piece in pieces)
     kv, queries = pl.pallas_call(
         gather_kernel,
@@ -219,7 +219,7 @@
         out_specs=(VMEM, VMEM),
         scratch_shapes=[pltpu.SemaphoreType.DMA((Q_COPIES,))],
         compiler_params=params(16),
-        cost_estimate=pl.CostEstimate(flops=10**9, bytes_accessed=2**22, transcendentals=0),
+        cost_estimate=pl.CostEstimate(flops=3 * 10**9, bytes_accessed=2**22, transcendentals=0),
         name="gather",
     )(pltpu.with_memory_space_constraint(q_new, pltpu.HBM), kv_new, *pieces)
     return pl.pallas_call(

time: 35.1 us -> 36.2 us (1.031)
  waiting for transfers between devices: 5.93 us -> 7.62 us
  starting transfers between devices: 20.8 us -> 20.2 us
    all_to_all x1, waiting for transfers between devices: 0.01 us -> 5.56 us  [on_device(): lax.all_to_all(routed, 'ctx', split_axis=0, concat_axis=0, tiled=True)]
    ppermute x18, waiting for transfers between devices: 5.92 us -> 2.06 us  [swap(): lax.ppermute(x, axis, [(i, i ^ distance) for i in range(lax.axis_size(axi...]
    ppermute x18, starting transfers between devices: 16.3 us -> 14.6 us  [swap(): lax.ppermute(x, axis, [(i, i ^ distance) for i in range(lax.axis_size(axi...]
    all_to_all x1, starting transfers between devices: 4.49 us -> 5.55 us  [on_device(): lax.all_to_all(routed, 'ctx', split_axis=0, concat_axis=0, tiled=True)]
  transfers between devices with their start and end apart: 19 -> 19, of which waited for: 2 -> 4; matrix products, arithmetic and copies ran while one was open for 0% -> 0% of each run, Pallas kernels for 6% -> 5%
where the time goes in v12:
time: 36.2 us; the launch traced here: 35.9 us
  starting transfers between devices  20.2 us (56%)
  Pallas kernels  8.02 us (22%)
  waiting for transfers between devices  7.62 us (21%)
    ppermute x18, starting transfers between devices, swap(): lax.ppermute(x, axis, [(i, i ^ distance) for i in range(lax.axis_size(axi...  14.6 us
    all_to_all x1, waiting for transfers between devices, on_device(): lax.all_to_all(routed, 'ctx', split_axis=0, concat_axis=0, tiled=True)  5.56 us
    all_to_all x1, starting transfers between devices, on_device(): lax.all_to_all(routed, 'ctx', split_axis=0, concat_axis=0, tiled=True)  5.55 us
    pallas_call x1, Pallas kernels, on_device(): pl.pallas_call(attend_kernel, out_shape=shape((tokens, q_width), jnp.bflo...  4.93 us
    ppermute x18, waiting for transfers between devices, swap(): lax.ppermute(x, axis, [(i, i ^ distance) for i in range(lax.axis_size(axi...  2.06 us
    pallas_call x1, Pallas kernels, on_device(): pl.pallas_call(gather_kernel, out_shape=(shape((key_count, 2 * width), jn...  1.23 us
    pallas_call x1, Pallas kernels, on_device(): pl.pallas_call(functools.partial(pack_kernel, dom_count), out_shape=(shap...  1.14 us
  transfers between devices with their start and end apart: 19, of which 4 were waited for; matrix products, arithmetic and copies ran while one was open for 0% of the time, Pallas kernels for 5%

profile of v12, /device:TPU:0, one launch (start us, length us, event | category | flops | bytes accessed | tf_op | source)
XLA Modules:
  0.0 35.9 jit_solution(61002991745949128)
XLA Ops:
  0.0 1.1 %pack.1 = (bf16[32,1024]{1,0:T(8,128)(2,1)S(1)}, bf16[4,8,1024]{2,1,0:T(8,128)(2,1)S(1)}, bf16[4,8,1024]{2,1,0:T(8,128)(2,1)S(1)}, bf16[4,8,1024]{2,1,0:T(8,128)...) custom-call(s32[32]{0:T(128)} %anc_hbm.1, s32[32]{0:T(128)} %len_hbm.1, ...), custom_call_target="tpu_custom_call" | custom-call | tf_op jit(solution)/shard_map/pack/pallas_call | solution.py:174
  1.2 0.4 %collective-permute-start.15 = (bf16[4,8,1024]{2,1,0:T(8,128)(2,1)S(1)}, bf16[4,8,1024]{2,1,0:T(8,128)(2,1)S(1)}, u32[]{:S(2)}, u32[]{:S(2)}) collective-permute-start(bf16[4,8,1024]{2,1,0:T(8,128)(2,1)S(1)} %get-tuple-element.20), channel_id=1, source_target_pairs={{0,8},{8,0},{16,24},{24,16},{1,9},{9,1},{17,25},{25,17},{2,10},{10... | collective-permute-start | bytes 196616 | tf_op jit(solution)/shard_map/ppermute | solution.py:163
  1.6 2.6 %collective-permute-start.16 = (bf16[4,8,1024]{2,1,0:T(8,128)(2,1)S(1)}, bf16[4,8,1024]{2,1,0:T(8,128)(2,1)S(1)}, u32[]{:S(2)}, u32[]{:S(2)}) collective-permute-start(bf16[4,8,1024]{2,1,0:T(8,128)(2,1)S(1)} %get-tuple-element.21), channel_id=1, source_target_pairs={{0,16},{8,24},{16,0},{24,8},{1,17},{9,25},{17,1},{25,9},{2,18},{10... | collective-permute-start | bytes 196616 | tf_op jit(solution)/shard_map/ppermute | solution.py:163
  4.2 0.1 collective-permute-start.17
  4.3 3.9 %collective-permute-start.2 = (bf16[32,1024]{1,0:T(8,128)(2,1)S(1)}, bf16[32,1024]{1,0:T(8,128)(2,1)S(1)}, u32[]{:S(2)}, u32[]{:S(2)}) collective-permute-start(bf16[32,1024]{1,0:T(8,128)(2,1)S(1)} %get-tuple-element.15.refs_0_), channel_id=1, source_target_pairs={{0,6},{1,7},{2,4},{3,5},{4,2},{5,3},{6,0},{7,1},{8,14},{9,15},{10,... | collective-permute-start | bytes 196616 | tf_op jit(solution)/shard_map/ppermute | solution.py:163
  8.1 0.0 collective-permute-start
  8.1 0.0 collective-permute-done.15.refs_1_
  8.1 1.5 %collective-permute-start.13 = (bf16[32,1024]{1,0:T(8,128)(2,1)S(1)}, bf16[32,1024]{1,0:T(8,128)(2,1)S(1)}, u32[]{:S(2)}, u32[]{:S(2)}) collective-permute-start(bf16[32,1024]{1,0:T(8,128)(2,1)S(1)} %get-tuple-element.15.refs_0_), channel_id=1, source_target_pairs={{0,1},{1,0},{2,3},{3,2},{4,5},{5,4},{6,7},{7,6},{8,9},{9,8},{10,11... | collective-permute-start | bytes 196616 | tf_op jit(solution)/shard_map/ppermute | solution.py:163
  9.7 0.0 collective-permute-done.16.refs_2_
  9.7 0.8 %collective-permute-start.1 = (bf16[32,1024]{1,0:T(8,128)(2,1)S(1)}, bf16[32,1024]{1,0:T(8,128)(2,1)S(1)}, u32[]{:S(2)}, u32[]{:S(2)}) collective-permute-start(bf16[32,1024]{1,0:T(8,128)(2,1)S(1)} %get-tuple-element.15.refs_0_), channel_id=1, source_target_pairs={{0,4},{1,5},{2,6},{3,7},{4,0},{5,1},{6,2},{7,3},{8,12},{9,13},{10,... | collective-permute-start | bytes 196616 | tf_op jit(solution)/shard_map/ppermute | solution.py:163
  10.5 0.0 collective-permute-done.17.refs_3_
  10.5 0.0 collective-permute-start.4
  10.5 0.7 %collective-permute-done.2.refs_3_ = bf16[32,1024]{1,0:T(8,128)(2,1)S(1)} collective-permute-done((bf16[32,1024]{1,0:T(8,128)(2,1)S(1)}, bf16[32,1024]{1,0:T(8,128)(2,1)S(1)}, u32[]{:S(2)}, u32[]{:S(2)}) %collective-permute-start.2) | collective-permute-done | bytes 65568 | tf_op jit(solution)/shard_map/ppermute | solution.py:163
  11.1 1.6 %collective-permute-start.9 = (bf16[32,1024]{1,0:T(8,128)(2,1)S(1)}, bf16[32,1024]{1,0:T(8,128)(2,1)S(1)}, u32[]{:S(2)}, u32[]{:S(2)}) collective-permute-start(bf16[32,1024]{1,0:T(8,128)(2,1)S(1)} %collective-permute-done.2.refs_3_), channel_id=1, source_target_pairs={{0,1},{1,0},{2,3},{3,2},{4,5},{5,4},{6,7},{7,6},{8,9},{9,8},{10,11... | collective-permute-start | bytes 196616 | tf_op jit(solution)/shard_map/ppermute | solution.py:163
  12.8 0.0 collective-permute-done.refs_1_
  12.8 1.9 %collective-permute-start.3 = (bf16[32,1024]{1,0:T(8,128)(2,1)S(1)}, bf16[32,1024]{1,0:T(8,128)(2,1)S(1)}, u32[]{:S(2)}, u32[]{:S(2)}) collective-permute-start(bf16[32,1024]{1,0:T(8,128)(2,1)S(1)} %collective-permute-done.refs_1_), channel_id=1, source_target_pairs={{0,1},{1,0},{2,3},{3,2},{4,5},{5,4},{6,7},{7,6},{8,9},{9,8},{10,11... | collective-permute-start | bytes 196616 | tf_op jit(solution)/shard_map/ppermute | solution.py:163
  14.6 0.0 collective-permute-done.13.refs_5_
  14.7 0.0 collective-permute-start.7
  14.7 0.9 %collective-permute-done.1.refs_2_ = bf16[32,1024]{1,0:T(8,128)(2,1)S(1)} collective-permute-done((bf16[32,1024]{1,0:T(8,128)(2,1)S(1)}, bf16[32,1024]{1,0:T(8,128)(2,1)S(1)}, u32[]{:S(2)}, u32[]{:S(2)}) %collective-permute-start.1) | collective-permute-done | bytes 65568 | tf_op jit(solution)/shard_map/ppermute | solution.py:163
  15.5 0.5 %collective-permute-start.11 = (bf16[32,1024]{1,0:T(8,128)(2,1)S(1)}, bf16[32,1024]{1,0:T(8,128)(2,1)S(1)}, u32[]{:S(2)}, u32[]{:S(2)}) collective-permute-start(bf16[32,1024]{1,0:T(8,128)(2,1)S(1)} %collective-permute-done.1.refs_2_), channel_id=1, source_target_pairs={{0,1},{1,0},{2,3},{3,2},{4,5},{5,4},{6,7},{7,6},{8,9},{9,8},{10,11... | collective-permute-start | bytes 196616 | tf_op jit(solution)/shard_map/ppermute | solution.py:163
  16.0 0.0 collective-permute-done.4.refs_5_
  16.0 0.0 collective-permute-start.6
  16.0 0.0 collective-permute-done.9.refs_3_
  16.1 0.5 %collective-permute-start.5 = (bf16[32,1024]{1,0:T(8,128)(2,1)S(1)}, bf16[32,1024]{1,0:T(8,128)(2,1)S(1)}, u32[]{:S(2)}, u32[]{:S(2)}) collective-permute-start(bf16[32,1024]{1,0:T(8,128)(2,1)S(1)} %collective-permute-done.refs_1_), channel_id=1, source_target_pairs={{0,8},{8,0},{16,24},{24,16},{1,9},{9,1},{17,25},{25,17},{2,10},{10... | collective-permute-start | bytes 196616 | tf_op jit(solution)/shard_map/ppermute | solution.py:163
  16.6 0.5 %collective-permute-done.3.refs_4_ = bf16[32,1024]{1,0:T(8,128)(2,1)S(1)} collective-permute-done((bf16[32,1024]{1,0:T(8,128)(2,1)S(1)}, bf16[32,1024]{1,0:T(8,128)(2,1)S(1)}, u32[]{:S(2)}, u32[]{:S(2)}) %collective-permute-start.3) | collective-permute-done | bytes 65568 | tf_op jit(solution)/shard_map/ppermute | solution.py:163
  17.0 0.0 collective-permute-start.8
  17.0 0.0 copy-start
  17.0 0.7 %route.1 = bf16[8,8,1024]{2,1,0:T(8,128)(2,1)} custom-call(bf16[2,8,128]{2,1,0:T(8,128)(2,1)S(1)} %get-tuple-element.18.far_ref, bf16[4,8,1024]{2,1,0:T(8,128)(2,1)S(1)} %get-tuple-element.19.refs_0_, bf16[4,8,1024]{2,1,0:T(8,128)(2,1)S(1)} %collective-permute-done.15.refs_1_, bf16[4,8,1024]{2,1,0:T(8,128)(2,1)S(1)} %collective-permute-done.16.refs_2_, ...), custom_call_target="tpu_custom_call" | custom-call | tf_op jit(solution)/shard_map/route/pallas_call | solution.py:201
  17.8 5.5 %all-to-all-start = ((bf16[8,8,1024]{2,1,0:T(8,128)(2,1)}), bf16[8,8,1024]{2,1,0:T(8,128)(2,1)S(1)}, u32[]{:S(2)}, u32[]{:S(2)}) async-start(bf16[8,8,1024]{2,1,0:T(8,128)(2,1)} %route.1), calls=%async_computation | async-start | bytes 262144 | tf_op jit(solution)/shard_map/all_to_all | solution.py:210
  23.3 0.0 collective-permute-done.7.refs_8_
  23.3 0.3 collective-permute-start.14
  23.6 0.0 collective-permute-done.11.refs_4_
  23.6 0.3 collective-permute-start.10
  23.9 0.0 collective-permute-done.6.refs_7_
  23.9 0.2 collective-permute-start.12
  24.1 0.0 collective-permute-done.5.refs_6_
  24.1 0.0 collective-permute-done.8.refs_9_
  24.1 0.0 copy-done
  24.1 1.2 %gather.1 = (bf16[448,1024]{1,0:T(8,128)(2,1)S(1)}, bf16[128,4096]{1,0:T(8,128)(2,1)S(1)}) custom-call(bf16[128,4096]{1,0:T(8,128)(2,1)} %q_hbm.1, bf16[128,2,512]{2,1,0:T(2,128)(2,1)S(1)} %copy-done, bf16[32,1024]{1,0:T(8,128)(2,1)S(1)} %get-tuple-element.15.refs_0_, bf16[32,1024]{1,0:T(8,128)(2,1)S(1)} %collective-permute-done.refs_1_, ...), custom_call_target="tpu_custom_call" | custom-call | flops 3000000000 | bytes 4194304 | tf_op jit(solution)/shard_map/gather/pallas_call | solution.py:215
  25.4 0.0 collective-permute-done.14.refs_2_
  25.4 0.0 collective-permute-done.10.refs_0_
  25.4 0.0 collective-permute-done.12.refs_1_
  25.4 5.6 %all-to-all-done = bf16[8,8,1024]{2,1,0:T(8,128)(2,1)S(1)} async-done(((bf16[8,8,1024]{2,1,0:T(8,128)(2,1)}), bf16[8,8,1024]{2,1,0:T(8,128)(2,1)S(1)}, u32[]{:S(2)}, u32[]{:S(2)}) %all-to-all-start) | async-done | bytes 131104 | tf_op jit(solution)/shard_map/all_to_all | solution.py:210
  31.0 4.9 %attend.1 = bf16[128,4096]{1,0:T(8,128)(2,1)} custom-call(s32[8,64]{1,0:T(8,128)S(1)} %get-tuple-element.14.limit_ref, bf16[128,4096]{1,0:T(8,128)(2,1)S(1)} %get-tuple-element.16.q_ref, bf16[448,1024]{1,0:T(8,128)(2,1)S(1)} %get-tuple-element.17.kv_ref, bf16[32,1024]{1,0:T(8,128)(2,1)S(1)} %collective-permute-done.10.refs_0_, ...), custom_call_target="tpu_custom_call" | custom-call | tf_op jit(solution)/shard_map/attend/pallas_call | solution.py:225
Async XLA Ops:
  1.2 7.0 %collective-permute-start.15 = (bf16[4,8,1024]{2,1,0:T(8,128)(2,1)S(1)}, bf16[4,8,1024]{2,1,0:T(8,128)(2,1)S(1)}, u32[]{:S(2)}, u32[]{:S(2)}) collective-permute-start(bf16[4,8,1024]{2,1,0:T(8,128)(2,1)S(1)} %get-tuple-element.20), channel_id=1, source_target_pairs={{0,8},{8,0},{16,24},{24,16},{1,9},{9,1},{17,25},{25,17},{2,10},{10... | collective-permute-start | bytes 196616 | tf_op jit(solution)/shard_map/ppermute | solution.py:163
  1.6 8.1 %collective-permute-start.16 = (bf16[4,8,1024]{2,1,0:T(8,128)(2,1)S(1)}, bf16[4,8,1024]{2,1,0:T(8,128)(2,1)S(1)}, u32[]{:S(2)}, u32[]{:S(2)}) collective-permute-start(bf16[4,8,1024]{2,1,0:T(8,128)(2,1)S(1)} %get-tuple-element.21), channel_id=1, source_target_pairs={{0,16},{8,24},{16,0},{24,8},{1,17},{9,25},{17,1},{25,9},{2,18},{10... | collective-permute-start | bytes 196616 | tf_op jit(solution)/shard_map/ppermute | solution.py:163
  4.2 6.3 %collective-permute-start.17 = (bf16[4,8,1024]{2,1,0:T(8,128)(2,1)S(1)}, bf16[4,8,1024]{2,1,0:T(8,128)(2,1)S(1)}, u32[]{:S(2)}, u32[]{:S(2)}) collective-permute-start(bf16[4,8,1024]{2,1,0:T(8,128)(2,1)S(1)} %get-tuple-element.22), channel_id=1, source_target_pairs={{0,24},{8,16},{16,8},{24,0},{1,25},{9,17},{17,9},{25,1},{2,26},{10... | collective-permute-start | bytes 196616 | tf_op jit(solution)/shard_map/ppermute | solution.py:163
  4.3 6.9 %collective-permute-start.2 = (bf16[32,1024]{1,0:T(8,128)(2,1)S(1)}, bf16[32,1024]{1,0:T(8,128)(2,1)S(1)}, u32[]{:S(2)}, u32[]{:S(2)}) collective-permute-start(bf16[32,1024]{1,0:T(8,128)(2,1)S(1)} %get-tuple-element.15.refs_0_), channel_id=1, source_target_pairs={{0,6},{1,7},{2,4},{3,5},{4,2},{5,3},{6,0},{7,1},{8,14},{9,15},{10,... | collective-permute-start | bytes 196616 | tf_op jit(solution)/shard_map/ppermute | solution.py:163
  8.1 4.6 %collective-permute-start = (bf16[32,1024]{1,0:T(8,128)(2,1)S(1)}, bf16[32,1024]{1,0:T(8,128)(2,1)S(1)}, u32[]{:S(2)}, u32[]{:S(2)}) collective-permute-start(bf16[32,1024]{1,0:T(8,128)(2,1)S(1)} %get-tuple-element.15.refs_0_), channel_id=1, source_target_pairs={{0,2},{1,3},{2,0},{3,1},{4,6},{5,7},{6,4},{7,5},{8,10},{9,11},{10,... | collective-permute-start | bytes 196616 | tf_op jit(solution)/shard_map/ppermute | solution.py:163
  8.1 6.5 %collective-permute-start.13 = (bf16[32,1024]{1,0:T(8,128)(2,1)S(1)}, bf16[32,1024]{1,0:T(8,128)(2,1)S(1)}, u32[]{:S(2)}, u32[]{:S(2)}) collective-permute-start(bf16[32,1024]{1,0:T(8,128)(2,1)S(1)} %get-tuple-element.15.refs_0_), channel_id=1, source_target_pairs={{0,1},{1,0},{2,3},{3,2},{4,5},{5,4},{6,7},{7,6},{8,9},{9,8},{10,11... | collective-permute-start | bytes 196616 | tf_op jit(solution)/shard_map/ppermute | solution.py:163
  9.7 5.9 %collective-permute-start.1 = (bf16[32,1024]{1,0:T(8,128)(2,1)S(1)}, bf16[32,1024]{1,0:T(8,128)(2,1)S(1)}, u32[]{:S(2)}, u32[]{:S(2)}) collective-permute-start(bf16[32,1024]{1,0:T(8,128)(2,1)S(1)} %get-tuple-element.15.refs_0_), channel_id=1, source_target_pairs={{0,4},{1,5},{2,6},{3,7},{4,0},{5,1},{6,2},{7,3},{8,12},{9,13},{10,... | collective-permute-start | bytes 196616 | tf_op jit(solution)/shard_map/ppermute | solution.py:163
  10.5 5.6 %collective-permute-start.4 = (bf16[32,1024]{1,0:T(8,128)(2,1)S(1)}, bf16[32,1024]{1,0:T(8,128)(2,1)S(1)}, u32[]{:S(2)}, u32[]{:S(2)}) collective-permute-start(bf16[32,1024]{1,0:T(8,128)(2,1)S(1)} %get-tuple-element.15.refs_0_), channel_id=1, source_target_pairs={{0,8},{8,0},{16,24},{24,16},{1,9},{9,1},{17,25},{25,17},{2,10},{10... | collective-permute-start | bytes 196616 | tf_op jit(solution)/shard_map/ppermute | solution.py:163
  11.1 4.9 %collective-permute-start.9 = (bf16[32,1024]{1,0:T(8,128)(2,1)S(1)}, bf16[32,1024]{1,0:T(8,128)(2,1)S(1)}, u32[]{:S(2)}, u32[]{:S(2)}) collective-permute-start(bf16[32,1024]{1,0:T(8,128)(2,1)S(1)} %collective-permute-done.2.refs_3_), channel_id=1, source_target_pairs={{0,1},{1,0},{2,3},{3,2},{4,5},{5,4},{6,7},{7,6},{8,9},{9,8},{10,11... | collective-permute-start | bytes 196616 | tf_op jit(solution)/shard_map/ppermute | solution.py:163
  12.8 4.3 %collective-permute-start.3 = (bf16[32,1024]{1,0:T(8,128)(2,1)S(1)}, bf16[32,1024]{1,0:T(8,128)(2,1)S(1)}, u32[]{:S(2)}, u32[]{:S(2)}) collective-permute-start(bf16[32,1024]{1,0:T(8,128)(2,1)S(1)} %collective-permute-done.refs_1_), channel_id=1, source_target_pairs={{0,1},{1,0},{2,3},{3,2},{4,5},{5,4},{6,7},{7,6},{8,9},{9,8},{10,11... | collective-permute-start | bytes 196616 | tf_op jit(solution)/shard_map/ppermute | solution.py:163
  14.7 8.7 %collective-permute-start.7 = (bf16[32,1024]{1,0:T(8,128)(2,1)S(1)}, bf16[32,1024]{1,0:T(8,128)(2,1)S(1)}, u32[]{:S(2)}, u32[]{:S(2)}) collective-permute-start(bf16[32,1024]{1,0:T(8,128)(2,1)S(1)} %collective-permute-done.2.refs_3_), channel_id=1, source_target_pairs={{0,8},{8,0},{16,24},{24,16},{1,9},{9,1},{17,25},{25,17},{2,10},{10... | collective-permute-start | bytes 196616 | tf_op jit(solution)/shard_map/ppermute | solution.py:163
  15.5 8.1 %collective-permute-start.11 = (bf16[32,1024]{1,0:T(8,128)(2,1)S(1)}, bf16[32,1024]{1,0:T(8,128)(2,1)S(1)}, u32[]{:S(2)}, u32[]{:S(2)}) collective-permute-start(bf16[32,1024]{1,0:T(8,128)(2,1)S(1)} %collective-permute-done.1.refs_2_), channel_id=1, source_target_pairs={{0,1},{1,0},{2,3},{3,2},{4,5},{5,4},{6,7},{7,6},{8,9},{9,8},{10,11... | collective-permute-start | bytes 196616 | tf_op jit(solution)/shard_map/ppermute | solution.py:163
  16.0 7.9 %collective-permute-start.6 = (bf16[32,1024]{1,0:T(8,128)(2,1)S(1)}, bf16[32,1024]{1,0:T(8,128)(2,1)S(1)}, u32[]{:S(2)}, u32[]{:S(2)}) collective-permute-start(bf16[32,1024]{1,0:T(8,128)(2,1)S(1)} %collective-permute-done.1.refs_2_), channel_id=1, source_target_pairs={{0,8},{8,0},{16,24},{24,16},{1,9},{9,1},{17,25},{25,17},{2,10},{10... | collective-permute-start | bytes 196616 | tf_op jit(solution)/shard_map/ppermute | solution.py:163
  16.1 8.1 %collective-permute-start.5 = (bf16[32,1024]{1,0:T(8,128)(2,1)S(1)}, bf16[32,1024]{1,0:T(8,128)(2,1)S(1)}, u32[]{:S(2)}, u32[]{:S(2)}) collective-permute-start(bf16[32,1024]{1,0:T(8,128)(2,1)S(1)} %collective-permute-done.refs_1_), channel_id=1, source_target_pairs={{0,8},{8,0},{16,24},{24,16},{1,9},{9,1},{17,25},{25,17},{2,10},{10... | collective-permute-start | bytes 196616 | tf_op jit(solution)/shard_map/ppermute | solution.py:163
  17.0 7.1 %collective-permute-start.8 = (bf16[32,1024]{1,0:T(8,128)(2,1)S(1)}, bf16[32,1024]{1,0:T(8,128)(2,1)S(1)}, u32[]{:S(2)}, u32[]{:S(2)}) collective-permute-start(bf16[32,1024]{1,0:T(8,128)(2,1)S(1)} %collective-permute-done.3.refs_4_), channel_id=1, source_target_pairs={{0,8},{8,0},{16,24},{24,16},{1,9},{9,1},{17,25},{25,17},{2,10},{10... | collective-permute-start | bytes 196616 | tf_op jit(solution)/shard_map/ppermute | solution.py:163
  17.0 7.1 %copy-start = (bf16[128,2,512]{2,1,0:T(2,128)(2,1)S(1)}, bf16[128,2,512]{2,1,0:T(2,128)(2,1)}, u32[]{:S(2)}) copy-start(bf16[128,2,512]{2,1,0:T(2,128)(2,1)} %new_ref.1) | copy-start | bytes 786436
  17.8 13.2 %all-to-all-start = ((bf16[8,8,1024]{2,1,0:T(8,128)(2,1)}), bf16[8,8,1024]{2,1,0:T(8,128)(2,1)S(1)}, u32[]{:S(2)}, u32[]{:S(2)}) async-start(bf16[8,8,1024]{2,1,0:T(8,128)(2,1)} %route.1), calls=%async_computation | async-start | bytes 262144 | tf_op jit(solution)/shard_map/all_to_all | solution.py:210
  23.3 2.1 %collective-permute-start.14 = (bf16[32,1024]{1,0:T(8,128)(2,1)S(1)}, bf16[32,1024]{1,0:T(8,128)(2,1)S(1)}, u32[]{:S(2)}, u32[]{:S(2)}) collective-permute-start(bf16[32,1024]{1,0:T(8,128)(2,1)S(1)} %collective-permute-done.13.refs_5_), channel_id=1, source_target_pairs={{0,8},{8,0},{16,24},{24,16},{1,9},{9,1},{17,25},{25,17},{2,10},{10... | collective-permute-start | bytes 196616 | tf_op jit(solution)/shard_map/ppermute | solution.py:163
  23.6 1.8 %collective-permute-start.10 = (bf16[32,1024]{1,0:T(8,128)(2,1)S(1)}, bf16[32,1024]{1,0:T(8,128)(2,1)S(1)}, u32[]{:S(2)}, u32[]{:S(2)}) collective-permute-start(bf16[32,1024]{1,0:T(8,128)(2,1)S(1)} %collective-permute-done.9.refs_3_), channel_id=1, source_target_pairs={{0,8},{8,0},{16,24},{24,16},{1,9},{9,1},{17,25},{25,17},{2,10},{10... | collective-permute-start | bytes 196616 | tf_op jit(solution)/shard_map/ppermute | solution.py:163
  23.9 1.5 %collective-permute-start.12 = (bf16[32,1024]{1,0:T(8,128)(2,1)S(1)}, bf16[32,1024]{1,0:T(8,128)(2,1)S(1)}, u32[]{:S(2)}, u32[]{:S(2)}) collective-permute-start(bf16[32,1024]{1,0:T(8,128)(2,1)S(1)} %collective-permute-done.11.refs_4_), channel_id=1, source_target_pairs={{0,8},{8,0},{16,24},{24,16},{1,9},{9,1},{17,25},{25,17},{2,10},{10... | collective-permute-start | bytes 196616 | tf_op jit(solution)/shard_map/ppermute | solution.py:163

commit v13 on v11

--- a/solution.py
+++ b/solution.py
@@ -61,8 +61,8 @@
                     out_ref[slot] = cache_ref[local].reshape(cache_ref.shape[1], width)
 
 
-def route_kernel(far_ref, *refs):
-    *in_refs, out_hbm, out_ref, sem = refs
+def route_kernel(dom_count, far_ref, *refs):
+    in_refs, (out_hbm, out_ref, sem) = refs[:dom_count], refs[-3:]
     width = out_ref.shape[2]
     for run in range(far_ref.shape[0]):
         far = far_ref[run]
@@ -199,14 +199,14 @@
 
     incoming = outgoing[:1] + [swap(outgoing[k], "dom", k) for k in range(1, dom_count)]
     routed = pl.pallas_call(
-        route_kernel,
+        functools.partial(route_kernel, dom_count),
         out_shape=pltpu.HBM((group, page_rows, 2 * width), jnp.bfloat16),
-        in_specs=[VMEM] * (1 + dom_count),
+        in_specs=[VMEM] * (1 + dom_count) + [pl.BlockSpec(memory_space=pl.ANY)] * (Z - 1),
         out_specs=HBM,
         scratch_shapes=[pltpu.VMEM((group, page_rows, 2 * width), jnp.bfloat16), pltpu.SemaphoreType.DMA],
         compiler_params=params(12),
         name="route",
-    )(far, *incoming)
+    )(far, *incoming, *pieces[1:Z])
     pages = lax.all_to_all(routed, "ctx", split_axis=0, concat_axis=0, tiled=True)
     pages = pages.reshape(ctx_count * page_rows, 2 * width)
 

time: 35.1 us -> 34.9 us (level)
  starting transfers between devices: 20.8 us -> 19.3 us
  waiting for transfers between devices: 5.93 us -> 7.3 us
    ppermute x18, starting transfers between devices: 16.3 us -> 14.6 us  [swap(): lax.ppermute(x, axis, [(i, i ^ distance) for i in range(lax.axis_size(axi...]
    ppermute x18, waiting for transfers between devices: 5.92 us -> 7.3 us  [swap(): lax.ppermute(x, axis, [(i, i ^ distance) for i in range(lax.axis_size(axi...]
  transfers between devices with their start and end apart: 19 -> 19, of which waited for: 2 -> 6; matrix products, arithmetic and copies ran while one was open for 0% -> 0% of each run, Pallas kernels for 6% -> 6%
where the time goes in v13:
time: 34.9 us; the launch traced here: 34.7 us
  starting transfers between devices  19.3 us (55%)
  Pallas kernels  7.98 us (23%)
  waiting for transfers between devices  7.3 us (21%)
    ppermute x18, starting transfers between devices, swap(): lax.ppermute(x, axis, [(i, i ^ distance) for i in range(lax.axis_size(axi...  14.6 us
    ppermute x18, waiting for transfers between devices, swap(): lax.ppermute(x, axis, [(i, i ^ distance) for i in range(lax.axis_size(axi...  7.3 us
    pallas_call x1, Pallas kernels, on_device(): pl.pallas_call(attend_kernel, out_shape=shape((tokens, q_width), jnp.bflo...  4.93 us
    all_to_all x1, starting transfers between devices, on_device(): lax.all_to_all(routed, 'ctx', split_axis=0, concat_axis=0, tiled=True)  4.72 us
    pallas_call x1, Pallas kernels, on_device(): pl.pallas_call(gather_kernel, out_shape=(shape((key_count, 2 * width), jn...  1.22 us
    pallas_call x1, Pallas kernels, on_device(): pl.pallas_call(functools.partial(pack_kernel, dom_count), out_shape=(shap...  1.1 us
    pallas_call x1, Pallas kernels, on_device(): pl.pallas_call(functools.partial(route_kernel, dom_count), out_shape=pltp...  0.72 us
  transfers between devices with their start and end apart: 19, of which 6 were waited for; matrix products, arithmetic and copies ran while one was open for 0% of the time, Pallas kernels for 6%

profile of v13, /device:TPU:0, one launch (start us, length us, event | category | flops | bytes accessed | tf_op | source)
XLA Modules:
  0.0 34.7 jit_solution(2250061033671925320)
XLA Ops:
  0.0 1.1 %pack.1 = (bf16[32,1024]{1,0:T(8,128)(2,1)S(1)}, bf16[4,8,1024]{2,1,0:T(8,128)(2,1)S(1)}, bf16[4,8,1024]{2,1,0:T(8,128)(2,1)S(1)}, bf16[4,8,1024]{2,1,0:T(8,128)...) custom-call(s32[32]{0:T(128)} %anc_hbm.1, s32[32]{0:T(128)} %len_hbm.1, ...), custom_call_target="tpu_custom_call" | custom-call | tf_op jit(solution)/shard_map/pack/pallas_call | solution.py:174
  1.1 0.6 %collective-permute-start.15 = (bf16[4,8,1024]{2,1,0:T(8,128)(2,1)S(1)}, bf16[4,8,1024]{2,1,0:T(8,128)(2,1)S(1)}, u32[]{:S(2)}, u32[]{:S(2)}) collective-permute-start(bf16[4,8,1024]{2,1,0:T(8,128)(2,1)S(1)} %get-tuple-element.20), channel_id=1, source_target_pairs={{0,8},{8,0},{16,24},{24,16},{1,9},{9,1},{17,25},{25,17},{2,10},{10... | collective-permute-start | bytes 196616 | tf_op jit(solution)/shard_map/ppermute | solution.py:163
  1.7 2.6 %collective-permute-start.16 = (bf16[4,8,1024]{2,1,0:T(8,128)(2,1)S(1)}, bf16[4,8,1024]{2,1,0:T(8,128)(2,1)S(1)}, u32[]{:S(2)}, u32[]{:S(2)}) collective-permute-start(bf16[4,8,1024]{2,1,0:T(8,128)(2,1)S(1)} %get-tuple-element.21), channel_id=1, source_target_pairs={{0,16},{8,24},{16,0},{24,8},{1,17},{9,25},{17,1},{25,9},{2,18},{10... | collective-permute-start | bytes 196616 | tf_op jit(solution)/shard_map/ppermute | solution.py:163
  4.3 0.1 collective-permute-start.17
  4.3 3.8 %collective-permute-start.2 = (bf16[32,1024]{1,0:T(8,128)(2,1)S(1)}, bf16[32,1024]{1,0:T(8,128)(2,1)S(1)}, u32[]{:S(2)}, u32[]{:S(2)}) collective-permute-start(bf16[32,1024]{1,0:T(8,128)(2,1)S(1)} %get-tuple-element.15.refs_0_), channel_id=1, source_target_pairs={{0,6},{1,7},{2,4},{3,5},{4,2},{5,3},{6,0},{7,1},{8,14},{9,15},{10,... | collective-permute-start | bytes 196616 | tf_op jit(solution)/shard_map/ppermute | solution.py:163
  8.1 0.0 collective-permute-start.1
  8.1 0.0 collective-permute-done.15.refs_1_
  8.1 0.6 %collective-permute-start = (bf16[32,1024]{1,0:T(8,128)(2,1)S(1)}, bf16[32,1024]{1,0:T(8,128)(2,1)S(1)}, u32[]{:S(2)}, u32[]{:S(2)}) collective-permute-start(bf16[32,1024]{1,0:T(8,128)(2,1)S(1)} %get-tuple-element.15.refs_0_), channel_id=1, source_target_pairs={{0,2},{1,3},{2,0},{3,1},{4,6},{5,7},{6,4},{7,5},{8,10},{9,11},{10,... | collective-permute-start | bytes 196616 | tf_op jit(solution)/shard_map/ppermute | solution.py:163
  8.7 0.0 collective-permute-done.16.refs_2_
  8.7 1.7 %collective-permute-start.3 = (bf16[32,1024]{1,0:T(8,128)(2,1)S(1)}, bf16[32,1024]{1,0:T(8,128)(2,1)S(1)}, u32[]{:S(2)}, u32[]{:S(2)}) collective-permute-start(bf16[32,1024]{1,0:T(8,128)(2,1)S(1)} %get-tuple-element.15.refs_0_), channel_id=1, source_target_pairs={{0,1},{1,0},{2,3},{3,2},{4,5},{5,4},{6,7},{7,6},{8,9},{9,8},{10,11... | collective-permute-start | bytes 196616 | tf_op jit(solution)/shard_map/ppermute | solution.py:163
  10.4 0.0 collective-permute-done.17.refs_3_
  10.4 0.5 %collective-permute-done.2.refs_3_.refs_6_ = bf16[32,1024]{1,0:T(8,128)(2,1)S(1)} collective-permute-done((bf16[32,1024]{1,0:T(8,128)(2,1)S(1)}, bf16[32,1024]{1,0:T(8,128)(2,1)S(1)}, u32[]{:S(2)}, u32[]{:S(2)}) %collective-permute-start.2) | collective-permute-done | bytes 65568 | tf_op jit(solution)/shard_map/ppermute | solution.py:163
  10.9 3.2 %collective-permute-done.1.refs_2_.refs_5_ = bf16[32,1024]{1,0:T(8,128)(2,1)S(1)} collective-permute-done((bf16[32,1024]{1,0:T(8,128)(2,1)S(1)}, bf16[32,1024]{1,0:T(8,128)(2,1)S(1)}, u32[]{:S(2)}, u32[]{:S(2)}) %collective-permute-start.1) | collective-permute-done | bytes 65568 | tf_op jit(solution)/shard_map/ppermute | solution.py:163
  14.1 0.0 collective-permute-done.refs_1_.refs_4_
  14.1 0.0 copy-start
  14.1 0.7 %route.1 = bf16[8,8,1024]{2,1,0:T(8,128)(2,1)} custom-call(bf16[2,8,128]{2,1,0:T(8,128)(2,1)S(1)} %get-tuple-element.18.far_ref, bf16[4,8,1024]{2,1,0:T(8,128)(2,1)S(1)} %get-tuple-element.19.refs_0_, bf16[4,8,1024]{2,1,0:T(8,128)(2,1)S(1)} %collective-permute-done.15.refs_1_, bf16[4,8,1024]{2,1,0:T(8,128)(2,1)S(1)} %collective-permute-done.16.refs_2_, ...), custom_call_target="tpu_custom_call" | custom-call | tf_op jit(solution)/shard_map/route/pallas_call | solution.py:201
  14.8 4.7 %all-to-all-start = ((bf16[8,8,1024]{2,1,0:T(8,128)(2,1)}), bf16[8,8,1024]{2,1,0:T(8,128)(2,1)S(1)}, u32[]{:S(2)}, u32[]{:S(2)}) async-start(bf16[8,8,1024]{2,1,0:T(8,128)(2,1)} %route.1), calls=%async_computation | async-start | bytes 262144 | tf_op jit(solution)/shard_map/all_to_all | solution.py:210
  19.5 0.0 collective-permute-start.5
  19.5 0.0 collective-permute-done.3.refs_4_
  19.5 0.5 %collective-permute-start.9 = (bf16[32,1024]{1,0:T(8,128)(2,1)S(1)}, bf16[32,1024]{1,0:T(8,128)(2,1)S(1)}, u32[]{:S(2)}, u32[]{:S(2)}) collective-permute-start(bf16[32,1024]{1,0:T(8,128)(2,1)S(1)} %collective-permute-done.3.refs_4_), channel_id=1, source_target_pairs={{0,8},{8,0},{16,24},{24,16},{1,9},{9,1},{17,25},{25,17},{2,10},{10... | collective-permute-start | bytes 196616 | tf_op jit(solution)/shard_map/ppermute | solution.py:163
  20.0 2.0 %collective-permute-start.11 = (bf16[32,1024]{1,0:T(8,128)(2,1)S(1)}, bf16[32,1024]{1,0:T(8,128)(2,1)S(1)}, u32[]{:S(2)}, u32[]{:S(2)}) collective-permute-start(bf16[32,1024]{1,0:T(8,128)(2,1)S(1)} %collective-permute-done.2.refs_3_.refs_6_), channel_id=1, source_target_pairs={{0,1},{1,0},{2,3},{3,2},{4,5},{5,4},{6,7},{7,6},{8,9},{9,8},{10,11... | collective-permute-start | bytes 196616 | tf_op jit(solution)/shard_map/ppermute | solution.py:163
  22.1 0.0 collective-permute-start.4
  22.1 0.0 collective-permute-start.8
  22.1 0.0 collective-permute-done.5.refs_6_
  22.1 2.0 %collective-permute-start.13 = (bf16[32,1024]{1,0:T(8,128)(2,1)S(1)}, bf16[32,1024]{1,0:T(8,128)(2,1)S(1)}, u32[]{:S(2)}, u32[]{:S(2)}) collective-permute-start(bf16[32,1024]{1,0:T(8,128)(2,1)S(1)} %collective-permute-done.1.refs_2_.refs_5_), channel_id=1, source_target_pairs={{0,1},{1,0},{2,3},{3,2},{4,5},{5,4},{6,7},{7,6},{8,9},{9,8},{10,11... | collective-permute-start | bytes 196616 | tf_op jit(solution)/shard_map/ppermute | solution.py:163
  24.1 0.0 collective-permute-done.9.refs_10_
  24.1 0.2 collective-permute-start.7
  24.3 1.1 %collective-permute-done.11.refs_2_ = bf16[32,1024]{1,0:T(8,128)(2,1)S(1)} collective-permute-done((bf16[32,1024]{1,0:T(8,128)(2,1)S(1)}, bf16[32,1024]{1,0:T(8,128)(2,1)S(1)}, u32[]{:S(2)}, u32[]{:S(2)}) %collective-permute-start.11) | collective-permute-done | bytes 65568 | tf_op jit(solution)/shard_map/ppermute | solution.py:163
  25.4 0.0 collective-permute-start.6
  25.4 1.8 %collective-permute-done.4.refs_5_ = bf16[32,1024]{1,0:T(8,128)(2,1)S(1)} collective-permute-done((bf16[32,1024]{1,0:T(8,128)(2,1)S(1)}, bf16[32,1024]{1,0:T(8,128)(2,1)S(1)}, u32[]{:S(2)}, u32[]{:S(2)}) %collective-permute-start.4) | collective-permute-done | bytes 65568 | tf_op jit(solution)/shard_map/ppermute | solution.py:163
  27.2 0.0 collective-permute-start.10
  27.2 0.0 collective-permute-done.8.refs_9_
  27.2 0.5 %collective-permute-start.12 = (bf16[32,1024]{1,0:T(8,128)(2,1)S(1)}, bf16[32,1024]{1,0:T(8,128)(2,1)S(1)}, u32[]{:S(2)}, u32[]{:S(2)}) collective-permute-start(bf16[32,1024]{1,0:T(8,128)(2,1)S(1)} %collective-permute-done.11.refs_2_), channel_id=1, source_target_pairs={{0,8},{8,0},{16,24},{24,16},{1,9},{9,1},{17,25},{25,17},{2,10},{10... | collective-permute-start | bytes 196616 | tf_op jit(solution)/shard_map/ppermute | solution.py:163
  27.7 0.5 %collective-permute-done.13.refs_3_ = bf16[32,1024]{1,0:T(8,128)(2,1)S(1)} collective-permute-done((bf16[32,1024]{1,0:T(8,128)(2,1)S(1)}, bf16[32,1024]{1,0:T(8,128)(2,1)S(1)}, u32[]{:S(2)}, u32[]{:S(2)}) %collective-permute-start.13) | collective-permute-done | bytes 65568 | tf_op jit(solution)/shard_map/ppermute | solution.py:163
  28.2 0.0 collective-permute-start.14
  28.2 0.0 collective-permute-done.7.refs_8_
  28.2 0.0 collective-permute-done.6.refs_7_
  28.3 0.2 collective-permute-done.10.refs_11_
  28.5 0.0 copy-done
  28.5 1.2 %gather.1 = (bf16[512,1024]{1,0:T(8,128)(2,1)S(1)}, bf16[128,4096]{1,0:T(8,128)(2,1)S(1)}) custom-call(bf16[128,4096]{1,0:T(8,128)(2,1)} %q_hbm.1, bf16[128,2,512]{2,1,0:T(2,128)(2,1)S(1)} %copy-done, bf16[32,1024]{1,0:T(8,128)(2,1)S(1)} %get-tuple-element.15.refs_0_, bf16[32,1024]{1,0:T(8,128)(2,1)S(1)} %collective-permute-done.refs_1_.refs_4_, ...), custom_call_target="tpu_custom_call" | custom-call | flops 1000000000 | bytes 4194304 | tf_op jit(solution)/shard_map/gather/pallas_call | solution.py:215
  29.7 0.0 collective-permute-done.12.refs_0_
  29.7 0.0 collective-permute-done.14.refs_1_
  29.7 0.0 all-to-all-done
  29.7 4.9 %attend.1 = bf16[128,4096]{1,0:T(8,128)(2,1)} custom-call(s32[8,64]{1,0:T(8,128)S(1)} %get-tuple-element.14.limit_ref, bf16[128,4096]{1,0:T(8,128)(2,1)S(1)} %get-tuple-element.16.q_ref, bf16[512,1024]{1,0:T(8,128)(2,1)S(1)} %get-tuple-element.17.kv_ref, bf16[32,1024]{1,0:T(8,128)(2,1)S(1)} %collective-permute-done.12.refs_0_, ...), custom_call_target="tpu_custom_call" | custom-call | tf_op jit(solution)/shard_map/attend/pallas_call | solution.py:225
Async XLA Ops:
  1.1 7.0 %collective-permute-start.15 = (bf16[4,8,1024]{2,1,0:T(8,128)(2,1)S(1)}, bf16[4,8,1024]{2,1,0:T(8,128)(2,1)S(1)}, u32[]{:S(2)}, u32[]{:S(2)}) collective-permute-start(bf16[4,8,1024]{2,1,0:T(8,128)(2,1)S(1)} %get-tuple-element.20), channel_id=1, source_target_pairs={{0,8},{8,0},{16,24},{24,16},{1,9},{9,1},{17,25},{25,17},{2,10},{10... | collective-permute-start | bytes 196616 | tf_op jit(solution)/shard_map/ppermute | solution.py:163
  1.7 7.0 %collective-permute-start.16 = (bf16[4,8,1024]{2,1,0:T(8,128)(2,1)S(1)}, bf16[4,8,1024]{2,1,0:T(8,128)(2,1)S(1)}, u32[]{:S(2)}, u32[]{:S(2)}) collective-permute-start(bf16[4,8,1024]{2,1,0:T(8,128)(2,1)S(1)} %get-tuple-element.21), channel_id=1, source_target_pairs={{0,16},{8,24},{16,0},{24,8},{1,17},{9,25},{17,1},{25,9},{2,18},{10... | collective-permute-start | bytes 196616 | tf_op jit(solution)/shard_map/ppermute | solution.py:163
  4.3 6.2 %collective-permute-start.17 = (bf16[4,8,1024]{2,1,0:T(8,128)(2,1)S(1)}, bf16[4,8,1024]{2,1,0:T(8,128)(2,1)S(1)}, u32[]{:S(2)}, u32[]{:S(2)}) collective-permute-start(bf16[4,8,1024]{2,1,0:T(8,128)(2,1)S(1)} %get-tuple-element.22), channel_id=1, source_target_pairs={{0,24},{8,16},{16,8},{24,0},{1,25},{9,17},{17,9},{25,1},{2,26},{10... | collective-permute-start | bytes 196616 | tf_op jit(solution)/shard_map/ppermute | solution.py:163
  4.3 6.6 %collective-permute-start.2 = (bf16[32,1024]{1,0:T(8,128)(2,1)S(1)}, bf16[32,1024]{1,0:T(8,128)(2,1)S(1)}, u32[]{:S(2)}, u32[]{:S(2)}) collective-permute-start(bf16[32,1024]{1,0:T(8,128)(2,1)S(1)} %get-tuple-element.15.refs_0_), channel_id=1, source_target_pairs={{0,6},{1,7},{2,4},{3,5},{4,2},{5,3},{6,0},{7,1},{8,14},{9,15},{10,... | collective-permute-start | bytes 196616 | tf_op jit(solution)/shard_map/ppermute | solution.py:163
  8.1 6.0 %collective-permute-start.1 = (bf16[32,1024]{1,0:T(8,128)(2,1)S(1)}, bf16[32,1024]{1,0:T(8,128)(2,1)S(1)}, u32[]{:S(2)}, u32[]{:S(2)}) collective-permute-start(bf16[32,1024]{1,0:T(8,128)(2,1)S(1)} %get-tuple-element.15.refs_0_), channel_id=1, source_target_pairs={{0,4},{1,5},{2,6},{3,7},{4,0},{5,1},{6,2},{7,3},{8,12},{9,13},{10,... | collective-permute-start | bytes 196616 | tf_op jit(solution)/shard_map/ppermute | solution.py:163
  8.1 6.0 %collective-permute-start = (bf16[32,1024]{1,0:T(8,128)(2,1)S(1)}, bf16[32,1024]{1,0:T(8,128)(2,1)S(1)}, u32[]{:S(2)}, u32[]{:S(2)}) collective-permute-start(bf16[32,1024]{1,0:T(8,128)(2,1)S(1)} %get-tuple-element.15.refs_0_), channel_id=1, source_target_pairs={{0,2},{1,3},{2,0},{3,1},{4,6},{5,7},{6,4},{7,5},{8,10},{9,11},{10,... | collective-permute-start | bytes 196616 | tf_op jit(solution)/shard_map/ppermute | solution.py:163
  8.7 10.8 %collective-permute-start.3 = (bf16[32,1024]{1,0:T(8,128)(2,1)S(1)}, bf16[32,1024]{1,0:T(8,128)(2,1)S(1)}, u32[]{:S(2)}, u32[]{:S(2)}) collective-permute-start(bf16[32,1024]{1,0:T(8,128)(2,1)S(1)} %get-tuple-element.15.refs_0_), channel_id=1, source_target_pairs={{0,1},{1,0},{2,3},{3,2},{4,5},{5,4},{6,7},{7,6},{8,9},{9,8},{10,11... | collective-permute-start | bytes 196616 | tf_op jit(solution)/shard_map/ppermute | solution.py:163
  14.1 14.4 %copy-start = (bf16[128,2,512]{2,1,0:T(2,128)(2,1)S(1)}, bf16[128,2,512]{2,1,0:T(2,128)(2,1)}, u32[]{:S(2)}) copy-start(bf16[128,2,512]{2,1,0:T(2,128)(2,1)} %new_ref.1) | copy-start | bytes 786436
  14.8 14.9 %all-to-all-start = ((bf16[8,8,1024]{2,1,0:T(8,128)(2,1)}), bf16[8,8,1024]{2,1,0:T(8,128)(2,1)S(1)}, u32[]{:S(2)}, u32[]{:S(2)}) async-start(bf16[8,8,1024]{2,1,0:T(8,128)(2,1)} %route.1), calls=%async_computation | async-start | bytes 262144 | tf_op jit(solution)/shard_map/all_to_all | solution.py:210
  19.5 2.6 %collective-permute-start.5 = (bf16[32,1024]{1,0:T(8,128)(2,1)S(1)}, bf16[32,1024]{1,0:T(8,128)(2,1)S(1)}, u32[]{:S(2)}, u32[]{:S(2)}) collective-permute-start(bf16[32,1024]{1,0:T(8,128)(2,1)S(1)} %get-tuple-element.15.refs_0_), channel_id=1, source_target_pairs={{0,8},{8,0},{16,24},{24,16},{1,9},{9,1},{17,25},{25,17},{2,10},{10... | collective-permute-start | bytes 196616 | tf_op jit(solution)/shard_map/ppermute | solution.py:163
  19.5 4.6 %collective-permute-start.9 = (bf16[32,1024]{1,0:T(8,128)(2,1)S(1)}, bf16[32,1024]{1,0:T(8,128)(2,1)S(1)}, u32[]{:S(2)}, u32[]{:S(2)}) collective-permute-start(bf16[32,1024]{1,0:T(8,128)(2,1)S(1)} %collective-permute-done.3.refs_4_), channel_id=1, source_target_pairs={{0,8},{8,0},{16,24},{24,16},{1,9},{9,1},{17,25},{25,17},{2,10},{10... | collective-permute-start | bytes 196616 | tf_op jit(solution)/shard_map/ppermute | solution.py:163
  20.0 5.4 %collective-permute-start.11 = (bf16[32,1024]{1,0:T(8,128)(2,1)S(1)}, bf16[32,1024]{1,0:T(8,128)(2,1)S(1)}, u32[]{:S(2)}, u32[]{:S(2)}) collective-permute-start(bf16[32,1024]{1,0:T(8,128)(2,1)S(1)} %collective-permute-done.2.refs_3_.refs_6_), channel_id=1, source_target_pairs={{0,1},{1,0},{2,3},{3,2},{4,5},{5,4},{6,7},{7,6},{8,9},{9,8},{10,11... | collective-permute-start | bytes 196616 | tf_op jit(solution)/shard_map/ppermute | solution.py:163
  22.1 5.2 %collective-permute-start.4 = (bf16[32,1024]{1,0:T(8,128)(2,1)S(1)}, bf16[32,1024]{1,0:T(8,128)(2,1)S(1)}, u32[]{:S(2)}, u32[]{:S(2)}) collective-permute-start(bf16[32,1024]{1,0:T(8,128)(2,1)S(1)} %collective-permute-done.refs_1_.refs_4_), channel_id=1, source_target_pairs={{0,1},{1,0},{2,3},{3,2},{4,5},{5,4},{6,7},{7,6},{8,9},{9,8},{10,11... | collective-permute-start | bytes 196616 | tf_op jit(solution)/shard_map/ppermute | solution.py:163
  22.1 5.1 %collective-permute-start.8 = (bf16[32,1024]{1,0:T(8,128)(2,1)S(1)}, bf16[32,1024]{1,0:T(8,128)(2,1)S(1)}, u32[]{:S(2)}, u32[]{:S(2)}) collective-permute-start(bf16[32,1024]{1,0:T(8,128)(2,1)S(1)} %collective-permute-done.2.refs_3_.refs_6_), channel_id=1, source_target_pairs={{0,8},{8,0},{16,24},{24,16},{1,9},{9,1},{17,25},{25,17},{2,10},{10... | collective-permute-start | bytes 196616 | tf_op jit(solution)/shard_map/ppermute | solution.py:163
  22.1 6.1 %collective-permute-start.13 = (bf16[32,1024]{1,0:T(8,128)(2,1)S(1)}, bf16[32,1024]{1,0:T(8,128)(2,1)S(1)}, u32[]{:S(2)}, u32[]{:S(2)}) collective-permute-start(bf16[32,1024]{1,0:T(8,128)(2,1)S(1)} %collective-permute-done.1.refs_2_.refs_5_), channel_id=1, source_target_pairs={{0,1},{1,0},{2,3},{3,2},{4,5},{5,4},{6,7},{7,6},{8,9},{9,8},{10,11... | collective-permute-start | bytes 196616 | tf_op jit(solution)/shard_map/ppermute | solution.py:163
  24.1 4.2 %collective-permute-start.7 = (bf16[32,1024]{1,0:T(8,128)(2,1)S(1)}, bf16[32,1024]{1,0:T(8,128)(2,1)S(1)}, u32[]{:S(2)}, u32[]{:S(2)}) collective-permute-start(bf16[32,1024]{1,0:T(8,128)(2,1)S(1)} %collective-permute-done.1.refs_2_.refs_5_), channel_id=1, source_target_pairs={{0,8},{8,0},{16,24},{24,16},{1,9},{9,1},{17,25},{25,17},{2,10},{10... | collective-permute-start | bytes 196616 | tf_op jit(solution)/shard_map/ppermute | solution.py:163
  25.4 2.8 %collective-permute-start.6 = (bf16[32,1024]{1,0:T(8,128)(2,1)S(1)}, bf16[32,1024]{1,0:T(8,128)(2,1)S(1)}, u32[]{:S(2)}, u32[]{:S(2)}) collective-permute-start(bf16[32,1024]{1,0:T(8,128)(2,1)S(1)} %collective-permute-done.refs_1_.refs_4_), channel_id=1, source_target_pairs={{0,8},{8,0},{16,24},{24,16},{1,9},{9,1},{17,25},{25,17},{2,10},{10... | collective-permute-start | bytes 196616 | tf_op jit(solution)/shard_map/ppermute | solution.py:163
  27.2 1.3 %collective-permute-start.10 = (bf16[32,1024]{1,0:T(8,128)(2,1)S(1)}, bf16[32,1024]{1,0:T(8,128)(2,1)S(1)}, u32[]{:S(2)}, u32[]{:S(2)}) collective-permute-start(bf16[32,1024]{1,0:T(8,128)(2,1)S(1)} %collective-permute-done.4.refs_5_), channel_id=1, source_target_pairs={{0,8},{8,0},{16,24},{24,16},{1,9},{9,1},{17,25},{25,17},{2,10},{10... | collective-permute-start | bytes 196616 | tf_op jit(solution)/shard_map/ppermute | solution.py:163
  27.2 2.5 %collective-permute-start.12 = (bf16[32,1024]{1,0:T(8,128)(2,1)S(1)}, bf16[32,1024]{1,0:T(8,128)(2,1)S(1)}, u32[]{:S(2)}, u32[]{:S(2)}) collective-permute-start(bf16[32,1024]{1,0:T(8,128)(2,1)S(1)} %collective-permute-done.11.refs_2_), channel_id=1, source_target_pairs={{0,8},{8,0},{16,24},{24,16},{1,9},{9,1},{17,25},{25,17},{2,10},{10... | collective-permute-start | bytes 196616 | tf_op jit(solution)/shard_map/ppermute | solution.py:163
  28.2 1.5 %collective-permute-start.14 = (bf16[32,1024]{1,0:T(8,128)(2,1)S(1)}, bf16[32,1024]{1,0:T(8,128)(2,1)S(1)}, u32[]{:S(2)}, u32[]{:S(2)}) collective-permute-start(bf16[32,1024]{1,0:T(8,128)(2,1)S(1)} %collective-permute-done.13.refs_3_), channel_id=1, source_target_pairs={{0,8},{8,0},{16,24},{24,16},{1,9},{9,1},{17,25},{25,17},{2,10},{10... | collective-permute-start | bytes 196616 | tf_op jit(solution)/shard_map/ppermute | solution.py:163

commit v14 on v13

--- a/solution.py
+++ b/solution.py
@@ -62,7 +62,7 @@
 
 
 def route_kernel(dom_count, far_ref, *refs):
-    in_refs, (out_hbm, out_ref, sem) = refs[:dom_count], refs[-3:]
+    in_refs, pieces, (out_hbm, rows_ref, out_ref, sem) = refs[:dom_count], refs[dom_count:-4], refs[-4:]
     width = out_ref.shape[2]
     for run in range(far_ref.shape[0]):
         far = far_ref[run]
@@ -74,6 +74,8 @@
             out_ref[run * RUN + slot] = picked
     out = pltpu.make_async_copy(out_ref, out_hbm, sem)
     out.start()
+    for number, piece in enumerate(pieces):
+        rows_ref[number * piece.shape[0] : (number + 1) * piece.shape[0], :] = piece[...]
     out.wait()
 
 
@@ -194,23 +196,26 @@
     outgoing, (far, limit) = rest[:dom_count], rest[dom_count:]
 
     pieces = [half] + [swap(half, "ctx", k * y_count) for k in range(1, Z)]
-    pieces += [swap(p, "ctx", k) for k in range(1, y_count) for p in pieces[:Z]]
-    pieces += [swap(p, "dom", 1) for p in pieces]
 
     incoming = outgoing[:1] + [swap(outgoing[k], "dom", k) for k in range(1, dom_count)]
-    routed = pl.pallas_call(
+    routed, rows = pl.pallas_call(
         functools.partial(route_kernel, dom_count),
-        out_shape=pltpu.HBM((group, page_rows, 2 * width), jnp.bfloat16),
-        in_specs=[VMEM] * (1 + dom_count) + [pl.BlockSpec(memory_space=pl.ANY)] * (Z - 1),
-        out_specs=HBM,
+        out_shape=(
+            pltpu.HBM((group, page_rows, 2 * width), jnp.bfloat16),
+            shape((Z * half_rows, 2 * width), jnp.bfloat16),
+        ),
+        in_specs=[VMEM] * (1 + dom_count + Z),
+        out_specs=(HBM, VMEM),
         scratch_shapes=[pltpu.VMEM((group, page_rows, 2 * width), jnp.bfloat16), pltpu.SemaphoreType.DMA],
         compiler_params=params(12),
         name="route",
-    )(far, *incoming, *pieces[1:Z])
+    )(far, *incoming, *pieces)
+    over_y = [swap(rows, "ctx", k) for k in range(1, y_count)]
+    pieces = [rows, swap(rows, "dom", 1), *over_y]
+    late = [swap(piece, "dom", 1) for piece in over_y]
     pages = lax.all_to_all(routed, "ctx", split_axis=0, concat_axis=0, tiled=True)
     pages = pages.reshape(ctx_count * page_rows, 2 * width)
 
-    late = [pieces.pop(at) for at in sorted((*range(Z + 2, 2 * Z), *range(len(pieces) - Z + 2, len(pieces))), reverse=True)]
     key_count = SPAN + sum(piece.shape[0] for piece in pieces)
     kv, queries = pl.pallas_call(
         gather_kernel,
@@ -219,7 +224,7 @@
         out_specs=(VMEM, VMEM),
         scratch_shapes=[pltpu.SemaphoreType.DMA((Q_COPIES,))],
         compiler_params=params(16),
-        cost_estimate=pl.CostEstimate(flops=10**9, bytes_accessed=2**22, transcendentals=0),
+        cost_estimate=pl.CostEstimate(flops=10**10, bytes_accessed=2**22, transcendentals=0),
         name="gather",
     )(pltpu.with_memory_space_constraint(q_new, pltpu.HBM), kv_new, *pieces)
     return pl.pallas_call(

time: 34.9 us -> 33 us (0.946)
  starting transfers between devices: 19.3 us -> 12.9 us
  waiting for transfers between devices: 7.3 us -> 11.8 us
    ppermute x18 -> x9, starting transfers between devices: 14.6 us -> 9.15 us  [swap(): lax.ppermute(x, axis, [(i, i ^ distance) for i in range(lax.axis_size(axi...]
    all_to_all x1, waiting for transfers between devices: 0.01 us -> 3.76 us  [on_device(): lax.all_to_all(routed, 'ctx', split_axis=0, concat_axis=0, tiled=True)]
    all_to_all x1, starting transfers between devices: 4.72 us -> 3.75 us  [on_device(): lax.all_to_all(routed, 'ctx', split_axis=0, concat_axis=0, tiled=True)]
    ppermute x18 -> x9, waiting for transfers between devices: 7.3 us -> 8.05 us  [swap(): lax.ppermute(x, axis, [(i, i ^ distance) for i in range(lax.axis_size(axi...]
  transfers between devices with their start and end apart: 19 -> 10, of which waited for: 6 -> 4; matrix products, arithmetic and copies ran while one was open for 0% -> 0% of each run, Pallas kernels for 6% -> 4%
where the time goes in v14:
time: 33 us; the launch traced here: 32.8 us
  starting transfers between devices  12.9 us (39%)
  waiting for transfers between devices  11.8 us (36%)
  Pallas kernels  8.04 us (24%)
    ppermute x9, starting transfers between devices, swap(): lax.ppermute(x, axis, [(i, i ^ distance) for i in range(lax.axis_size(axi...  9.15 us
    ppermute x9, waiting for transfers between devices, swap(): lax.ppermute(x, axis, [(i, i ^ distance) for i in range(lax.axis_size(axi...  8.05 us
    pallas_call x1, Pallas kernels, on_device(): pl.pallas_call(attend_kernel, out_shape=shape((tokens, q_width), jnp.bflo...  4.93 us
    all_to_all x1, waiting for transfers between devices, on_device(): lax.all_to_all(routed, 'ctx', split_axis=0, concat_axis=0, tiled=True)  3.76 us
    all_to_all x1, starting transfers between devices, on_device(): lax.all_to_all(routed, 'ctx', split_axis=0, concat_axis=0, tiled=True)  3.75 us
    pallas_call x1, Pallas kernels, on_device(): pl.pallas_call(gather_kernel, out_shape=(shape((key_count, 2 * width), jn...  1.23 us
    pallas_call x1, Pallas kernels, on_device(): pl.pallas_call(functools.partial(pack_kernel, dom_count), out_shape=(shap...  1.14 us
    pallas_call x1, Pallas kernels, on_device(): pl.pallas_call(functools.partial(route_kernel, dom_count), out_shape=(plt...  0.74 us
  transfers between devices with their start and end apart: 10, of which 4 were waited for; matrix products, arithmetic and copies ran while one was open for 0% of the time, Pallas kernels for 4%

profile of v14, /device:TPU:0, one launch (start us, length us, event | category | flops | bytes accessed | tf_op | source)
XLA Modules:
  0.0 32.8 jit_solution(3438054918974721108)
XLA Ops:
  0.0 1.1 %pack.1 = (bf16[32,1024]{1,0:T(8,128)(2,1)S(1)}, bf16[4,8,1024]{2,1,0:T(8,128)(2,1)S(1)}, bf16[4,8,1024]{2,1,0:T(8,128)(2,1)S(1)}, bf16[4,8,1024]{2,1,0:T(8,128)...) custom-call(s32[32]{0:T(128)} %anc_hbm.1, s32[32]{0:T(128)} %len_hbm.1, ...), custom_call_target="tpu_custom_call" | custom-call | tf_op jit(solution)/shard_map/pack/pallas_call | solution.py:176
  1.2 0.5 %collective-permute-start = (bf16[4,8,1024]{2,1,0:T(8,128)(2,1)S(1)}, bf16[4,8,1024]{2,1,0:T(8,128)(2,1)S(1)}, u32[]{:S(2)}, u32[]{:S(2)}) collective-permute-start(bf16[4,8,1024]{2,1,0:T(8,128)(2,1)S(1)} %get-tuple-element.19), channel_id=1, source_target_pairs={{0,8},{8,0},{16,24},{24,16},{1,9},{9,1},{17,25},{25,17},{2,10},{10... | collective-permute-start | bytes 196616 | tf_op jit(solution)/shard_map/ppermute | solution.py:165
  1.6 2.6 %collective-permute-start.1 = (bf16[4,8,1024]{2,1,0:T(8,128)(2,1)S(1)}, bf16[4,8,1024]{2,1,0:T(8,128)(2,1)S(1)}, u32[]{:S(2)}, u32[]{:S(2)}) collective-permute-start(bf16[4,8,1024]{2,1,0:T(8,128)(2,1)S(1)} %get-tuple-element.20), channel_id=1, source_target_pairs={{0,16},{8,24},{16,0},{24,8},{1,17},{9,25},{17,1},{25,9},{2,18},{10... | collective-permute-start | bytes 196616 | tf_op jit(solution)/shard_map/ppermute | solution.py:165
  4.2 0.1 collective-permute-start.2
  4.3 3.9 %collective-permute-start.5 = (bf16[32,1024]{1,0:T(8,128)(2,1)S(1)}, bf16[32,1024]{1,0:T(8,128)(2,1)S(1)}, u32[]{:S(2)}, u32[]{:S(2)}) collective-permute-start(bf16[32,1024]{1,0:T(8,128)(2,1)S(1)} %get-tuple-element.22.refs_4_), channel_id=1, source_target_pairs={{0,6},{1,7},{2,4},{3,5},{4,2},{5,3},{6,0},{7,1},{8,14},{9,15},{10,... | collective-permute-start | bytes 196616 | tf_op jit(solution)/shard_map/ppermute | solution.py:165
  8.1 0.0 collective-permute-start.4
  8.1 0.0 collective-permute-done.refs_1_
  8.1 0.6 %collective-permute-start.3 = (bf16[32,1024]{1,0:T(8,128)(2,1)S(1)}, bf16[32,1024]{1,0:T(8,128)(2,1)S(1)}, u32[]{:S(2)}, u32[]{:S(2)}) collective-permute-start(bf16[32,1024]{1,0:T(8,128)(2,1)S(1)} %get-tuple-element.22.refs_4_), channel_id=1, source_target_pairs={{0,2},{1,3},{2,0},{3,1},{4,6},{5,7},{6,4},{7,5},{8,10},{9,11},{10,... | collective-permute-start | bytes 196616 | tf_op jit(solution)/shard_map/ppermute | solution.py:165
  8.7 0.0 collective-permute-done.1.refs_2_
  8.7 0.0 collective-permute-done.2.refs_3_
  8.7 2.2 %collective-permute-done.5.refs_7_ = bf16[32,1024]{1,0:T(8,128)(2,1)S(1)} collective-permute-done((bf16[32,1024]{1,0:T(8,128)(2,1)S(1)}, bf16[32,1024]{1,0:T(8,128)(2,1)S(1)}, u32[]{:S(2)}, u32[]{:S(2)}) %collective-permute-start.5) | collective-permute-done | bytes 65568 | tf_op jit(solution)/shard_map/ppermute | solution.py:165
  10.9 3.2 %collective-permute-done.4.refs_6_ = bf16[32,1024]{1,0:T(8,128)(2,1)S(1)} collective-permute-done((bf16[32,1024]{1,0:T(8,128)(2,1)S(1)}, bf16[32,1024]{1,0:T(8,128)(2,1)S(1)}, u32[]{:S(2)}, u32[]{:S(2)}) %collective-permute-start.4) | collective-permute-done | bytes 65568 | tf_op jit(solution)/shard_map/ppermute | solution.py:165
  14.1 0.0 collective-permute-done.3.refs_5_
  14.1 0.7 %route.1 = (bf16[8,8,1024]{2,1,0:T(8,128)(2,1)}, bf16[128,1024]{1,0:T(8,128)(2,1)S(1)}) custom-call(bf16[2,8,128]{2,1,0:T(8,128)(2,1)S(1)} %get-tuple-element.17.far_ref, bf16[4,8,1024]{2,1,0:T(8,128)(2,1)S(1)} %get-tuple-element.18.refs_0_, bf16[4,8,1024]{2,1,0:T(8,128)(2,1)S(1)} %collective-permute-done.refs_1_, ...), custom_call_target="tpu_custom_call" | custom-call | tf_op jit(solution)/shard_map/route/pallas_call | solution.py:201
  14.9 0.0 copy-start
  14.9 1.6 %collective-permute-start.7 = (bf16[128,1024]{1,0:T(8,128)(2,1)S(1)}, bf16[128,1024]{1,0:T(8,128)(2,1)S(1)}, u32[]{:S(2)}, u32[]{:S(2)}) collective-permute-start(bf16[128,1024]{1,0:T(8,128)(2,1)S(1)} %get-tuple-element.23.refs_0_), channel_id=1, source_target_pairs={{0,1},{1,0},{2,3},{3,2},{4,5},{5,4},{6,7},{7,6},{8,9},{9,8},{10,11... | collective-permute-start | bytes 786440 | tf_op jit(solution)/shard_map/ppermute | solution.py:165
  16.5 0.0 collective-permute-start.6
  16.5 3.8 %all-to-all-start = ((bf16[8,8,1024]{2,1,0:T(8,128)(2,1)}), bf16[8,8,1024]{2,1,0:T(8,128)(2,1)S(1)}, u32[]{:S(2)}, u32[]{:S(2)}) async-start(bf16[8,8,1024]{2,1,0:T(8,128)(2,1)} %get-tuple-element.26), calls=%async_computation | async-start | bytes 262144 | tf_op jit(solution)/shard_map/all_to_all | solution.py:216
  20.2 2.6 %collective-permute-done.7.refs_2_ = bf16[128,1024]{1,0:T(8,128)(2,1)S(1)} collective-permute-done((bf16[128,1024]{1,0:T(8,128)(2,1)S(1)}, bf16[128,1024]{1,0:T(8,128)(2,1)S(1)}, u32[]{:S(2)}, u32[]{:S(2)}) %collective-permute-start.7) | collective-permute-done | bytes 262176 | tf_op jit(solution)/shard_map/ppermute | solution.py:165
  22.9 0.0 collective-permute-start.8
  22.9 0.0 collective-permute-done.6.refs_1_
  22.9 0.0 copy-done
  22.9 1.2 %gather.1 = (bf16[512,1024]{1,0:T(8,128)(2,1)S(1)}, bf16[128,4096]{1,0:T(8,128)(2,1)S(1)}) custom-call(bf16[128,4096]{1,0:T(8,128)(2,1)} %q_hbm.1, bf16[128,2,512]{2,1,0:T(2,128)(2,1)S(1)} %copy-done, bf16[128,1024]{1,0:T(8,128)(2,1)S(1)} %get-tuple-element.23.refs_0_, bf16[128,1024]{1,0:T(8,128)(2,1)S(1)} %collective-permute-done.6.refs_1_, ...), custom_call_target="tpu_custom_call" | custom-call | flops 10000000000 | bytes 4194304 | tf_op jit(solution)/shard_map/gather/pallas_call | solution.py:220
  24.1 3.8 %all-to-all-done = bf16[8,8,1024]{2,1,0:T(8,128)(2,1)S(1)} async-done(((bf16[8,8,1024]{2,1,0:T(8,128)(2,1)}), bf16[8,8,1024]{2,1,0:T(8,128)(2,1)S(1)}, u32[]{:S(2)}, u32[]{:S(2)}) %all-to-all-start) | async-done | bytes 131104 | tf_op jit(solution)/shard_map/all_to_all | solution.py:216
  27.9 0.0 collective-permute-done.8.refs_0_
  27.9 4.9 %attend.1 = bf16[128,4096]{1,0:T(8,128)(2,1)} custom-call(s32[8,64]{1,0:T(8,128)S(1)} %get-tuple-element.16.limit_ref, bf16[128,4096]{1,0:T(8,128)(2,1)S(1)} %get-tuple-element.24.q_ref, bf16[512,1024]{1,0:T(8,128)(2,1)S(1)} %get-tuple-element.25.kv_ref, bf16[128,1024]{1,0:T(8,128)(2,1)S(1)} %collective-permute-done.8.refs_0_, bf16[64,1024]{1,0:T(8,128)(2,1)S(1)} %bitcast.1), custom_call_target="tpu_custom_call" | custom-call | tf_op jit(solution)/shard_map/attend/pallas_call | solution.py:230
Async XLA Ops:
  1.2 7.0 %collective-permute-start = (bf16[4,8,1024]{2,1,0:T(8,128)(2,1)S(1)}, bf16[4,8,1024]{2,1,0:T(8,128)(2,1)S(1)}, u32[]{:S(2)}, u32[]{:S(2)}) collective-permute-start(bf16[4,8,1024]{2,1,0:T(8,128)(2,1)S(1)} %get-tuple-element.19), channel_id=1, source_target_pairs={{0,8},{8,0},{16,24},{24,16},{1,9},{9,1},{17,25},{25,17},{2,10},{10... | collective-permute-start | bytes 196616 | tf_op jit(solution)/shard_map/ppermute | solution.py:165
  1.6 7.1 %collective-permute-start.1 = (bf16[4,8,1024]{2,1,0:T(8,128)(2,1)S(1)}, bf16[4,8,1024]{2,1,0:T(8,128)(2,1)S(1)}, u32[]{:S(2)}, u32[]{:S(2)}) collective-permute-start(bf16[4,8,1024]{2,1,0:T(8,128)(2,1)S(1)} %get-tuple-element.20), channel_id=1, source_target_pairs={{0,16},{8,24},{16,0},{24,8},{1,17},{9,25},{17,1},{25,9},{2,18},{10... | collective-permute-start | bytes 196616 | tf_op jit(solution)/shard_map/ppermute | solution.py:165
  4.2 4.5 %collective-permute-start.2 = (bf16[4,8,1024]{2,1,0:T(8,128)(2,1)S(1)}, bf16[4,8,1024]{2,1,0:T(8,128)(2,1)S(1)}, u32[]{:S(2)}, u32[]{:S(2)}) collective-permute-start(bf16[4,8,1024]{2,1,0:T(8,128)(2,1)S(1)} %get-tuple-element.21), channel_id=1, source_target_pairs={{0,24},{8,16},{16,8},{24,0},{1,25},{9,17},{17,9},{25,1},{2,26},{10... | collective-permute-start | bytes 196616 | tf_op jit(solution)/shard_map/ppermute | solution.py:165
  4.3 6.7 %collective-permute-start.5 = (bf16[32,1024]{1,0:T(8,128)(2,1)S(1)}, bf16[32,1024]{1,0:T(8,128)(2,1)S(1)}, u32[]{:S(2)}, u32[]{:S(2)}) collective-permute-start(bf16[32,1024]{1,0:T(8,128)(2,1)S(1)} %get-tuple-element.22.refs_4_), channel_id=1, source_target_pairs={{0,6},{1,7},{2,4},{3,5},{4,2},{5,3},{6,0},{7,1},{8,14},{9,15},{10,... | collective-permute-start | bytes 196616 | tf_op jit(solution)/shard_map/ppermute | solution.py:165
  8.1 6.0 %collective-permute-start.4 = (bf16[32,1024]{1,0:T(8,128)(2,1)S(1)}, bf16[32,1024]{1,0:T(8,128)(2,1)S(1)}, u32[]{:S(2)}, u32[]{:S(2)}) collective-permute-start(bf16[32,1024]{1,0:T(8,128)(2,1)S(1)} %get-tuple-element.22.refs_4_), channel_id=1, source_target_pairs={{0,4},{1,5},{2,6},{3,7},{4,0},{5,1},{6,2},{7,3},{8,12},{9,13},{10,... | collective-permute-start | bytes 196616 | tf_op jit(solution)/shard_map/ppermute | solution.py:165
  8.1 6.0 %collective-permute-start.3 = (bf16[32,1024]{1,0:T(8,128)(2,1)S(1)}, bf16[32,1024]{1,0:T(8,128)(2,1)S(1)}, u32[]{:S(2)}, u32[]{:S(2)}) collective-permute-start(bf16[32,1024]{1,0:T(8,128)(2,1)S(1)} %get-tuple-element.22.refs_4_), channel_id=1, source_target_pairs={{0,2},{1,3},{2,0},{3,1},{4,6},{5,7},{6,4},{7,5},{8,10},{9,11},{10,... | collective-permute-start | bytes 196616 | tf_op jit(solution)/shard_map/ppermute | solution.py:165
  14.9 8.0 %copy-start = (bf16[128,2,512]{2,1,0:T(2,128)(2,1)S(1)}, bf16[128,2,512]{2,1,0:T(2,128)(2,1)}, u32[]{:S(2)}) copy-start(bf16[128,2,512]{2,1,0:T(2,128)(2,1)} %new_ref.1) | copy-start | bytes 786436
  14.9 8.0 %collective-permute-start.7 = (bf16[128,1024]{1,0:T(8,128)(2,1)S(1)}, bf16[128,1024]{1,0:T(8,128)(2,1)S(1)}, u32[]{:S(2)}, u32[]{:S(2)}) collective-permute-start(bf16[128,1024]{1,0:T(8,128)(2,1)S(1)} %get-tuple-element.23.refs_0_), channel_id=1, source_target_pairs={{0,1},{1,0},{2,3},{3,2},{4,5},{5,4},{6,7},{7,6},{8,9},{9,8},{10,11... | collective-permute-start | bytes 786440 | tf_op jit(solution)/shard_map/ppermute | solution.py:165
  16.5 6.4 %collective-permute-start.6 = (bf16[128,1024]{1,0:T(8,128)(2,1)S(1)}, bf16[128,1024]{1,0:T(8,128)(2,1)S(1)}, u32[]{:S(2)}, u32[]{:S(2)}) collective-permute-start(bf16[128,1024]{1,0:T(8,128)(2,1)S(1)} %get-tuple-element.23.refs_0_), channel_id=1, source_target_pairs={{0,8},{8,0},{16,24},{24,16},{1,9},{9,1},{17,25},{25,17},{2,10},{10... | collective-permute-start | bytes 786440 | tf_op jit(solution)/shard_map/ppermute | solution.py:165
  16.5 11.4 %all-to-all-start = ((bf16[8,8,1024]{2,1,0:T(8,128)(2,1)}), bf16[8,8,1024]{2,1,0:T(8,128)(2,1)S(1)}, u32[]{:S(2)}, u32[]{:S(2)}) async-start(bf16[8,8,1024]{2,1,0:T(8,128)(2,1)} %get-tuple-element.26), calls=%async_computation | async-start | bytes 262144 | tf_op jit(solution)/shard_map/all_to_all | solution.py:216
  22.9 5.0 %collective-permute-start.8 = (bf16[128,1024]{1,0:T(8,128)(2,1)S(1)}, bf16[128,1024]{1,0:T(8,128)(2,1)S(1)}, u32[]{:S(2)}, u32[]{:S(2)}) collective-permute-start(bf16[128,1024]{1,0:T(8,128)(2,1)S(1)} %collective-permute-done.7.refs_2_), channel_id=1, source_target_pairs={{0,8},{8,0},{16,24},{24,16},{1,9},{9,1},{17,25},{25,17},{2,10},{10... | collective-permute-start | bytes 786440 | tf_op jit(solution)/shard_map/ppermute | solution.py:165

commit v15 on v14

--- a/solution.py
+++ b/solution.py
@@ -61,22 +61,33 @@
                     out_ref[slot] = cache_ref[local].reshape(cache_ref.shape[1], width)
 
 
-def route_kernel(dom_count, far_ref, *refs):
-    in_refs, pieces, (out_hbm, rows_ref, out_ref, sem) = refs[:dom_count], refs[dom_count:-4], refs[-4:]
-    width = out_ref.shape[2]
-    for run in range(far_ref.shape[0]):
-        far = far_ref[run]
-        for slot in range(RUN):
-            picked = in_refs[0][slot]
-            for k in range(1, len(in_refs)):
-                here = jnp.concatenate([far == k] * (width // far.shape[1]), axis=1)
-                picked = jnp.where(here, in_refs[k][slot], picked)
-            out_ref[run * RUN + slot] = picked
-    out = pltpu.make_async_copy(out_ref, out_hbm, sem)
-    out.start()
+def route_kernel(y_count, far_ref, *refs):
+    in_refs, out_refs = refs[:-Z], refs[-Z:]
+    own_z = lax.axis_index("ctx") // y_count
+    width = out_refs[0].shape[2]
+    for k, out_ref in enumerate(out_refs):
+        for y in range(y_count):
+            to = (own_z ^ k) * y_count + y
+            far = far_ref[to // RUN]
+            picked = in_refs[0][to % RUN]
+            for at in range(1, len(in_refs)):
+                here = jnp.concatenate([far == at] * (width // far.shape[1]), axis=1)
+                picked = jnp.where(here, in_refs[at][to % RUN], picked)
+            out_ref[y] = picked
+
+
+def turn_kernel(*refs):
+    in_refs, out_refs = refs[:Z], refs[Z:]
+    own_y = lax.axis_index("ctx") % len(out_refs)
+    for j, out_ref in enumerate(out_refs):
+        for k, in_ref in enumerate(in_refs):
+            out_ref[k] = in_ref[own_y ^ j]
+
+
+def stack_kernel(*refs):
+    *pieces, rows_ref = refs
     for number, piece in enumerate(pieces):
         rows_ref[number * piece.shape[0] : (number + 1) * piece.shape[0], :] = piece[...]
-    out.wait()
 
 
 def head_rows(q_ref, g, gq):
@@ -110,23 +121,29 @@
         copy.wait()
 
 
-def attend_kernel(limit_ref, q_ref, kv_ref, *refs):
-    late, (cache_ref, out_ref, stage, sems) = refs[:-4], refs[-4:]
+def attend_kernel(y_count, limit_ref, q_ref, kv_ref, *refs):
+    late, pages, (out_ref, stage, sems) = refs[: -3 - y_count], refs[-3 - y_count : -3], refs[-3:]
     width = kv_ref.shape[1] // 2
-    gen = cache_ref.shape[0]
+    page_rows = pages[0].shape[0] // Z
+    gen = page_rows * Z * y_count
     kvh = width // HD
     gq = q_ref.shape[1] // width
     old = kv_ref.shape[0] - SPAN + sum(piece.shape[0] for piece in late)
     token = lax.broadcasted_iota(jnp.int32, (SPAN, SPAN), 0)
     causal = lax.broadcasted_iota(jnp.int32, (SPAN, SPAN), 1) <= token
-    visible = lax.broadcasted_iota(jnp.int32, (SPAN, gen), 1) < jnp.broadcast_to(limit_ref[:1], (SPAN, gen))
+    at = lax.broadcasted_iota(jnp.int32, (SPAN, gen), 1)
+    ctx = lax.axis_index("ctx")
+    page_z = (at // page_rows % Z) ^ (ctx // y_count)
+    page_y = (at // (page_rows * Z)) ^ (ctx % y_count)
+    at = (page_z * y_count + page_y) * page_rows + at % page_rows
+    visible = at < jnp.broadcast_to(limit_ref[:1], (SPAN, gen))
     ones = jnp.ones((SPAN + old + gen, HD), jnp.bfloat16)
     keys, values = [], []
     for g in range(kvh):
         k_at = slice(g * HD, (g + 1) * HD)
         v_at = slice(width + g * HD, width + (g + 1) * HD)
-        keys.append(jnp.concatenate([ref[:, k_at] for ref in (kv_ref, *late, cache_ref)], axis=0))
-        value = jnp.concatenate([ref[:, v_at] for ref in (kv_ref, *late, cache_ref)], axis=0)
+        keys.append(jnp.concatenate([ref[:, k_at] for ref in (kv_ref, *late, *pages)], axis=0))
+        value = jnp.concatenate([ref[:, v_at] for ref in (kv_ref, *late, *pages)], axis=0)
         values.append(jnp.concatenate([value, ones], axis=1))
     chunk = CHUNK * HD
     per_group = gq // CHUNK
@@ -150,7 +167,7 @@
             top = jnp.max(s, axis=1, keepdims=True)
             weights.append(jnp.exp2((s - top) * SCALE2).astype(jnp.bfloat16))
         out = dot_nn(jnp.concatenate(weights, axis=0), values[c // per_group])
-        out = (out[:, :HD] / out[:, HD:]).astype(jnp.bfloat16)
+        out = (out[:, :HD] * pl.reciprocal(out[:, HD:], approx=True)).astype(jnp.bfloat16)
         for j in range(CHUNK):
             stage[:, (c * CHUNK + j) * HD : (c * CHUNK + j + 1) * HD] = out[j * SPAN : (j + 1) * SPAN]
         columns = pl.ds(c * chunk, chunk)
@@ -198,24 +215,36 @@
     pieces = [half] + [swap(half, "ctx", k * y_count) for k in range(1, Z)]
 
     incoming = outgoing[:1] + [swap(outgoing[k], "dom", k) for k in range(1, dom_count)]
-    routed, rows = pl.pallas_call(
-        functools.partial(route_kernel, dom_count),
-        out_shape=(
-            pltpu.HBM((group, page_rows, 2 * width), jnp.bfloat16),
-            shape((Z * half_rows, 2 * width), jnp.bfloat16),
-        ),
-        in_specs=[VMEM] * (1 + dom_count + Z),
-        out_specs=(HBM, VMEM),
-        scratch_shapes=[pltpu.VMEM((group, page_rows, 2 * width), jnp.bfloat16), pltpu.SemaphoreType.DMA],
+    routed = pl.pallas_call(
+        functools.partial(route_kernel, y_count),
+        out_shape=(shape((y_count, page_rows, 2 * width), jnp.bfloat16),) * Z,
+        in_specs=[VMEM] * (1 + dom_count),
+        out_specs=(VMEM,) * Z,
         compiler_params=params(12),
         name="route",
-    )(far, *incoming, *pieces)
+    )(far, *incoming)
+    routed = routed[:1] + tuple(swap(routed[k], "ctx", k * y_count) for k in range(1, Z))
+    pages = pl.pallas_call(
+        turn_kernel,
+        out_shape=(shape((Z, page_rows, 2 * width), jnp.bfloat16),) * y_count,
+        in_specs=[VMEM] * Z,
+        out_specs=(VMEM,) * y_count,
+        compiler_params=params(12),
+        name="turn",
+    )(*routed)
+    pages = pages[:1] + tuple(swap(pages[j], "ctx", j) for j in range(1, y_count))
+    pages = [page.reshape(Z * page_rows, 2 * width) for page in pages]
+    rows = pl.pallas_call(
+        stack_kernel,
+        out_shape=shape((Z * half_rows, 2 * width), jnp.bfloat16),
+        in_specs=[VMEM] * Z,
+        out_specs=VMEM,
+        compiler_params=params(12),
+        name="stack",
+    )(*pieces)
     over_y = [swap(rows, "ctx", k) for k in range(1, y_count)]
     pieces = [rows, swap(rows, "dom", 1), *over_y]
     late = [swap(piece, "dom", 1) for piece in over_y]
-    pages = lax.all_to_all(routed, "ctx", split_axis=0, concat_axis=0, tiled=True)
-    pages = pages.reshape(ctx_count * page_rows, 2 * width)
-
     key_count = SPAN + sum(piece.shape[0] for piece in pieces)
     kv, queries = pl.pallas_call(
         gather_kernel,
@@ -228,14 +257,14 @@
         name="gather",
     )(pltpu.with_memory_space_constraint(q_new, pltpu.HBM), kv_new, *pieces)
     return pl.pallas_call(
-        attend_kernel,
+        functools.partial(attend_kernel, y_count),
         out_shape=shape((tokens, q_width), jnp.bfloat16),
-        in_specs=[VMEM] * (4 + len(late)),
+        in_specs=[VMEM] * (3 + len(late) + len(pages)),
         out_specs=HBM,
         scratch_shapes=[pltpu.VMEM((tokens, q_width), jnp.bfloat16), pltpu.SemaphoreType.DMA((q_width // (CHUNK * HD),))],
         compiler_params=params(40 if prompt_kv.shape[0] * ctx_count > 1024 else 24),
         name="attend",
-    )(limit, queries, kv, *late, pages)
+    )(limit, queries, kv, *late, *pages)
 
 
 def solution(mesh):

time: 33 us -> 38.3 us (1.16)
  waiting for transfers between devices: 11.8 us -> 16.2 us
  starting transfers between devices: 12.9 us -> 14.5 us
  Pallas kernels: 8.04 us -> 7.42 us
    ppermute x9 -> x13, waiting for transfers between devices: 8.05 us -> 16.2 us  [swap(): lax.ppermute(x, axis, [(i, i ^ distance) for i in range(lax.axis_size(axi...]
    ppermute x9 -> x13, starting transfers between devices: 9.15 us -> 14.5 us  [swap(): lax.ppermute(x, axis, [(i, i ^ distance) for i in range(lax.axis_size(axi...]
    all_to_all x1 -> x0, waiting for transfers between devices: 3.76 us -> none  [on_device(): lax.all_to_all(routed, 'ctx', split_axis=0, concat_axis=0, tiled=True)]
    all_to_all x1 -> x0, starting transfers between devices: 3.75 us -> none  [on_device(): lax.all_to_all(routed, 'ctx', split_axis=0, concat_axis=0, tiled=True)]
    pallas_call x2 -> x4, Pallas kernels: 5.67 us -> 5.05 us  [the longest x1 4.95 us: on_device(): pl.pallas_call(functools.partial(attend_kernel, y_count), out_shape=shape...]
  transfers between devices with their start and end apart: 10 -> 13, of which waited for: 4 -> 7; matrix products, arithmetic and copies ran while one was open for 0% -> 0% of each run, Pallas kernels for 4% -> 3%
where the time goes in v15:
time: 38.3 us; the launch traced here: 38.1 us
  waiting for transfers between devices  16.2 us (42%)
  starting transfers between devices  14.5 us (38%)
  Pallas kernels  7.42 us (19%)
    ppermute x13, waiting for transfers between devices, swap(): lax.ppermute(x, axis, [(i, i ^ distance) for i in range(lax.axis_size(axi...  16.2 us
    ppermute x13, starting transfers between devices, swap(): lax.ppermute(x, axis, [(i, i ^ distance) for i in range(lax.axis_size(axi...  14.5 us
    pallas_call x1, Pallas kernels, on_device(): pl.pallas_call(functools.partial(attend_kernel, y_count), out_shape=shape...  4.95 us
    pallas_call x1, Pallas kernels, on_device(): pl.pallas_call(gather_kernel, out_shape=(shape((key_count, 2 * width), jn...  1.23 us
    pallas_call x1, Pallas kernels, on_device(): pl.pallas_call(functools.partial(pack_kernel, dom_count), out_shape=(shap...  1.14 us
  transfers between devices with their start and end apart: 13, of which 7 were waited for; matrix products, arithmetic and copies ran while one was open for 0% of the time, Pallas kernels for 3%

profile of v15, /device:TPU:0, one launch (start us, length us, event | category | flops | bytes accessed | tf_op | source)
XLA Modules:
  0.0 38.1 jit_solution(7575271952775876073)
XLA Ops:
  0.0 1.1 %pack.1 = (bf16[32,1024]{1,0:T(8,128)(2,1)S(1)}, bf16[4,8,1024]{2,1,0:T(8,128)(2,1)S(1)}, bf16[4,8,1024]{2,1,0:T(8,128)(2,1)S(1)}, bf16[4,8,1024]{2,1,0:T(8,128)...) custom-call(s32[32]{0:T(128)} %anc_hbm.1, s32[32]{0:T(128)} %len_hbm.1, ...), custom_call_target="tpu_custom_call" | custom-call | tf_op jit(solution)/shard_map/pack/pallas_call | solution.py:193
  1.2 5.1 %collective-permute-start.2 = (bf16[32,1024]{1,0:T(8,128)(2,1)S(1)}, bf16[32,1024]{1,0:T(8,128)(2,1)S(1)}, u32[]{:S(2)}, u32[]{:S(2)}) collective-permute-start(bf16[32,1024]{1,0:T(8,128)(2,1)S(1)} %get-tuple-element.21.refs_0_), channel_id=1, source_target_pairs={{0,6},{1,7},{2,4},{3,5},{4,2},{5,3},{6,0},{7,1},{8,14},{9,15},{10,... | collective-permute-start | bytes 196616 | tf_op jit(solution)/shard_map/ppermute | solution.py:182
  6.3 0.0 collective-permute-start.1
  6.3 0.6 %collective-permute-start = (bf16[32,1024]{1,0:T(8,128)(2,1)S(1)}, bf16[32,1024]{1,0:T(8,128)(2,1)S(1)}, u32[]{:S(2)}, u32[]{:S(2)}) collective-permute-start(bf16[32,1024]{1,0:T(8,128)(2,1)S(1)} %get-tuple-element.21.refs_0_), channel_id=1, source_target_pairs={{0,2},{1,3},{2,0},{3,1},{4,6},{5,7},{6,4},{7,5},{8,10},{9,11},{10,... | collective-permute-start | bytes 196616 | tf_op jit(solution)/shard_map/ppermute | solution.py:182
  6.9 2.0 %collective-permute-done.2.refs_3_ = bf16[32,1024]{1,0:T(8,128)(2,1)S(1)} collective-permute-done((bf16[32,1024]{1,0:T(8,128)(2,1)S(1)}, bf16[32,1024]{1,0:T(8,128)(2,1)S(1)}, u32[]{:S(2)}, u32[]{:S(2)}) %collective-permute-start.2) | collective-permute-done | bytes 65568 | tf_op jit(solution)/shard_map/ppermute | solution.py:182
  8.9 2.9 %collective-permute-done.1.refs_2_ = bf16[32,1024]{1,0:T(8,128)(2,1)S(1)} collective-permute-done((bf16[32,1024]{1,0:T(8,128)(2,1)S(1)}, bf16[32,1024]{1,0:T(8,128)(2,1)S(1)}, u32[]{:S(2)}, u32[]{:S(2)}) %collective-permute-start.1) | collective-permute-done | bytes 65568 | tf_op jit(solution)/shard_map/ppermute | solution.py:182
  11.8 0.0 collective-permute-done.refs_1_
  11.8 0.0 copy-start
  11.9 1.6 %collective-permute-start.4 = (bf16[128,1024]{1,0:T(8,128)(2,1)S(1)}, bf16[128,1024]{1,0:T(8,128)(2,1)S(1)}, u32[]{:S(2)}, u32[]{:S(2)}) collective-permute-start(bf16[128,1024]{1,0:T(8,128)(2,1)S(1)} %stack.1.refs_0_), channel_id=1, source_target_pairs={{0,1},{1,0},{2,3},{3,2},{4,5},{5,4},{6,7},{7,6},{8,9},{9,8},{10,11... | collective-permute-start | bytes 786440 | tf_op jit(solution)/shard_map/ppermute | solution.py:182
  13.5 0.0 collective-permute-start.3
  13.5 0.5 %collective-permute-start.6 = (bf16[4,8,1024]{2,1,0:T(8,128)(2,1)S(1)}, bf16[4,8,1024]{2,1,0:T(8,128)(2,1)S(1)}, u32[]{:S(2)}, u32[]{:S(2)}) collective-permute-start(bf16[4,8,1024]{2,1,0:T(8,128)(2,1)S(1)} %get-tuple-element.26), channel_id=1, source_target_pairs={{0,8},{8,0},{16,24},{24,16},{1,9},{9,1},{17,25},{25,17},{2,10},{10... | collective-permute-start | bytes 196616 | tf_op jit(solution)/shard_map/ppermute | solution.py:182
  14.0 1.5 %collective-permute-start.7 = (bf16[4,8,1024]{2,1,0:T(8,128)(2,1)S(1)}, bf16[4,8,1024]{2,1,0:T(8,128)(2,1)S(1)}, u32[]{:S(2)}, u32[]{:S(2)}) collective-permute-start(bf16[4,8,1024]{2,1,0:T(8,128)(2,1)S(1)} %get-tuple-element.27), channel_id=1, source_target_pairs={{0,16},{8,24},{16,0},{24,8},{1,17},{9,25},{17,1},{25,9},{2,18},{10... | collective-permute-start | bytes 196616 | tf_op jit(solution)/shard_map/ppermute | solution.py:182
  15.5 0.0 collective-permute-start.8
  15.5 0.0 collective-permute-done.6.refs_1_
  15.5 2.7 %collective-permute-done.7.refs_2_ = bf16[4,8,1024]{2,1,0:T(8,128)(2,1)S(1)} collective-permute-done((bf16[4,8,1024]{2,1,0:T(8,128)(2,1)S(1)}, bf16[4,8,1024]{2,1,0:T(8,128)(2,1)S(1)}, u32[]{:S(2)}, u32[]{:S(2)}) %collective-permute-start.7) | collective-permute-done | bytes 65568 | tf_op jit(solution)/shard_map/ppermute | solution.py:182
  18.3 1.6 %collective-permute-done.8.refs_3_ = bf16[4,8,1024]{2,1,0:T(8,128)(2,1)S(1)} collective-permute-done((bf16[4,8,1024]{2,1,0:T(8,128)(2,1)S(1)}, bf16[4,8,1024]{2,1,0:T(8,128)(2,1)S(1)}, u32[]{:S(2)}, u32[]{:S(2)}) %collective-permute-start.8) | collective-permute-done | bytes 65568 | tf_op jit(solution)/shard_map/ppermute | solution.py:182
  19.8 0.1 route.1
  19.9 1.1 %collective-permute-start.9 = (bf16[2,8,1024]{2,1,0:T(8,128)(2,1)S(1)}, bf16[2,8,1024]{2,1,0:T(8,128)(2,1)S(1)}, u32[]{:S(2)}, u32[]{:S(2)}) collective-permute-start(bf16[2,8,1024]{2,1,0:T(8,128)(2,1)S(1)} %get-tuple-element.30), channel_id=1, source_target_pairs={{0,2},{1,3},{2,0},{3,1},{4,6},{5,7},{6,4},{7,5},{8,10},{9,11},{10,... | collective-permute-start | bytes 98312 | tf_op jit(solution)/shard_map/ppermute | solution.py:182
  21.0 2.1 %collective-permute-start.10 = (bf16[2,8,1024]{2,1,0:T(8,128)(2,1)S(1)}, bf16[2,8,1024]{2,1,0:T(8,128)(2,1)S(1)}, u32[]{:S(2)}, u32[]{:S(2)}) collective-permute-start(bf16[2,8,1024]{2,1,0:T(8,128)(2,1)S(1)} %get-tuple-element.31), channel_id=1, source_target_pairs={{0,4},{1,5},{2,6},{3,7},{4,0},{5,1},{6,2},{7,3},{8,12},{9,13},{10,... | collective-permute-start | bytes 98312 | tf_op jit(solution)/shard_map/ppermute | solution.py:182
  23.1 1.2 %collective-permute-start.11 = (bf16[2,8,1024]{2,1,0:T(8,128)(2,1)S(1)}, bf16[2,8,1024]{2,1,0:T(8,128)(2,1)S(1)}, u32[]{:S(2)}, u32[]{:S(2)}) collective-permute-start(bf16[2,8,1024]{2,1,0:T(8,128)(2,1)S(1)} %get-tuple-element.32), channel_id=1, source_target_pairs={{0,6},{1,7},{2,4},{3,5},{4,2},{5,3},{6,0},{7,1},{8,14},{9,15},{10,... | collective-permute-start | bytes 98312 | tf_op jit(solution)/shard_map/ppermute | solution.py:182
  24.3 0.0 collective-permute-done.9.refs_1_
  24.4 1.5 %collective-permute-done.10.refs_2_ = bf16[2,8,1024]{2,1,0:T(8,128)(2,1)S(1)} collective-permute-done((bf16[2,8,1024]{2,1,0:T(8,128)(2,1)S(1)}, bf16[2,8,1024]{2,1,0:T(8,128)(2,1)S(1)}, u32[]{:S(2)}, u32[]{:S(2)}) %collective-permute-start.10) | collective-permute-done | bytes 32800 | tf_op jit(solution)/shard_map/ppermute | solution.py:182
  25.9 3.0 %collective-permute-done.11.refs_3_ = bf16[2,8,1024]{2,1,0:T(8,128)(2,1)S(1)} collective-permute-done((bf16[2,8,1024]{2,1,0:T(8,128)(2,1)S(1)}, bf16[2,8,1024]{2,1,0:T(8,128)(2,1)S(1)}, u32[]{:S(2)}, u32[]{:S(2)}) %collective-permute-start.11) | collective-permute-done | bytes 32800 | tf_op jit(solution)/shard_map/ppermute | solution.py:182
  28.9 0.6 %collective-permute-start.12 = (bf16[4,8,1024]{2,1,0:T(8,128)(2,1)S(1)}, bf16[4,8,1024]{2,1,0:T(8,128)(2,1)S(1)}, u32[]{:S(2)}, u32[]{:S(2)}) collective-permute-start(bf16[4,8,1024]{2,1,0:T(8,128)(2,1)S(1)} %get-tuple-element.34), channel_id=1, source_target_pairs={{0,1},{1,0},{2,3},{3,2},{4,5},{5,4},{6,7},{7,6},{8,9},{9,8},{10,11... | collective-permute-start | bytes 196616 | tf_op jit(solution)/shard_map/ppermute | solution.py:182
  29.4 0.0 collective-permute-done.4.refs_2_
  29.4 0.0 collective-permute-start.5
  29.4 0.0 collective-permute-done.3.refs_1_
  29.4 0.0 copy-done
  29.4 1.2 %gather.1 = (bf16[512,1024]{1,0:T(8,128)(2,1)S(1)}, bf16[128,4096]{1,0:T(8,128)(2,1)S(1)}) custom-call(bf16[128,4096]{1,0:T(8,128)(2,1)} %q_hbm.1, bf16[128,2,512]{2,1,0:T(2,128)(2,1)S(1)} %copy-done, bf16[128,1024]{1,0:T(8,128)(2,1)S(1)} %stack.1.refs_0_, bf16[128,1024]{1,0:T(8,128)(2,1)S(1)} %collective-permute-done.3.refs_1_, ...), custom_call_target="tpu_custom_call" | custom-call | flops 10000000000 | bytes 4194304 | tf_op jit(solution)/shard_map/gather/pallas_call | solution.py:249
  30.7 2.5 %collective-permute-done.12 = bf16[4,8,1024]{2,1,0:T(8,128)(2,1)S(1)} collective-permute-done((bf16[4,8,1024]{2,1,0:T(8,128)(2,1)S(1)}, bf16[4,8,1024]{2,1,0:T(8,128)(2,1)S(1)}, u32[]{:S(2)}, u32[]{:S(2)}) %collective-permute-start.12) | collective-permute-done | bytes 65568 | tf_op jit(solution)/shard_map/ppermute | solution.py:182
  33.2 0.0 collective-permute-done.5.refs_0_
  33.2 4.9 %attend.1 = bf16[128,4096]{1,0:T(8,128)(2,1)} custom-call(s32[8,64]{1,0:T(8,128)S(1)} %get-tuple-element.20.limit_ref, bf16[128,4096]{1,0:T(8,128)(2,1)S(1)} %get-tuple-element.22.q_ref, bf16[512,1024]{1,0:T(8,128)(2,1)S(1)} %get-tuple-element.23.kv_ref, bf16[128,1024]{1,0:T(8,128)(2,1)S(1)} %collective-permute-done.5.refs_0_, bf16[32,1024]{1,0:T(8,128)(2,1)S(1)} %bitcast.2, ...), custom_call_target="tpu_custom_call" | custom-call | tf_op jit(solution)/shard_map/attend/pallas_call | solution.py:259
  (2 shorter events, 0.0 us)
Async XLA Ops:
  1.2 7.8 %collective-permute-start.2 = (bf16[32,1024]{1,0:T(8,128)(2,1)S(1)}, bf16[32,1024]{1,0:T(8,128)(2,1)S(1)}, u32[]{:S(2)}, u32[]{:S(2)}) collective-permute-start(bf16[32,1024]{1,0:T(8,128)(2,1)S(1)} %get-tuple-element.21.refs_0_), channel_id=1, source_target_pairs={{0,6},{1,7},{2,4},{3,5},{4,2},{5,3},{6,0},{7,1},{8,14},{9,15},{10,... | collective-permute-start | bytes 196616 | tf_op jit(solution)/shard_map/ppermute | solution.py:182
  6.3 5.5 %collective-permute-start.1 = (bf16[32,1024]{1,0:T(8,128)(2,1)S(1)}, bf16[32,1024]{1,0:T(8,128)(2,1)S(1)}, u32[]{:S(2)}, u32[]{:S(2)}) collective-permute-start(bf16[32,1024]{1,0:T(8,128)(2,1)S(1)} %get-tuple-element.21.refs_0_), channel_id=1, source_target_pairs={{0,4},{1,5},{2,6},{3,7},{4,0},{5,1},{6,2},{7,3},{8,12},{9,13},{10,... | collective-permute-start | bytes 196616 | tf_op jit(solution)/shard_map/ppermute | solution.py:182
  6.3 5.5 %collective-permute-start = (bf16[32,1024]{1,0:T(8,128)(2,1)S(1)}, bf16[32,1024]{1,0:T(8,128)(2,1)S(1)}, u32[]{:S(2)}, u32[]{:S(2)}) collective-permute-start(bf16[32,1024]{1,0:T(8,128)(2,1)S(1)} %get-tuple-element.21.refs_0_), channel_id=1, source_target_pairs={{0,2},{1,3},{2,0},{3,1},{4,6},{5,7},{6,4},{7,5},{8,10},{9,11},{10,... | collective-permute-start | bytes 196616 | tf_op jit(solution)/shard_map/ppermute | solution.py:182
  11.8 17.6 %copy-start = (bf16[128,2,512]{2,1,0:T(2,128)(2,1)S(1)}, bf16[128,2,512]{2,1,0:T(2,128)(2,1)}, u32[]{:S(2)}) copy-start(bf16[128,2,512]{2,1,0:T(2,128)(2,1)} %new_ref.1) | copy-start | bytes 786436
  11.9 17.6 %collective-permute-start.4 = (bf16[128,1024]{1,0:T(8,128)(2,1)S(1)}, bf16[128,1024]{1,0:T(8,128)(2,1)S(1)}, u32[]{:S(2)}, u32[]{:S(2)}) collective-permute-start(bf16[128,1024]{1,0:T(8,128)(2,1)S(1)} %stack.1.refs_0_), channel_id=1, source_target_pairs={{0,1},{1,0},{2,3},{3,2},{4,5},{5,4},{6,7},{7,6},{8,9},{9,8},{10,11... | collective-permute-start | bytes 786440 | tf_op jit(solution)/shard_map/ppermute | solution.py:182
  13.5 16.0 %collective-permute-start.3 = (bf16[128,1024]{1,0:T(8,128)(2,1)S(1)}, bf16[128,1024]{1,0:T(8,128)(2,1)S(1)}, u32[]{:S(2)}, u32[]{:S(2)}) collective-permute-start(bf16[128,1024]{1,0:T(8,128)(2,1)S(1)} %stack.1.refs_0_), channel_id=1, source_target_pairs={{0,8},{8,0},{16,24},{24,16},{1,9},{9,1},{17,25},{25,17},{2,10},{10... | collective-permute-start | bytes 786440 | tf_op jit(solution)/shard_map/ppermute | solution.py:182
  13.5 2.1 %collective-permute-start.6 = (bf16[4,8,1024]{2,1,0:T(8,128)(2,1)S(1)}, bf16[4,8,1024]{2,1,0:T(8,128)(2,1)S(1)}, u32[]{:S(2)}, u32[]{:S(2)}) collective-permute-start(bf16[4,8,1024]{2,1,0:T(8,128)(2,1)S(1)} %get-tuple-element.26), channel_id=1, source_target_pairs={{0,8},{8,0},{16,24},{24,16},{1,9},{9,1},{17,25},{25,17},{2,10},{10... | collective-permute-start | bytes 196616 | tf_op jit(solution)/shard_map/ppermute | solution.py:182
  14.0 4.3 %collective-permute-start.7 = (bf16[4,8,1024]{2,1,0:T(8,128)(2,1)S(1)}, bf16[4,8,1024]{2,1,0:T(8,128)(2,1)S(1)}, u32[]{:S(2)}, u32[]{:S(2)}) collective-permute-start(bf16[4,8,1024]{2,1,0:T(8,128)(2,1)S(1)} %get-tuple-element.27), channel_id=1, source_target_pairs={{0,16},{8,24},{16,0},{24,8},{1,17},{9,25},{17,1},{25,9},{2,18},{10... | collective-permute-start | bytes 196616 | tf_op jit(solution)/shard_map/ppermute | solution.py:182
  15.5 4.3 %collective-permute-start.8 = (bf16[4,8,1024]{2,1,0:T(8,128)(2,1)S(1)}, bf16[4,8,1024]{2,1,0:T(8,128)(2,1)S(1)}, u32[]{:S(2)}, u32[]{:S(2)}) collective-permute-start(bf16[4,8,1024]{2,1,0:T(8,128)(2,1)S(1)} %get-tuple-element.28), channel_id=1, source_target_pairs={{0,24},{8,16},{16,8},{24,0},{1,25},{9,17},{17,9},{25,1},{2,26},{10... | collective-permute-start | bytes 196616 | tf_op jit(solution)/shard_map/ppermute | solution.py:182
  19.9 4.5 %collective-permute-start.9 = (bf16[2,8,1024]{2,1,0:T(8,128)(2,1)S(1)}, bf16[2,8,1024]{2,1,0:T(8,128)(2,1)S(1)}, u32[]{:S(2)}, u32[]{:S(2)}) collective-permute-start(bf16[2,8,1024]{2,1,0:T(8,128)(2,1)S(1)} %get-tuple-element.30), channel_id=1, source_target_pairs={{0,2},{1,3},{2,0},{3,1},{4,6},{5,7},{6,4},{7,5},{8,10},{9,11},{10,... | collective-permute-start | bytes 98312 | tf_op jit(solution)/shard_map/ppermute | solution.py:182
  21.0 4.8 %collective-permute-start.10 = (bf16[2,8,1024]{2,1,0:T(8,128)(2,1)S(1)}, bf16[2,8,1024]{2,1,0:T(8,128)(2,1)S(1)}, u32[]{:S(2)}, u32[]{:S(2)}) collective-permute-start(bf16[2,8,1024]{2,1,0:T(8,128)(2,1)S(1)} %get-tuple-element.31), channel_id=1, source_target_pairs={{0,4},{1,5},{2,6},{3,7},{4,0},{5,1},{6,2},{7,3},{8,12},{9,13},{10,... | collective-permute-start | bytes 98312 | tf_op jit(solution)/shard_map/ppermute | solution.py:182
  23.1 5.7 %collective-permute-start.11 = (bf16[2,8,1024]{2,1,0:T(8,128)(2,1)S(1)}, bf16[2,8,1024]{2,1,0:T(8,128)(2,1)S(1)}, u32[]{:S(2)}, u32[]{:S(2)}) collective-permute-start(bf16[2,8,1024]{2,1,0:T(8,128)(2,1)S(1)} %get-tuple-element.32), channel_id=1, source_target_pairs={{0,6},{1,7},{2,4},{3,5},{4,2},{5,3},{6,0},{7,1},{8,14},{9,15},{10,... | collective-permute-start | bytes 98312 | tf_op jit(solution)/shard_map/ppermute | solution.py:182
  28.9 4.3 %collective-permute-start.12 = (bf16[4,8,1024]{2,1,0:T(8,128)(2,1)S(1)}, bf16[4,8,1024]{2,1,0:T(8,128)(2,1)S(1)}, u32[]{:S(2)}, u32[]{:S(2)}) collective-permute-start(bf16[4,8,1024]{2,1,0:T(8,128)(2,1)S(1)} %get-tuple-element.34), channel_id=1, source_target_pairs={{0,1},{1,0},{2,3},{3,2},{4,5},{5,4},{6,7},{7,6},{8,9},{9,8},{10,11... | collective-permute-start | bytes 196616 | tf_op jit(solution)/shard_map/ppermute | solution.py:182
  29.4 3.8 %collective-permute-start.5 = (bf16[128,1024]{1,0:T(8,128)(2,1)S(1)}, bf16[128,1024]{1,0:T(8,128)(2,1)S(1)}, u32[]{:S(2)}, u32[]{:S(2)}) collective-permute-start(bf16[128,1024]{1,0:T(8,128)(2,1)S(1)} %collective-permute-done.4.refs_2_), channel_id=1, source_target_pairs={{0,8},{8,0},{16,24},{24,16},{1,9},{9,1},{17,25},{25,17},{2,10},{10... | collective-permute-start | bytes 786440 | tf_op jit(solution)/shard_map/ppermute | solution.py:182

commit v16 on v14

--- a/solution.py
+++ b/solution.py
@@ -148,9 +148,9 @@
             s_cache = jnp.where(visible, s[:, SPAN + old :], NEGATIVE)
             s = jnp.concatenate([s_new, s[:, SPAN : SPAN + old], s_cache], axis=1)
             top = jnp.max(s, axis=1, keepdims=True)
-            weights.append(jnp.exp2((s - top) * SCALE2).astype(jnp.bfloat16))
+            weights.append(jnp.exp2(((s - top) * SCALE2).astype(jnp.bfloat16)))
         out = dot_nn(jnp.concatenate(weights, axis=0), values[c // per_group])
-        out = (out[:, :HD] / out[:, HD:]).astype(jnp.bfloat16)
+        out = (out[:, :HD] * pl.reciprocal(out[:, HD:], approx=True)).astype(jnp.bfloat16)
         for j in range(CHUNK):
             stage[:, (c * CHUNK + j) * HD : (c * CHUNK + j + 1) * HD] = out[j * SPAN : (j + 1) * SPAN]
         columns = pl.ds(c * chunk, chunk)

time: 33 us -> 33.2 us (level)
  no operation moved by 1% of the time
where the time goes in v16:
time: 33.2 us; the launch traced here: 32.9 us
  starting transfers between devices  13 us (39%)
  waiting for transfers between devices  11.7 us (35%)
  Pallas kernels  8.14 us (25%)
    ppermute x9, starting transfers between devices, swap(): lax.ppermute(x, axis, [(i, i ^ distance) for i in range(lax.axis_size(axi...  9.26 us
    ppermute x9, waiting for transfers between devices, swap(): lax.ppermute(x, axis, [(i, i ^ distance) for i in range(lax.axis_size(axi...  7.93 us
    pallas_call x1, Pallas kernels, on_device(): pl.pallas_call(attend_kernel, out_shape=shape((tokens, q_width), jnp.bflo...  5.16 us
    all_to_all x1, waiting for transfers between devices, on_device(): lax.all_to_all(routed, 'ctx', split_axis=0, concat_axis=0, tiled=True)  3.76 us
    all_to_all x1, starting transfers between devices, on_device(): lax.all_to_all(routed, 'ctx', split_axis=0, concat_axis=0, tiled=True)  3.75 us
    pallas_call x1, Pallas kernels, on_device(): pl.pallas_call(gather_kernel, out_shape=(shape((key_count, 2 * width), jn...  1.23 us
    pallas_call x1, Pallas kernels, on_device(): pl.pallas_call(functools.partial(pack_kernel, dom_count), out_shape=(shap...  1.01 us
    pallas_call x1, Pallas kernels, on_device(): pl.pallas_call(functools.partial(route_kernel, dom_count), out_shape=(plt...  0.74 us
  transfers between devices with their start and end apart: 10, of which 4 were waited for; matrix products, arithmetic and copies ran while one was open for 0% of the time, Pallas kernels for 4%

profile of v16, /device:TPU:0, one launch (start us, length us, event | category | flops | bytes accessed | tf_op | source)
XLA Modules:
  0.0 32.9 jit_solution(15791925657614523029)
XLA Ops:
  0.0 1.0 %pack.1 = (bf16[32,1024]{1,0:T(8,128)(2,1)S(1)}, bf16[4,8,1024]{2,1,0:T(8,128)(2,1)S(1)}, bf16[4,8,1024]{2,1,0:T(8,128)(2,1)S(1)}, bf16[4,8,1024]{2,1,0:T(8,128)...) custom-call(s32[32]{0:T(128)} %anc_hbm.1, s32[32]{0:T(128)} %len_hbm.1, ...), custom_call_target="tpu_custom_call" | custom-call | tf_op jit(solution)/shard_map/pack/pallas_call | solution.py:176
  1.0 0.6 %collective-permute-start = (bf16[4,8,1024]{2,1,0:T(8,128)(2,1)S(1)}, bf16[4,8,1024]{2,1,0:T(8,128)(2,1)S(1)}, u32[]{:S(2)}, u32[]{:S(2)}) collective-permute-start(bf16[4,8,1024]{2,1,0:T(8,128)(2,1)S(1)} %get-tuple-element.19), channel_id=1, source_target_pairs={{0,8},{8,0},{16,24},{24,16},{1,9},{9,1},{17,25},{25,17},{2,10},{10... | collective-permute-start | bytes 196616 | tf_op jit(solution)/shard_map/ppermute | solution.py:165
  1.7 2.6 %collective-permute-start.1 = (bf16[4,8,1024]{2,1,0:T(8,128)(2,1)S(1)}, bf16[4,8,1024]{2,1,0:T(8,128)(2,1)S(1)}, u32[]{:S(2)}, u32[]{:S(2)}) collective-permute-start(bf16[4,8,1024]{2,1,0:T(8,128)(2,1)S(1)} %get-tuple-element.20), channel_id=1, source_target_pairs={{0,16},{8,24},{16,0},{24,8},{1,17},{9,25},{17,1},{25,9},{2,18},{10... | collective-permute-start | bytes 196616 | tf_op jit(solution)/shard_map/ppermute | solution.py:165
  4.2 0.1 collective-permute-start.2
  4.3 3.7 %collective-permute-start.5 = (bf16[32,1024]{1,0:T(8,128)(2,1)S(1)}, bf16[32,1024]{1,0:T(8,128)(2,1)S(1)}, u32[]{:S(2)}, u32[]{:S(2)}) collective-permute-start(bf16[32,1024]{1,0:T(8,128)(2,1)S(1)} %get-tuple-element.22.refs_4_), channel_id=1, source_target_pairs={{0,6},{1,7},{2,4},{3,5},{4,2},{5,3},{6,0},{7,1},{8,14},{9,15},{10,... | collective-permute-start | bytes 196616 | tf_op jit(solution)/shard_map/ppermute | solution.py:165
  8.0 0.0 collective-permute-start.4
  8.0 0.0 collective-permute-done.refs_1_
  8.0 0.7 %collective-permute-start.3 = (bf16[32,1024]{1,0:T(8,128)(2,1)S(1)}, bf16[32,1024]{1,0:T(8,128)(2,1)S(1)}, u32[]{:S(2)}, u32[]{:S(2)}) collective-permute-start(bf16[32,1024]{1,0:T(8,128)(2,1)S(1)} %get-tuple-element.22.refs_4_), channel_id=1, source_target_pairs={{0,2},{1,3},{2,0},{3,1},{4,6},{5,7},{6,4},{7,5},{8,10},{9,11},{10,... | collective-permute-start | bytes 196616 | tf_op jit(solution)/shard_map/ppermute | solution.py:165
  8.7 0.0 collective-permute-done.1.refs_2_
  8.7 0.0 collective-permute-done.2.refs_3_
  8.7 2.1 %collective-permute-done.5.refs_7_ = bf16[32,1024]{1,0:T(8,128)(2,1)S(1)} collective-permute-done((bf16[32,1024]{1,0:T(8,128)(2,1)S(1)}, bf16[32,1024]{1,0:T(8,128)(2,1)S(1)}, u32[]{:S(2)}, u32[]{:S(2)}) %collective-permute-start.5) | collective-permute-done | bytes 65568 | tf_op jit(solution)/shard_map/ppermute | solution.py:165
  10.8 3.1 %collective-permute-done.4.refs_6_ = bf16[32,1024]{1,0:T(8,128)(2,1)S(1)} collective-permute-done((bf16[32,1024]{1,0:T(8,128)(2,1)S(1)}, bf16[32,1024]{1,0:T(8,128)(2,1)S(1)}, u32[]{:S(2)}, u32[]{:S(2)}) %collective-permute-start.4) | collective-permute-done | bytes 65568 | tf_op jit(solution)/shard_map/ppermute | solution.py:165
  14.0 0.0 collective-permute-done.3.refs_5_
  14.0 0.7 %route.1 = (bf16[8,8,1024]{2,1,0:T(8,128)(2,1)}, bf16[128,1024]{1,0:T(8,128)(2,1)S(1)}) custom-call(bf16[2,8,128]{2,1,0:T(8,128)(2,1)S(1)} %get-tuple-element.17.far_ref, bf16[4,8,1024]{2,1,0:T(8,128)(2,1)S(1)} %get-tuple-element.18.refs_0_, bf16[4,8,1024]{2,1,0:T(8,128)(2,1)S(1)} %collective-permute-done.refs_1_, ...), custom_call_target="tpu_custom_call" | custom-call | tf_op jit(solution)/shard_map/route/pallas_call | solution.py:201
  14.7 0.0 copy-start
  14.7 1.6 %collective-permute-start.7 = (bf16[128,1024]{1,0:T(8,128)(2,1)S(1)}, bf16[128,1024]{1,0:T(8,128)(2,1)S(1)}, u32[]{:S(2)}, u32[]{:S(2)}) collective-permute-start(bf16[128,1024]{1,0:T(8,128)(2,1)S(1)} %get-tuple-element.23.refs_0_), channel_id=1, source_target_pairs={{0,1},{1,0},{2,3},{3,2},{4,5},{5,4},{6,7},{7,6},{8,9},{9,8},{10,11... | collective-permute-start | bytes 786440 | tf_op jit(solution)/shard_map/ppermute | solution.py:165
  16.3 0.0 collective-permute-start.6
  16.3 3.8 %all-to-all-start = ((bf16[8,8,1024]{2,1,0:T(8,128)(2,1)}), bf16[8,8,1024]{2,1,0:T(8,128)(2,1)S(1)}, u32[]{:S(2)}, u32[]{:S(2)}) async-start(bf16[8,8,1024]{2,1,0:T(8,128)(2,1)} %get-tuple-element.26), calls=%async_computation | async-start | bytes 262144 | tf_op jit(solution)/shard_map/all_to_all | solution.py:216
  20.1 2.6 %collective-permute-done.7.refs_2_ = bf16[128,1024]{1,0:T(8,128)(2,1)S(1)} collective-permute-done((bf16[128,1024]{1,0:T(8,128)(2,1)S(1)}, bf16[128,1024]{1,0:T(8,128)(2,1)S(1)}, u32[]{:S(2)}, u32[]{:S(2)}) %collective-permute-start.7) | collective-permute-done | bytes 262176 | tf_op jit(solution)/shard_map/ppermute | solution.py:165
  22.7 0.0 collective-permute-start.8
  22.7 0.0 collective-permute-done.6.refs_1_
  22.7 0.0 copy-done
  22.7 1.2 %gather.1 = (bf16[512,1024]{1,0:T(8,128)(2,1)S(1)}, bf16[128,4096]{1,0:T(8,128)(2,1)S(1)}) custom-call(bf16[128,4096]{1,0:T(8,128)(2,1)} %q_hbm.1, bf16[128,2,512]{2,1,0:T(2,128)(2,1)S(1)} %copy-done, bf16[128,1024]{1,0:T(8,128)(2,1)S(1)} %get-tuple-element.23.refs_0_, bf16[128,1024]{1,0:T(8,128)(2,1)S(1)} %collective-permute-done.6.refs_1_, ...), custom_call_target="tpu_custom_call" | custom-call | flops 10000000000 | bytes 4194304 | tf_op jit(solution)/shard_map/gather/pallas_call | solution.py:220
  24.0 3.8 %all-to-all-done = bf16[8,8,1024]{2,1,0:T(8,128)(2,1)S(1)} async-done(((bf16[8,8,1024]{2,1,0:T(8,128)(2,1)}), bf16[8,8,1024]{2,1,0:T(8,128)(2,1)S(1)}, u32[]{:S(2)}, u32[]{:S(2)}) %all-to-all-start) | async-done | bytes 131104 | tf_op jit(solution)/shard_map/all_to_all | solution.py:216
  27.7 0.0 collective-permute-done.8.refs_0_
  27.7 5.2 %attend.1 = bf16[128,4096]{1,0:T(8,128)(2,1)} custom-call(s32[8,64]{1,0:T(8,128)S(1)} %get-tuple-element.16.limit_ref, bf16[128,4096]{1,0:T(8,128)(2,1)S(1)} %get-tuple-element.24.q_ref, bf16[512,1024]{1,0:T(8,128)(2,1)S(1)} %get-tuple-element.25.kv_ref, bf16[128,1024]{1,0:T(8,128)(2,1)S(1)} %collective-permute-done.8.refs_0_, bf16[64,1024]{1,0:T(8,128)(2,1)S(1)} %bitcast.1), custom_call_target="tpu_custom_call" | custom-call | tf_op jit(solution)/shard_map/attend/pallas_call | solution.py:230
Async XLA Ops:
  1.0 7.0 %collective-permute-start = (bf16[4,8,1024]{2,1,0:T(8,128)(2,1)S(1)}, bf16[4,8,1024]{2,1,0:T(8,128)(2,1)S(1)}, u32[]{:S(2)}, u32[]{:S(2)}) collective-permute-start(bf16[4,8,1024]{2,1,0:T(8,128)(2,1)S(1)} %get-tuple-element.19), channel_id=1, source_target_pairs={{0,8},{8,0},{16,24},{24,16},{1,9},{9,1},{17,25},{25,17},{2,10},{10... | collective-permute-start | bytes 196616 | tf_op jit(solution)/shard_map/ppermute | solution.py:165
  1.7 7.0 %collective-permute-start.1 = (bf16[4,8,1024]{2,1,0:T(8,128)(2,1)S(1)}, bf16[4,8,1024]{2,1,0:T(8,128)(2,1)S(1)}, u32[]{:S(2)}, u32[]{:S(2)}) collective-permute-start(bf16[4,8,1024]{2,1,0:T(8,128)(2,1)S(1)} %get-tuple-element.20), channel_id=1, source_target_pairs={{0,16},{8,24},{16,0},{24,8},{1,17},{9,25},{17,1},{25,9},{2,18},{10... | collective-permute-start | bytes 196616 | tf_op jit(solution)/shard_map/ppermute | solution.py:165
  4.2 4.5 %collective-permute-start.2 = (bf16[4,8,1024]{2,1,0:T(8,128)(2,1)S(1)}, bf16[4,8,1024]{2,1,0:T(8,128)(2,1)S(1)}, u32[]{:S(2)}, u32[]{:S(2)}) collective-permute-start(bf16[4,8,1024]{2,1,0:T(8,128)(2,1)S(1)} %get-tuple-element.21), channel_id=1, source_target_pairs={{0,24},{8,16},{16,8},{24,0},{1,25},{9,17},{17,9},{25,1},{2,26},{10... | collective-permute-start | bytes 196616 | tf_op jit(solution)/shard_map/ppermute | solution.py:165
  4.3 6.5 %collective-permute-start.5 = (bf16[32,1024]{1,0:T(8,128)(2,1)S(1)}, bf16[32,1024]{1,0:T(8,128)(2,1)S(1)}, u32[]{:S(2)}, u32[]{:S(2)}) collective-permute-start(bf16[32,1024]{1,0:T(8,128)(2,1)S(1)} %get-tuple-element.22.refs_4_), channel_id=1, source_target_pairs={{0,6},{1,7},{2,4},{3,5},{4,2},{5,3},{6,0},{7,1},{8,14},{9,15},{10,... | collective-permute-start | bytes 196616 | tf_op jit(solution)/shard_map/ppermute | solution.py:165
  8.0 6.0 %collective-permute-start.4 = (bf16[32,1024]{1,0:T(8,128)(2,1)S(1)}, bf16[32,1024]{1,0:T(8,128)(2,1)S(1)}, u32[]{:S(2)}, u32[]{:S(2)}) collective-permute-start(bf16[32,1024]{1,0:T(8,128)(2,1)S(1)} %get-tuple-element.22.refs_4_), channel_id=1, source_target_pairs={{0,4},{1,5},{2,6},{3,7},{4,0},{5,1},{6,2},{7,3},{8,12},{9,13},{10,... | collective-permute-start | bytes 196616 | tf_op jit(solution)/shard_map/ppermute | solution.py:165
  8.0 6.0 %collective-permute-start.3 = (bf16[32,1024]{1,0:T(8,128)(2,1)S(1)}, bf16[32,1024]{1,0:T(8,128)(2,1)S(1)}, u32[]{:S(2)}, u32[]{:S(2)}) collective-permute-start(bf16[32,1024]{1,0:T(8,128)(2,1)S(1)} %get-tuple-element.22.refs_4_), channel_id=1, source_target_pairs={{0,2},{1,3},{2,0},{3,1},{4,6},{5,7},{6,4},{7,5},{8,10},{9,11},{10,... | collective-permute-start | bytes 196616 | tf_op jit(solution)/shard_map/ppermute | solution.py:165
  14.7 8.0 %copy-start = (bf16[128,2,512]{2,1,0:T(2,128)(2,1)S(1)}, bf16[128,2,512]{2,1,0:T(2,128)(2,1)}, u32[]{:S(2)}) copy-start(bf16[128,2,512]{2,1,0:T(2,128)(2,1)} %new_ref.1) | copy-start | bytes 786436
  14.7 8.0 %collective-permute-start.7 = (bf16[128,1024]{1,0:T(8,128)(2,1)S(1)}, bf16[128,1024]{1,0:T(8,128)(2,1)S(1)}, u32[]{:S(2)}, u32[]{:S(2)}) collective-permute-start(bf16[128,1024]{1,0:T(8,128)(2,1)S(1)} %get-tuple-element.23.refs_0_), channel_id=1, source_target_pairs={{0,1},{1,0},{2,3},{3,2},{4,5},{5,4},{6,7},{7,6},{8,9},{9,8},{10,11... | collective-permute-start | bytes 786440 | tf_op jit(solution)/shard_map/ppermute | solution.py:165
  16.3 6.4 %collective-permute-start.6 = (bf16[128,1024]{1,0:T(8,128)(2,1)S(1)}, bf16[128,1024]{1,0:T(8,128)(2,1)S(1)}, u32[]{:S(2)}, u32[]{:S(2)}) collective-permute-start(bf16[128,1024]{1,0:T(8,128)(2,1)S(1)} %get-tuple-element.23.refs_0_), channel_id=1, source_target_pairs={{0,8},{8,0},{16,24},{24,16},{1,9},{9,1},{17,25},{25,17},{2,10},{10... | collective-permute-start | bytes 786440 | tf_op jit(solution)/shard_map/ppermute | solution.py:165
  16.3 11.4 %all-to-all-start = ((bf16[8,8,1024]{2,1,0:T(8,128)(2,1)}), bf16[8,8,1024]{2,1,0:T(8,128)(2,1)S(1)}, u32[]{:S(2)}, u32[]{:S(2)}) async-start(bf16[8,8,1024]{2,1,0:T(8,128)(2,1)} %get-tuple-element.26), calls=%async_computation | async-start | bytes 262144 | tf_op jit(solution)/shard_map/all_to_all | solution.py:216
  22.7 5.0 %collective-permute-start.8 = (bf16[128,1024]{1,0:T(8,128)(2,1)S(1)}, bf16[128,1024]{1,0:T(8,128)(2,1)S(1)}, u32[]{:S(2)}, u32[]{:S(2)}) collective-permute-start(bf16[128,1024]{1,0:T(8,128)(2,1)S(1)} %collective-permute-done.7.refs_2_), channel_id=1, source_target_pairs={{0,8},{8,0},{16,24},{24,16},{1,9},{9,1},{17,25},{25,17},{2,10},{10... | collective-permute-start | bytes 786440 | tf_op jit(solution)/shard_map/ppermute | solution.py:165

commit v17 on v13

--- a/solution.py
+++ b/solution.py
@@ -77,6 +77,14 @@
     out.wait()
 
 
+def stack_kernel(*refs):
+    pieces, out_refs = refs[:Z], refs[-2:]
+    half = len(pieces) // 2
+    for number, piece in enumerate(pieces):
+        at = number % half * piece.shape[0]
+        out_refs[number // half][at : at + piece.shape[0], :] = piece[...]
+
+
 def head_rows(q_ref, g, gq):
     return jnp.concatenate(
         [q_ref[:, (g * gq + j) * HD : (g * gq + j + 1) * HD] for j in range(gq)], axis=0
@@ -194,23 +202,31 @@
     outgoing, (far, limit) = rest[:dom_count], rest[dom_count:]
 
     pieces = [half] + [swap(half, "ctx", k * y_count) for k in range(1, Z)]
-    pieces += [swap(p, "ctx", k) for k in range(1, y_count) for p in pieces[:Z]]
-    pieces += [swap(p, "dom", 1) for p in pieces]
 
     incoming = outgoing[:1] + [swap(outgoing[k], "dom", k) for k in range(1, dom_count)]
     routed = pl.pallas_call(
         functools.partial(route_kernel, dom_count),
         out_shape=pltpu.HBM((group, page_rows, 2 * width), jnp.bfloat16),
-        in_specs=[VMEM] * (1 + dom_count) + [pl.BlockSpec(memory_space=pl.ANY)] * (Z - 1),
+        in_specs=[VMEM] * (1 + dom_count),
         out_specs=HBM,
         scratch_shapes=[pltpu.VMEM((group, page_rows, 2 * width), jnp.bfloat16), pltpu.SemaphoreType.DMA],
         compiler_params=params(12),
         name="route",
-    )(far, *incoming, *pieces[1:Z])
+    )(far, *incoming)
+    stacks = pl.pallas_call(
+        stack_kernel,
+        out_shape=(shape((Z // 2 * half_rows, 2 * width), jnp.bfloat16),) * 2,
+        in_specs=[VMEM] * Z + [pl.BlockSpec(memory_space=pl.ANY)] * (dom_count - 1),
+        out_specs=(VMEM, VMEM),
+        compiler_params=params(12),
+        name="stack",
+    )(*pieces, *incoming[1:])
+    pieces = [*stacks, *(swap(rows, "dom", 1) for rows in stacks)]
+    late = [swap(rows, "ctx", k) for k in range(1, y_count) for rows in stacks]
+    late += [swap(rows, "dom", 1) for rows in late]
     pages = lax.all_to_all(routed, "ctx", split_axis=0, concat_axis=0, tiled=True)
     pages = pages.reshape(ctx_count * page_rows, 2 * width)
 
-    late = [pieces.pop(at) for at in sorted((*range(Z + 2, 2 * Z), *range(len(pieces) - Z + 2, len(pieces))), reverse=True)]
     key_count = SPAN + sum(piece.shape[0] for piece in pieces)
     kv, queries = pl.pallas_call(
         gather_kernel,

time: 34.9 us -> 34.2 us (0.980)
  starting transfers between devices: 19.3 us -> 15.4 us
  waiting for transfers between devices: 7.3 us -> 10.5 us
    all_to_all x1, waiting for transfers between devices: 0.01 us -> 4.57 us  [on_device(): lax.all_to_all(routed, 'ctx', split_axis=0, concat_axis=0, tiled=True)]
    ppermute x18 -> x12, starting transfers between devices: 14.6 us -> 10.7 us  [swap(): lax.ppermute(x, axis, [(i, i ^ distance) for i in range(lax.axis_size(axi...]
    ppermute x18 -> x12, waiting for transfers between devices: 7.3 us -> 5.92 us  [swap(): lax.ppermute(x, axis, [(i, i ^ distance) for i in range(lax.axis_size(axi...]
  transfers between devices with their start and end apart: 19 -> 13, of which waited for: 6 -> 5; matrix products, arithmetic and copies ran while one was open for 0% -> 0% of each run, Pallas kernels for 6% -> 6%
where the time goes in v17:
time: 34.2 us; the launch traced here: 34 us
  starting transfers between devices  15.4 us (45%)
  waiting for transfers between devices  10.5 us (31%)
  Pallas kernels  8.06 us (24%)
    ppermute x12, starting transfers between devices, swap(): lax.ppermute(x, axis, [(i, i ^ distance) for i in range(lax.axis_size(axi...  10.7 us
    ppermute x12, waiting for transfers between devices, swap(): lax.ppermute(x, axis, [(i, i ^ distance) for i in range(lax.axis_size(axi...  5.92 us
    pallas_call x1, Pallas kernels, on_device(): pl.pallas_call(attend_kernel, out_shape=shape((tokens, q_width), jnp.bflo...  4.93 us
    all_to_all x1, starting transfers between devices, on_device(): lax.all_to_all(routed, 'ctx', split_axis=0, concat_axis=0, tiled=True)  4.72 us
    all_to_all x1, waiting for transfers between devices, on_device(): lax.all_to_all(routed, 'ctx', split_axis=0, concat_axis=0, tiled=True)  4.57 us
    pallas_call x1, Pallas kernels, on_device(): pl.pallas_call(gather_kernel, out_shape=(shape((key_count, 2 * width), jn...  1.22 us
    pallas_call x1, Pallas kernels, on_device(): pl.pallas_call(functools.partial(pack_kernel, dom_count), out_shape=(shap...  1.17 us
    pallas_call x1, Pallas kernels, on_device(): pl.pallas_call(functools.partial(route_kernel, dom_count), out_shape=pltp...  0.72 us
  transfers between devices with their start and end apart: 13, of which 5 were waited for; matrix products, arithmetic and copies ran while one was open for 0% of the time, Pallas kernels for 6%

profile of v17, /device:TPU:0, one launch (start us, length us, event | category | flops | bytes accessed | tf_op | source)
XLA Modules:
  0.0 34.0 jit_solution(13454160778543397219)
XLA Ops:
  0.0 1.2 %pack.1 = (bf16[32,1024]{1,0:T(8,128)(2,1)S(1)}, bf16[4,8,1024]{2,1,0:T(8,128)(2,1)S(1)}, bf16[4,8,1024]{2,1,0:T(8,128)(2,1)S(1)}, bf16[4,8,1024]{2,1,0:T(8,128)...) custom-call(s32[32]{0:T(128)} %anc_hbm.1, s32[32]{0:T(128)} %len_hbm.1, ...), custom_call_target="tpu_custom_call" | custom-call | tf_op jit(solution)/shard_map/pack/pallas_call | solution.py:182
  1.2 0.5 %collective-permute-start.3 = (bf16[4,8,1024]{2,1,0:T(8,128)(2,1)S(1)}, bf16[4,8,1024]{2,1,0:T(8,128)(2,1)S(1)}, u32[]{:S(2)}, u32[]{:S(2)}) collective-permute-start(bf16[4,8,1024]{2,1,0:T(8,128)(2,1)S(1)} %get-tuple-element.18), channel_id=1, source_target_pairs={{0,8},{8,0},{16,24},{24,16},{1,9},{9,1},{17,25},{25,17},{2,10},{10... | collective-permute-start | bytes 196616 | tf_op jit(solution)/shard_map/ppermute | solution.py:171
  1.6 2.5 %collective-permute-start.4 = (bf16[4,8,1024]{2,1,0:T(8,128)(2,1)S(1)}, bf16[4,8,1024]{2,1,0:T(8,128)(2,1)S(1)}, u32[]{:S(2)}, u32[]{:S(2)}) collective-permute-start(bf16[4,8,1024]{2,1,0:T(8,128)(2,1)S(1)} %get-tuple-element.19), channel_id=1, source_target_pairs={{0,16},{8,24},{16,0},{24,8},{1,17},{9,25},{17,1},{25,9},{2,18},{10... | collective-permute-start | bytes 196616 | tf_op jit(solution)/shard_map/ppermute | solution.py:171
  4.1 0.1 collective-permute-start.5
  4.2 4.0 %collective-permute-start.2 = (bf16[32,1024]{1,0:T(8,128)(2,1)S(1)}, bf16[32,1024]{1,0:T(8,128)(2,1)S(1)}, u32[]{:S(2)}, u32[]{:S(2)}) collective-permute-start(bf16[32,1024]{1,0:T(8,128)(2,1)S(1)} %get-tuple-element.17.refs_0_), channel_id=1, source_target_pairs={{0,6},{1,7},{2,4},{3,5},{4,2},{5,3},{6,0},{7,1},{8,14},{9,15},{10,... | collective-permute-start | bytes 196616 | tf_op jit(solution)/shard_map/ppermute | solution.py:171
  8.2 0.0 collective-permute-start.1
  8.2 0.0 collective-permute-done.3.refs_4_.refs_1_
  8.2 0.6 %collective-permute-start = (bf16[32,1024]{1,0:T(8,128)(2,1)S(1)}, bf16[32,1024]{1,0:T(8,128)(2,1)S(1)}, u32[]{:S(2)}, u32[]{:S(2)}) collective-permute-start(bf16[32,1024]{1,0:T(8,128)(2,1)S(1)} %get-tuple-element.17.refs_0_), channel_id=1, source_target_pairs={{0,2},{1,3},{2,0},{3,1},{4,6},{5,7},{6,4},{7,5},{8,10},{9,11},{10,... | collective-permute-start | bytes 196616 | tf_op jit(solution)/shard_map/ppermute | solution.py:171
  8.7 0.0 collective-permute-done.4.refs_5_.refs_2_
  8.7 0.0 collective-permute-done.5.refs_6_.refs_3_
  8.8 2.2 %collective-permute-done.2.refs_3_ = bf16[32,1024]{1,0:T(8,128)(2,1)S(1)} collective-permute-done((bf16[32,1024]{1,0:T(8,128)(2,1)S(1)}, bf16[32,1024]{1,0:T(8,128)(2,1)S(1)}, u32[]{:S(2)}, u32[]{:S(2)}) %collective-permute-start.2) | collective-permute-done | bytes 65568 | tf_op jit(solution)/shard_map/ppermute | solution.py:171
  11.0 3.2 %collective-permute-done.1.refs_2_ = bf16[32,1024]{1,0:T(8,128)(2,1)S(1)} collective-permute-done((bf16[32,1024]{1,0:T(8,128)(2,1)S(1)}, bf16[32,1024]{1,0:T(8,128)(2,1)S(1)}, u32[]{:S(2)}, u32[]{:S(2)}) %collective-permute-start.1) | collective-permute-done | bytes 65568 | tf_op jit(solution)/shard_map/ppermute | solution.py:171
  14.1 0.0 collective-permute-done.refs_1_
  14.2 1.6 %collective-permute-start.8 = (bf16[64,1024]{1,0:T(8,128)(2,1)S(1)}, bf16[64,1024]{1,0:T(8,128)(2,1)S(1)}, u32[]{:S(2)}, u32[]{:S(2)}) collective-permute-start(bf16[64,1024]{1,0:T(8,128)(2,1)S(1)} %get-tuple-element.21.refs_0_), channel_id=1, source_target_pairs={{0,1},{1,0},{2,3},{3,2},{4,5},{5,4},{6,7},{7,6},{8,9},{9,8},{10,11... | collective-permute-start | bytes 393224 | tf_op jit(solution)/shard_map/ppermute | solution.py:171
  15.8 0.5 %collective-permute-start.9 = (bf16[64,1024]{1,0:T(8,128)(2,1)S(1)}, bf16[64,1024]{1,0:T(8,128)(2,1)S(1)}, u32[]{:S(2)}, u32[]{:S(2)}) collective-permute-start(bf16[64,1024]{1,0:T(8,128)(2,1)S(1)} %get-tuple-element.22.refs_1_), channel_id=1, source_target_pairs={{0,1},{1,0},{2,3},{3,2},{4,5},{5,4},{6,7},{7,6},{8,9},{9,8},{10,11... | collective-permute-start | bytes 393224 | tf_op jit(solution)/shard_map/ppermute | solution.py:171
  16.3 0.0 copy-start
  16.3 0.7 %route.1 = bf16[8,8,1024]{2,1,0:T(8,128)(2,1)} custom-call(bf16[2,8,128]{2,1,0:T(8,128)(2,1)S(1)} %get-tuple-element.25.far_ref, bf16[4,8,1024]{2,1,0:T(8,128)(2,1)S(1)} %get-tuple-element.26.refs_0_, bf16[4,8,1024]{2,1,0:T(8,128)(2,1)S(1)} %collective-permute-done.3.refs_4_.refs_1_, bf16[4,8,1024]{2,1,0:T(8,128)(2,1)S(1)} %collective-permute-done.4.refs_5_.refs_2_, ...), custom_call_target="tpu_custom_call" | custom-call | tf_op jit(solution)/shard_map/route/pallas_call | solution.py:207
  17.0 4.7 %all-to-all-start = ((bf16[8,8,1024]{2,1,0:T(8,128)(2,1)}), bf16[8,8,1024]{2,1,0:T(8,128)(2,1)S(1)}, u32[]{:S(2)}, u32[]{:S(2)}) async-start(bf16[8,8,1024]{2,1,0:T(8,128)(2,1)} %route.1), calls=%async_computation | async-start | bytes 262144 | tf_op jit(solution)/shard_map/all_to_all | solution.py:227
  21.7 0.0 collective-permute-start.6
  21.7 0.5 %collective-permute-start.7 = (bf16[64,1024]{1,0:T(8,128)(2,1)S(1)}, bf16[64,1024]{1,0:T(8,128)(2,1)S(1)}, u32[]{:S(2)}, u32[]{:S(2)}) collective-permute-start(bf16[64,1024]{1,0:T(8,128)(2,1)S(1)} %get-tuple-element.22.refs_1_), channel_id=1, source_target_pairs={{0,8},{8,0},{16,24},{24,16},{1,9},{9,1},{17,25},{25,17},{2,10},{10... | collective-permute-start | bytes 393224 | tf_op jit(solution)/shard_map/ppermute | solution.py:171
  22.2 0.0 collective-permute-done.8.refs_0_
  22.2 0.1 collective-permute-start.10
  22.3 0.0 collective-permute-done.9.refs_1_
  22.3 0.4 %collective-permute-start.11 = (bf16[64,1024]{1,0:T(8,128)(2,1)S(1)}, bf16[64,1024]{1,0:T(8,128)(2,1)S(1)}, u32[]{:S(2)}, u32[]{:S(2)}) collective-permute-start(bf16[64,1024]{1,0:T(8,128)(2,1)S(1)} %collective-permute-done.9.refs_1_), channel_id=1, source_target_pairs={{0,8},{8,0},{16,24},{24,16},{1,9},{9,1},{17,25},{25,17},{2,10},{10... | collective-permute-start | bytes 393224 | tf_op jit(solution)/shard_map/ppermute | solution.py:171
  22.7 0.3 collective-permute-done.6.refs_2_
  23.1 0.2 collective-permute-done.7.refs_3_
  23.2 0.0 copy-done
  23.2 1.2 %gather.1 = (bf16[384,1024]{1,0:T(8,128)(2,1)S(1)}, bf16[128,4096]{1,0:T(8,128)(2,1)S(1)}) custom-call(bf16[128,4096]{1,0:T(8,128)(2,1)} %q_hbm.1, bf16[128,2,512]{2,1,0:T(2,128)(2,1)S(1)} %copy-done, bf16[64,1024]{1,0:T(8,128)(2,1)S(1)} %get-tuple-element.21.refs_0_, bf16[64,1024]{1,0:T(8,128)(2,1)S(1)} %get-tuple-element.22.refs_1_, ...), custom_call_target="tpu_custom_call" | custom-call | flops 1000000000 | bytes 4194304 | tf_op jit(solution)/shard_map/gather/pallas_call | solution.py:231
  24.5 4.6 %all-to-all-done = bf16[8,8,1024]{2,1,0:T(8,128)(2,1)S(1)} async-done(((bf16[8,8,1024]{2,1,0:T(8,128)(2,1)}), bf16[8,8,1024]{2,1,0:T(8,128)(2,1)S(1)}, u32[]{:S(2)}, u32[]{:S(2)}) %all-to-all-start) | async-done | bytes 131104 | tf_op jit(solution)/shard_map/all_to_all | solution.py:227
  29.1 0.0 collective-permute-done.10.refs_2_
  29.1 0.0 collective-permute-done.11.refs_3_
  29.1 4.9 %attend.1 = bf16[128,4096]{1,0:T(8,128)(2,1)} custom-call(s32[8,64]{1,0:T(8,128)S(1)} %get-tuple-element.16.limit_ref, bf16[128,4096]{1,0:T(8,128)(2,1)S(1)} %get-tuple-element.23.q_ref, bf16[384,1024]{1,0:T(8,128)(2,1)S(1)} %get-tuple-element.24.kv_ref, bf16[64,1024]{1,0:T(8,128)(2,1)S(1)} %collective-permute-done.8.refs_0_, ...), custom_call_target="tpu_custom_call" | custom-call | tf_op jit(solution)/shard_map/attend/pallas_call | solution.py:241
  (1 shorter events, 0.0 us)
Async XLA Ops:
  1.2 7.0 %collective-permute-start.3 = (bf16[4,8,1024]{2,1,0:T(8,128)(2,1)S(1)}, bf16[4,8,1024]{2,1,0:T(8,128)(2,1)S(1)}, u32[]{:S(2)}, u32[]{:S(2)}) collective-permute-start(bf16[4,8,1024]{2,1,0:T(8,128)(2,1)S(1)} %get-tuple-element.18), channel_id=1, source_target_pairs={{0,8},{8,0},{16,24},{24,16},{1,9},{9,1},{17,25},{25,17},{2,10},{10... | collective-permute-start | bytes 196616 | tf_op jit(solution)/shard_map/ppermute | solution.py:171
  1.6 7.1 %collective-permute-start.4 = (bf16[4,8,1024]{2,1,0:T(8,128)(2,1)S(1)}, bf16[4,8,1024]{2,1,0:T(8,128)(2,1)S(1)}, u32[]{:S(2)}, u32[]{:S(2)}) collective-permute-start(bf16[4,8,1024]{2,1,0:T(8,128)(2,1)S(1)} %get-tuple-element.19), channel_id=1, source_target_pairs={{0,16},{8,24},{16,0},{24,8},{1,17},{9,25},{17,1},{25,9},{2,18},{10... | collective-permute-start | bytes 196616 | tf_op jit(solution)/shard_map/ppermute | solution.py:171
  4.1 4.6 %collective-permute-start.5 = (bf16[4,8,1024]{2,1,0:T(8,128)(2,1)S(1)}, bf16[4,8,1024]{2,1,0:T(8,128)(2,1)S(1)}, u32[]{:S(2)}, u32[]{:S(2)}) collective-permute-start(bf16[4,8,1024]{2,1,0:T(8,128)(2,1)S(1)} %get-tuple-element.20), channel_id=1, source_target_pairs={{0,24},{8,16},{16,8},{24,0},{1,25},{9,17},{17,9},{25,1},{2,26},{10... | collective-permute-start | bytes 196616 | tf_op jit(solution)/shard_map/ppermute | solution.py:171
  4.2 6.8 %collective-permute-start.2 = (bf16[32,1024]{1,0:T(8,128)(2,1)S(1)}, bf16[32,1024]{1,0:T(8,128)(2,1)S(1)}, u32[]{:S(2)}, u32[]{:S(2)}) collective-permute-start(bf16[32,1024]{1,0:T(8,128)(2,1)S(1)} %get-tuple-element.17.refs_0_), channel_id=1, source_target_pairs={{0,6},{1,7},{2,4},{3,5},{4,2},{5,3},{6,0},{7,1},{8,14},{9,15},{10,... | collective-permute-start | bytes 196616 | tf_op jit(solution)/shard_map/ppermute | solution.py:171
  8.2 6.0 %collective-permute-start.1 = (bf16[32,1024]{1,0:T(8,128)(2,1)S(1)}, bf16[32,1024]{1,0:T(8,128)(2,1)S(1)}, u32[]{:S(2)}, u32[]{:S(2)}) collective-permute-start(bf16[32,1024]{1,0:T(8,128)(2,1)S(1)} %get-tuple-element.17.refs_0_), channel_id=1, source_target_pairs={{0,4},{1,5},{2,6},{3,7},{4,0},{5,1},{6,2},{7,3},{8,12},{9,13},{10,... | collective-permute-start | bytes 196616 | tf_op jit(solution)/shard_map/ppermute | solution.py:171
  8.2 6.0 %collective-permute-start = (bf16[32,1024]{1,0:T(8,128)(2,1)S(1)}, bf16[32,1024]{1,0:T(8,128)(2,1)S(1)}, u32[]{:S(2)}, u32[]{:S(2)}) collective-permute-start(bf16[32,1024]{1,0:T(8,128)(2,1)S(1)} %get-tuple-element.17.refs_0_), channel_id=1, source_target_pairs={{0,2},{1,3},{2,0},{3,1},{4,6},{5,7},{6,4},{7,5},{8,10},{9,11},{10,... | collective-permute-start | bytes 196616 | tf_op jit(solution)/shard_map/ppermute | solution.py:171
  14.2 8.1 %collective-permute-start.8 = (bf16[64,1024]{1,0:T(8,128)(2,1)S(1)}, bf16[64,1024]{1,0:T(8,128)(2,1)S(1)}, u32[]{:S(2)}, u32[]{:S(2)}) collective-permute-start(bf16[64,1024]{1,0:T(8,128)(2,1)S(1)} %get-tuple-element.21.refs_0_), channel_id=1, source_target_pairs={{0,1},{1,0},{2,3},{3,2},{4,5},{5,4},{6,7},{7,6},{8,9},{9,8},{10,11... | collective-permute-start | bytes 393224 | tf_op jit(solution)/shard_map/ppermute | solution.py:171
  15.8 6.5 %collective-permute-start.9 = (bf16[64,1024]{1,0:T(8,128)(2,1)S(1)}, bf16[64,1024]{1,0:T(8,128)(2,1)S(1)}, u32[]{:S(2)}, u32[]{:S(2)}) collective-permute-start(bf16[64,1024]{1,0:T(8,128)(2,1)S(1)} %get-tuple-element.22.refs_1_), channel_id=1, source_target_pairs={{0,1},{1,0},{2,3},{3,2},{4,5},{5,4},{6,7},{7,6},{8,9},{9,8},{10,11... | collective-permute-start | bytes 393224 | tf_op jit(solution)/shard_map/ppermute | solution.py:171
  16.3 7.0 %copy-start = (bf16[128,2,512]{2,1,0:T(2,128)(2,1)S(1)}, bf16[128,2,512]{2,1,0:T(2,128)(2,1)}, u32[]{:S(2)}) copy-start(bf16[128,2,512]{2,1,0:T(2,128)(2,1)} %new_ref.1) | copy-start | bytes 786436
  17.0 12.1 %all-to-all-start = ((bf16[8,8,1024]{2,1,0:T(8,128)(2,1)}), bf16[8,8,1024]{2,1,0:T(8,128)(2,1)S(1)}, u32[]{:S(2)}, u32[]{:S(2)}) async-start(bf16[8,8,1024]{2,1,0:T(8,128)(2,1)} %route.1), calls=%async_computation | async-start | bytes 262144 | tf_op jit(solution)/shard_map/all_to_all | solution.py:227
  21.7 1.3 %collective-permute-start.6 = (bf16[64,1024]{1,0:T(8,128)(2,1)S(1)}, bf16[64,1024]{1,0:T(8,128)(2,1)S(1)}, u32[]{:S(2)}, u32[]{:S(2)}) collective-permute-start(bf16[64,1024]{1,0:T(8,128)(2,1)S(1)} %get-tuple-element.21.refs_0_), channel_id=1, source_target_pairs={{0,8},{8,0},{16,24},{24,16},{1,9},{9,1},{17,25},{25,17},{2,10},{10... | collective-permute-start | bytes 393224 | tf_op jit(solution)/shard_map/ppermute | solution.py:171
  21.7 1.5 %collective-permute-start.7 = (bf16[64,1024]{1,0:T(8,128)(2,1)S(1)}, bf16[64,1024]{1,0:T(8,128)(2,1)S(1)}, u32[]{:S(2)}, u32[]{:S(2)}) collective-permute-start(bf16[64,1024]{1,0:T(8,128)(2,1)S(1)} %get-tuple-element.22.refs_1_), channel_id=1, source_target_pairs={{0,8},{8,0},{16,24},{24,16},{1,9},{9,1},{17,25},{25,17},{2,10},{10... | collective-permute-start | bytes 393224 | tf_op jit(solution)/shard_map/ppermute | solution.py:171
  22.2 6.8 %collective-permute-start.10 = (bf16[64,1024]{1,0:T(8,128)(2,1)S(1)}, bf16[64,1024]{1,0:T(8,128)(2,1)S(1)}, u32[]{:S(2)}, u32[]{:S(2)}) collective-permute-start(bf16[64,1024]{1,0:T(8,128)(2,1)S(1)} %collective-permute-done.8.refs_0_), channel_id=1, source_target_pairs={{0,8},{8,0},{16,24},{24,16},{1,9},{9,1},{17,25},{25,17},{2,10},{10... | collective-permute-start | bytes 393224 | tf_op jit(solution)/shard_map/ppermute | solution.py:171
  22.3 6.8 %collective-permute-start.11 = (bf16[64,1024]{1,0:T(8,128)(2,1)S(1)}, bf16[64,1024]{1,0:T(8,128)(2,1)S(1)}, u32[]{:S(2)}, u32[]{:S(2)}) collective-permute-start(bf16[64,1024]{1,0:T(8,128)(2,1)S(1)} %collective-permute-done.9.refs_1_), channel_id=1, source_target_pairs={{0,8},{8,0},{16,24},{24,16},{1,9},{9,1},{17,25},{25,17},{2,10},{10... | collective-permute-start | bytes 393224 | tf_op jit(solution)/shard_map/ppermute | solution.py:171

commit v18 on v17

--- a/solution.py
+++ b/solution.py
@@ -78,11 +78,9 @@
 
 
 def stack_kernel(*refs):
-    pieces, out_refs = refs[:Z], refs[-2:]
-    half = len(pieces) // 2
+    pieces, rows_ref = refs[:Z], refs[-1]
     for number, piece in enumerate(pieces):
-        at = number % half * piece.shape[0]
-        out_refs[number // half][at : at + piece.shape[0], :] = piece[...]
+        rows_ref[number * piece.shape[0] : (number + 1) * piece.shape[0], :] = piece[...]
 
 
 def head_rows(q_ref, g, gq):
@@ -213,17 +211,17 @@
         compiler_params=params(12),
         name="route",
     )(far, *incoming)
-    stacks = pl.pallas_call(
+    rows = pl.pallas_call(
         stack_kernel,
-        out_shape=(shape((Z // 2 * half_rows, 2 * width), jnp.bfloat16),) * 2,
-        in_specs=[VMEM] * Z + [pl.BlockSpec(memory_space=pl.ANY)] * (dom_count - 1),
-        out_specs=(VMEM, VMEM),
+        out_shape=shape((Z * half_rows, 2 * width), jnp.bfloat16),
+        in_specs=[VMEM] * Z + [HBM],
+        out_specs=VMEM,
         compiler_params=params(12),
         name="stack",
-    )(*pieces, *incoming[1:])
-    pieces = [*stacks, *(swap(rows, "dom", 1) for rows in stacks)]
-    late = [swap(rows, "ctx", k) for k in range(1, y_count) for rows in stacks]
-    late += [swap(rows, "dom", 1) for rows in late]
+    )(*pieces, pltpu.with_memory_space_constraint(routed, pltpu.HBM))
+    over_y = [swap(rows, "ctx", k) for k in range(1, y_count)]
+    pieces = [rows, swap(rows, "dom", 1), *over_y]
+    late = [swap(piece, "dom", 1) for piece in over_y]
     pages = lax.all_to_all(routed, "ctx", split_axis=0, concat_axis=0, tiled=True)
     pages = pages.reshape(ctx_count * page_rows, 2 * width)
 
@@ -235,7 +233,7 @@
         out_specs=(VMEM, VMEM),
         scratch_shapes=[pltpu.SemaphoreType.DMA((Q_COPIES,))],
         compiler_params=params(16),
-        cost_estimate=pl.CostEstimate(flops=10**9, bytes_accessed=2**22, transcendentals=0),
+        cost_estimate=pl.CostEstimate(flops=10**10, bytes_accessed=2**22, transcendentals=0),
         name="gather",
     )(pltpu.with_memory_space_constraint(q_new, pltpu.HBM), kv_new, *pieces)
     return pl.pallas_call(

time: 34.2 us -> 32.2 us (0.942)
  starting transfers between devices: 15.4 us -> 12.9 us
  waiting for transfers between devices: 10.5 us -> 11.1 us
    ppermute x12 -> x9, starting transfers between devices: 10.7 us -> 9.15 us  [swap(): lax.ppermute(x, axis, [(i, i ^ distance) for i in range(lax.axis_size(axi...]
    ppermute x12 -> x9, waiting for transfers between devices: 5.92 us -> 7.31 us  [swap(): lax.ppermute(x, axis, [(i, i ^ distance) for i in range(lax.axis_size(axi...]
    all_to_all x1, starting transfers between devices: 4.72 us -> 3.75 us  [on_device(): lax.all_to_all(routed, 'ctx', split_axis=0, concat_axis=0, tiled=True)]
    all_to_all x1, waiting for transfers between devices: 4.57 us -> 3.76 us  [on_device(): lax.all_to_all(routed, 'ctx', split_axis=0, concat_axis=0, tiled=True)]
  transfers between devices with their start and end apart: 13 -> 10, of which waited for: 5 -> 4; matrix products, arithmetic and copies ran while one was open for 0% -> 0% of each run, Pallas kernels for 6% -> 6%
where the time goes in v18:
time: 32.2 us; the launch traced here: 31.9 us
  starting transfers between devices  12.9 us (40%)
  waiting for transfers between devices  11.1 us (34%)
  Pallas kernels  7.89 us (25%)
    ppermute x9, starting transfers between devices, swap(): lax.ppermute(x, axis, [(i, i ^ distance) for i in range(lax.axis_size(axi...  9.15 us
    ppermute x9, waiting for transfers between devices, swap(): lax.ppermute(x, axis, [(i, i ^ distance) for i in range(lax.axis_size(axi...  7.31 us
    pallas_call x1, Pallas kernels, on_device(): pl.pallas_call(attend_kernel, out_shape=shape((tokens, q_width), jnp.bflo...  4.81 us
    all_to_all x1, waiting for transfers between devices, on_device(): lax.all_to_all(routed, 'ctx', split_axis=0, concat_axis=0, tiled=True)  3.76 us
    all_to_all x1, starting transfers between devices, on_device(): lax.all_to_all(routed, 'ctx', split_axis=0, concat_axis=0, tiled=True)  3.75 us
    pallas_call x1, Pallas kernels, on_device(): pl.pallas_call(gather_kernel, out_shape=(shape((key_count, 2 * width), jn...  1.23 us
    pallas_call x1, Pallas kernels, on_device(): pl.pallas_call(functools.partial(pack_kernel, dom_count), out_shape=(shap...  1.12 us
    pallas_call x1, Pallas kernels, on_device(): pl.pallas_call(functools.partial(route_kernel, dom_count), out_shape=pltp...  0.72 us
  transfers between devices with their start and end apart: 10, of which 4 were waited for; matrix products, arithmetic and copies ran while one was open for 0% of the time, Pallas kernels for 6%

profile of v18, /device:TPU:0, one launch (start us, length us, event | category | flops | bytes accessed | tf_op | source)
XLA Modules:
  0.0 31.9 jit_solution(13874578430957361900)
XLA Ops:
  0.0 1.1 %pack.1 = (bf16[32,1024]{1,0:T(8,128)(2,1)S(1)}, bf16[4,8,1024]{2,1,0:T(8,128)(2,1)S(1)}, bf16[4,8,1024]{2,1,0:T(8,128)(2,1)S(1)}, bf16[4,8,1024]{2,1,0:T(8,128)...) custom-call(s32[32]{0:T(128)} %anc_hbm.1, s32[32]{0:T(128)} %len_hbm.1, ...), custom_call_target="tpu_custom_call" | custom-call | tf_op jit(solution)/shard_map/pack/pallas_call | solution.py:180
  1.1 0.5 %collective-permute-start.3 = (bf16[4,8,1024]{2,1,0:T(8,128)(2,1)S(1)}, bf16[4,8,1024]{2,1,0:T(8,128)(2,1)S(1)}, u32[]{:S(2)}, u32[]{:S(2)}) collective-permute-start(bf16[4,8,1024]{2,1,0:T(8,128)(2,1)S(1)} %get-tuple-element.18), channel_id=1, source_target_pairs={{0,8},{8,0},{16,24},{24,16},{1,9},{9,1},{17,25},{25,17},{2,10},{10... | collective-permute-start | bytes 196616 | tf_op jit(solution)/shard_map/ppermute | solution.py:169
  1.6 2.6 %collective-permute-start.4 = (bf16[4,8,1024]{2,1,0:T(8,128)(2,1)S(1)}, bf16[4,8,1024]{2,1,0:T(8,128)(2,1)S(1)}, u32[]{:S(2)}, u32[]{:S(2)}) collective-permute-start(bf16[4,8,1024]{2,1,0:T(8,128)(2,1)S(1)} %get-tuple-element.19), channel_id=1, source_target_pairs={{0,16},{8,24},{16,0},{24,8},{1,17},{9,25},{17,1},{25,9},{2,18},{10... | collective-permute-start | bytes 196616 | tf_op jit(solution)/shard_map/ppermute | solution.py:169
  4.2 0.1 collective-permute-start.5
  4.3 3.8 %collective-permute-start.2 = (bf16[32,1024]{1,0:T(8,128)(2,1)S(1)}, bf16[32,1024]{1,0:T(8,128)(2,1)S(1)}, u32[]{:S(2)}, u32[]{:S(2)}) collective-permute-start(bf16[32,1024]{1,0:T(8,128)(2,1)S(1)} %get-tuple-element.15.refs_0_), channel_id=1, source_target_pairs={{0,6},{1,7},{2,4},{3,5},{4,2},{5,3},{6,0},{7,1},{8,14},{9,15},{10,... | collective-permute-start | bytes 196616 | tf_op jit(solution)/shard_map/ppermute | solution.py:169
  8.1 0.0 collective-permute-start.1
  8.1 0.0 collective-permute-done.3.refs_1_
  8.1 0.6 %collective-permute-start = (bf16[32,1024]{1,0:T(8,128)(2,1)S(1)}, bf16[32,1024]{1,0:T(8,128)(2,1)S(1)}, u32[]{:S(2)}, u32[]{:S(2)}) collective-permute-start(bf16[32,1024]{1,0:T(8,128)(2,1)S(1)} %get-tuple-element.15.refs_0_), channel_id=1, source_target_pairs={{0,2},{1,3},{2,0},{3,1},{4,6},{5,7},{6,4},{7,5},{8,10},{9,11},{10,... | collective-permute-start | bytes 196616 | tf_op jit(solution)/shard_map/ppermute | solution.py:169
  8.7 0.0 collective-permute-done.4.refs_2_
  8.7 0.0 collective-permute-done.5.refs_3_
  8.7 0.7 %route.1.refs_4_ = bf16[8,8,1024]{2,1,0:T(8,128)(2,1)} custom-call(bf16[2,8,128]{2,1,0:T(8,128)(2,1)S(1)} %get-tuple-element.16.far_ref, bf16[4,8,1024]{2,1,0:T(8,128)(2,1)S(1)} %get-tuple-element.17.refs_0_, bf16[4,8,1024]{2,1,0:T(8,128)(2,1)S(1)} %collective-permute-done.3.refs_1_, bf16[4,8,1024]{2,1,0:T(8,128)(2,1)S(1)} %collective-permute-done.4.refs_2_, ...), custom_call_target="tpu_custom_call" | custom-call | tf_op jit(solution)/shard_map/route/pallas_call | solution.py:205
  9.4 0.0 copy-start
  9.4 1.5 %collective-permute-done.2.refs_3_ = bf16[32,1024]{1,0:T(8,128)(2,1)S(1)} collective-permute-done((bf16[32,1024]{1,0:T(8,128)(2,1)S(1)}, bf16[32,1024]{1,0:T(8,128)(2,1)S(1)}, u32[]{:S(2)}, u32[]{:S(2)}) %collective-permute-start.2) | collective-permute-done | bytes 65568 | tf_op jit(solution)/shard_map/ppermute | solution.py:169
  10.9 3.2 %collective-permute-done.1.refs_2_ = bf16[32,1024]{1,0:T(8,128)(2,1)S(1)} collective-permute-done((bf16[32,1024]{1,0:T(8,128)(2,1)S(1)}, bf16[32,1024]{1,0:T(8,128)(2,1)S(1)}, u32[]{:S(2)}, u32[]{:S(2)}) %collective-permute-start.1) | collective-permute-done | bytes 65568 | tf_op jit(solution)/shard_map/ppermute | solution.py:169
  14.1 0.0 collective-permute-done.refs_1_
  14.1 1.6 %collective-permute-start.7 = (bf16[128,1024]{1,0:T(8,128)(2,1)S(1)}, bf16[128,1024]{1,0:T(8,128)(2,1)S(1)}, u32[]{:S(2)}, u32[]{:S(2)}) collective-permute-start(bf16[128,1024]{1,0:T(8,128)(2,1)S(1)} %stack.1.refs_0_), channel_id=1, source_target_pairs={{0,1},{1,0},{2,3},{3,2},{4,5},{5,4},{6,7},{7,6},{8,9},{9,8},{10,11... | collective-permute-start | bytes 786440 | tf_op jit(solution)/shard_map/ppermute | solution.py:169
  15.7 0.0 collective-permute-start.6
  15.7 3.8 %all-to-all-start = ((bf16[8,8,1024]{2,1,0:T(8,128)(2,1)}), bf16[8,8,1024]{2,1,0:T(8,128)(2,1)S(1)}, u32[]{:S(2)}, u32[]{:S(2)}) async-start(bf16[8,8,1024]{2,1,0:T(8,128)(2,1)} %route.1.refs_4_), calls=%async_computation | async-start | bytes 262144 | tf_op jit(solution)/shard_map/all_to_all | solution.py:225
  19.4 2.6 %collective-permute-done.7.refs_2_ = bf16[128,1024]{1,0:T(8,128)(2,1)S(1)} collective-permute-done((bf16[128,1024]{1,0:T(8,128)(2,1)S(1)}, bf16[128,1024]{1,0:T(8,128)(2,1)S(1)}, u32[]{:S(2)}, u32[]{:S(2)}) %collective-permute-start.7) | collective-permute-done | bytes 262176 | tf_op jit(solution)/shard_map/ppermute | solution.py:169
  22.1 0.0 collective-permute-start.8
  22.1 0.0 collective-permute-done.6.refs_1_
  22.1 0.0 copy-done
  22.1 1.2 %gather.1 = (bf16[512,1024]{1,0:T(8,128)(2,1)S(1)}, bf16[128,4096]{1,0:T(8,128)(2,1)S(1)}) custom-call(bf16[128,4096]{1,0:T(8,128)(2,1)} %q_hbm.1, bf16[128,2,512]{2,1,0:T(2,128)(2,1)S(1)} %copy-done, bf16[128,1024]{1,0:T(8,128)(2,1)S(1)} %stack.1.refs_0_, bf16[128,1024]{1,0:T(8,128)(2,1)S(1)} %collective-permute-done.6.refs_1_, ...), custom_call_target="tpu_custom_call" | custom-call | flops 10000000000 | bytes 4194304 | tf_op jit(solution)/shard_map/gather/pallas_call | solution.py:229
  23.3 3.8 %all-to-all-done = bf16[8,8,1024]{2,1,0:T(8,128)(2,1)S(1)} async-done(((bf16[8,8,1024]{2,1,0:T(8,128)(2,1)}), bf16[8,8,1024]{2,1,0:T(8,128)(2,1)S(1)}, u32[]{:S(2)}, u32[]{:S(2)}) %all-to-all-start) | async-done | bytes 131104 | tf_op jit(solution)/shard_map/all_to_all | solution.py:225
  27.1 0.0 collective-permute-done.8.refs_0_
  27.1 4.8 %attend.1 = bf16[128,4096]{1,0:T(8,128)(2,1)} custom-call(s32[8,64]{1,0:T(8,128)S(1)} %get-tuple-element.14.limit_ref, bf16[128,4096]{1,0:T(8,128)(2,1)S(1)} %get-tuple-element.21.q_ref, bf16[512,1024]{1,0:T(8,128)(2,1)S(1)} %get-tuple-element.22.kv_ref, bf16[128,1024]{1,0:T(8,128)(2,1)S(1)} %collective-permute-done.8.refs_0_, bf16[64,1024]{1,0:T(8,128)(2,1)S(1)} %bitcast.1), custom_call_target="tpu_custom_call" | custom-call | tf_op jit(solution)/shard_map/attend/pallas_call | solution.py:239
  (1 shorter events, 0.0 us)
Async XLA Ops:
  1.1 7.0 %collective-permute-start.3 = (bf16[4,8,1024]{2,1,0:T(8,128)(2,1)S(1)}, bf16[4,8,1024]{2,1,0:T(8,128)(2,1)S(1)}, u32[]{:S(2)}, u32[]{:S(2)}) collective-permute-start(bf16[4,8,1024]{2,1,0:T(8,128)(2,1)S(1)} %get-tuple-element.18), channel_id=1, source_target_pairs={{0,8},{8,0},{16,24},{24,16},{1,9},{9,1},{17,25},{25,17},{2,10},{10... | collective-permute-start | bytes 196616 | tf_op jit(solution)/shard_map/ppermute | solution.py:169
  1.6 7.1 %collective-permute-start.4 = (bf16[4,8,1024]{2,1,0:T(8,128)(2,1)S(1)}, bf16[4,8,1024]{2,1,0:T(8,128)(2,1)S(1)}, u32[]{:S(2)}, u32[]{:S(2)}) collective-permute-start(bf16[4,8,1024]{2,1,0:T(8,128)(2,1)S(1)} %get-tuple-element.19), channel_id=1, source_target_pairs={{0,16},{8,24},{16,0},{24,8},{1,17},{9,25},{17,1},{25,9},{2,18},{10... | collective-permute-start | bytes 196616 | tf_op jit(solution)/shard_map/ppermute | solution.py:169
  4.2 4.5 %collective-permute-start.5 = (bf16[4,8,1024]{2,1,0:T(8,128)(2,1)S(1)}, bf16[4,8,1024]{2,1,0:T(8,128)(2,1)S(1)}, u32[]{:S(2)}, u32[]{:S(2)}) collective-permute-start(bf16[4,8,1024]{2,1,0:T(8,128)(2,1)S(1)} %get-tuple-element.20), channel_id=1, source_target_pairs={{0,24},{8,16},{16,8},{24,0},{1,25},{9,17},{17,9},{25,1},{2,26},{10... | collective-permute-start | bytes 196616 | tf_op jit(solution)/shard_map/ppermute | solution.py:169
  4.3 6.6 %collective-permute-start.2 = (bf16[32,1024]{1,0:T(8,128)(2,1)S(1)}, bf16[32,1024]{1,0:T(8,128)(2,1)S(1)}, u32[]{:S(2)}, u32[]{:S(2)}) collective-permute-start(bf16[32,1024]{1,0:T(8,128)(2,1)S(1)} %get-tuple-element.15.refs_0_), channel_id=1, source_target_pairs={{0,6},{1,7},{2,4},{3,5},{4,2},{5,3},{6,0},{7,1},{8,14},{9,15},{10,... | collective-permute-start | bytes 196616 | tf_op jit(solution)/shard_map/ppermute | solution.py:169
  8.1 6.0 %collective-permute-start.1 = (bf16[32,1024]{1,0:T(8,128)(2,1)S(1)}, bf16[32,1024]{1,0:T(8,128)(2,1)S(1)}, u32[]{:S(2)}, u32[]{:S(2)}) collective-permute-start(bf16[32,1024]{1,0:T(8,128)(2,1)S(1)} %get-tuple-element.15.refs_0_), channel_id=1, source_target_pairs={{0,4},{1,5},{2,6},{3,7},{4,0},{5,1},{6,2},{7,3},{8,12},{9,13},{10,... | collective-permute-start | bytes 196616 | tf_op jit(solution)/shard_map/ppermute | solution.py:169
  8.1 6.0 %collective-permute-start = (bf16[32,1024]{1,0:T(8,128)(2,1)S(1)}, bf16[32,1024]{1,0:T(8,128)(2,1)S(1)}, u32[]{:S(2)}, u32[]{:S(2)}) collective-permute-start(bf16[32,1024]{1,0:T(8,128)(2,1)S(1)} %get-tuple-element.15.refs_0_), channel_id=1, source_target_pairs={{0,2},{1,3},{2,0},{3,1},{4,6},{5,7},{6,4},{7,5},{8,10},{9,11},{10,... | collective-permute-start | bytes 196616 | tf_op jit(solution)/shard_map/ppermute | solution.py:169
  9.4 12.7 %copy-start = (bf16[128,2,512]{2,1,0:T(2,128)(2,1)S(1)}, bf16[128,2,512]{2,1,0:T(2,128)(2,1)}, u32[]{:S(2)}) copy-start(bf16[128,2,512]{2,1,0:T(2,128)(2,1)} %new_ref.1) | copy-start | bytes 786436
  14.1 8.0 %collective-permute-start.7 = (bf16[128,1024]{1,0:T(8,128)(2,1)S(1)}, bf16[128,1024]{1,0:T(8,128)(2,1)S(1)}, u32[]{:S(2)}, u32[]{:S(2)}) collective-permute-start(bf16[128,1024]{1,0:T(8,128)(2,1)S(1)} %stack.1.refs_0_), channel_id=1, source_target_pairs={{0,1},{1,0},{2,3},{3,2},{4,5},{5,4},{6,7},{7,6},{8,9},{9,8},{10,11... | collective-permute-start | bytes 786440 | tf_op jit(solution)/shard_map/ppermute | solution.py:169
  15.7 6.4 %collective-permute-start.6 = (bf16[128,1024]{1,0:T(8,128)(2,1)S(1)}, bf16[128,1024]{1,0:T(8,128)(2,1)S(1)}, u32[]{:S(2)}, u32[]{:S(2)}) collective-permute-start(bf16[128,1024]{1,0:T(8,128)(2,1)S(1)} %stack.1.refs_0_), channel_id=1, source_target_pairs={{0,8},{8,0},{16,24},{24,16},{1,9},{9,1},{17,25},{25,17},{2,10},{10... | collective-permute-start | bytes 786440 | tf_op jit(solution)/shard_map/ppermute | solution.py:169
  15.7 11.4 %all-to-all-start = ((bf16[8,8,1024]{2,1,0:T(8,128)(2,1)}), bf16[8,8,1024]{2,1,0:T(8,128)(2,1)S(1)}, u32[]{:S(2)}, u32[]{:S(2)}) async-start(bf16[8,8,1024]{2,1,0:T(8,128)(2,1)} %route.1.refs_4_), calls=%async_computation | async-start | bytes 262144 | tf_op jit(solution)/shard_map/all_to_all | solution.py:225
  22.1 5.0 %collective-permute-start.8 = (bf16[128,1024]{1,0:T(8,128)(2,1)S(1)}, bf16[128,1024]{1,0:T(8,128)(2,1)S(1)}, u32[]{:S(2)}, u32[]{:S(2)}) collective-permute-start(bf16[128,1024]{1,0:T(8,128)(2,1)S(1)} %collective-permute-done.7.refs_2_), channel_id=1, source_target_pairs={{0,8},{8,0},{16,24},{24,16},{1,9},{9,1},{17,25},{25,17},{2,10},{10... | collective-permute-start | bytes 786440 | tf_op jit(solution)/shard_map/ppermute | solution.py:169
